TPU v7x, 32 devices: a whole 2x2x4 slice. The times are simulated.
32 devices in a mesh: rows: 16 (over z, x, core), cols: 2 (over y).
Axes of the slice: x: 2, y: 2, z: 4, core: 2. Of those that a mesh axis runs over, the one named last changes fastest.
Arguments:
- features: bfloat16 [49152, 256], P(('rows', 'cols')), may hold values from -6 to 6
- adj_values: bfloat16 [384, 3, 128, 128], P(('rows', 'cols')), may hold values from -0.3125 to 0.3125
- adj_offset: int32 [384, 3], P(('rows', 'cols')), may hold values from -2 to 2, as said below
- adj_count: int32 [384], P(('rows', 'cols')), may hold values from 1 to 3, as said below
- weight: bfloat16 [256, 256], replicated, may hold values from -0.375 to 0.375
- bias_vector: float32 [256], replicated, may hold values from -4 to 4
- cotangent: bfloat16 [49152, 256], P(('rows', 'cols')), may hold values from -6 to 6
Outputs:
- activated: bfloat16 [49152, 256], P(('rows', 'cols'))
- grad_features: bfloat16 [49152, 256], P(('rows', 'cols'))
- grad_weight: float32 [256, 256], replicated
- grad_bias: float32 [256], replicated
Inputs may be any that keep to these rules, and one draw needn't show every extreme that they name: Slot 0 of every row block has offset 0; the offsets of one row block are distinct, and for row block i every i + adj_offset[i, s] lies in 0 to 383. Row block i uses its slots 0 to adj_count[i] - 1; the values and offsets of its other slots are ignored. In every draw all row blocks of one device, drawn from the seed, use all 3 slots.
All inputs are finite; a program needn't handle non-finite values.
Results may differ from a plain program's by a relative error of at most 0.0075.
Values may be sent and summed in bfloat16 or wider, within the bound.
No kernel may reach another device: no remote copies, remote signals or barrier semaphores. Data moves between devices by JAX's collectives and lax.ppermute only.
A program may use at most 64 MiB of HBM per device.

v0:
```python
import math

import jax
import jax.numpy as jnp
from jax import lax
from jax.sharding import PartitionSpec as P

BAND = 2


def shifted(value, axis, steps):
    count = lax.axis_size(axis)
    pairs = [(source, (source + steps) % count) for source in range(count)]
    return lax.ppermute(value, axis, pairs)


def from_behind(value, axis, steps):
    count = lax.axis_size(axis)
    initial, last = (max(0, -steps), min(count, count - steps))
    return lax.ppermute(value, axis, [(source, source + steps) for source in range(initial, last)])


def fetch_lower(rim_piece):
    narrow_step = shifted(rim_piece, "cols", 1)
    wide_step = from_behind(narrow_step, "rows", 1)
    return jnp.where(lax.axis_index("cols") == 0, wide_step, narrow_step)


def fetch_upper(rim_piece):
    narrow_step = shifted(rim_piece, "cols", -1)
    wide_step = from_behind(narrow_step, "rows", -1)
    return jnp.where(lax.axis_index("cols") == lax.axis_size("cols") - 1, wide_step, narrow_step)


def spill_lower(rim_piece):
    narrow_step = shifted(rim_piece, "cols", 1)
    wide_step = from_behind(narrow_step, "rows", 1)
    return jnp.where(lax.axis_index("cols") == 0, wide_step, narrow_step)


def spill_upper(rim_piece):
    narrow_step = shifted(rim_piece, "cols", -1)
    wide_step = from_behind(narrow_step, "rows", -1)
    return jnp.where(lax.axis_index("cols") == lax.axis_size("cols") - 1, wide_step, narrow_step)


def on_device(features, adj_values, adj_offset, adj_count, weight, bias_vector, cotangent):
    blocks = adj_offset.shape[0]
    slot_total = adj_offset.shape[1]
    block_rows = adj_values.shape[2]
    feat_width = features.shape[1]
    band_reach = BAND
    span_blocks = blocks + 2 * band_reach
    rim_rows = band_reach * block_rows
    slot_index = lax.broadcasted_iota(jnp.int32, (blocks, slot_total), 1)
    block_index = lax.broadcasted_iota(jnp.int32, (blocks, slot_total), 0)
    active = slot_index < adj_count[:, None]
    target = block_index + band_reach + adj_offset
    from_below = fetch_lower(features[features.shape[0] - rim_rows :])
    from_above = fetch_upper(features[:rim_rows])
    extended = jnp.concatenate([from_below, features, from_above], 0)
    window = extended.reshape(span_blocks, block_rows, feat_width)
    picked = window[target]
    picked = jnp.where(active[:, :, None, None], picked, jnp.zeros_like(picked))
    summed = jnp.einsum("bsac,bscf->baf", adj_values, picked, preferred_element_type=jnp.float32)
    aggregated = summed.reshape(-1, feat_width).astype(jnp.bfloat16)
    preact = jnp.dot(aggregated, weight, preferred_element_type=jnp.float32) + bias_vector
    activated = jax.nn.silu(preact).astype(jnp.bfloat16)
    sigmoid_pre = jax.nn.sigmoid(preact)
    grad_pre = (
        cotangent.astype(jnp.float32) * sigmoid_pre * (1.0 + preact * (1.0 - sigmoid_pre))
    ).astype(jnp.bfloat16)
    partial_weight = lax.dot_general(
        aggregated, grad_pre, (((0,), (0,)), ((), ())), preferred_element_type=jnp.float32
    )
    partial_bias = jnp.sum(grad_pre.astype(jnp.float32), axis=0)
    total_weight, total_bias = lax.psum((partial_weight, partial_bias), ("rows", "cols"))
    nodes_total = features.shape[0] * lax.axis_size("rows") * lax.axis_size("cols")
    norm_scale = 1.0 / math.sqrt(nodes_total)
    grad_weight = total_weight * norm_scale
    grad_bias = total_bias * norm_scale
    upstream = lax.dot_general(
        grad_pre, weight, (((1,), (1,)), ((), ())), preferred_element_type=jnp.float32
    ).astype(jnp.bfloat16)
    slot_terms = jnp.einsum(
        "bsac,baf->bscf",
        adj_values,
        upstream.reshape(blocks, block_rows, feat_width),
        preferred_element_type=jnp.float32,
    )
    slot_terms = jnp.where(active[:, :, None, None], slot_terms, jnp.zeros_like(slot_terms))
    empty = jnp.zeros((span_blocks, block_rows, feat_width), jnp.float32)
    spread = empty.at[target.reshape(-1)].add(slot_terms.reshape(-1, block_rows, feat_width))
    lower_part = spread[:band_reach]
    middle = spread[band_reach : band_reach + blocks]
    upper_part = spread[band_reach + blocks :]
    from_above_dev = spill_upper(lower_part)
    from_below_dev = spill_lower(upper_part)
    combined = middle.at[:band_reach].add(from_below_dev)
    combined = combined.at[blocks - band_reach :].add(from_above_dev)
    grad_features = combined.reshape(-1, feat_width).astype(jnp.bfloat16)
    return (activated, grad_features, grad_weight, grad_bias)


def solution(mesh):
    return jax.shard_map(
        on_device,
        mesh=mesh,
        in_specs=(
            P(("rows", "cols"), None),
            P(("rows", "cols"), None, None, None),
            P(("rows", "cols"), None),
            P(("rows", "cols")),
            P(),
            P(),
            P(("rows", "cols"), None),
        ),
        out_specs=(P(("rows", "cols"), None), P(("rows", "cols"), None), P(), P()),
        check_vma=False,
    )
```

profile of v0, /device:TPU:0, one launch (start us, length us, event | category | flops | bytes accessed | tf_op | source)
XLA Modules:
  0.0 197.7 jit_solution(1919197538032877157)
XLA Ops:
  7.2 1.1 fusion.11
  8.4 3.0 %collective-permute-start = (bf16[256,256]{1,0:T(8,128)(2,1)S(1)}, bf16[256,256]{1,0:T(8,128)(2,1)S(1)}, u32[]{:S(2)}, u32[]{:S(2)}) collective-permute-start(bf16[256,256]{1,0:T(8,128)(2,1)S(1)} %get-tuple-element.35), channel_id=1, source_target_pairs={{0,1},{1,0},{2,3},{3,2},{4,5},{5,4},{6,7},{7,6},{8,9},{9,8},{10,11... | collective-permute-start | bytes 393224 | tf_op jit(solution)/shard_map/ppermute | solution.py:14
  11.5 0.7 compare_select_fusion
  12.3 0.7 iota_compare_fusion
  13.1 2.6 %collective-permute-done = bf16[256,256]{1,0:T(8,128)(2,1)S(1)} collective-permute-done((bf16[256,256]{1,0:T(8,128)(2,1)S(1)}, bf16[256,256]{1,0:T(8,128)(2,1)S(1)}, u32[]{:S(2)}, u32[]{:S(2)}) %collective-permute-start) | collective-permute-done | bytes 131104 | tf_op jit(solution)/shard_map/ppermute | solution.py:14
  15.7 1.3 collective-permute-start.1
  17.2 0.5 collective-permute-done.2
  17.7 1.3 collective-permute-start.3
  19.0 3.7 %collective-permute-done.3 = bf16[256,256]{1,0:T(8,128)(2,1)S(1)} collective-permute-done((bf16[256,256]{1,0:T(8,128)(2,1)S(1)}, bf16[256,256]{1,0:T(8,128)(2,1)S(1)}, u32[]{:S(2)}, u32[]{:S(2)}) %collective-permute-start.3) | collective-permute-done | bytes 131104 | tf_op jit(solution)/shard_map/ppermute | solution.py:20
  22.8 2.3 %gather_fusion = bf16[36,128,256]{2,1,0:T(8,128)(2,1)} fusion(bf16[16,128,256]{2,1,0:T(8,128)(2,1)S(1)} %bitcast.29, s32[1024]{0:T(1024)S(1)} %pad_clamp_fusion), kind=kCustom, calls=%fused_computation | custom fusion | bytes 4718736 | tf_op jit(solution)/shard_map/gather | solution.py:63
  25.1 2.4 %bitcast_convert_fusion = bf16[12,256,128]{1,2,0:T(8,128)(2,1)S(1)} fusion(bf16[12,3,128,128]{3,2,1,0:T(8,128)(2,1)S(1)} %copy-done, bf16[12,3,128,256]{3,2,1,0:T(8,128)(2,1)} %bitcast.31, pred[12,3]{1,0:T(8,128)(4,1)S(1)} %iota_compare_fusion), kind=kOutput, calls=%fused_computation.8 | convolution fusion | flops 303562752 | bytes 4325412 | tf_op jit(solution)/shard_map/bsac,bscf->baf/dot_general | solution.py:65
  27.6 1.8 convert_reduce_fusion
  29.4 0.9 copy-done.2
  30.3 0.4 convolution_convert_fusion
  30.7 3.1 %broadcast_select_fusion = f32[12,256,3,128]{3,1,2,0:T(8,128)} fusion(pred[12,3]{1,0:T(8,128)(4,1)S(1)} %iota_compare_fusion, bf16[12,128,256,1]{2,1,3,0:T(8,128)(2,1)S(1)} %bitcast.30, bf16[12,3,128,128]{3,2,1,0:T(8,128)(2,1)S(1)} %copy-done), kind=kOutput, calls=%fused_computation.4 | convolution fusion | flops 303169536 | bytes 6684708 | tf_op jit(solution)/shard_map/bsac,baf->bscf/dot_general | solution.py:85
  33.8 6.1 %copy.17 = f32[36,128,256]{2,1,0:T(8,128)} copy(f32[36,128,256]{1,2,0:T(8,128)} %bitcast.28) | data formatting | bytes 9437184 | tf_op jit(solution)/shard_map/reshape | solution.py:93
  39.9 0.2 broadcast_in_dim.36
  40.1 8.9 %scatter_fusion = f32[16,128,256]{2,1,0:T(8,128)S(1)} fusion(f32[16,128,256]{2,1,0:T(8,128)S(1)} %broadcast_in_dim.36, s32[36]{0:T(128)S(1)} %fusion.8, f32[36,128,256]{2,1,0:T(8,128)} %copy.17), kind=kCustom, calls=%fused_computation.1 | custom fusion | flops 1179648 | bytes 14155920 | tf_op jit(solution)/shard_map/scatter-add | solution.py:93
  49.0 0.8 fusion.10
  49.8 1.5 collective-permute-start.4
  51.4 0.5 collective-permute-start.6
  51.9 2.5 %fusion.12 = f32[256,256]{1,0:T(8,128)} fusion(bf16[1536,256]{1,0:T(8,128)(2,1)} %bitcast.34, bf16[1536,256]{1,0:T(8,128)(2,1)} %copy-done.2), kind=kOutput, calls=%fused_computation.33 | convolution fusion | flops 201326592 | bytes 1835008 | tf_op jit(solution)/shard_map/dot_general | solution.py:73
  54.4 47.8 %psum.15 = f32[256]{0:T(256)S(1)} all-reduce(f32[256]{0:T(256)S(1)} %get-tuple-element.28), channel_id=1, replica_groups=mesh['rows'=16,'cols'=2] {'rows','cols'}, use_global_device_ids=true, to_apply=%region_3.4 | all-reduce | flops 256 | bytes 2048 | tf_op jit(solution)/shard_map/psum | solution.py:77
  102.2 2.4 %collective-permute-start.5 = (f32[2,128,256]{2,1,0:T(8,128)}, f32[2,128,256]{2,1,0:T(8,128)}, u32[]{:S(2)}, u32[]{:S(2)}) collective-permute-start(f32[2,128,256]{2,1,0:T(8,128)} %collective-permute-done.4), channel_id=1, source_target_pairs={{0,2},{2,4},{4,6},{6,8},{8,10},{10,12},{12,14},{14,16},{16,18},{18... | collective-permute-start | bytes 786440 | tf_op jit(solution)/shard_map/ppermute | solution.py:20
  104.6 0.6 broadcast_multiply_fusion.1
  105.1 1.3 slice.73
  106.5 1.3 collective-permute-start.7
  107.8 75.6 %all-reduce.2.cloned.1.call-done = f32[256,256]{1,0:T(8,128)} async-done(((f32[256,256]{1,0:T(8,128)}), f32[256,256]{1,0:T(8,128)}) %all-reduce.2.cloned.1.call-update) | async-done | bytes 262160 | tf_op jit(solution)/shard_map/psum | solution.py:77
  183.4 1.7 broadcast_multiply_fusion
  185.1 1.7 fusion.7
  186.8 1.7 fusion.6
  188.5 2.4 %convert_element_type.37 = bf16[12,128,256]{2,1,0:T(8,128)(2,1)} convert(f32[12,128,256]{2,1,0:T(8,128)} %fusion.6) | non-fusion elementwise | flops 393216 | bytes 2359296 | tf_op jit(solution)/shard_map/convert_element_type | solution.py:101
  (31 shorter events, 0.7 us)
Async XLA Ops:
  7.2 18.0 %copy-start = (bf16[12,3,128,128]{3,2,1,0:T(8,128)(2,1)S(1)}, bf16[12,3,128,128]{3,2,1,0:T(8,128)(2,1)}, u32[]{:S(2)}) copy-start(bf16[12,3,128,128]{3,2,1,0:T(8,128)(2,1)} %param.12) | copy-start | bytes 3538948
  7.2 15.6 %copy-start.1 = (bf16[1536,256]{1,0:T(8,128)(2,1)S(1)}, bf16[1536,256]{1,0:T(8,128)(2,1)}, u32[]{:S(2)}) copy-start(bf16[1536,256]{1,0:T(8,128)(2,1)} %param.11) | copy-start | bytes 2359300
  7.2 176.2 %all-reduce.2.cloned.1.call-start = ((), (), s32[]{:S(2)}) async-start(), calls=%async_computation | async-start | bytes 524288 | tf_op jit(solution)/shard_map/psum | solution.py:77
  8.4 7.4 %collective-permute-start = (bf16[256,256]{1,0:T(8,128)(2,1)S(1)}, bf16[256,256]{1,0:T(8,128)(2,1)S(1)}, u32[]{:S(2)}, u32[]{:S(2)}) collective-permute-start(bf16[256,256]{1,0:T(8,128)(2,1)S(1)} %get-tuple-element.35), channel_id=1, source_target_pairs={{0,1},{1,0},{2,3},{3,2},{4,5},{5,4},{6,7},{7,6},{8,9},{9,8},{10,11... | collective-permute-start | bytes 393224 | tf_op jit(solution)/shard_map/ppermute | solution.py:14
  11.4 6.3 %collective-permute-start.2 = (bf16[256,256]{1,0:T(8,128)(2,1)S(1)}, bf16[256,256]{1,0:T(8,128)(2,1)S(1)}, u32[]{:S(2)}, u32[]{:S(2)}) collective-permute-start(bf16[256,256]{1,0:T(8,128)(2,1)S(1)} %get-tuple-element.36), channel_id=1, source_target_pairs={{0,1},{1,0},{2,3},{3,2},{4,5},{5,4},{6,7},{7,6},{8,9},{9,8},{10,11... | collective-permute-start | bytes 393224 | tf_op jit(solution)/shard_map/ppermute | solution.py:14
  15.7 3.3 %collective-permute-start.1 = (bf16[256,256]{1,0:T(8,128)(2,1)S(1)}, bf16[256,256]{1,0:T(8,128)(2,1)S(1)}, u32[]{:S(2)}, u32[]{:S(2)}) collective-permute-start(bf16[256,256]{1,0:T(8,128)(2,1)S(1)} %collective-permute-done), channel_id=1, source_target_pairs={{0,2},{2,4},{4,6},{6,8},{8,10},{10,12},{12,14},{14,16},{16,18},{18... | collective-permute-start | bytes 393224 | tf_op jit(solution)/shard_map/ppermute | solution.py:20
  17.7 5.0 %collective-permute-start.3 = (bf16[256,256]{1,0:T(8,128)(2,1)S(1)}, bf16[256,256]{1,0:T(8,128)(2,1)S(1)}, u32[]{:S(2)}, u32[]{:S(2)}) collective-permute-start(bf16[256,256]{1,0:T(8,128)(2,1)S(1)} %collective-permute-done.2), channel_id=1, source_target_pairs={{2,0},{4,2},{6,4},{8,6},{10,8},{12,10},{14,12},{16,14},{18,16},{20... | collective-permute-start | bytes 393224 | tf_op jit(solution)/shard_map/ppermute | solution.py:20
  25.1 2.4 %copy-start.3 = (bf16[256,256]{1,0:T(8,128)(2,1)S(1)}, bf16[256,256]{1,0:T(8,128)(2,1)}, u32[]{:S(2)}) copy-start(bf16[256,256]{1,0:T(8,128)(2,1)} %param.15) | copy-start | bytes 393220
  25.1 2.4 %copy-start.4 = (bf16[1536,256]{1,0:T(8,128)(2,1)S(1)}, bf16[1536,256]{1,0:T(8,128)(2,1)}, u32[]{:S(2)}) copy-start(bf16[1536,256]{1,0:T(8,128)(2,1)} %param.17) | copy-start | bytes 2359300
  25.1 2.5 %copy-start.5 = (f32[256]{0:T(256)S(1)}, f32[256]{0:T(256)}, u32[]{:S(2)}) copy-start(f32[256]{0:T(256)} %param.16) | copy-start | bytes 3076
  27.5 1.9 copy-start.6
  29.4 0.9 copy-start.2
  49.8 52.3 %collective-permute-start.4 = (f32[2,128,256]{2,1,0:T(8,128)}, f32[2,128,256]{2,1,0:T(8,128)}, u32[]{:S(2)}, u32[]{:S(2)}) collective-permute-start(f32[2,128,256]{2,1,0:T(8,128)} %get-tuple-element.33), channel_id=1, source_target_pairs={{0,1},{1,0},{2,3},{3,2},{4,5},{5,4},{6,7},{7,6},{8,9},{9,8},{10,11... | collective-permute-start | bytes 786440 | tf_op jit(solution)/shard_map/ppermute | solution.py:14
  51.4 55.1 %collective-permute-start.6 = (f32[2,128,256]{2,1,0:T(8,128)}, f32[2,128,256]{2,1,0:T(8,128)S(1)}, u32[]{:S(2)}, u32[]{:S(2)}) collective-permute-start(f32[2,128,256]{2,1,0:T(8,128)} %get-tuple-element.32), channel_id=1, source_target_pairs={{0,1},{1,0},{2,3},{3,2},{4,5},{5,4},{6,7},{7,6},{8,9},{9,8},{10,11... | collective-permute-start | bytes 786440 | tf_op jit(solution)/shard_map/ppermute | solution.py:14
  102.2 82.9 %collective-permute-start.5 = (f32[2,128,256]{2,1,0:T(8,128)}, f32[2,128,256]{2,1,0:T(8,128)}, u32[]{:S(2)}, u32[]{:S(2)}) collective-permute-start(f32[2,128,256]{2,1,0:T(8,128)} %collective-permute-done.4), channel_id=1, source_target_pairs={{0,2},{2,4},{4,6},{6,8},{8,10},{10,12},{12,14},{14,16},{16,18},{18... | collective-permute-start | bytes 786440 | tf_op jit(solution)/shard_map/ppermute | solution.py:20
  106.5 80.3 %collective-permute-start.7 = (f32[2,128,256]{2,1,0:T(8,128)S(1)}, f32[2,128,256]{2,1,0:T(8,128)}, u32[]{:S(2)}, u32[]{:S(2)}) collective-permute-start(f32[2,128,256]{2,1,0:T(8,128)S(1)} %collective-permute-done.6), channel_id=1, source_target_pairs={{2,0},{4,2},{6,4},{8,6},{10,8},{12,10},{14,12},{16,14},{18,16},{20... | collective-permute-start | bytes 786440 | tf_op jit(solution)/shard_map/ppermute | solution.py:20
Sparse Core Ops, SparseCore 0:
  54.5 128.8 all-reduce.1
where the time goes:
time: 198 us
  waiting for transfers between devices  82.5 us (42%)
  blocking collectives  47.8 us (24%)
  other arithmetic  18.4 us (9%)
  between operations  14.2 us (7%)
  local copies, waits for them, and re-layouts  13.2 us (7%)
  starting transfers between devices  11.4 us (6%)
  matrix products  10.2 us (5%)
    psum x1, waiting for transfers between devices, on_device(): lax.psum((partial_weight, partial_bias), ('rows', 'cols'))  75.6 us
    psum x1, blocking collectives, on_device(): lax.psum((partial_weight, partial_bias), ('rows', 'cols'))  47.8 us
    scatter-add x1, other arithmetic, on_device(): empty.at[target.reshape(-1)]  8.85 us
    ppermute x4, starting transfers between devices, from_behind(): lax.ppermute(value, axis, [(source, source + steps) for source in range(i...  6.27 us
    reshape x1, local copies, waits for them, and re-layouts, on_device(): slot_terms.reshape(-1, block_rows, feat_width)  6.15 us
    ppermute x4, starting transfers between devices, shifted(): return lax.ppermute(value, axis, pairs)  5.14 us
  transfers between devices with their start and end apart: 9, of which 4 were waited for; matrix products, arithmetic and copies ran while one was open for 5% of the time, Pallas kernels for 0%

commit v1 on v0

v1 whole, which is shorter than its diff:
```python
import math

import jax
import jax.numpy as jnp
from jax import lax
from jax.experimental import pallas as pl
from jax.experimental.pallas import tpu as pltpu
from jax.sharding import PartitionSpec as P

BAND = 2
AXES = ("rows", "cols")
LANES = 128


def targets(off_ref, cnt_ref, block, slots, blocks):
    dump = blocks + 2 * BAND
    return [
        jnp.where(slot < cnt_ref[block], block + BAND + off_ref[block, slot], dump)
        for slot in range(slots)
    ]


def forward_kernel(
    off_ref, cnt_ref, feat_ref, lower_ref, upper_ref, adj_ref, weight_ref, bias_ref, cot_ref,
    act_ref, upstream_ref, partial_ref,
    window, agg_all, grad_all,
):
    blocks, slots, block_rows, _ = adj_ref.shape
    width = feat_ref.shape[1]
    rim = BAND * block_rows
    rows = blocks * block_rows
    window[:rim] = lower_ref[...]
    window[rim : rim + rows] = feat_ref[...]
    window[rim + rows : 2 * rim + rows] = upper_ref[...]
    window[2 * rim + rows :] = jnp.zeros((block_rows, width), jnp.bfloat16)
    weight = weight_ref[...]
    bias = bias_ref[...]
    bias_sum = jnp.zeros((8, width), jnp.float32)
    for block in range(blocks):
        here = pl.ds(block * block_rows, block_rows)
        picked = jnp.concatenate(
            [
                window[pl.ds(pl.multiple_of(target * block_rows, block_rows), block_rows)]
                for target in targets(off_ref, cnt_ref, block, slots, blocks)
            ],
            0,
        )
        row = jnp.concatenate([adj_ref[block, slot] for slot in range(slots)], 1)
        agg = jnp.dot(row, picked, preferred_element_type=jnp.float32).astype(jnp.bfloat16)
        agg_all[here] = agg
        preact = jnp.dot(agg, weight, preferred_element_type=jnp.float32) + bias
        gate = 1.0 / (1.0 + jnp.exp(-preact))
        act_ref[here] = (preact * gate).astype(jnp.bfloat16)
        grad = cot_ref[here].astype(jnp.float32) * gate * (1.0 + preact * (1.0 - gate))
        grad = grad.astype(jnp.bfloat16)
        grad_all[here] = grad
        bias_sum = bias_sum + jnp.sum(
            grad.astype(jnp.float32).reshape(block_rows // 8, 8, width), axis=0
        )
        upstream_ref[block] = lax.dot_general(
            weight, grad, (((1,), (1,)), ((), ())), preferred_element_type=jnp.float32
        ).astype(jnp.bfloat16)
    partial = lax.dot_general(
        agg_all[...], grad_all[...], (((0,), (0,)), ((), ())), preferred_element_type=jnp.float32
    )
    partial_ref[:, :width] = partial.astype(jnp.bfloat16)
    bias_row = jnp.sum(bias_sum, axis=0, keepdims=True)
    partial_ref[:, width:] = jnp.broadcast_to(bias_row, (LANES, width)).T.astype(jnp.bfloat16)


def backward_kernel(
    off_ref, cnt_ref, adj_ref, upstream_ref, grad_ref, edge_ref, lower_ref, upper_ref, spread
):
    blocks, slots, block_rows, _ = adj_ref.shape
    spread[...] = jnp.zeros_like(spread)
    for block in range(blocks):
        row = jnp.concatenate([adj_ref[block, slot] for slot in range(slots)], 1)
        terms = jnp.dot(upstream_ref[block], row, preferred_element_type=jnp.float32)
        for slot, target in enumerate(targets(off_ref, cnt_ref, block, slots, blocks)):
            spread[target] += terms[:, slot * block_rows : (slot + 1) * block_rows]
    for block in range(BAND):
        here = pl.ds(block * block_rows, block_rows)
        lower_ref[here] = spread[block].T.astype(jnp.bfloat16)
        upper_ref[here] = spread[BAND + blocks + block].T.astype(jnp.bfloat16)
    for block in range(blocks):
        value = spread[BAND + block].T
        if block < BAND:
            edge_ref[block * block_rows : (block + 1) * block_rows] = value
        elif block >= blocks - BAND:
            place = block - blocks + 2 * BAND
            edge_ref[place * block_rows : (place + 1) * block_rows] = value
        else:
            grad_ref[block * block_rows : (block + 1) * block_rows] = value.astype(jnp.bfloat16)


def edge_kernel(whole_ref, edge_ref, spill_ref, out_ref):
    out_ref[...] = (edge_ref[...] + spill_ref[...].astype(jnp.float32)).astype(jnp.bfloat16)


def reduce_kernel(gathered_ref, spread_ref):
    count = gathered_ref.shape[0]
    total = jnp.sum(gathered_ref[...].astype(jnp.float32), axis=0).astype(jnp.bfloat16)
    spread_ref[...] = jnp.broadcast_to(total[None], (count,) + total.shape)


def neighbour(value, steps, count):
    initial, last = max(0, -steps), min(count, count - steps)
    return lax.ppermute(value, AXES, [(source, source + steps) for source in range(initial, last)])


def sum_devices(partial, count):
    rows, lanes = partial.shape
    axes = AXES
    if rows % count:
        axes = "rows"
        count = lax.axis_size("rows")
    gathered = lax.all_to_all(partial, axes, 0, 0, tiled=True).reshape(count, rows // count, lanes)
    if axes == "rows":
        share = jnp.sum(gathered.astype(jnp.float32), axis=0)
        share = lax.psum(share, "cols").astype(jnp.bfloat16)
        shares = jnp.broadcast_to(share[None], gathered.shape)
    else:
        shares = pl.pallas_call(
            reduce_kernel,
            out_shape=jax.ShapeDtypeStruct(gathered.shape, jnp.bfloat16),
            name="reduce_share",
        )(gathered)
    return lax.all_to_all(shares.reshape(rows, lanes), axes, 0, 0, tiled=True)


def on_device(features, adj_values, adj_offset, adj_count, weight, bias_vector, cotangent):
    blocks, slots = adj_offset.shape
    block_rows = adj_values.shape[2]
    rows, width = features.shape
    rim = BAND * block_rows
    count = lax.axis_size("rows") * lax.axis_size("cols")
    smem = pl.BlockSpec(memory_space=pltpu.SMEM)
    vmem = pl.BlockSpec(memory_space=pltpu.VMEM)
    params = pltpu.CompilerParams(vmem_limit_bytes=40 * 1024 * 1024)

    from_below = neighbour(features[rows - rim :], 1, count)
    from_above = neighbour(features[:rim], -1, count)
    activated, upstream, partial = pl.pallas_call(
        forward_kernel,
        out_shape=(
            jax.ShapeDtypeStruct((rows, width), jnp.bfloat16),
            jax.ShapeDtypeStruct((blocks, width, block_rows), jnp.bfloat16),
            jax.ShapeDtypeStruct((width, width + LANES), jnp.bfloat16),
        ),
        in_specs=[smem, smem] + [vmem] * 7,
        out_specs=(vmem, vmem, vmem),
        scratch_shapes=[
            pltpu.VMEM((rows + 2 * rim + block_rows, width), jnp.bfloat16),
            pltpu.VMEM((rows, width), jnp.bfloat16),
            pltpu.VMEM((rows, width), jnp.bfloat16),
        ],
        compiler_params=params,
        cost_estimate=pl.CostEstimate(
            flops=1_000_000_000, bytes_accessed=5_000_000, transcendentals=800_000
        ),
        name="layer_forward",
    )(
        adj_offset, adj_count, features, from_below, from_above, adj_values, weight,
        bias_vector.reshape(1, width), cotangent,
    )
    grad_inner, edges, lower_part, upper_part = pl.pallas_call(
        backward_kernel,
        out_shape=(
            jax.ShapeDtypeStruct((rows, width), jnp.bfloat16),
            jax.ShapeDtypeStruct((2 * rim, width), jnp.float32),
            jax.ShapeDtypeStruct((rim, width), jnp.bfloat16),
            jax.ShapeDtypeStruct((rim, width), jnp.bfloat16),
        ),
        in_specs=[smem, smem, vmem, vmem],
        out_specs=(vmem, vmem, vmem, vmem),
        scratch_shapes=[
            pltpu.VMEM((blocks + 2 * BAND + 1, width, block_rows), jnp.float32),
        ],
        compiler_params=params,
        cost_estimate=pl.CostEstimate(
            flops=400_000_000, bytes_accessed=4_000_000, transcendentals=0
        ),
        name="layer_backward",
    )(adj_offset, adj_count, adj_values, upstream)
    from_above_dev = neighbour(lower_part, -1, count)
    from_below_dev = neighbour(upper_part, 1, count)
    summed = sum_devices(partial, count)
    norm_scale = 1.0 / math.sqrt(rows * count)
    grad_weight = summed[:, :width].astype(jnp.float32) * norm_scale
    grad_bias = summed[:, width].astype(jnp.float32) * norm_scale
    last = rows // rim - 1
    spills = jnp.concatenate([from_below_dev, from_above_dev], 0)
    grad_features = pl.pallas_call(
        edge_kernel,
        grid=(2,),
        out_shape=jax.ShapeDtypeStruct((rows, width), jnp.bfloat16),
        in_specs=[
            pl.BlockSpec(memory_space=pl.ANY),
            pl.BlockSpec((rim, width), lambda step: (step, 0)),
            pl.BlockSpec((rim, width), lambda step: (step, 0)),
        ],
        out_specs=pl.BlockSpec((rim, width), lambda step: (step * last, 0)),
        input_output_aliases={0: 0},
        name="join_edges",
    )(grad_inner, edges, spills)
    return (activated, grad_features, grad_weight, grad_bias)


def solution(mesh):
    return jax.shard_map(
        on_device,
        mesh=mesh,
        in_specs=(
            P(AXES, None),
            P(AXES, None, None, None),
            P(AXES, None),
            P(AXES),
            P(),
            P(),
            P(AXES, None),
        ),
        out_specs=(P(AXES, None), P(AXES, None), P(), P()),
        check_vma=False,
    )
```

time: 198 us -> 62.8 us (0.32)
  waiting for transfers between devices: 82.5 us -> 10.9 us
  blocking collectives: 47.8 us -> 15.1 us
  other arithmetic: 18.4 us -> 2.12 us
  between operations: 14.2 us -> 0.7 us
  Pallas kernels: 0 us -> 11.5 us
  matrix products: 10.2 us -> 0 us
  local copies, waits for them, and re-layouts: 13.2 us -> 8.33 us
  starting transfers between devices: 11.4 us -> 13.6 us
    psum x1 -> x0, waiting for transfers between devices: 75.6 us -> none  [on_device(): lax.psum((partial_weight, partial_bias), ('rows', 'cols'))]
    psum x1 -> x0, blocking collectives: 47.8 us -> none  [on_device(): lax.psum((partial_weight, partial_bias), ('rows', 'cols'))]
    all_to_all x0 -> x1, blocking collectives: none -> 15.1 us  [sum_devices(): lax.all_to_all(partial, axes, 0, 0, tiled=True)]
    scatter-add x3 -> x0, other arithmetic: 12.3 us -> none  [the longest x1 8.85 us: on_device(): empty.at[target.reshape(-1)]]
    pallas_call x0 -> x4, Pallas kernels: none -> 11.5 us  [the longest x1 5.21 us: on_device(): pl.pallas_call(forward_kernel, out_shape=(jax.ShapeDtypeStruct((rows, wid...]
    dot_general x5 -> x0, matrix products: 10.2 us -> none  [the longest x1 3.07 us: on_device(): jnp.einsum('bsac,baf->bscf', adj_values, upstream.reshape(blocks, block_r...]
    unnamed x14 -> x19, local copies, waits for them, and re-layouts: 0.92 us -> 7.34 us
    reshape x2 -> x0, local copies, waits for them, and re-layouts: 6.23 us -> none  [the longest x1 6.15 us: on_device(): slot_terms.reshape(-1, block_rows, feat_width)]
  transfers between devices with their start and end apart: 9 -> 5, of which waited for: 4 -> 4; matrix products, arithmetic and copies ran while one was open for 5% -> 2% of each run, Pallas kernels for 0% -> 7%
where the time goes in v1:
time: 62.8 us; the launch traced here: 62.2 us
  blocking collectives  15.1 us (24%)
  starting transfers between devices  13.6 us (22%)
  Pallas kernels  11.5 us (18%)
  waiting for transfers between devices  10.9 us (17%)
  local copies, waits for them, and re-layouts  8.33 us (13%)
  other arithmetic  2.12 us (3%)
  between operations  0.7 us (1%)
    all_to_all x1, blocking collectives, sum_devices(): lax.all_to_all(partial, axes, 0, 0, tiled=True)  15.1 us
    ppermute x4, starting transfers between devices, neighbour(): lax.ppermute(value, AXES, [(source, source + steps) for source in range(i...  11 us
    ppermute x4, waiting for transfers between devices, neighbour(): lax.ppermute(value, AXES, [(source, source + steps) for source in range(i...  10.9 us
    unnamed x19, local copies, waits for them, and re-layouts  7.34 us
    pallas_call x1, Pallas kernels, on_device(): pl.pallas_call(forward_kernel, out_shape=(jax.ShapeDtypeStruct((rows, wid...  5.21 us
    pallas_call x1, Pallas kernels, on_device(): pl.pallas_call(backward_kernel, out_shape=(jax.ShapeDtypeStruct((rows, wi...  2.85 us
    all_to_all x1, starting transfers between devices, sum_devices(): return lax.all_to_all(shares.reshape(rows, lanes), axes, 0, 0, tiled=True)  2.58 us
    pallas_call x1, Pallas kernels, on_device(): pl.pallas_call(edge_kernel, grid=(2,), out_shape=jax.ShapeDtypeStruct((ro...  1.81 us
  transfers between devices with their start and end apart: 5, of which 4 were waited for; matrix products, arithmetic and copies ran while one was open for 2% of the time, Pallas kernels for 7%

profile of v1, /device:TPU:0, one launch (start us, length us, event | category | flops | bytes accessed | tf_op | source)
XLA Modules:
  0.0 62.2 jit_solution(8628657021141902080)
XLA Ops:
  0.6 1.0 %fusion = (bf16[256,256]{1,0:T(8,128)(2,1)S(1)}, bf16[256,256]{1,0:T(8,128)(2,1)S(1)}) fusion(bf16[1536,256]{1,0:T(8,128)(2,1)} %feat_ref.1), kind=kLoop, calls=%fused_computation.3 | loop fusion | bytes 524288 | tf_op jit(solution)/shard_map/slice | solution.py:142
  1.6 4.9 %collective-permute-start = (bf16[256,256]{1,0:T(8,128)(2,1)S(1)}, bf16[256,256]{1,0:T(8,128)(2,1)S(1)}, u32[]{:S(2)}, u32[]{:S(2)}) collective-permute-start(bf16[256,256]{1,0:T(8,128)(2,1)S(1)} %get-tuple-element.19), channel_id=1, source_target_pairs={{0,1},{1,2},{2,3},{3,4},{4,5},{5,6},{6,7},{7,8},{8,9},{9,10},{10,1... | collective-permute-start | bytes 393224 | tf_op jit(solution)/shard_map/ppermute | solution.py:108
  6.5 1.3 %collective-permute-start.1 = (bf16[256,256]{1,0:T(8,128)(2,1)S(1)}, bf16[256,256]{1,0:T(8,128)(2,1)S(1)}, u32[]{:S(2)}, u32[]{:S(2)}) collective-permute-start(bf16[256,256]{1,0:T(8,128)(2,1)S(1)} %get-tuple-element.18), channel_id=1, source_target_pairs={{1,0},{2,1},{3,2},{4,3},{5,4},{6,5},{7,6},{8,7},{9,8},{10,9},{11,1... | collective-permute-start | bytes 393224 | tf_op jit(solution)/shard_map/ppermute | solution.py:108
  7.8 0.8 %copy.14.off_ref = s32[12,3]{1,0:T(8,128)S(1)} copy(s32[12,3]{0,1:T(4,128)} %param.9) | data formatting | bytes 288 | tf_op args[2]
  8.6 0.9 %collective-permute-done.lower_ref = bf16[256,256]{1,0:T(8,128)(2,1)S(1)} collective-permute-done((bf16[256,256]{1,0:T(8,128)(2,1)S(1)}, bf16[256,256]{1,0:T(8,128)(2,1)S(1)}, u32[]{:S(2)}, u32[]{:S(2)}) %collective-permute-start) | collective-permute-done | bytes 131104 | tf_op jit(solution)/shard_map/ppermute | solution.py:108
  9.5 4.1 %collective-permute-done.1.upper_ref = bf16[256,256]{1,0:T(8,128)(2,1)S(1)} collective-permute-done((bf16[256,256]{1,0:T(8,128)(2,1)S(1)}, bf16[256,256]{1,0:T(8,128)(2,1)S(1)}, u32[]{:S(2)}, u32[]{:S(2)}) %collective-permute-start.1) | collective-permute-done | bytes 131104 | tf_op jit(solution)/shard_map/ppermute | solution.py:108
  13.6 0.0 copy-start
  13.6 1.3 %copy-done = bf16[12,3,128,128]{3,2,1,0:T(8,128)(2,1)S(1)} copy-done((bf16[12,3,128,128]{3,2,1,0:T(8,128)(2,1)S(1)}, bf16[12,3,128,128]{3,2,1,0:T(8,128)(2,1)}, u32[]{:S(2)}) %copy-start) | copy-done | bytes 1179672
  14.9 0.0 copy-start.3
  14.9 1.1 %copy-done.3 = bf16[1536,256]{1,0:T(8,128)(2,1)S(1)} copy-done((bf16[1536,256]{1,0:T(8,128)(2,1)S(1)}, bf16[1536,256]{1,0:T(8,128)(2,1)}, u32[]{:S(2)}) %copy-start.3) | copy-done | bytes 786456
  16.0 0.0 copy-start.4
  16.0 0.7 %copy-done.4 = s32[12]{0:T(128)S(1)} copy-done((s32[12]{0:T(128)S(1)}, s32[12]{0:T(128)}, u32[]{:S(2)}) %copy-start.4) | copy-done | bytes 72
  16.7 1.1 %copy-done.6 = bf16[1536,256]{1,0:T(8,128)(2,1)S(1)} copy-done((bf16[1536,256]{1,0:T(8,128)(2,1)S(1)}, bf16[1536,256]{1,0:T(8,128)(2,1)}, u32[]{:S(2)}) %copy-start.6) | copy-done | bytes 786456
  17.8 0.9 %copy-done.7 = bf16[256,256]{1,0:T(8,128)(2,1)S(1)} copy-done((bf16[256,256]{1,0:T(8,128)(2,1)S(1)}, bf16[256,256]{1,0:T(8,128)(2,1)}, u32[]{:S(2)}) %copy-start.7) | copy-done | bytes 131096
  18.7 0.7 %copy-done.8 = f32[256]{0:T(256)S(1)} copy-done((f32[256]{0:T(256)S(1)}, f32[256]{0:T(256)}, u32[]{:S(2)}) %copy-start.8) | copy-done | bytes 1048
  19.4 5.2 %layer_forward.1 = (bf16[1536,256]{1,0:T(8,128)(2,1)}, bf16[12,256,128]{2,1,0:T(8,128)(2,1)S(1)}, bf16[256,384]{1,0:T(8,128)(2,1)S(1)}) custom-call(s32[12,3]{1,0:T(8,128)S(1)} %copy.14.off_ref, s32[12]{0:T(128)S(1)} %copy-done.4, bf16[1536,256]{1,0:T(8,128)(2,1)S(1)} %copy-done.3, bf16[256,256]{1,0:T(8,128)(2,1)S(1)} %collective-permute-done.lower_ref, ...), custom_call_target="tpu_custom_call" | custom-call | flops 1000000000 | bytes 5000000 | tf_op jit(solution)/shard_map/layer_forward/pallas_call | solution.py:143
  24.6 15.1 %all_to_all.18.gathered_ref = bf16[32,8,384]{2,1,0:T(8,128)(2,1)} all-to-all(bf16[32,8,384]{2,1,0:T(8,128)(2,1)S(1)} %bitcast.3), channel_id=1, replica_groups=mesh['rows'=16,'cols'=2] {'rows','cols'}, dimensions={0} | all-to-all | bytes 393216 | tf_op jit(solution)/shard_map/all_to_all | solution.py:117
  39.7 1.7 %reduce_share.1 = bf16[32,8,384]{2,1,0:T(8,128)(2,1)} custom-call(bf16[32,8,384]{2,1,0:T(8,128)(2,1)} %all_to_all.18.gathered_ref), custom_call_target="tpu_custom_call" | custom-call | tf_op jit(solution)/shard_map/reduce_share/pallas_call | solution.py:123
  41.3 2.6 %all-to-all-start.1 = ((bf16[32,8,384]{2,1,0:T(8,128)(2,1)}), bf16[32,8,384]{2,1,0:T(8,128)(2,1)S(1)}, u32[]{:S(2)}, u32[]{:S(2)}) async-start(bf16[32,8,384]{2,1,0:T(8,128)(2,1)} %reduce_share.1), calls=%async_computation.1 | async-start | bytes 393216 | tf_op jit(solution)/shard_map/all_to_all | solution.py:128
  43.9 0.0 copy-done.1
  43.9 0.0 copy-done.5
  43.9 2.8 %layer_backward.1 = (bf16[1536,256]{1,0:T(8,128)(2,1)}, f32[512,256]{1,0:T(8,128)S(1)}, bf16[256,256]{1,0:T(8,128)(2,1)S(1)}, bf16[256,256]{1,0:T(8,128)(2,1)S(1)}) custom-call(s32[12,3]{1,0:T(8,128)S(1)} %copy.14.off_ref, s32[12]{0:T(128)S(1)} %copy-done.5, bf16[12,3,128,128]{3,2,1,0:T(8,128)(2,1)S(1)} %copy-done.1, ...), custom_call_target="tpu_custom_call" | custom-call | flops 400000000 | bytes 4000000 | tf_op jit(solution)/shard_map/layer_backward/pallas_call | solution.py:166
  46.8 0.8 %copy-done.2 = f32[512,256]{1,0:T(8,128)} copy-done((f32[512,256]{1,0:T(8,128)}, f32[512,256]{1,0:T(8,128)S(1)}, u32[]{:S(2)}) %copy-start.2) | copy-done | bytes 524312
  47.6 3.5 %collective-permute-start.2 = (bf16[256,256]{1,0:T(8,128)(2,1)S(1)}, bf16[256,256]{1,0:T(8,128)(2,1)S(1)}, u32[]{:S(2)}, u32[]{:S(2)}) collective-permute-start(bf16[256,256]{1,0:T(8,128)(2,1)S(1)} %get-tuple-element.15), channel_id=1, source_target_pairs={{0,1},{1,2},{2,3},{3,4},{4,5},{5,6},{6,7},{7,8},{8,9},{9,10},{10,1... | collective-permute-start | bytes 393224 | tf_op jit(solution)/shard_map/ppermute | solution.py:108
  51.1 1.3 %collective-permute-start.3 = (bf16[256,256]{1,0:T(8,128)(2,1)S(1)}, bf16[256,256]{1,0:T(8,128)(2,1)S(1)}, u32[]{:S(2)}, u32[]{:S(2)}) collective-permute-start(bf16[256,256]{1,0:T(8,128)(2,1)S(1)} %get-tuple-element.16), channel_id=1, source_target_pairs={{1,0},{2,1},{3,2},{4,3},{5,4},{6,5},{7,6},{8,7},{9,8},{10,9},{11,1... | collective-permute-start | bytes 393224 | tf_op jit(solution)/shard_map/ppermute | solution.py:108
  52.4 2.3 %collective-permute-done.2 = bf16[256,256]{1,0:T(8,128)(2,1)S(1)} collective-permute-done((bf16[256,256]{1,0:T(8,128)(2,1)S(1)}, bf16[256,256]{1,0:T(8,128)(2,1)S(1)}, u32[]{:S(2)}, u32[]{:S(2)}) %collective-permute-start.2) | collective-permute-done | bytes 131104 | tf_op jit(solution)/shard_map/ppermute | solution.py:108
  54.7 3.6 %collective-permute-done.3 = bf16[256,256]{1,0:T(8,128)(2,1)S(1)} collective-permute-done((bf16[256,256]{1,0:T(8,128)(2,1)S(1)}, bf16[256,256]{1,0:T(8,128)(2,1)S(1)}, u32[]{:S(2)}, u32[]{:S(2)}) %collective-permute-start.3) | collective-permute-done | bytes 131104 | tf_op jit(solution)/shard_map/ppermute | solution.py:108
  58.3 0.7 %pad_maximum_fusion.spill_ref = bf16[512,256]{1,0:T(8,128)(2,1)} fusion(bf16[256,256]{1,0:T(8,128)(2,1)S(1)} %collective-permute-done.3, bf16[256,256]{1,0:T(8,128)(2,1)S(1)} %collective-permute-done.2), kind=kLoop, calls=%fused_computation | loop fusion | flops 524288 | bytes 524288 | tf_op jit(solution)/shard_map/concatenate | solution.py:192
  59.0 1.8 %join_edges.1 = bf16[1536,256]{1,0:T(8,128)(2,1)} custom-call(bf16[1536,256]{1,0:T(8,128)(2,1)} %get-tuple-element.13.whole_ref, f32[512,256]{1,0:T(8,128)} %copy-done.2, bf16[512,256]{1,0:T(8,128)(2,1)} %pad_maximum_fusion.spill_ref), custom_call_target="tpu_custom_call", output_to_operand_aliasing={{}: (0, {})} | custom-call | tf_op jit(solution)/shard_map/join_edges/pallas_call | solution.py:193
  60.8 0.0 all-to-all-done.1
  60.8 0.7 %convert_multiply_fusion = f32[256,256]{1,0:T(8,128)} fusion(bf16[256,384]{1,0:T(8,128)(2,1)S(1)} %bitcast.5), kind=kLoop, calls=%fused_computation.1 | loop fusion | flops 131072 | bytes 393216 | tf_op jit(solution)/shard_map/mul | solution.py:189
  61.5 0.7 %multiply_reduce_fusion = f32[256]{0:T(256)} fusion(bf16[256,384]{1,0:T(8,128)(2,1)S(1)} %bitcast.6), kind=kLoop, calls=%fused_computation.2 | loop fusion | flops 512 | bytes 1536 | tf_op jit(solution)/shard_map/mul | solution.py:190
  (6 shorter events, 0.0 us)
Async XLA Ops:
  1.6 7.9 %collective-permute-start = (bf16[256,256]{1,0:T(8,128)(2,1)S(1)}, bf16[256,256]{1,0:T(8,128)(2,1)S(1)}, u32[]{:S(2)}, u32[]{:S(2)}) collective-permute-start(bf16[256,256]{1,0:T(8,128)(2,1)S(1)} %get-tuple-element.19), channel_id=1, source_target_pairs={{0,1},{1,2},{2,3},{3,4},{4,5},{5,6},{6,7},{7,8},{8,9},{9,10},{10,1... | collective-permute-start | bytes 393224 | tf_op jit(solution)/shard_map/ppermute | solution.py:108
  6.5 7.1 %collective-permute-start.1 = (bf16[256,256]{1,0:T(8,128)(2,1)S(1)}, bf16[256,256]{1,0:T(8,128)(2,1)S(1)}, u32[]{:S(2)}, u32[]{:S(2)}) collective-permute-start(bf16[256,256]{1,0:T(8,128)(2,1)S(1)} %get-tuple-element.18), channel_id=1, source_target_pairs={{1,0},{2,1},{3,2},{4,3},{5,4},{6,5},{7,6},{8,7},{9,8},{10,9},{11,1... | collective-permute-start | bytes 393224 | tf_op jit(solution)/shard_map/ppermute | solution.py:108
  13.6 1.3 %copy-start = (bf16[12,3,128,128]{3,2,1,0:T(8,128)(2,1)S(1)}, bf16[12,3,128,128]{3,2,1,0:T(8,128)(2,1)}, u32[]{:S(2)}) copy-start(bf16[12,3,128,128]{3,2,1,0:T(8,128)(2,1)} %adj_ref.3) | copy-start | bytes 3538948
  14.9 1.1 %copy-start.3 = (bf16[1536,256]{1,0:T(8,128)(2,1)S(1)}, bf16[1536,256]{1,0:T(8,128)(2,1)}, u32[]{:S(2)}) copy-start(bf16[1536,256]{1,0:T(8,128)(2,1)} %feat_ref.1) | copy-start | bytes 2359300
  16.0 0.7 %copy-start.4 = (s32[12]{0:T(128)S(1)}, s32[12]{0:T(128)}, u32[]{:S(2)}) copy-start(s32[12]{0:T(128)} %cnt_ref.3) | copy-start | bytes 148
  16.7 1.1 %copy-start.6 = (bf16[1536,256]{1,0:T(8,128)(2,1)S(1)}, bf16[1536,256]{1,0:T(8,128)(2,1)}, u32[]{:S(2)}) copy-start(bf16[1536,256]{1,0:T(8,128)(2,1)} %cot_ref.1) | copy-start | bytes 2359300
  17.8 0.9 %copy-start.7 = (bf16[256,256]{1,0:T(8,128)(2,1)S(1)}, bf16[256,256]{1,0:T(8,128)(2,1)}, u32[]{:S(2)}) copy-start(bf16[256,256]{1,0:T(8,128)(2,1)} %weight_ref.1) | copy-start | bytes 393220
  18.7 0.7 %copy-start.8 = (f32[256]{0:T(256)S(1)}, f32[256]{0:T(256)}, u32[]{:S(2)}) copy-start(f32[256]{0:T(256)} %param.12) | copy-start | bytes 3076
  24.6 19.3 %copy-start.1 = (bf16[12,3,128,128]{3,2,1,0:T(8,128)(2,1)S(1)}, bf16[12,3,128,128]{3,2,1,0:T(8,128)(2,1)}, u32[]{:S(2)}) copy-start(bf16[12,3,128,128]{3,2,1,0:T(8,128)(2,1)} %adj_ref.3) | copy-start | bytes 3538948
  24.6 19.3 %copy-start.5 = (s32[12]{0:T(128)S(1)}, s32[12]{0:T(128)}, u32[]{:S(2)}) copy-start(s32[12]{0:T(128)} %cnt_ref.3) | copy-start | bytes 148
  41.3 19.5 %all-to-all-start.1 = ((bf16[32,8,384]{2,1,0:T(8,128)(2,1)}), bf16[32,8,384]{2,1,0:T(8,128)(2,1)S(1)}, u32[]{:S(2)}, u32[]{:S(2)}) async-start(bf16[32,8,384]{2,1,0:T(8,128)(2,1)} %reduce_share.1), calls=%async_computation.1 | async-start | bytes 393216 | tf_op jit(solution)/shard_map/all_to_all | solution.py:128
  46.8 0.8 %copy-start.2 = (f32[512,256]{1,0:T(8,128)}, f32[512,256]{1,0:T(8,128)S(1)}, u32[]{:S(2)}) copy-start(f32[512,256]{1,0:T(8,128)S(1)} %get-tuple-element.14.edge_ref) | copy-start | bytes 1572868
  47.6 7.1 %collective-permute-start.2 = (bf16[256,256]{1,0:T(8,128)(2,1)S(1)}, bf16[256,256]{1,0:T(8,128)(2,1)S(1)}, u32[]{:S(2)}, u32[]{:S(2)}) collective-permute-start(bf16[256,256]{1,0:T(8,128)(2,1)S(1)} %get-tuple-element.15), channel_id=1, source_target_pairs={{0,1},{1,2},{2,3},{3,4},{4,5},{5,6},{6,7},{7,8},{8,9},{9,10},{10,1... | collective-permute-start | bytes 393224 | tf_op jit(solution)/shard_map/ppermute | solution.py:108
  51.1 7.2 %collective-permute-start.3 = (bf16[256,256]{1,0:T(8,128)(2,1)S(1)}, bf16[256,256]{1,0:T(8,128)(2,1)S(1)}, u32[]{:S(2)}, u32[]{:S(2)}) collective-permute-start(bf16[256,256]{1,0:T(8,128)(2,1)S(1)} %get-tuple-element.16), channel_id=1, source_target_pairs={{1,0},{2,1},{3,2},{4,3},{5,4},{6,5},{7,6},{8,7},{9,8},{10,9},{11,1... | collective-permute-start | bytes 393224 | tf_op jit(solution)/shard_map/ppermute | solution.py:108

commit v2 on v0

v2 whole, which is shorter than its diff:
```python
import math

import jax
import jax.numpy as jnp
from jax import lax
from jax.experimental import pallas as pl
from jax.experimental.pallas import tpu as pltpu
from jax.sharding import Mesh, PartitionSpec as P

BAND = 2
AXES = ("outer", "inner", "cols")
GROUP = ("inner", "cols")
LANES = 128
MIB = 1024 * 1024


def row_of(adj_ref, block, slots):
    return jnp.concatenate([adj_ref[block, slot] for slot in range(slots)], 1)


def pick(source, places, block_rows):
    return jnp.concatenate(
        [
            source[pl.ds(pl.multiple_of(place * block_rows, block_rows), block_rows)]
            for place in places
        ],
        0,
    )


def places_of(off_ref, cnt_ref, block, shift, dump, slots):
    return [
        jnp.where(slot < cnt_ref[block], block + shift + off_ref[slot, block], dump)
        for slot in range(slots)
    ]


def activate(preact, cotangent):
    gate = 1.0 / (1.0 + jnp.exp(-preact))
    grad = cotangent.astype(jnp.float32) * gate * (1.0 + preact * (1.0 - gate))
    return (preact * gate).astype(jnp.bfloat16), grad.astype(jnp.bfloat16)


def column_sums(grad):
    rows, width = grad.shape
    return jnp.sum(grad.astype(jnp.float32).reshape(rows // 8, 8, width), axis=0)


def to_upstream(weight, grad):
    return lax.dot_general(
        weight, grad, (((1,), (1,)), ((), ())), preferred_element_type=jnp.float32
    ).astype(jnp.bfloat16)


def weight_terms(agg, grad):
    return lax.dot_general(
        agg, grad, (((0,), (0,)), ((), ())), preferred_element_type=jnp.float32
    )


def inner_kernel(
    off_ref, cnt_ref, weight_hbm, bias_hbm, feat_hbm, adj_hbm, cot_hbm,
    act_hbm, grad_hbm, spread, partial_ref, sums_ref, weight_ref, bias_ref, feat_rim, adj_rim,
    cot_rim,
    feat, adj, cot, act, out, agg_all, grad_all, sems,
):
    blocks, slots, block_rows, _ = adj_hbm.shape
    rows, width = feat_hbm.shape
    count = blocks - 2 * BAND
    rim = BAND * block_rows
    half = 2 * rim
    inner = count * block_rows
    copies = [
        pltpu.make_async_copy(feat_hbm, feat.at[pl.ds(0, rows)], sems.at[0]),
        pltpu.make_async_copy(adj_hbm.at[pl.ds(BAND, count)], adj, sems.at[1]),
        pltpu.make_async_copy(weight_hbm, weight_ref, sems.at[11]),
        pltpu.make_async_copy(bias_hbm, bias_ref, sems.at[12]),
        pltpu.make_async_copy(cot_hbm.at[pl.ds(rim, inner)], cot, sems.at[2]),
        pltpu.make_async_copy(feat_hbm.at[pl.ds(0, half)], feat_rim.at[pl.ds(0, half)], sems.at[3]),
        pltpu.make_async_copy(
            feat_hbm.at[pl.ds(rows - half, half)], feat_rim.at[pl.ds(half, half)], sems.at[4]
        ),
        pltpu.make_async_copy(adj_hbm.at[pl.ds(0, BAND)], adj_rim.at[pl.ds(0, BAND)], sems.at[5]),
        pltpu.make_async_copy(
            adj_hbm.at[pl.ds(blocks - BAND, BAND)], adj_rim.at[pl.ds(BAND, BAND)], sems.at[6]
        ),
        pltpu.make_async_copy(cot_hbm.at[pl.ds(0, rim)], cot_rim.at[pl.ds(0, rim)], sems.at[7]),
        pltpu.make_async_copy(
            cot_hbm.at[pl.ds(rows - rim, rim)], cot_rim.at[pl.ds(rim, rim)], sems.at[8]
        ),
    ]
    for copy in copies:
        copy.start()
    feat[rows:] = jnp.zeros((block_rows, width), jnp.bfloat16)
    spread[...] = jnp.zeros_like(spread)
    for copy in copies[:5]:
        copy.wait()
    weight = weight_ref[...]
    bias = bias_ref[...]
    sums = jnp.zeros((8, width), jnp.float32)
    for step in range(count):
        here = pl.ds(step * block_rows, block_rows)
        places = places_of(off_ref, cnt_ref, step + BAND, 0, blocks, slots)
        row = row_of(adj, step, slots)
        agg = jnp.dot(row, pick(feat, places, block_rows), preferred_element_type=jnp.float32)
        agg = agg.astype(jnp.bfloat16)
        agg_all[here] = agg
        preact = jnp.dot(agg, weight, preferred_element_type=jnp.float32) + bias
        act[here], grad = activate(preact, cot[here])
        grad_all[here] = grad
        sums = sums + column_sums(grad)
        terms = jnp.dot(to_upstream(weight, grad), row, preferred_element_type=jnp.float32)
        for slot, place in enumerate(places):
            spread[place] += terms[:, slot * block_rows : (slot + 1) * block_rows]
    act_out = pltpu.make_async_copy(act, act_hbm.at[pl.ds(rim, inner)], sems.at[9])
    act_out.start()
    done = blocks - 4 * BAND
    for step in range(done):
        here = pl.ds(step * block_rows, block_rows)
        out[here] = spread[2 * BAND + step].T.astype(jnp.bfloat16)
    grad_out = pltpu.make_async_copy(
        out, grad_hbm.at[pl.ds(half, done * block_rows)], sems.at[10]
    )
    grad_out.start()
    sums_ref[...] = sums
    partial_ref[...] = weight_terms(agg_all[...], grad_all[...])
    for copy in copies[5:]:
        copy.wait()
    act_out.wait()
    grad_out.wait()


def rim_places(off_ref, cnt_ref, step, blocks, slots):
    if step < BAND:
        return places_of(off_ref, cnt_ref, step, BAND, 6 * BAND, slots)
    block = blocks - 2 * BAND + step
    return places_of(off_ref, cnt_ref, block, 5 * BAND - blocks, 6 * BAND, slots)


def rim_kernel(
    off_ref, cnt_ref, weight_ref, bias_ref, feat_ref, lower_ref, upper_ref, adj_ref, cot_ref,
    partial_ref, sums_ref,
    act_ref, grad_ref, payload_ref,
    window, agg_all,
):
    blocks = off_ref.shape[1]
    steps, slots, block_rows, _ = adj_ref.shape
    width = feat_ref.shape[1]
    rim = BAND * block_rows
    window[:rim] = lower_ref[...]
    window[rim : 5 * rim] = feat_ref[...]
    window[5 * rim : 6 * rim] = upper_ref[...]
    window[6 * rim :] = jnp.zeros((block_rows, width), jnp.bfloat16)
    weight = weight_ref[...]
    bias = bias_ref[...]
    sums = sums_ref[...]
    for step in range(steps):
        here = pl.ds(step * block_rows, block_rows)
        places = rim_places(off_ref, cnt_ref, step, blocks, slots)
        agg = jnp.dot(
            row_of(adj_ref, step, slots), pick(window, places, block_rows),
            preferred_element_type=jnp.float32,
        ).astype(jnp.bfloat16)
        agg_all[here] = agg
        preact = jnp.dot(agg, weight, preferred_element_type=jnp.float32) + bias
        act_ref[here], grad = activate(preact, cot_ref[here])
        grad_ref[here] = grad
        sums = sums + column_sums(grad)
    partial = partial_ref[...] + weight_terms(agg_all[...], grad_ref[...])
    payload_ref[:, :width] = partial.astype(jnp.bfloat16)
    sum_row = jnp.sum(sums, axis=0, keepdims=True)
    payload_ref[:, width:] = jnp.broadcast_to(sum_row, (LANES, width)).T.astype(jnp.bfloat16)


def rim_back_kernel(
    off_ref, cnt_ref, weight_ref, adj_ref, grad_ref, act_ref, inner_ref, act_in, whole_in,
    act_hbm, whole_hbm, edge_ref, lower_ref, upper_ref,
    spread, out, sems,
):
    blocks = off_ref.shape[1]
    steps, slots, block_rows, _ = adj_ref.shape
    rim = BAND * block_rows
    rows = blocks * block_rows
    copies = [
        pltpu.make_async_copy(act_ref.at[pl.ds(0, rim)], act_hbm.at[pl.ds(0, rim)], sems.at[0]),
        pltpu.make_async_copy(
            act_ref.at[pl.ds(rim, rim)], act_hbm.at[pl.ds(rows - rim, rim)], sems.at[1]
        ),
    ]
    for copy in copies:
        copy.start()
    zero = jnp.zeros((BAND,) + spread.shape[1:], jnp.float32)
    spread[:BAND] = zero
    spread[BAND : 3 * BAND] = inner_ref[: 2 * BAND]
    spread[3 * BAND : 5 * BAND] = inner_ref[blocks - 2 * BAND : blocks]
    spread[5 * BAND : 6 * BAND] = zero
    weight = weight_ref[...]
    for step in range(steps):
        here = pl.ds(step * block_rows, block_rows)
        places = rim_places(off_ref, cnt_ref, step, blocks, slots)
        terms = jnp.dot(
            to_upstream(weight, grad_ref[here]), row_of(adj_ref, step, slots),
            preferred_element_type=jnp.float32,
        )
        for slot, place in enumerate(places):
            spread[place] += terms[:, slot * block_rows : (slot + 1) * block_rows]
    for block in range(BAND):
        here = pl.ds(block * block_rows, block_rows)
        after = pl.ds(rim + block * block_rows, block_rows)
        lower_ref[here] = spread[block].T.astype(jnp.bfloat16)
        upper_ref[here] = spread[5 * BAND + block].T.astype(jnp.bfloat16)
        edge_ref[here] = spread[BAND + block].T
        edge_ref[after] = spread[4 * BAND + block].T
        out[here] = spread[2 * BAND + block].T.astype(jnp.bfloat16)
        out[after] = spread[3 * BAND + block].T.astype(jnp.bfloat16)
    finals = [
        pltpu.make_async_copy(out.at[pl.ds(0, rim)], whole_hbm.at[pl.ds(rim, rim)], sems.at[2]),
        pltpu.make_async_copy(
            out.at[pl.ds(rim, rim)], whole_hbm.at[pl.ds(rows - 2 * rim, rim)], sems.at[3]
        ),
    ]
    for copy in finals:
        copy.start()
    for copy in copies + finals:
        copy.wait()


def share_kernel(gathered_ref, spread_ref):
    total = jnp.sum(gathered_ref[...].astype(jnp.float32), axis=0).astype(jnp.bfloat16)
    spread_ref[...] = jnp.broadcast_to(total[None], spread_ref.shape)


def last_kernel(
    scale, summed_ref, edge_ref, below_ref, above_ref, whole_in,
    weight_out, bias_out, whole_hbm, out, sems,
):
    width = weight_out.shape[1]
    rim = below_ref.shape[0]
    rows = whole_hbm.shape[0]
    out[:rim] = (edge_ref[:rim] + below_ref[...].astype(jnp.float32)).astype(jnp.bfloat16)
    out[rim:] = (edge_ref[rim:] + above_ref[...].astype(jnp.float32)).astype(jnp.bfloat16)
    copies = [
        pltpu.make_async_copy(out.at[pl.ds(0, rim)], whole_hbm.at[pl.ds(0, rim)], sems.at[0]),
        pltpu.make_async_copy(
            out.at[pl.ds(rim, rim)], whole_hbm.at[pl.ds(rows - rim, rim)], sems.at[1]
        ),
    ]
    for copy in copies:
        copy.start()
    weight_out[...] = summed_ref[:, :width].astype(jnp.float32) * scale
    bias_out[...] = summed_ref[:, width:].astype(jnp.float32).T[:1] * scale
    for copy in copies:
        copy.wait()


def neighbour(value, steps, count):
    initial, last = max(0, -steps), min(count, count - steps)
    return lax.ppermute(value, AXES, [(source, source + steps) for source in range(initial, last)])


def add_up(gathered, copies):
    return pl.pallas_call(
        share_kernel,
        out_shape=jax.ShapeDtypeStruct((copies,) + gathered.shape[1:], jnp.bfloat16),
        compiler_params=pltpu.CompilerParams(vmem_limit_bytes=4 * MIB),
        cost_estimate=pl.CostEstimate(
            flops=gathered.size, bytes_accessed=4 * gathered.size, transcendentals=0
        ),
        name="add_up",
    )(gathered)


def sum_devices(payload):
    rows, lanes = payload.shape
    group = lax.axis_size("inner") * lax.axis_size("cols")
    outer = lax.axis_size("outer")
    parts = lax.all_to_all(payload, GROUP, 0, 0, tiled=True).reshape(group, rows // group, lanes)
    shares = add_up(parts, outer).reshape(outer * (rows // group), lanes)
    shares = lax.all_to_all(shares, "outer", 0, 0, tiled=True).reshape(outer, rows // group, lanes)
    return lax.all_to_all(add_up(shares, group).reshape(rows, lanes), GROUP, 0, 0, tiled=True)


def on_device(features, adj_values, adj_offset, adj_count, weight, bias_vector, cotangent):
    blocks, slots = adj_offset.shape
    block_rows = adj_values.shape[2]
    rows, width = features.shape
    rim = BAND * block_rows
    inner = rows - 2 * rim
    count = lax.axis_size("outer") * lax.axis_size("inner") * lax.axis_size("cols")
    smem = pl.BlockSpec(memory_space=pltpu.SMEM)
    vmem = pl.BlockSpec(memory_space=pltpu.VMEM)
    hbm = pl.BlockSpec(memory_space=pltpu.HBM)
    bias_row = bias_vector.reshape(1, width)

    def in_hbm(value):
        return pltpu.with_memory_space_constraint(value, pltpu.HBM)

    def shape(*sizes, dtype=jnp.bfloat16):
        return jax.ShapeDtypeStruct(sizes, dtype)

    def params(mib):
        return pltpu.CompilerParams(vmem_limit_bytes=mib * MIB)

    def cost(share):
        return pl.CostEstimate(
            flops=int(1.2e9 * share), bytes_accessed=int(6e6 * share),
            transcendentals=int(8e5 * share),
        )

    offsets = in_hbm(adj_offset.T)
    counts = in_hbm(adj_count)
    from_below = neighbour(features[rows - rim :], 1, count)
    from_above = neighbour(features[:rim], -1, count)
    (
        activated, grad_whole, spread, partial, sums, weight_near, bias_near, feat_rim, adj_rim,
        cot_rim,
    ) = pl.pallas_call(
        inner_kernel,
        out_shape=(
            shape(rows, width),
            shape(rows, width),
            shape(blocks + 1, width, block_rows, dtype=jnp.float32),
            shape(width, width, dtype=jnp.float32),
            shape(8, width, dtype=jnp.float32),
            shape(width, width),
            shape(1, width, dtype=jnp.float32),
            shape(4 * rim, width),
            shape(2 * BAND, slots, block_rows, block_rows),
            shape(2 * rim, width),
        ),
        in_specs=[smem, smem] + [hbm] * 5,
        out_specs=(hbm, hbm) + (vmem,) * 8,
        scratch_shapes=[
            pltpu.VMEM((rows + block_rows, width), jnp.bfloat16),
            pltpu.VMEM((blocks - 2 * BAND, slots, block_rows, block_rows), jnp.bfloat16),
            pltpu.VMEM((inner, width), jnp.bfloat16),
            pltpu.VMEM((inner, width), jnp.bfloat16),
            pltpu.VMEM((rows - 4 * rim, width), jnp.bfloat16),
            pltpu.VMEM((inner, width), jnp.bfloat16),
            pltpu.VMEM((inner, width), jnp.bfloat16),
            pltpu.SemaphoreType.DMA((13,)),
        ],
        compiler_params=params(20),
        cost_estimate=cost(0.7),
        name="inner_rows",
    )(
        offsets, counts,
        *(in_hbm(x) for x in (weight, bias_row, features, adj_values, cotangent)),
    )
    act_rim, grad_rim, payload = pl.pallas_call(
        rim_kernel,
        out_shape=(shape(2 * rim, width), shape(2 * rim, width), shape(width, width + LANES)),
        in_specs=[smem, smem] + [vmem] * 9,
        out_specs=(vmem,) * 3,
        scratch_shapes=[
            pltpu.VMEM((6 * rim + block_rows, width), jnp.bfloat16),
            pltpu.VMEM((2 * rim, width), jnp.bfloat16),
        ],
        compiler_params=params(12),
        cost_estimate=cost(0.15),
        name="rim_rows",
    )(
        offsets, counts, weight_near, bias_near, feat_rim, from_below, from_above, adj_rim,
        cot_rim, partial, sums,
    )
    activated, grad_whole, edges, lower_part, upper_part = pl.pallas_call(
        rim_back_kernel,
        out_shape=(
            shape(rows, width),
            shape(rows, width),
            shape(2 * rim, width, dtype=jnp.float32),
            shape(rim, width),
            shape(rim, width),
        ),
        in_specs=[smem, smem] + [vmem] * 5 + [hbm, hbm],
        out_specs=(hbm, hbm, vmem, vmem, vmem),
        scratch_shapes=[
            pltpu.VMEM((6 * BAND + 1, width, block_rows), jnp.float32),
            pltpu.VMEM((2 * rim, width), jnp.bfloat16),
            pltpu.SemaphoreType.DMA((4,)),
        ],
        input_output_aliases={7: 0, 8: 1},
        compiler_params=params(12),
        cost_estimate=cost(0.15),
        name="rim_rows_back",
    )(
        offsets, counts, weight_near, adj_rim, grad_rim, act_rim, spread, activated, grad_whole
    )
    from_above_dev = neighbour(lower_part, -1, count)
    from_below_dev = neighbour(upper_part, 1, count)
    summed = sum_devices(payload)
    norm_scale = 1.0 / math.sqrt(rows * count)
    grad_weight, grad_bias, grad_features = pl.pallas_call(
        lambda *refs: last_kernel(norm_scale, *refs),
        out_shape=(
            shape(width, width, dtype=jnp.float32),
            shape(1, width, dtype=jnp.float32),
            shape(rows, width),
        ),
        in_specs=[vmem] * 4 + [hbm],
        out_specs=(vmem, vmem, hbm),
        scratch_shapes=[
            pltpu.VMEM((2 * rim, width), jnp.bfloat16),
            pltpu.SemaphoreType.DMA((2,)),
        ],
        input_output_aliases={4: 2},
        compiler_params=params(8),
        name="last_step",
    )(summed, edges, from_below_dev, from_above_dev, grad_whole)
    return (activated, grad_features, grad_weight, grad_bias.reshape(width))


def solution(mesh):
    rows, cols = mesh.devices.shape
    inner = math.gcd(rows, 4)
    parts = Mesh(mesh.devices.reshape(rows // inner, inner, cols), AXES)
    return jax.shard_map(
        on_device,
        mesh=parts,
        in_specs=(
            P(AXES, None),
            P(AXES, None, None, None),
            P(AXES, None),
            P(AXES),
            P(),
            P(),
            P(AXES, None),
        ),
        out_specs=(P(AXES, None), P(AXES, None), P(), P()),
        check_vma=False,
    )
```

time: 198 us -> 57.6 us (0.29)
  waiting for transfers between devices: 82.5 us -> 5.87 us
  blocking collectives: 47.8 us -> 19.9 us
  other arithmetic: 18.4 us -> 0 us
  Pallas kernels: 0 us -> 14.3 us
  between operations: 14.2 us -> 0.72 us
  local copies, waits for them, and re-layouts: 13.2 us -> 0.99 us
  matrix products: 10.2 us -> 0 us
  starting transfers between devices: 11.4 us -> 15.3 us
    psum x1 -> x0, waiting for transfers between devices: 75.6 us -> none  [on_device(): lax.psum((partial_weight, partial_bias), ('rows', 'cols'))]
    psum x1 -> x0, blocking collectives: 47.8 us -> none  [on_device(): lax.psum((partial_weight, partial_bias), ('rows', 'cols'))]
    all_to_all x0 -> x2, blocking collectives: none -> 19.9 us  [the longest x1 10.3 us: sum_devices(): lax.all_to_all(payload, GROUP, 0, 0, tiled=True)]
    pallas_call x0 -> x6, Pallas kernels: none -> 14.3 us  [the longest x1 7.55 us: on_device(): pl.pallas_call(inner_kernel, out_shape=(shape(rows, width), shape(rows, w...]
    scatter-add x3 -> x0, other arithmetic: 12.3 us -> none  [the longest x1 8.85 us: on_device(): empty.at[target.reshape(-1)]]
    dot_general x5 -> x0, matrix products: 10.2 us -> none  [the longest x1 3.07 us: on_device(): jnp.einsum('bsac,baf->bscf', adj_values, upstream.reshape(blocks, block_r...]
    reshape x2 -> x0, local copies, waits for them, and re-layouts: 6.23 us -> none  [the longest x1 6.15 us: on_device(): slot_terms.reshape(-1, block_rows, feat_width)]
    all_to_all x0 -> x1, starting transfers between devices: none -> 3.39 us  [sum_devices(): lax.all_to_all(add_up(shares, group).reshape(rows, lanes), GROUP, 0, 0, t...]
  transfers between devices with their start and end apart: 9 -> 5, of which waited for: 4 -> 2; matrix products, arithmetic and copies ran while one was open for 5% -> 0% of each run, Pallas kernels for 0% -> 18%
where the time goes in v2:
time: 57.6 us; the launch traced here: 57.1 us
  blocking collectives  19.9 us (35%)
  starting transfers between devices  15.3 us (27%)
  Pallas kernels  14.3 us (25%)
  waiting for transfers between devices  5.87 us (10%)
  local copies, waits for them, and re-layouts  0.99 us (2%)
  between operations  0.72 us (1%)
    ppermute x4, starting transfers between devices, neighbour(): lax.ppermute(value, AXES, [(source, source + steps) for source in range(i...  11.9 us
    all_to_all x1, blocking collectives, sum_devices(): lax.all_to_all(payload, GROUP, 0, 0, tiled=True)  10.3 us
    all_to_all x1, blocking collectives, sum_devices(): lax.all_to_all(shares, 'outer', 0, 0, tiled=True)  9.65 us
    pallas_call x1, Pallas kernels, on_device(): pl.pallas_call(inner_kernel, out_shape=(shape(rows, width), shape(rows, w...  7.55 us
    ppermute x4, waiting for transfers between devices, neighbour(): lax.ppermute(value, AXES, [(source, source + steps) for source in range(i...  5.86 us
    all_to_all x1, starting transfers between devices, sum_devices(): lax.all_to_all(add_up(shares, group).reshape(rows, lanes), GROUP, 0, 0, t...  3.39 us
    pallas_call x1, Pallas kernels, on_device(): pl.pallas_call(rim_back_kernel, out_shape=(shape(rows, width), shape(rows...  2.64 us
    pallas_call x1, Pallas kernels, on_device(): pl.pallas_call(rim_kernel, out_shape=(shape(2 * rim, width), shape(2 * ri...  1.9 us
  transfers between devices with their start and end apart: 5, of which 2 were waited for; matrix products, arithmetic and copies ran while one was open for 0% of the time, Pallas kernels for 18%

profile of v2, /device:TPU:0, one launch (start us, length us, event | category | flops | bytes accessed | tf_op | source)
XLA Modules:
  0.0 57.1 jit_solution(15314688662884217028)
XLA Ops:
  0.6 1.0 %fusion = (bf16[256,256]{1,0:T(8,128)(2,1)S(1)}, bf16[256,256]{1,0:T(8,128)(2,1)S(1)}) fusion(bf16[1536,256]{1,0:T(8,128)(2,1)} %feat_hbm.1), kind=kLoop, calls=%fused_computation | loop fusion | bytes 524288 | tf_op jit(solution)/shard_map/slice | solution.py:313
  1.6 1.3 %collective-permute-start.1 = (bf16[256,256]{1,0:T(8,128)(2,1)S(1)}, bf16[256,256]{1,0:T(8,128)(2,1)S(1)}, u32[]{:S(2)}, u32[]{:S(2)}) collective-permute-start(bf16[256,256]{1,0:T(8,128)(2,1)S(1)} %get-tuple-element.46), channel_id=1, source_target_pairs={{1,0},{2,1},{3,2},{4,3},{5,4},{6,5},{7,6},{8,7},{9,8},{10,9},{11,1... | collective-permute-start | bytes 393224 | tf_op jit(solution)/shard_map/ppermute | solution.py:258
  2.9 5.5 %collective-permute-start = (bf16[256,256]{1,0:T(8,128)(2,1)S(1)}, bf16[256,256]{1,0:T(8,128)(2,1)S(1)}, u32[]{:S(2)}, u32[]{:S(2)}) collective-permute-start(bf16[256,256]{1,0:T(8,128)(2,1)S(1)} %get-tuple-element.47), channel_id=1, source_target_pairs={{0,1},{1,2},{2,3},{3,4},{4,5},{5,6},{6,7},{7,8},{8,9},{9,10},{10,1... | collective-permute-start | bytes 393224 | tf_op jit(solution)/shard_map/ppermute | solution.py:258
  8.4 7.5 %inner_rows.1 = (bf16[1536,256]{1,0:T(8,128)(2,1)}, bf16[1536,256]{1,0:T(8,128)(2,1)}, f32[13,256,128]{2,1,0:T(8,128)S(1)}, f32[256,256]{1,0:T(8,128)S(1)}, f32[...) custom-call(s32[3,12]{1,0:T(4,128)} %bitcast.7, ...), custom_call_target="tpu_custom_call" | custom-call | flops 840000000 | bytes 4200000 | tf_op jit(solution)/shard_map/inner_rows/pallas_call | solution.py:317
  16.0 0.0 collective-permute-done.1.upper_ref
  16.0 0.0 collective-permute-done.lower_ref
  16.0 1.9 %rim_rows.1 = (bf16[512,256]{1,0:T(8,128)(2,1)S(1)}, bf16[512,256]{1,0:T(8,128)(2,1)S(1)}, bf16[256,384]{1,0:T(8,128)(2,1)S(1)}) custom-call(s32[3,12]{1,0:T(4,128)} %bitcast.8, s32[12]{0:T(128)} %cnt_ref.5, bf16[256,256]{1,0:T(8,128)(2,1)S(1)} %get-tuple-element.25.weight_ref, f32[1,256]{1,0:T(1,128)S(1)} %get-tuple-element.27.bias_ref, ...), custom_call_target="tpu_custom_call" | custom-call | flops 180000000 | bytes 900000 | tf_op jit(solution)/shard_map/rim_rows/pallas_call | solution.py:350
  17.9 10.3 %all_to_all.23.gathered_ref = bf16[8,32,384]{2,1,0:T(8,128)(2,1)S(1)} all-to-all(bf16[8,32,384]{2,1,0:T(8,128)(2,1)S(1)} %bitcast.6), channel_id=1, replica_groups=mesh['outer'=4,'inner'=4,'cols'=2] {'inner','cols'}, dimensions={0} | all-to-all | bytes 393216 | tf_op jit(solution)/shard_map/all_to_all | solution.py:277
  28.3 9.6 %all_to_all.24.gathered_ref = bf16[4,32,384]{2,1,0:T(8,128)(2,1)S(1)} all-to-all(bf16[4,32,384]{2,1,0:T(8,128)(2,1)S(1)} %add_up.2), channel_id=1, replica_groups=mesh['outer'=4,'inner'=4,'cols'=2] {'outer'}, dimensions={0} | all-to-all | bytes 196608 | tf_op jit(solution)/shard_map/all_to_all | solution.py:279
  37.9 0.7 %add_up.3 = bf16[8,32,384]{2,1,0:T(8,128)(2,1)} custom-call(bf16[4,32,384]{2,1,0:T(8,128)(2,1)S(1)} %all_to_all.24.gathered_ref), custom_call_target="tpu_custom_call" | custom-call | flops 49152 | bytes 196608 | tf_op jit(solution)/shard_map/add_up/pallas_call | solution.py:262
  38.6 3.4 %all-to-all-start.2 = ((bf16[8,32,384]{2,1,0:T(8,128)(2,1)}), bf16[8,32,384]{2,1,0:T(8,128)(2,1)S(1)}, u32[]{:S(2)}, u32[]{:S(2)}) async-start(bf16[8,32,384]{2,1,0:T(8,128)(2,1)} %add_up.3), calls=%async_computation.2 | async-start | bytes 393216 | tf_op jit(solution)/shard_map/all_to_all | solution.py:280
  42.0 2.6 %rim_rows_back.1 = (bf16[1536,256]{1,0:T(8,128)(2,1)}, bf16[1536,256]{1,0:T(8,128)(2,1)}, f32[512,256]{1,0:T(8,128)S(1)}, bf16[256,256]{1,0:T(8,128)(2,1)S(1)}, bf16[256,256]{1,0:T(8,128)(2,1)S(1)}) custom-call(s32[3,12]{1,0:T(4,128)} %bitcast.9, s32[12]{0:T(128)} %cnt_ref.5, ...), custom_call_target="tpu_custom_call", output_to_operand_aliasing={{0}: (7, {}), {1}: (8, {})} | custom-call | flops 180000000 | bytes 900000 | tf_op jit(solution)/shard_map/rim_rows_back/pallas_call | solution.py:366
  44.7 3.8 %collective-permute-start.2 = (bf16[256,256]{1,0:T(8,128)(2,1)S(1)}, bf16[256,256]{1,0:T(8,128)(2,1)S(1)}, u32[]{:S(2)}, u32[]{:S(2)}) collective-permute-start(bf16[256,256]{1,0:T(8,128)(2,1)S(1)} %get-tuple-element.40), channel_id=1, source_target_pairs={{0,1},{1,2},{2,3},{3,4},{4,5},{5,6},{6,7},{7,8},{8,9},{9,10},{10,1... | collective-permute-start | bytes 393224 | tf_op jit(solution)/shard_map/ppermute | solution.py:258
  48.5 1.3 %collective-permute-start.3 = (bf16[256,256]{1,0:T(8,128)(2,1)S(1)}, bf16[256,256]{1,0:T(8,128)(2,1)S(1)}, u32[]{:S(2)}, u32[]{:S(2)}) collective-permute-start(bf16[256,256]{1,0:T(8,128)(2,1)S(1)} %get-tuple-element.41), channel_id=1, source_target_pairs={{1,0},{2,1},{3,2},{4,3},{5,4},{6,5},{7,6},{8,7},{9,8},{10,9},{11,1... | collective-permute-start | bytes 393224 | tf_op jit(solution)/shard_map/ppermute | solution.py:258
  49.8 2.2 %collective-permute-done.2.refs_2_ = bf16[256,256]{1,0:T(8,128)(2,1)S(1)} collective-permute-done((bf16[256,256]{1,0:T(8,128)(2,1)S(1)}, bf16[256,256]{1,0:T(8,128)(2,1)S(1)}, u32[]{:S(2)}, u32[]{:S(2)}) %collective-permute-start.2) | collective-permute-done | bytes 131104 | tf_op jit(solution)/shard_map/ppermute | solution.py:258
  52.0 3.7 %collective-permute-done.3.refs_3_ = bf16[256,256]{1,0:T(8,128)(2,1)S(1)} collective-permute-done((bf16[256,256]{1,0:T(8,128)(2,1)S(1)}, bf16[256,256]{1,0:T(8,128)(2,1)S(1)}, u32[]{:S(2)}, u32[]{:S(2)}) %collective-permute-start.3) | collective-permute-done | bytes 131104 | tf_op jit(solution)/shard_map/ppermute | solution.py:258
  55.6 0.0 all-to-all-done.2
  55.6 1.5 %last_step.1 = (f32[256,256]{1,0:T(8,128)}, f32[1,256]{1,0:T(1,128)}, bf16[1536,256]{1,0:T(8,128)(2,1)}) custom-call(bf16[256,384]{1,0:T(8,128)(2,1)S(1)} %bitcast.5, f32[512,256]{1,0:T(8,128)S(1)} %get-tuple-element.39.refs_1_, bf16[256,256]{1,0:T(8,128)(2,1)S(1)} %collective-permute-done.2.refs_2_, ...), custom_call_target="tpu_custom_call", output_to_operand_aliasing={{2}: (4, {})} | custom-call | tf_op jit(solution)/shard_map/last_step/pallas_call | solution.py:393
  (1 shorter events, 0.0 us)
Async XLA Ops:
  1.6 14.4 %collective-permute-start.1 = (bf16[256,256]{1,0:T(8,128)(2,1)S(1)}, bf16[256,256]{1,0:T(8,128)(2,1)S(1)}, u32[]{:S(2)}, u32[]{:S(2)}) collective-permute-start(bf16[256,256]{1,0:T(8,128)(2,1)S(1)} %get-tuple-element.46), channel_id=1, source_target_pairs={{1,0},{2,1},{3,2},{4,3},{5,4},{6,5},{7,6},{8,7},{9,8},{10,9},{11,1... | collective-permute-start | bytes 393224 | tf_op jit(solution)/shard_map/ppermute | solution.py:258
  2.9 13.1 %collective-permute-start = (bf16[256,256]{1,0:T(8,128)(2,1)S(1)}, bf16[256,256]{1,0:T(8,128)(2,1)S(1)}, u32[]{:S(2)}, u32[]{:S(2)}) collective-permute-start(bf16[256,256]{1,0:T(8,128)(2,1)S(1)} %get-tuple-element.47), channel_id=1, source_target_pairs={{0,1},{1,2},{2,3},{3,4},{4,5},{5,6},{6,7},{7,8},{8,9},{9,10},{10,1... | collective-permute-start | bytes 393224 | tf_op jit(solution)/shard_map/ppermute | solution.py:258
  38.6 17.0 %all-to-all-start.2 = ((bf16[8,32,384]{2,1,0:T(8,128)(2,1)}), bf16[8,32,384]{2,1,0:T(8,128)(2,1)S(1)}, u32[]{:S(2)}, u32[]{:S(2)}) async-start(bf16[8,32,384]{2,1,0:T(8,128)(2,1)} %add_up.3), calls=%async_computation.2 | async-start | bytes 393216 | tf_op jit(solution)/shard_map/all_to_all | solution.py:280
  44.7 7.3 %collective-permute-start.2 = (bf16[256,256]{1,0:T(8,128)(2,1)S(1)}, bf16[256,256]{1,0:T(8,128)(2,1)S(1)}, u32[]{:S(2)}, u32[]{:S(2)}) collective-permute-start(bf16[256,256]{1,0:T(8,128)(2,1)S(1)} %get-tuple-element.40), channel_id=1, source_target_pairs={{0,1},{1,2},{2,3},{3,4},{4,5},{5,6},{6,7},{7,8},{8,9},{9,10},{10,1... | collective-permute-start | bytes 393224 | tf_op jit(solution)/shard_map/ppermute | solution.py:258
  48.5 7.2 %collective-permute-start.3 = (bf16[256,256]{1,0:T(8,128)(2,1)S(1)}, bf16[256,256]{1,0:T(8,128)(2,1)S(1)}, u32[]{:S(2)}, u32[]{:S(2)}) collective-permute-start(bf16[256,256]{1,0:T(8,128)(2,1)S(1)} %get-tuple-element.41), channel_id=1, source_target_pairs={{1,0},{2,1},{3,2},{4,3},{5,4},{6,5},{7,6},{8,7},{9,8},{10,9},{11,1... | collective-permute-start | bytes 393224 | tf_op jit(solution)/shard_map/ppermute | solution.py:258

commit v3 on v2

v3 whole, which is shorter than its diff:
```python
import math

import jax
import jax.numpy as jnp
from jax import lax
from jax.experimental import pallas as pl
from jax.experimental.pallas import tpu as pltpu
from jax.sharding import PartitionSpec as P

BAND = 2
TAIL = 16
AXES = ("rows", "cols")
MIB = 1024 * 1024


def row_of(adj_ref, block, slots):
    return jnp.concatenate([adj_ref[block, slot] for slot in range(slots)], 1)


def pick(source, places, block_rows):
    return jnp.concatenate(
        [
            source[pl.ds(pl.multiple_of(place * block_rows, block_rows), block_rows)]
            for place in places
        ],
        0,
    )


def places_of(off_ref, cnt_ref, block, shift, dump, slots):
    return [
        jnp.where(slot < cnt_ref[block], block + shift + off_ref[slot, block], dump)
        for slot in range(slots)
    ]


def activate(preact, cotangent):
    gate = 1.0 / (1.0 + jnp.exp(-preact))
    grad = cotangent.astype(jnp.float32) * gate * (1.0 + preact * (1.0 - gate))
    return (preact * gate).astype(jnp.bfloat16), grad.astype(jnp.bfloat16)


def column_sums(grad):
    rows, width = grad.shape
    return jnp.sum(grad.astype(jnp.float32).reshape(rows // 8, 8, width), axis=0)


def to_upstream(weight, grad):
    return lax.dot_general(
        weight, grad, (((1,), (1,)), ((), ())), preferred_element_type=jnp.float32
    ).astype(jnp.bfloat16)


def weight_terms(agg, grad):
    return lax.dot_general(
        agg, grad, (((0,), (0,)), ((), ())), preferred_element_type=jnp.float32
    )


def inner_kernel(
    off_ref, cnt_ref, weight_hbm, bias_hbm, feat_hbm, adj_hbm, cot_hbm,
    act_hbm, grad_ref, partial_ref, sums_ref, weight_ref, bias_ref, feat_rim, adj_rim, cot_rim,
    feat, adj, cot, act, agg_all, sems,
):
    blocks, slots, block_rows, _ = adj_hbm.shape
    rows, width = feat_hbm.shape
    count = blocks - 2 * BAND
    rim = BAND * block_rows
    half = 2 * rim
    inner = count * block_rows
    copies = [
        pltpu.make_async_copy(feat_hbm, feat.at[pl.ds(0, rows)], sems.at[0]),
        pltpu.make_async_copy(adj_hbm.at[pl.ds(BAND, count)], adj, sems.at[1]),
        pltpu.make_async_copy(weight_hbm, weight_ref, sems.at[2]),
        pltpu.make_async_copy(bias_hbm, bias_ref, sems.at[3]),
        pltpu.make_async_copy(cot_hbm.at[pl.ds(rim, inner)], cot, sems.at[4]),
        pltpu.make_async_copy(feat_hbm.at[pl.ds(0, half)], feat_rim.at[pl.ds(0, half)], sems.at[5]),
        pltpu.make_async_copy(
            feat_hbm.at[pl.ds(rows - half, half)], feat_rim.at[pl.ds(half, half)], sems.at[6]
        ),
        pltpu.make_async_copy(adj_hbm.at[pl.ds(0, BAND)], adj_rim.at[pl.ds(0, BAND)], sems.at[7]),
        pltpu.make_async_copy(
            adj_hbm.at[pl.ds(blocks - BAND, BAND)], adj_rim.at[pl.ds(BAND, BAND)], sems.at[8]
        ),
        pltpu.make_async_copy(cot_hbm.at[pl.ds(0, rim)], cot_rim.at[pl.ds(0, rim)], sems.at[9]),
        pltpu.make_async_copy(
            cot_hbm.at[pl.ds(rows - rim, rim)], cot_rim.at[pl.ds(rim, rim)], sems.at[10]
        ),
    ]
    for copy in copies:
        copy.start()
    feat[rows:] = jnp.zeros((block_rows, width), jnp.bfloat16)
    for copy in copies[:5]:
        copy.wait()
    weight = weight_ref[...]
    bias = bias_ref[...]
    sums = jnp.zeros((8, width), jnp.float32)
    for step in range(0, count, 2):
        for block in (step, step + 1):
            places = places_of(off_ref, cnt_ref, block + BAND, 0, blocks, slots)
            agg_all[block * block_rows : (block + 1) * block_rows] = jnp.dot(
                row_of(adj, block, slots), pick(feat, places, block_rows),
                preferred_element_type=jnp.float32,
            ).astype(jnp.bfloat16)
        here = pl.ds(step * block_rows, 2 * block_rows)
        preact = jnp.dot(agg_all[here], weight, preferred_element_type=jnp.float32) + bias
        act[here], grad = activate(preact, cot[here])
        grad_ref[here] = grad
        sums = sums + column_sums(grad)
    act_out = pltpu.make_async_copy(act, act_hbm.at[pl.ds(rim, inner)], sems.at[11])
    act_out.start()
    sums_ref[...] = sums
    partial_ref[...] = weight_terms(agg_all[...], grad_ref[...])
    for copy in copies[5:]:
        copy.wait()
    act_out.wait()


def rim_places(off_ref, cnt_ref, step, blocks, slots):
    if step < BAND:
        return places_of(off_ref, cnt_ref, step, BAND, 6 * BAND, slots)
    block = blocks - 2 * BAND + step
    return places_of(off_ref, cnt_ref, block, 5 * BAND - blocks, 6 * BAND, slots)


def rim_kernel(
    off_ref, cnt_ref, side_ref, weight_ref, bias_ref, feat_ref, lower_ref, upper_ref, adj_ref,
    cot_ref, partial_ref, sums_ref,
    act_ref, grad_ref, send_ref, keep_ref,
    window, agg_all, payload,
):
    blocks = off_ref.shape[1]
    steps, slots, block_rows, _ = adj_ref.shape
    width = feat_ref.shape[1]
    rim = BAND * block_rows
    window[:rim] = lower_ref[...]
    window[rim : 5 * rim] = feat_ref[...]
    window[5 * rim : 6 * rim] = upper_ref[...]
    window[6 * rim :] = jnp.zeros((block_rows, width), jnp.bfloat16)
    weight = weight_ref[...]
    bias = bias_ref[...]
    sums = sums_ref[...]
    for step in range(0, steps, 2):
        for block in (step, step + 1):
            places = rim_places(off_ref, cnt_ref, block, blocks, slots)
            agg_all[block * block_rows : (block + 1) * block_rows] = jnp.dot(
                row_of(adj_ref, block, slots), pick(window, places, block_rows),
                preferred_element_type=jnp.float32,
            ).astype(jnp.bfloat16)
        here = pl.ds(step * block_rows, 2 * block_rows)
        preact = jnp.dot(agg_all[here], weight, preferred_element_type=jnp.float32) + bias
        act_ref[here], grad = activate(preact, cot_ref[here])
        grad_ref[here] = grad
        sums = sums + column_sums(grad)
    half = width // 2
    partial = partial_ref[...] + weight_terms(agg_all[...], grad_ref[...])
    payload[0, :half] = partial[:half]
    payload[1, :half] = partial[half:]
    tail = jnp.zeros((TAIL, width), jnp.float32)
    payload[0, half:] = jnp.broadcast_to(jnp.sum(sums, axis=0, keepdims=True), tail.shape)
    payload[1, half:] = tail
    side = side_ref[0]
    keep_ref[...] = payload[side]
    send_ref[...] = payload[1 - side]


def rim_back_kernel(
    off_ref, cnt_ref, weight_ref, adj_ref, grad_ref, act_ref, act_in,
    act_hbm, spread, lower_ref, upper_ref, mark_ref,
    sems,
):
    blocks = off_ref.shape[1]
    steps, slots, block_rows, _ = adj_ref.shape
    rim = BAND * block_rows
    rows = blocks * block_rows
    copies = [
        pltpu.make_async_copy(act_ref.at[pl.ds(0, rim)], act_hbm.at[pl.ds(0, rim)], sems.at[0]),
        pltpu.make_async_copy(
            act_ref.at[pl.ds(rim, rim)], act_hbm.at[pl.ds(rows - rim, rim)], sems.at[1]
        ),
    ]
    for copy in copies:
        copy.start()
    spread[...] = jnp.zeros_like(spread)
    weight = weight_ref[...]
    for step in range(steps):
        here = pl.ds(step * block_rows, block_rows)
        places = rim_places(off_ref, cnt_ref, step, blocks, slots)
        terms = jnp.dot(
            to_upstream(weight, grad_ref[here]), row_of(adj_ref, step, slots),
            preferred_element_type=jnp.float32,
        )
        for slot, place in enumerate(places):
            spread[place] += terms[:, slot * block_rows : (slot + 1) * block_rows]
    for block in range(BAND):
        here = pl.ds(block * block_rows, block_rows)
        lower_ref[here] = spread[block].T.astype(jnp.bfloat16)
        upper_ref[here] = spread[5 * BAND + block].T.astype(jnp.bfloat16)
    mark_ref[...] = jnp.zeros_like(mark_ref)
    for copy in copies:
        copy.wait()


def inner_back_kernel(
    off_ref, cnt_ref, weight_ref, adj_hbm, grad_ref, rim_spread,
    whole_hbm, edge_ref, mark_ref,
    adj, spread, out, sems,
):
    blocks, slots, block_rows, _ = adj_hbm.shape
    count = blocks - 2 * BAND
    rim = BAND * block_rows
    fetch = pltpu.make_async_copy(adj_hbm.at[pl.ds(BAND, count)], adj, sems.at[0])
    fetch.start()
    spread[: 2 * BAND] = rim_spread[BAND : 3 * BAND]
    spread[2 * BAND :] = jnp.zeros_like(spread[2 * BAND :])
    spread[blocks - 2 * BAND : blocks] = rim_spread[3 * BAND : 5 * BAND]
    weight = weight_ref[...]
    fetch.wait()
    for step in range(count):
        here = pl.ds(step * block_rows, block_rows)
        places = places_of(off_ref, cnt_ref, step + BAND, 0, blocks, slots)
        terms = jnp.dot(
            to_upstream(weight, grad_ref[here]), row_of(adj, step, slots),
            preferred_element_type=jnp.float32,
        )
        for slot, place in enumerate(places):
            spread[place] += terms[:, slot * block_rows : (slot + 1) * block_rows]
    for step in range(count):
        here = pl.ds(step * block_rows, block_rows)
        out[here] = spread[BAND + step].T.astype(jnp.bfloat16)
    finish = pltpu.make_async_copy(out, whole_hbm.at[pl.ds(rim, count * block_rows)], sems.at[1])
    finish.start()
    mark_ref[...] = jnp.zeros_like(mark_ref)
    for block in range(BAND):
        edge_ref[block * block_rows : (block + 1) * block_rows] = spread[block].T
        after = BAND + block
        edge_ref[after * block_rows : (after + 1) * block_rows] = spread[blocks - BAND + block].T
    finish.wait()


def edge_kernel(edge_ref, below_ref, above_ref, whole_in, whole_hbm, mark_ref, out, sems):
    rim = below_ref.shape[0]
    rows = whole_hbm.shape[0]
    out[:rim] = (edge_ref[:rim] + below_ref[...].astype(jnp.float32)).astype(jnp.bfloat16)
    out[rim:] = (edge_ref[rim:] + above_ref[...].astype(jnp.float32)).astype(jnp.bfloat16)
    copies = [
        pltpu.make_async_copy(out.at[pl.ds(0, rim)], whole_hbm.at[pl.ds(0, rim)], sems.at[0]),
        pltpu.make_async_copy(
            out.at[pl.ds(rim, rim)], whole_hbm.at[pl.ds(rows - rim, rim)], sems.at[1]
        ),
    ]
    for copy in copies:
        copy.start()
    mark_ref[...] = jnp.zeros_like(mark_ref)
    for copy in copies:
        copy.wait()


def add_kernel(left_ref, right_ref, *rest):
    total_ref = rest[-1]
    total = left_ref[...].astype(jnp.float32) + right_ref[...].astype(jnp.float32)
    total_ref[...] = total.astype(total_ref.dtype)


def last_kernel(scale, side_ref, own_ref, other_ref, weight_out, bias_out):
    half = weight_out.shape[0] // 2
    side = side_ref[0]
    own_rows = pl.ds(pl.multiple_of(side * half, half), half)
    other_rows = pl.ds(pl.multiple_of((1 - side) * half, half), half)
    weight_out[own_rows] = own_ref[:half] * scale
    weight_out[other_rows] = other_ref[:half] * scale
    first = jnp.where(side == 0, own_ref[half : half + 1], other_ref[half : half + 1])
    bias_out[...] = first * scale


def neighbour(value, steps, count):
    initial, last = max(0, -steps), min(count, count - steps)
    return lax.ppermute(value, AXES, [(source, source + steps) for source in range(initial, last)])


def add(left, right, dtype, after=()):
    return pl.pallas_call(
        add_kernel,
        out_shape=jax.ShapeDtypeStruct(left.shape, dtype),
        in_specs=[pl.BlockSpec(memory_space=pltpu.VMEM)] * 2
        + [pl.BlockSpec(memory_space=pl.ANY)] * len(after),
        compiler_params=pltpu.CompilerParams(vmem_limit_bytes=2 * MIB),
        cost_estimate=pl.CostEstimate(
            flops=left.size, bytes_accessed=6 * left.size, transcendentals=0
        ),
        name="add_halves",
    )(left, right, *after)


def swap(value, bits):
    return lax.ppermute(value, AXES, [(i, i ^ (1 << bit)) for i, bit in enumerate(bits)])


def sum_halves(send, keep, count, core_bit, marks):
    others = [bit for bit in range(count.bit_length() - 1) if bit != core_bit]
    orders = (others, others[::-1])
    total = add(keep, swap(send, [core_bit] * count), jnp.bfloat16, marks.get(0, ()))
    for step in range(len(others)):
        bits = [orders[(i >> core_bit) & 1][step] for i in range(count)]
        last = step == len(others) - 1
        dtype = jnp.float32 if last else jnp.bfloat16
        total = add(total, swap(total, bits), dtype, marks.get(-1 if last else step + 1, ()))
    return total


def on_device(features, adj_values, adj_offset, adj_count, weight, bias_vector, cotangent):
    blocks, slots = adj_offset.shape
    block_rows = adj_values.shape[2]
    rows, width = features.shape
    rim = BAND * block_rows
    inner = rows - 2 * rim
    cols = lax.axis_size("cols")
    count = lax.axis_size("rows") * cols
    smem = pl.BlockSpec(memory_space=pltpu.SMEM)
    vmem = pl.BlockSpec(memory_space=pltpu.VMEM)
    hbm = pl.BlockSpec(memory_space=pltpu.HBM)
    bias_row = bias_vector.reshape(1, width)

    def in_hbm(value):
        return pltpu.with_memory_space_constraint(value, pltpu.HBM)

    def shape(*sizes, dtype=jnp.bfloat16):
        return jax.ShapeDtypeStruct(sizes, dtype)

    def params(mib):
        return pltpu.CompilerParams(vmem_limit_bytes=mib * MIB)

    def cost(share):
        return pl.CostEstimate(
            flops=int(1.2e9 * share), bytes_accessed=int(6e6 * share),
            transcendentals=int(8e5 * share),
        )

    offsets = in_hbm(adj_offset.T)
    counts = in_hbm(adj_count)
    core_bit = cols.bit_length() - 1
    side = (lax.axis_index("rows") & 1).reshape(1)
    from_below = neighbour(features[rows - rim :], 1, count)
    from_above = neighbour(features[:rim], -1, count)
    (
        activated, grad_inner, partial, sums, weight_near, bias_near, feat_rim, adj_rim, cot_rim,
    ) = pl.pallas_call(
        inner_kernel,
        out_shape=(
            shape(rows, width),
            shape(inner, width),
            shape(width, width, dtype=jnp.float32),
            shape(8, width, dtype=jnp.float32),
            shape(width, width),
            shape(1, width, dtype=jnp.float32),
            shape(4 * rim, width),
            shape(2 * BAND, slots, block_rows, block_rows),
            shape(2 * rim, width),
        ),
        in_specs=[smem, smem] + [hbm] * 5,
        out_specs=(hbm,) + (vmem,) * 8,
        scratch_shapes=[
            pltpu.VMEM((rows + block_rows, width), jnp.bfloat16),
            pltpu.VMEM((blocks - 2 * BAND, slots, block_rows, block_rows), jnp.bfloat16),
            pltpu.VMEM((inner, width), jnp.bfloat16),
            pltpu.VMEM((inner, width), jnp.bfloat16),
            pltpu.VMEM((inner, width), jnp.bfloat16),
            pltpu.SemaphoreType.DMA((12,)),
        ],
        compiler_params=params(20),
        cost_estimate=cost(0.5),
        name="inner_rows",
    )(
        offsets, counts,
        *(in_hbm(x) for x in (weight, bias_row, features, adj_values, cotangent)),
    )
    half_shape = (width // 2 + TAIL, width)
    act_rim, grad_rim, send, keep = pl.pallas_call(
        rim_kernel,
        out_shape=(
            shape(2 * rim, width),
            shape(2 * rim, width),
            shape(*half_shape, dtype=jnp.float32),
            shape(*half_shape, dtype=jnp.float32),
        ),
        in_specs=[smem] * 3 + [vmem] * 9,
        out_specs=(vmem,) * 4,
        scratch_shapes=[
            pltpu.VMEM((6 * rim + block_rows, width), jnp.bfloat16),
            pltpu.VMEM((2 * rim, width), jnp.bfloat16),
            pltpu.VMEM((2,) + half_shape, jnp.float32),
        ],
        compiler_params=params(12),
        cost_estimate=cost(0.2),
        name="rim_rows",
    )(
        offsets, counts, side, weight_near, bias_near, feat_rim, from_below, from_above, adj_rim,
        cot_rim, partial, sums,
    )
    mark = shape(8, 128, dtype=jnp.float32)
    activated, rim_spread, lower_part, upper_part, first_mark = pl.pallas_call(
        rim_back_kernel,
        out_shape=(
            shape(rows, width),
            shape(6 * BAND + 1, width, block_rows, dtype=jnp.float32),
            shape(rim, width),
            shape(rim, width),
            mark,
        ),
        in_specs=[smem, smem] + [vmem] * 4 + [hbm],
        out_specs=(hbm,) + (vmem,) * 4,
        scratch_shapes=[pltpu.SemaphoreType.DMA((2,))],
        input_output_aliases={6: 0},
        compiler_params=params(12),
        cost_estimate=cost(0.2),
        name="rim_rows_back",
    )(offsets, counts, weight_near, adj_rim, grad_rim, act_rim, activated)
    from_above_dev = neighbour(lower_part, -1, count)
    from_below_dev = neighbour(upper_part, 1, count)
    grad_whole, edges, second_mark = pl.pallas_call(
        inner_back_kernel,
        out_shape=(shape(rows, width), shape(2 * rim, width, dtype=jnp.float32), mark),
        in_specs=[smem, smem, vmem, hbm, vmem, vmem],
        out_specs=(hbm, vmem, vmem),
        scratch_shapes=[
            pltpu.VMEM((blocks - 2 * BAND, slots, block_rows, block_rows), jnp.bfloat16),
            pltpu.VMEM((blocks + 1, width, block_rows), jnp.float32),
            pltpu.VMEM((inner, width), jnp.bfloat16),
            pltpu.SemaphoreType.DMA((2,)),
        ],
        compiler_params=params(12),
        cost_estimate=cost(0.3),
        name="inner_rows_back",
    )(offsets, counts, weight_near, in_hbm(adj_values), grad_inner, rim_spread)
    grad_features, third_mark = pl.pallas_call(
        edge_kernel,
        out_shape=(shape(rows, width), mark),
        in_specs=[vmem] * 3 + [hbm],
        out_specs=(hbm, vmem),
        scratch_shapes=[
            pltpu.VMEM((2 * rim, width), jnp.bfloat16),
            pltpu.SemaphoreType.DMA((2,)),
        ],
        input_output_aliases={3: 0},
        compiler_params=params(8),
        cost_estimate=cost(0.05),
        name="join_edges",
    )(edges, from_below_dev, from_above_dev, grad_whole)
    marks = {0: (first_mark,), 2: (second_mark,), -1: (third_mark,)}
    own_half = sum_halves(send, keep, count, core_bit, marks)
    other_half = swap(own_half, [core_bit] * count)
    norm_scale = 1.0 / math.sqrt(rows * count)
    grad_weight, grad_bias = pl.pallas_call(
        lambda *refs: last_kernel(norm_scale, *refs),
        out_shape=(
            shape(width, width, dtype=jnp.float32),
            shape(1, width, dtype=jnp.float32),
        ),
        in_specs=[smem, vmem, vmem],
        out_specs=(vmem, vmem),
        compiler_params=params(8),
        name="last_step",
    )(side, own_half, other_half)
    return (activated, grad_features, grad_weight, grad_bias.reshape(width))


def solution(mesh):
    return jax.shard_map(
        on_device,
        mesh=mesh,
        in_specs=(
            P(AXES, None),
            P(AXES, None, None, None),
            P(AXES, None),
            P(AXES),
            P(),
            P(),
            P(AXES, None),
        ),
        out_specs=(P(AXES, None), P(AXES, None), P(), P()),
        check_vma=False,
    )
```

time: 57.6 us -> 47.3 us (0.82)
  blocking collectives: 19.9 us -> 0 us
  starting transfers between devices: 15.3 us -> 23.6 us
  waiting for transfers between devices: 5.87 us -> 7.32 us
    all_to_all x2 -> x0, blocking collectives: 19.9 us -> none  [the longest x1 10.3 us: sum_devices(): lax.all_to_all(payload, GROUP, 0, 0, tiled=True)]
    ppermute x0 -> x6, starting transfers between devices: none -> 11.7 us  [swap(): lax.ppermute(value, AXES, [(i, i ^ 1 << bit) for i, bit in enumerate(bits)])]
    ppermute x0 -> x6, waiting for transfers between devices: none -> 6.45 us  [swap(): lax.ppermute(value, AXES, [(i, i ^ 1 << bit) for i, bit in enumerate(bits)])]
    ppermute x4, waiting for transfers between devices: 5.86 us -> 0.87 us  [neighbour(): lax.ppermute(value, AXES, [(source, source + steps) for source in range(i...]
    all_to_all x1 -> x0, starting transfers between devices: 3.39 us -> none  [sum_devices(): lax.all_to_all(add_up(shares, group).reshape(rows, lanes), GROUP, 0, 0, t...]
    pallas_call x4 -> x9, Pallas kernels: 10.9 us -> 11.8 us  [the longest x1 4.51 us: on_device(): pl.pallas_call(inner_back_kernel, out_shape=(shape(rows, width), shape(2...]
    pallas_call x1, Pallas kernels: 1.49 us -> 0.73 us  [on_device(): pl.pallas_call(lambda *refs: last_kernel(norm_scale, *refs), out_shape=(s...]
  transfers between devices with their start and end apart: 5 -> 10, of which waited for: 2 -> 4; matrix products, arithmetic and copies ran while one was open for 0% -> 0% of each run, Pallas kernels for 18% -> 25%
where the time goes in v3:
time: 47.3 us; the launch traced here: 47 us
  starting transfers between devices  23.6 us (50%)
  Pallas kernels  14.3 us (30%)
  waiting for transfers between devices  7.32 us (15%)
  local copies, waits for them, and re-layouts  0.99 us (2%)
  between operations  0.79 us (2%)
    ppermute x4, starting transfers between devices, neighbour(): lax.ppermute(value, AXES, [(source, source + steps) for source in range(i...  11.9 us
    ppermute x6, starting transfers between devices, swap(): lax.ppermute(value, AXES, [(i, i ^ 1 << bit) for i, bit in enumerate(bits)])  11.7 us
    ppermute x6, waiting for transfers between devices, swap(): lax.ppermute(value, AXES, [(i, i ^ 1 << bit) for i, bit in enumerate(bits)])  6.45 us
    pallas_call x1, Pallas kernels, on_device(): pl.pallas_call(inner_back_kernel, out_shape=(shape(rows, width), shape(2...  4.51 us
    pallas_call x1, Pallas kernels, on_device(): pl.pallas_call(inner_kernel, out_shape=(shape(rows, width), shape(inner,...  4.41 us
    pallas_call x1, Pallas kernels, on_device(): pl.pallas_call(rim_back_kernel, out_shape=(shape(rows, width), shape(6 *...  2.02 us
    pallas_call x1, Pallas kernels, on_device(): pl.pallas_call(rim_kernel, out_shape=(shape(2 * rim, width), shape(2 * ri...  1.71 us
    slice x1, local copies, waits for them, and re-layouts, on_device(): from_above = neighbour(features[:rim], -1, count)  0.99 us
  transfers between devices with their start and end apart: 10, of which 4 were waited for; matrix products, arithmetic and copies ran while one was open for 0% of the time, Pallas kernels for 25%

profile of v3, /device:TPU:0, one launch (start us, length us, event | category | flops | bytes accessed | tf_op | source)
XLA Modules:
  0.0 47.0 jit_solution(2114460785710261531)
XLA Ops:
  0.6 1.0 %fusion = (bf16[256,256]{1,0:T(8,128)(2,1)S(1)}, bf16[256,256]{1,0:T(8,128)(2,1)S(1)}) fusion(bf16[1536,256]{1,0:T(8,128)(2,1)} %feat_hbm.1), kind=kLoop, calls=%fused_computation | loop fusion | bytes 524288 | tf_op jit(solution)/shard_map/slice | solution.py:344
  1.6 1.3 %collective-permute-start.1 = (bf16[256,256]{1,0:T(8,128)(2,1)S(1)}, bf16[256,256]{1,0:T(8,128)(2,1)S(1)}, u32[]{:S(2)}, u32[]{:S(2)}) collective-permute-start(bf16[256,256]{1,0:T(8,128)(2,1)S(1)} %get-tuple-element.54), channel_id=1, source_target_pairs={{1,0},{2,1},{3,2},{4,3},{5,4},{6,5},{7,6},{8,7},{9,8},{10,9},{11,1... | collective-permute-start | bytes 393224 | tf_op jit(solution)/shard_map/ppermute | solution.py:278
  2.9 5.5 %collective-permute-start = (bf16[256,256]{1,0:T(8,128)(2,1)S(1)}, bf16[256,256]{1,0:T(8,128)(2,1)S(1)}, u32[]{:S(2)}, u32[]{:S(2)}) collective-permute-start(bf16[256,256]{1,0:T(8,128)(2,1)S(1)} %get-tuple-element.55), channel_id=1, source_target_pairs={{0,1},{1,2},{2,3},{3,4},{4,5},{5,6},{6,7},{7,8},{8,9},{9,10},{10,1... | collective-permute-start | bytes 393224 | tf_op jit(solution)/shard_map/ppermute | solution.py:278
  8.4 4.4 %inner_rows.1 = (bf16[1536,256]{1,0:T(8,128)(2,1)}, bf16[1024,256]{1,0:T(8,128)(2,1)S(1)}, f32[256,256]{1,0:T(8,128)S(1)}, f32[8,256]{1,0:T(8,128)S(1)}, bf16[25...) custom-call(s32[3,12]{1,0:T(4,128)} %bitcast.4, ...), custom_call_target="tpu_custom_call" | custom-call | flops 600000000 | bytes 3000000 | tf_op jit(solution)/shard_map/inner_rows/pallas_call | solution.py:347
  12.9 0.0 collective-permute-done.1.upper_ref
  12.9 0.0 collective-permute-done.lower_ref
  12.9 1.7 %rim_rows.1 = (bf16[512,256]{1,0:T(8,128)(2,1)S(1)}, bf16[512,256]{1,0:T(8,128)(2,1)S(1)}, f32[144,256]{1,0:T(8,128)S(1)}, f32[144,256]{1,0:T(8,128)S(1)}) custom-call(s32[3,12]{1,0:T(4,128)} %bitcast.5, s32[12]{0:T(128)} %cnt_ref.7, s32[1]{0:T(128)} %bitcast.2.side_ref.refs_0_, bf16[256,256]{1,0:T(8,128)(2,1)S(1)} %get-tuple-element.29.weight_ref, ...), custom_call_target="tpu_custom_call" | custom-call | flops 240000000 | bytes 1200000 | tf_op jit(solution)/shard_map/rim_rows/pallas_call | solution.py:378
  14.6 0.2 collective-permute-start.4
  14.8 2.0 %rim_rows_back.1 = (bf16[1536,256]{1,0:T(8,128)(2,1)}, f32[13,256,128]{2,1,0:T(8,128)S(1)}, bf16[256,256]{1,0:T(8,128)(2,1)S(1)}, bf16[256,256]{1,0:T(8,128)(2,1)S(1)}, f32[8,128]{1,0:T(8,128)S(1)}) custom-call(s32[3,12]{1,0:T(4,128)} %bitcast.6, s32[12]{0:T(128)} %cnt_ref.7, ...), custom_call_target="tpu_custom_call", output_to_operand_aliasing={{0}: (6, {})} | custom-call | flops 240000000 | bytes 1200000 | tf_op jit(solution)/shard_map/rim_rows_back/pallas_call | solution.py:401
  16.8 0.0 collective-permute-done.4.right_ref
  16.8 2.4 %collective-permute-start.5 = (bf16[144,256]{1,0:T(8,128)(2,1)S(1)}, bf16[144,256]{1,0:T(8,128)(2,1)S(1)}, u32[]{:S(2)}, u32[]{:S(2)}) collective-permute-start(bf16[144,256]{1,0:T(8,128)(2,1)S(1)} %add_halves.5.left_ref), channel_id=1, source_target_pairs={{0,1},{1,0},{2,18},{3,19},{4,5},{5,4},{6,22},{7,23},{8,9},{9,8},{1... | collective-permute-start | bytes 221192 | tf_op jit(solution)/shard_map/ppermute | solution.py:296
  19.2 2.3 %collective-permute-done.5.right_ref = bf16[144,256]{1,0:T(8,128)(2,1)S(1)} collective-permute-done((bf16[144,256]{1,0:T(8,128)(2,1)S(1)}, bf16[144,256]{1,0:T(8,128)(2,1)S(1)}, u32[]{:S(2)}, u32[]{:S(2)}) %collective-permute-start.5) | collective-permute-done | bytes 73760 | tf_op jit(solution)/shard_map/ppermute | solution.py:296
  21.6 2.5 %collective-permute-start.6 = (bf16[144,256]{1,0:T(8,128)(2,1)S(1)}, bf16[144,256]{1,0:T(8,128)(2,1)S(1)}, u32[]{:S(2)}, u32[]{:S(2)}) collective-permute-start(bf16[144,256]{1,0:T(8,128)(2,1)S(1)} %add_halves.6.left_ref), channel_id=1, source_target_pairs={{0,4},{1,5},{2,10},{3,11},{4,0},{5,1},{6,14},{7,15},{8,12},{9,13},... | collective-permute-start | bytes 221192 | tf_op jit(solution)/shard_map/ppermute | solution.py:296
  24.1 4.5 %inner_rows_back.1 = (bf16[1536,256]{1,0:T(8,128)(2,1)}, f32[512,256]{1,0:T(8,128)S(1)}, f32[8,128]{1,0:T(8,128)S(1)}) custom-call(s32[3,12]{1,0:T(4,128)} %bitcast.7, s32[12]{0:T(128)} %cnt_ref.7, bf16[256,256]{1,0:T(8,128)(2,1)S(1)} %get-tuple-element.29.weight_ref, bf16[12,3,128,128]{3,2,1,0:T(8,128)(2,1)} %adj_hbm.3, ...), custom_call_target="tpu_custom_call" | custom-call | flops 360000000 | bytes 1800000 | tf_op jit(solution)/shard_map/inner_rows_back/pallas_call | solution.py:420
  28.7 0.0 collective-permute-done.6.right_ref
  28.7 1.6 %collective-permute-start.7 = (bf16[144,256]{1,0:T(8,128)(2,1)S(1)}, bf16[144,256]{1,0:T(8,128)(2,1)S(1)}, u32[]{:S(2)}, u32[]{:S(2)}) collective-permute-start(bf16[144,256]{1,0:T(8,128)(2,1)S(1)} %add_halves.7.left_ref), channel_id=1, source_target_pairs={{0,8},{1,9},{2,6},{3,7},{4,12},{5,13},{6,2},{7,3},{8,0},{9,1},{10,... | collective-permute-start | bytes 221192 | tf_op jit(solution)/shard_map/ppermute | solution.py:296
  30.3 3.8 %collective-permute-start.2 = (bf16[256,256]{1,0:T(8,128)(2,1)S(1)}, bf16[256,256]{1,0:T(8,128)(2,1)S(1)}, u32[]{:S(2)}, u32[]{:S(2)}) collective-permute-start(bf16[256,256]{1,0:T(8,128)(2,1)S(1)} %get-tuple-element.43), channel_id=1, source_target_pairs={{0,1},{1,2},{2,3},{3,4},{4,5},{5,6},{6,7},{7,8},{8,9},{9,10},{10,1... | collective-permute-start | bytes 393224 | tf_op jit(solution)/shard_map/ppermute | solution.py:278
  34.2 1.3 %collective-permute-start.3 = (bf16[256,256]{1,0:T(8,128)(2,1)S(1)}, bf16[256,256]{1,0:T(8,128)(2,1)S(1)}, u32[]{:S(2)}, u32[]{:S(2)}) collective-permute-start(bf16[256,256]{1,0:T(8,128)(2,1)S(1)} %get-tuple-element.44), channel_id=1, source_target_pairs={{1,0},{2,1},{3,2},{4,3},{5,4},{6,5},{7,6},{8,7},{9,8},{10,9},{11,1... | collective-permute-start | bytes 393224 | tf_op jit(solution)/shard_map/ppermute | solution.py:278
  35.5 0.0 collective-permute-done.7.right_ref
  35.5 4.9 %collective-permute-start.8 = (bf16[144,256]{1,0:T(8,128)(2,1)S(1)}, bf16[144,256]{1,0:T(8,128)(2,1)S(1)}, u32[]{:S(2)}, u32[]{:S(2)}) collective-permute-start(bf16[144,256]{1,0:T(8,128)(2,1)S(1)} %add_halves.8.left_ref), channel_id=1, source_target_pairs={{0,16},{1,17},{2,3},{3,2},{4,20},{5,21},{6,7},{7,6},{8,24},{9,25},... | collective-permute-start | bytes 221192 | tf_op jit(solution)/shard_map/ppermute | solution.py:296
  40.4 0.0 collective-permute-done.2.below_ref
  40.4 0.9 %collective-permute-done.3.above_ref = bf16[256,256]{1,0:T(8,128)(2,1)S(1)} collective-permute-done((bf16[256,256]{1,0:T(8,128)(2,1)S(1)}, bf16[256,256]{1,0:T(8,128)(2,1)S(1)}, u32[]{:S(2)}, u32[]{:S(2)}) %collective-permute-start.3) | collective-permute-done | bytes 131104 | tf_op jit(solution)/shard_map/ppermute | solution.py:278
  41.3 0.8 %join_edges.1 = (bf16[1536,256]{1,0:T(8,128)(2,1)}, f32[8,128]{1,0:T(8,128)S(1)}) custom-call(f32[512,256]{1,0:T(8,128)S(1)} %get-tuple-element.42.edge_ref, bf16[256,256]{1,0:T(8,128)(2,1)S(1)} %collective-permute-done.2.below_ref, bf16[256,256]{1,0:T(8,128)(2,1)S(1)} %collective-permute-done.3.above_ref, ...), custom_call_target="tpu_custom_call", output_to_operand_aliasing={{0}: (3, {})} | custom-call | flops 60000000 | bytes 300000 | tf_op jit(solution)/shard_map/join_edges/pallas_call | solution.py:435
  42.0 2.8 %collective-permute-done.8.right_ref = bf16[144,256]{1,0:T(8,128)(2,1)S(1)} collective-permute-done((bf16[144,256]{1,0:T(8,128)(2,1)S(1)}, bf16[144,256]{1,0:T(8,128)(2,1)S(1)}, u32[]{:S(2)}, u32[]{:S(2)}) %collective-permute-start.8) | collective-permute-done | bytes 73760 | tf_op jit(solution)/shard_map/ppermute | solution.py:296
  44.8 0.1 collective-permute-start.9
  44.9 1.4 %collective-permute-done.9.refs_2_ = f32[144,256]{1,0:T(8,128)S(1)} collective-permute-done((f32[144,256]{1,0:T(8,128)S(1)}, f32[144,256]{1,0:T(8,128)S(1)}, u32[]{:S(2)}, u32[]{:S(2)}) %collective-permute-start.9) | collective-permute-done | bytes 147488 | tf_op jit(solution)/shard_map/ppermute | solution.py:296
  46.3 0.7 %last_step.1 = (f32[256,256]{1,0:T(8,128)}, f32[1,256]{1,0:T(1,128)}) custom-call(s32[1]{0:T(128)} %bitcast.2.side_ref.refs_0_, f32[144,256]{1,0:T(8,128)S(1)} %add_halves.9.refs_1_, f32[144,256]{1,0:T(8,128)S(1)} %collective-permute-done.9.refs_2_), custom_call_target="tpu_custom_call" | custom-call | tf_op jit(solution)/shard_map/last_step/pallas_call | solution.py:453
  (5 shorter events, 0.1 us)
Async XLA Ops:
  1.6 11.2 %collective-permute-start.1 = (bf16[256,256]{1,0:T(8,128)(2,1)S(1)}, bf16[256,256]{1,0:T(8,128)(2,1)S(1)}, u32[]{:S(2)}, u32[]{:S(2)}) collective-permute-start(bf16[256,256]{1,0:T(8,128)(2,1)S(1)} %get-tuple-element.54), channel_id=1, source_target_pairs={{1,0},{2,1},{3,2},{4,3},{5,4},{6,5},{7,6},{8,7},{9,8},{10,9},{11,1... | collective-permute-start | bytes 393224 | tf_op jit(solution)/shard_map/ppermute | solution.py:278
  2.9 9.9 %collective-permute-start = (bf16[256,256]{1,0:T(8,128)(2,1)S(1)}, bf16[256,256]{1,0:T(8,128)(2,1)S(1)}, u32[]{:S(2)}, u32[]{:S(2)}) collective-permute-start(bf16[256,256]{1,0:T(8,128)(2,1)S(1)} %get-tuple-element.55), channel_id=1, source_target_pairs={{0,1},{1,2},{2,3},{3,4},{4,5},{5,6},{6,7},{7,8},{8,9},{9,10},{10,1... | collective-permute-start | bytes 393224 | tf_op jit(solution)/shard_map/ppermute | solution.py:278
  14.6 2.2 %collective-permute-start.4 = (f32[144,256]{1,0:T(8,128)S(1)}, f32[144,256]{1,0:T(8,128)S(1)}, u32[]{:S(2)}, u32[]{:S(2)}) collective-permute-start(f32[144,256]{1,0:T(8,128)S(1)} %get-tuple-element.48), channel_id=1, source_target_pairs={{0,2},{1,3},{2,0},{3,1},{4,6},{5,7},{6,4},{7,5},{8,10},{9,11},{10,... | collective-permute-start | bytes 442376 | tf_op jit(solution)/shard_map/ppermute | solution.py:296
  16.8 4.7 %collective-permute-start.5 = (bf16[144,256]{1,0:T(8,128)(2,1)S(1)}, bf16[144,256]{1,0:T(8,128)(2,1)S(1)}, u32[]{:S(2)}, u32[]{:S(2)}) collective-permute-start(bf16[144,256]{1,0:T(8,128)(2,1)S(1)} %add_halves.5.left_ref), channel_id=1, source_target_pairs={{0,1},{1,0},{2,18},{3,19},{4,5},{5,4},{6,22},{7,23},{8,9},{9,8},{1... | collective-permute-start | bytes 221192 | tf_op jit(solution)/shard_map/ppermute | solution.py:296
  21.6 7.1 %collective-permute-start.6 = (bf16[144,256]{1,0:T(8,128)(2,1)S(1)}, bf16[144,256]{1,0:T(8,128)(2,1)S(1)}, u32[]{:S(2)}, u32[]{:S(2)}) collective-permute-start(bf16[144,256]{1,0:T(8,128)(2,1)S(1)} %add_halves.6.left_ref), channel_id=1, source_target_pairs={{0,4},{1,5},{2,10},{3,11},{4,0},{5,1},{6,14},{7,15},{8,12},{9,13},... | collective-permute-start | bytes 221192 | tf_op jit(solution)/shard_map/ppermute | solution.py:296
  28.7 6.8 %collective-permute-start.7 = (bf16[144,256]{1,0:T(8,128)(2,1)S(1)}, bf16[144,256]{1,0:T(8,128)(2,1)S(1)}, u32[]{:S(2)}, u32[]{:S(2)}) collective-permute-start(bf16[144,256]{1,0:T(8,128)(2,1)S(1)} %add_halves.7.left_ref), channel_id=1, source_target_pairs={{0,8},{1,9},{2,6},{3,7},{4,12},{5,13},{6,2},{7,3},{8,0},{9,1},{10,... | collective-permute-start | bytes 221192 | tf_op jit(solution)/shard_map/ppermute | solution.py:296
  30.3 10.1 %collective-permute-start.2 = (bf16[256,256]{1,0:T(8,128)(2,1)S(1)}, bf16[256,256]{1,0:T(8,128)(2,1)S(1)}, u32[]{:S(2)}, u32[]{:S(2)}) collective-permute-start(bf16[256,256]{1,0:T(8,128)(2,1)S(1)} %get-tuple-element.43), channel_id=1, source_target_pairs={{0,1},{1,2},{2,3},{3,4},{4,5},{5,6},{6,7},{7,8},{8,9},{9,10},{10,1... | collective-permute-start | bytes 393224 | tf_op jit(solution)/shard_map/ppermute | solution.py:278
  34.2 7.1 %collective-permute-start.3 = (bf16[256,256]{1,0:T(8,128)(2,1)S(1)}, bf16[256,256]{1,0:T(8,128)(2,1)S(1)}, u32[]{:S(2)}, u32[]{:S(2)}) collective-permute-start(bf16[256,256]{1,0:T(8,128)(2,1)S(1)} %get-tuple-element.44), channel_id=1, source_target_pairs={{1,0},{2,1},{3,2},{4,3},{5,4},{6,5},{7,6},{8,7},{9,8},{10,9},{11,1... | collective-permute-start | bytes 393224 | tf_op jit(solution)/shard_map/ppermute | solution.py:278
  35.5 9.3 %collective-permute-start.8 = (bf16[144,256]{1,0:T(8,128)(2,1)S(1)}, bf16[144,256]{1,0:T(8,128)(2,1)S(1)}, u32[]{:S(2)}, u32[]{:S(2)}) collective-permute-start(bf16[144,256]{1,0:T(8,128)(2,1)S(1)} %add_halves.8.left_ref), channel_id=1, source_target_pairs={{0,16},{1,17},{2,3},{3,2},{4,20},{5,21},{6,7},{7,6},{8,24},{9,25},... | collective-permute-start | bytes 221192 | tf_op jit(solution)/shard_map/ppermute | solution.py:296
  44.8 1.4 %collective-permute-start.9 = (f32[144,256]{1,0:T(8,128)S(1)}, f32[144,256]{1,0:T(8,128)S(1)}, u32[]{:S(2)}, u32[]{:S(2)}) collective-permute-start(f32[144,256]{1,0:T(8,128)S(1)} %add_halves.9.refs_1_), channel_id=1, source_target_pairs={{0,2},{1,3},{2,0},{3,1},{4,6},{5,7},{6,4},{7,5},{8,10},{9,11},{10,... | collective-permute-start | bytes 442376 | tf_op jit(solution)/shard_map/ppermute | solution.py:296

commit v4 on v3

--- a/solution.py
+++ b/solution.py
@@ -1,3 +1,4 @@
+import functools
 import math
 
 import jax
@@ -32,6 +33,32 @@
         jnp.where(slot < cnt_ref[block], block + shift + off_ref[slot, block], dump)
         for slot in range(slots)
     ]
+
+
+def place_in_mesh():
+    return lax.axis_index("rows") * lax.axis_size("cols") + lax.axis_index("cols")
+
+
+def core_side():
+    return lax.axis_index("rows") & 1
+
+
+def halo_kernel(feat_hbm, first_ref, second_ref, sems):
+    rows = feat_hbm.shape[0]
+    rim = first_ref.shape[0]
+    odd = place_in_mesh() & 1
+    last = rows - rim
+    starts = ((1 - odd) * last, odd * last)
+    copies = [
+        pltpu.make_async_copy(
+            feat_hbm.at[pl.ds(pl.multiple_of(start, rim), rim)], out_ref, sems.at[i]
+        )
+        for i, (start, out_ref) in enumerate(zip(starts, (first_ref, second_ref)))
+    ]
+    for copy in copies:
+        copy.start()
+    for copy in copies:
+        copy.wait()
 
 
 def activate(preact, cotangent):
@@ -124,7 +151,7 @@
 
 
 def rim_kernel(
-    off_ref, cnt_ref, side_ref, weight_ref, bias_ref, feat_ref, lower_ref, upper_ref, adj_ref,
+    off_ref, cnt_ref, weight_ref, bias_ref, feat_ref, first_ref, second_ref, adj_ref,
     cot_ref, partial_ref, sums_ref,
     act_ref, grad_ref, send_ref, keep_ref,
     window, agg_all, payload,
@@ -133,9 +160,10 @@
     steps, slots, block_rows, _ = adj_ref.shape
     width = feat_ref.shape[1]
     rim = BAND * block_rows
-    window[:rim] = lower_ref[...]
+    odd = place_in_mesh() & 1
+    window[pl.ds(pl.multiple_of((1 - odd) * 5 * rim, rim), rim)] = first_ref[...]
+    window[pl.ds(pl.multiple_of(odd * 5 * rim, rim), rim)] = second_ref[...]
     window[rim : 5 * rim] = feat_ref[...]
-    window[5 * rim : 6 * rim] = upper_ref[...]
     window[6 * rim :] = jnp.zeros((block_rows, width), jnp.bfloat16)
     weight = weight_ref[...]
     bias = bias_ref[...]
@@ -159,14 +187,14 @@
     tail = jnp.zeros((TAIL, width), jnp.float32)
     payload[0, half:] = jnp.broadcast_to(jnp.sum(sums, axis=0, keepdims=True), tail.shape)
     payload[1, half:] = tail
-    side = side_ref[0]
+    side = core_side()
     keep_ref[...] = payload[side]
     send_ref[...] = payload[1 - side]
 
 
 def rim_back_kernel(
     off_ref, cnt_ref, weight_ref, adj_ref, grad_ref, act_ref, act_in,
-    act_hbm, spread, lower_ref, upper_ref, mark_ref,
+    act_hbm, spread, first_ref, second_ref, mark_ref,
     sems,
 ):
     blocks = off_ref.shape[1]
@@ -192,45 +220,71 @@
         )
         for slot, place in enumerate(places):
             spread[place] += terms[:, slot * block_rows : (slot + 1) * block_rows]
+    odd = place_in_mesh() & 1
     for block in range(BAND):
         here = pl.ds(block * block_rows, block_rows)
-        lower_ref[here] = spread[block].T.astype(jnp.bfloat16)
-        upper_ref[here] = spread[5 * BAND + block].T.astype(jnp.bfloat16)
+        first_ref[here] = spread[(1 - odd) * 5 * BAND + block].T.astype(jnp.bfloat16)
+        second_ref[here] = spread[odd * 5 * BAND + block].T.astype(jnp.bfloat16)
     mark_ref[...] = jnp.zeros_like(mark_ref)
     for copy in copies:
         copy.wait()
 
 
-def inner_back_kernel(
-    off_ref, cnt_ref, weight_ref, adj_hbm, grad_ref, rim_spread,
+def scatter_rows(off_ref, cnt_ref, weight, adj, grad_ref, spread, steps, blocks, slots):
+    block_rows = adj.shape[2]
+    for i, step in enumerate(steps):
+        here = pl.ds(step * block_rows, block_rows)
+        places = places_of(off_ref, cnt_ref, step + BAND, 0, blocks, slots)
+        terms = jnp.dot(
+            to_upstream(weight, grad_ref[here]), row_of(adj, i, slots),
+            preferred_element_type=jnp.float32,
+        )
+        for slot, place in enumerate(places):
+            spread[place] += terms[:, slot * block_rows : (slot + 1) * block_rows]
+
+
+def inner_back_first(
+    off_ref, cnt_ref, weight_ref, adj_hbm, grad_ref, rim_spread, spread, mark_ref, adj, sems
+):
+    blocks, slots, _, _ = adj_hbm.shape
+    count = adj.shape[0]
+    fetch = pltpu.make_async_copy(adj_hbm.at[pl.ds(BAND, count)], adj, sems.at[0])
+    fetch.start()
+    spread[: 2 * BAND] = rim_spread[BAND : 3 * BAND]
+    spread[2 * BAND :] = jnp.zeros_like(spread[2 * BAND :])
+    spread[blocks - 2 * BAND : blocks] = rim_spread[3 * BAND : 5 * BAND]
+    mark_ref[...] = jnp.zeros_like(mark_ref)
+    fetch.wait()
+    scatter_rows(
+        off_ref, cnt_ref, weight_ref[...], adj, grad_ref, spread, range(count), blocks, slots
+    )
+
+
+def inner_back_second(
+    off_ref, cnt_ref, weight_ref, adj_hbm, grad_ref, half_spread,
     whole_hbm, edge_ref, mark_ref,
     adj, spread, out, sems,
 ):
     blocks, slots, block_rows, _ = adj_hbm.shape
     count = blocks - 2 * BAND
+    first = count - adj.shape[0]
     rim = BAND * block_rows
-    fetch = pltpu.make_async_copy(adj_hbm.at[pl.ds(BAND, count)], adj, sems.at[0])
+    fetch = pltpu.make_async_copy(
+        adj_hbm.at[pl.ds(BAND + first, count - first)], adj, sems.at[0]
+    )
     fetch.start()
-    spread[: 2 * BAND] = rim_spread[BAND : 3 * BAND]
-    spread[2 * BAND :] = jnp.zeros_like(spread[2 * BAND :])
-    spread[blocks - 2 * BAND : blocks] = rim_spread[3 * BAND : 5 * BAND]
-    weight = weight_ref[...]
+    spread[...] = half_spread[...]
+    mark_ref[...] = jnp.zeros_like(mark_ref)
     fetch.wait()
-    for step in range(count):
-        here = pl.ds(step * block_rows, block_rows)
-        places = places_of(off_ref, cnt_ref, step + BAND, 0, blocks, slots)
-        terms = jnp.dot(
-            to_upstream(weight, grad_ref[here]), row_of(adj, step, slots),
-            preferred_element_type=jnp.float32,
-        )
-        for slot, place in enumerate(places):
-            spread[place] += terms[:, slot * block_rows : (slot + 1) * block_rows]
+    scatter_rows(
+        off_ref, cnt_ref, weight_ref[...], adj, grad_ref, spread, range(first, count), blocks,
+        slots,
+    )
     for step in range(count):
         here = pl.ds(step * block_rows, block_rows)
         out[here] = spread[BAND + step].T.astype(jnp.bfloat16)
     finish = pltpu.make_async_copy(out, whole_hbm.at[pl.ds(rim, count * block_rows)], sems.at[1])
     finish.start()
-    mark_ref[...] = jnp.zeros_like(mark_ref)
     for block in range(BAND):
         edge_ref[block * block_rows : (block + 1) * block_rows] = spread[block].T
         after = BAND + block
@@ -238,11 +292,13 @@
     finish.wait()
 
 
-def edge_kernel(edge_ref, below_ref, above_ref, whole_in, whole_hbm, mark_ref, out, sems):
-    rim = below_ref.shape[0]
+def edge_kernel(edge_ref, first_ref, second_ref, whole_in, whole_hbm, mark_ref, out, sems):
+    rim = first_ref.shape[0]
     rows = whole_hbm.shape[0]
-    out[:rim] = (edge_ref[:rim] + below_ref[...].astype(jnp.float32)).astype(jnp.bfloat16)
-    out[rim:] = (edge_ref[rim:] + above_ref[...].astype(jnp.float32)).astype(jnp.bfloat16)
+    odd = place_in_mesh() & 1
+    for base, spill_ref in (((1 - odd) * rim, first_ref), (odd * rim, second_ref)):
+        here = pl.ds(pl.multiple_of(base, rim), rim)
+        out[here] = (edge_ref[here] + spill_ref[...].astype(jnp.float32)).astype(jnp.bfloat16)
     copies = [
         pltpu.make_async_copy(out.at[pl.ds(0, rim)], whole_hbm.at[pl.ds(0, rim)], sems.at[0]),
         pltpu.make_async_copy(
@@ -256,15 +312,17 @@
         copy.wait()
 
 
-def add_kernel(left_ref, right_ref, *rest):
-    total_ref = rest[-1]
-    total = left_ref[...].astype(jnp.float32) + right_ref[...].astype(jnp.float32)
-    total_ref[...] = total.astype(total_ref.dtype)
-
-
-def last_kernel(scale, side_ref, own_ref, other_ref, weight_out, bias_out):
+def add_kernel(parts, *refs):
+    values = [ref[...].astype(jnp.float32) for ref in refs[:parts]]
+    total = values[0] + values[1]
+    if parts == 4:
+        total = total + (values[2] + values[3])
+    refs[-1][...] = total.astype(refs[-1].dtype)
+
+
+def last_kernel(scale, own_ref, other_ref, weight_out, bias_out):
     half = weight_out.shape[0] // 2
-    side = side_ref[0]
+    side = core_side()
     own_rows = pl.ds(pl.multiple_of(side * half, half), half)
     other_rows = pl.ds(pl.multiple_of((1 - side) * half, half), half)
     weight_out[own_rows] = own_ref[:half] * scale
@@ -273,38 +331,49 @@
     bias_out[...] = first * scale
 
 
-def neighbour(value, steps, count):
-    initial, last = max(0, -steps), min(count, count - steps)
-    return lax.ppermute(value, AXES, [(source, source + steps) for source in range(initial, last)])
-
-
-def add(left, right, dtype, after=()):
+def add(values, dtype, after=()):
+    size = values[0].size
     return pl.pallas_call(
-        add_kernel,
-        out_shape=jax.ShapeDtypeStruct(left.shape, dtype),
-        in_specs=[pl.BlockSpec(memory_space=pltpu.VMEM)] * 2
+        functools.partial(add_kernel, len(values)),
+        out_shape=jax.ShapeDtypeStruct(values[0].shape, dtype),
+        in_specs=[pl.BlockSpec(memory_space=pltpu.VMEM)] * len(values)
         + [pl.BlockSpec(memory_space=pl.ANY)] * len(after),
         compiler_params=pltpu.CompilerParams(vmem_limit_bytes=2 * MIB),
         cost_estimate=pl.CostEstimate(
-            flops=left.size, bytes_accessed=6 * left.size, transcendentals=0
+            flops=size * len(values), bytes_accessed=8 * size, transcendentals=0
         ),
         name="add_halves",
-    )(left, right, *after)
-
-
-def swap(value, bits):
-    return lax.ppermute(value, AXES, [(i, i ^ (1 << bit)) for i, bit in enumerate(bits)])
+    )(*values, *after)
+
+
+def swap(value, masks):
+    pairs = [(i, i ^ mask) for i, mask in enumerate(masks) if mask]
+    return lax.ppermute(value, AXES, pairs)
+
+
+def with_next(value, count):
+    pairs = [(i, i + 1 if i & 1 else i - 1) for i in range(1, count - 1)]
+    return lax.ppermute(value, AXES, pairs)
 
 
 def sum_halves(send, keep, count, core_bit, marks):
     others = [bit for bit in range(count.bit_length() - 1) if bit != core_bit]
-    orders = (others, others[::-1])
-    total = add(keep, swap(send, [core_bit] * count), jnp.bfloat16, marks.get(0, ()))
-    for step in range(len(others)):
-        bits = [orders[(i >> core_bit) & 1][step] for i in range(count)]
-        last = step == len(others) - 1
-        dtype = jnp.float32 if last else jnp.bfloat16
-        total = add(total, swap(total, bits), dtype, marks.get(-1 if last else step + 1, ()))
+    groups = [others[i : i + 2] for i in range(0, len(others), 2)]
+    total = add([keep, swap(send, [1 << core_bit] * count)], jnp.bfloat16, marks.get("core", ()))
+    for step in range(len(groups)):
+        masks = []
+        for group in (groups[step], groups[len(groups) - 1 - step]):
+            if len(groups[0]) != len(groups[-1]):
+                group = groups[step]
+            low = 1 << group[0]
+            masks.append((low, 1 << group[1], low | 1 << group[1]) if group[1:] else (low,))
+        parts = [total] + [
+            swap(total, [masks[(i >> core_bit) & 1][k] for i in range(count)])
+            for k in range(len(masks[0]))
+        ]
+        last = step == len(groups) - 1
+        name = "last" if last else step
+        total = add(parts, jnp.float32 if last else jnp.bfloat16, marks.get(name, ()))
     return total
 
 
@@ -339,9 +408,18 @@
     offsets = in_hbm(adj_offset.T)
     counts = in_hbm(adj_count)
     core_bit = cols.bit_length() - 1
-    side = (lax.axis_index("rows") & 1).reshape(1)
-    from_below = neighbour(features[rows - rim :], 1, count)
-    from_above = neighbour(features[:rim], -1, count)
+    first_rim, second_rim = pl.pallas_call(
+        halo_kernel,
+        out_shape=(shape(rim, width), shape(rim, width)),
+        in_specs=[hbm],
+        out_specs=(vmem, vmem),
+        scratch_shapes=[pltpu.SemaphoreType.DMA((2,))],
+        compiler_params=params(2),
+        cost_estimate=cost(0.05),
+        name="halo_rows",
+    )(in_hbm(features))
+    first_halo = swap(first_rim, [1] * count)
+    second_halo = with_next(second_rim, count)
     (
         activated, grad_inner, partial, sums, weight_near, bias_near, feat_rim, adj_rim, cot_rim,
     ) = pl.pallas_call(
@@ -383,7 +461,7 @@
             shape(*half_shape, dtype=jnp.float32),
             shape(*half_shape, dtype=jnp.float32),
         ),
-        in_specs=[smem] * 3 + [vmem] * 9,
+        in_specs=[smem] * 2 + [vmem] * 9,
         out_specs=(vmem,) * 4,
         scratch_shapes=[
             pltpu.VMEM((6 * rim + block_rows, width), jnp.bfloat16),
@@ -394,11 +472,11 @@
         cost_estimate=cost(0.2),
         name="rim_rows",
     )(
-        offsets, counts, side, weight_near, bias_near, feat_rim, from_below, from_above, adj_rim,
+        offsets, counts, weight_near, bias_near, feat_rim, first_halo, second_halo, adj_rim,
         cot_rim, partial, sums,
     )
     mark = shape(8, 128, dtype=jnp.float32)
-    activated, rim_spread, lower_part, upper_part, first_mark = pl.pallas_call(
+    activated, rim_spread, first_spill, second_spill, first_mark = pl.pallas_call(
         rim_back_kernel,
         out_shape=(
             shape(rows, width),
@@ -415,24 +493,39 @@
         cost_estimate=cost(0.2),
         name="rim_rows_back",
     )(offsets, counts, weight_near, adj_rim, grad_rim, act_rim, activated)
-    from_above_dev = neighbour(lower_part, -1, count)
-    from_below_dev = neighbour(upper_part, 1, count)
-    grad_whole, edges, second_mark = pl.pallas_call(
-        inner_back_kernel,
+    first_part = swap(first_spill, [1] * count)
+    second_part = with_next(second_spill, count)
+    spread_shape = (blocks + 1, width, block_rows)
+    steps = inner // block_rows
+    half_spread, second_mark = pl.pallas_call(
+        inner_back_first,
+        out_shape=(shape(*spread_shape, dtype=jnp.float32), mark),
+        in_specs=[smem, smem, vmem, hbm, vmem, vmem],
+        out_specs=(vmem, vmem),
+        scratch_shapes=[
+            pltpu.VMEM((steps // 2, slots, block_rows, block_rows), jnp.bfloat16),
+            pltpu.SemaphoreType.DMA((1,)),
+        ],
+        compiler_params=params(12),
+        cost_estimate=cost(0.15),
+        name="inner_back_first",
+    )(offsets, counts, weight_near, in_hbm(adj_values), grad_inner, rim_spread)
+    grad_whole, edges, third_mark = pl.pallas_call(
+        inner_back_second,
         out_shape=(shape(rows, width), shape(2 * rim, width, dtype=jnp.float32), mark),
         in_specs=[smem, smem, vmem, hbm, vmem, vmem],
         out_specs=(hbm, vmem, vmem),
         scratch_shapes=[
-            pltpu.VMEM((blocks - 2 * BAND, slots, block_rows, block_rows), jnp.bfloat16),
-            pltpu.VMEM((blocks + 1, width, block_rows), jnp.float32),
+            pltpu.VMEM((steps - steps // 2, slots, block_rows, block_rows), jnp.bfloat16),
+            pltpu.VMEM(spread_shape, jnp.float32),
             pltpu.VMEM((inner, width), jnp.bfloat16),
             pltpu.SemaphoreType.DMA((2,)),
         ],
         compiler_params=params(12),
-        cost_estimate=cost(0.3),
-        name="inner_rows_back",
-    )(offsets, counts, weight_near, in_hbm(adj_values), grad_inner, rim_spread)
-    grad_features, third_mark = pl.pallas_call(
+        cost_estimate=cost(0.15),
+        name="inner_back_second",
+    )(offsets, counts, weight_near, in_hbm(adj_values), grad_inner, half_spread)
+    grad_features, last_mark = pl.pallas_call(
         edge_kernel,
         out_shape=(shape(rows, width), mark),
         in_specs=[vmem] * 3 + [hbm],
@@ -445,22 +538,22 @@
         compiler_params=params(8),
         cost_estimate=cost(0.05),
         name="join_edges",
-    )(edges, from_below_dev, from_above_dev, grad_whole)
-    marks = {0: (first_mark,), 2: (second_mark,), -1: (third_mark,)}
+    )(edges, first_part, second_part, grad_whole)
+    marks = {"core": (first_mark,), 0: (second_mark,), "last": (third_mark, last_mark)}
     own_half = sum_halves(send, keep, count, core_bit, marks)
-    other_half = swap(own_half, [core_bit] * count)
+    other_half = swap(own_half, [1 << core_bit] * count)
     norm_scale = 1.0 / math.sqrt(rows * count)
     grad_weight, grad_bias = pl.pallas_call(
-        lambda *refs: last_kernel(norm_scale, *refs),
+        functools.partial(last_kernel, norm_scale),
         out_shape=(
             shape(width, width, dtype=jnp.float32),
             shape(1, width, dtype=jnp.float32),
         ),
-        in_specs=[smem, vmem, vmem],
+        in_specs=[vmem, vmem],
         out_specs=(vmem, vmem),
         compiler_params=params(8),
         name="last_step",
-    )(side, own_half, other_half)
+    )(own_half, other_half)
     return (activated, grad_features, grad_weight, grad_bias.reshape(width))
 
 

time: 47.3 us -> 38.3 us (0.81)
  waiting for transfers between devices: 7.32 us -> 1.59 us
  starting transfers between devices: 23.6 us -> 18.3 us
  Pallas kernels: 14.3 us -> 17.2 us
  local copies, waits for them, and re-layouts: 0.99 us -> 0 us
    ppermute x10 -> x12, waiting for transfers between devices: 7.32 us -> 1.59 us  [the longest x10 1.59 us: swap(): return lax.ppermute(value, AXES, pairs)]
    ppermute x10 -> x12, starting transfers between devices: 23.6 us -> 18.3 us  [the longest x10 17 us: swap(): return lax.ppermute(value, AXES, pairs)]
    pallas_call x7, Pallas kernels: 5.35 us -> 7.98 us  [the longest x1 3.58 us: on_device(): pl.pallas_call(inner_back_second, out_shape=(shape(rows, width), shape(2...]
    slice x1 -> x0, local copies, waits for them, and re-layouts: 0.99 us -> none  [on_device(): from_above = neighbour(features[:rim], -1, count)]
  transfers between devices with their start and end apart: 10 -> 12, of which waited for: 4 -> 2; matrix products, arithmetic and copies ran while one was open for 0% -> 0% of each run, Pallas kernels for 25% -> 36%
where the time goes in v4:
time: 38.3 us; the launch traced here: 37.9 us
  starting transfers between devices  18.3 us (48%)
  Pallas kernels  17.2 us (45%)
  waiting for transfers between devices  1.59 us (4%)
  between operations  0.8 us (2%)
    ppermute x10, starting transfers between devices, swap(): return lax.ppermute(value, AXES, pairs)  17 us
    pallas_call x1, Pallas kernels, on_device(): pl.pallas_call(inner_kernel, out_shape=(shape(rows, width), shape(inner,...  4.41 us
    pallas_call x1, Pallas kernels, on_device(): pl.pallas_call(inner_back_second, out_shape=(shape(rows, width), shape(2...  3.58 us
    pallas_call x1, Pallas kernels, on_device(): pl.pallas_call(inner_back_first, out_shape=(shape(*spread_shape, dtype=jn...  2.58 us
    pallas_call x1, Pallas kernels, on_device(): pl.pallas_call(rim_back_kernel, out_shape=(shape(rows, width), shape(6 *...  2.27 us
    pallas_call x1, Pallas kernels, on_device(): pl.pallas_call(rim_kernel, out_shape=(shape(2 * rim, width), shape(2 * ri...  1.74 us
    ppermute x10, waiting for transfers between devices, swap(): return lax.ppermute(value, AXES, pairs)  1.59 us
    ppermute x2, starting transfers between devices, with_next(): return lax.ppermute(value, AXES, pairs)  1.31 us
  transfers between devices with their start and end apart: 12, of which 2 were waited for; matrix products, arithmetic and copies ran while one was open for 0% of the time, Pallas kernels for 36%

profile of v4, /device:TPU:0, one launch (start us, length us, event | category | flops | bytes accessed | tf_op | source)
XLA Modules:
  0.0 37.9 jit_solution(17121550007609100164)
XLA Ops:
  0.6 1.0 %halo_rows.1 = (bf16[256,256]{1,0:T(8,128)(2,1)S(1)}, bf16[256,256]{1,0:T(8,128)(2,1)S(1)}) custom-call(bf16[1536,256]{1,0:T(8,128)(2,1)} %feat_hbm.3), custom_call_target="tpu_custom_call" | custom-call | flops 60000000 | bytes 300000 | tf_op jit(solution)/shard_map/halo_rows/pallas_call | solution.py:411
  1.6 3.0 %collective-permute-start = (bf16[256,256]{1,0:T(8,128)(2,1)S(1)}, bf16[256,256]{1,0:T(8,128)(2,1)S(1)}, u32[]{:S(2)}, u32[]{:S(2)}) collective-permute-start(bf16[256,256]{1,0:T(8,128)(2,1)S(1)} %get-tuple-element.37), channel_id=1, source_target_pairs={{0,1},{1,0},{2,3},{3,2},{4,5},{5,4},{6,7},{7,6},{8,9},{9,8},{10,11... | collective-permute-start | bytes 393224 | tf_op jit(solution)/shard_map/ppermute | solution.py:351
  4.7 0.7 %collective-permute-start.1 = (bf16[256,256]{1,0:T(8,128)(2,1)S(1)}, bf16[256,256]{1,0:T(8,128)(2,1)S(1)}, u32[]{:S(2)}, u32[]{:S(2)}) collective-permute-start(bf16[256,256]{1,0:T(8,128)(2,1)S(1)} %get-tuple-element.38), channel_id=1, source_target_pairs={{1,2},{2,1},{3,4},{4,3},{5,6},{6,5},{7,8},{8,7},{9,10},{10,9},{11,... | collective-permute-start | bytes 393224 | tf_op jit(solution)/shard_map/ppermute | solution.py:356
  5.3 4.4 %inner_rows.1 = (bf16[1536,256]{1,0:T(8,128)(2,1)}, bf16[1024,256]{1,0:T(8,128)(2,1)S(1)}, f32[256,256]{1,0:T(8,128)S(1)}, f32[8,256]{1,0:T(8,128)S(1)}, bf16[25...) custom-call(s32[3,12]{1,0:T(4,128)} %bitcast.3, ...), custom_call_target="tpu_custom_call" | custom-call | flops 600000000 | bytes 3000000 | tf_op jit(solution)/shard_map/inner_rows/pallas_call | solution.py:425
  9.7 0.0 collective-permute-done.first_ref
  9.8 0.0 collective-permute-done.1.second_ref
  9.8 1.7 %rim_rows.1 = (bf16[512,256]{1,0:T(8,128)(2,1)S(1)}, bf16[512,256]{1,0:T(8,128)(2,1)S(1)}, f32[144,256]{1,0:T(8,128)S(1)}, f32[144,256]{1,0:T(8,128)S(1)}) custom-call(s32[3,12]{1,0:T(4,128)} %bitcast.4, s32[12]{0:T(128)} %cnt_ref.9, bf16[256,256]{1,0:T(8,128)(2,1)S(1)} %get-tuple-element.33.weight_ref, f32[1,256]{1,0:T(1,128)S(1)} %get-tuple-element.35.bias_ref, ...), custom_call_target="tpu_custom_call" | custom-call | flops 240000000 | bytes 1200000 | tf_op jit(solution)/shard_map/rim_rows/pallas_call | solution.py:456
  11.5 1.5 %collective-permute-start.4 = (f32[144,256]{1,0:T(8,128)S(1)}, f32[144,256]{1,0:T(8,128)S(1)}, u32[]{:S(2)}, u32[]{:S(2)}) collective-permute-start(f32[144,256]{1,0:T(8,128)S(1)} %get-tuple-element.55), channel_id=1, source_target_pairs={{0,2},{1,3},{2,0},{3,1},{4,6},{5,7},{6,4},{7,5},{8,10},{9,11},{10,... | collective-permute-start | bytes 442376 | tf_op jit(solution)/shard_map/ppermute | solution.py:351
  13.0 2.3 %rim_rows_back.1 = (bf16[1536,256]{1,0:T(8,128)(2,1)}, f32[13,256,128]{2,1,0:T(8,128)S(1)}, bf16[256,256]{1,0:T(8,128)(2,1)S(1)}, bf16[256,256]{1,0:T(8,128)(2,1)S(1)}, f32[8,128]{1,0:T(8,128)S(1)}) custom-call(s32[3,12]{1,0:T(4,128)} %bitcast.5, s32[12]{0:T(128)} %cnt_ref.9, ...), custom_call_target="tpu_custom_call", output_to_operand_aliasing={{0}: (6, {})} | custom-call | flops 240000000 | bytes 1200000 | tf_op jit(solution)/shard_map/rim_rows_back/pallas_call | solution.py:479
  15.2 0.0 collective-permute-done.4.refs_1_
  15.3 4.0 %collective-permute-start.7 = (bf16[144,256]{1,0:T(8,128)(2,1)S(1)}, bf16[144,256]{1,0:T(8,128)(2,1)S(1)}, u32[]{:S(2)}, u32[]{:S(2)}) collective-permute-start(bf16[144,256]{1,0:T(8,128)(2,1)S(1)} %add_halves.3.refs_0_), channel_id=1, source_target_pairs={{0,5},{1,4},{2,26},{3,27},{4,1},{5,0},{6,30},{7,31},{8,13},{9,12},... | collective-permute-start | bytes 221192 | tf_op jit(solution)/shard_map/ppermute | solution.py:351
  19.2 0.5 %collective-permute-start.6 = (bf16[144,256]{1,0:T(8,128)(2,1)S(1)}, bf16[144,256]{1,0:T(8,128)(2,1)S(1)}, u32[]{:S(2)}, u32[]{:S(2)}) collective-permute-start(bf16[144,256]{1,0:T(8,128)(2,1)S(1)} %add_halves.3.refs_0_), channel_id=1, source_target_pairs={{0,4},{1,5},{2,18},{3,19},{4,0},{5,1},{6,22},{7,23},{8,12},{9,13},... | collective-permute-start | bytes 221192 | tf_op jit(solution)/shard_map/ppermute | solution.py:351
  19.7 0.2 collective-permute-start.5
  19.9 1.9 %collective-permute-start.2 = (bf16[256,256]{1,0:T(8,128)(2,1)S(1)}, bf16[256,256]{1,0:T(8,128)(2,1)S(1)}, u32[]{:S(2)}, u32[]{:S(2)}) collective-permute-start(bf16[256,256]{1,0:T(8,128)(2,1)S(1)} %get-tuple-element.50), channel_id=1, source_target_pairs={{0,1},{1,0},{2,3},{3,2},{4,5},{5,4},{6,7},{7,6},{8,9},{9,8},{10,11... | collective-permute-start | bytes 393224 | tf_op jit(solution)/shard_map/ppermute | solution.py:351
  21.8 0.7 %collective-permute-start.3 = (bf16[256,256]{1,0:T(8,128)(2,1)S(1)}, bf16[256,256]{1,0:T(8,128)(2,1)S(1)}, u32[]{:S(2)}, u32[]{:S(2)}) collective-permute-start(bf16[256,256]{1,0:T(8,128)(2,1)S(1)} %get-tuple-element.51), channel_id=1, source_target_pairs={{1,2},{2,1},{3,4},{4,3},{5,6},{6,5},{7,8},{8,7},{9,10},{10,9},{11,... | collective-permute-start | bytes 393224 | tf_op jit(solution)/shard_map/ppermute | solution.py:356
  22.4 2.6 %inner_back_first.1 = (f32[13,256,128]{2,1,0:T(8,128)S(1)}, f32[8,128]{1,0:T(8,128)S(1)}) custom-call(s32[3,12]{1,0:T(4,128)} %bitcast.6, s32[12]{0:T(128)} %cnt_ref.9, bf16[256,256]{1,0:T(8,128)(2,1)S(1)} %get-tuple-element.33.weight_ref, bf16[12,3,128,128]{3,2,1,0:T(8,128)(2,1)} %adj_hbm.5, bf16[1024,256]{1,0:T(8,128)(2,1)S(1)} %get-tuple-element.46.grad_ref, ...), custom_call_target="tpu_custom_call" | custom-call | flops 180000000 | bytes 900000 | tf_op jit(solution)/shard_map/inner_back_first/pallas_call | solution.py:500
  25.0 0.0 collective-permute-done.7.refs_3_
  25.0 0.0 collective-permute-done.6.refs_2_
  25.0 0.0 collective-permute-done.5.refs_1_
  25.1 5.3 %collective-permute-start.10 = (bf16[144,256]{1,0:T(8,128)(2,1)S(1)}, bf16[144,256]{1,0:T(8,128)(2,1)S(1)}, u32[]{:S(2)}, u32[]{:S(2)}) collective-permute-start(bf16[144,256]{1,0:T(8,128)(2,1)S(1)} %add_halves.4.refs_0_), channel_id=1, source_target_pairs={{0,24},{1,25},{2,7},{3,6},{4,28},{5,29},{6,3},{7,2},{8,16},{9,17},... | collective-permute-start | bytes 221192 | tf_op jit(solution)/shard_map/ppermute | solution.py:351
  30.4 0.0 collective-permute-start.9
  30.4 0.6 %collective-permute-start.8 = (bf16[144,256]{1,0:T(8,128)(2,1)S(1)}, bf16[144,256]{1,0:T(8,128)(2,1)S(1)}, u32[]{:S(2)}, u32[]{:S(2)}) collective-permute-start(bf16[144,256]{1,0:T(8,128)(2,1)S(1)} %add_halves.4.refs_0_), channel_id=1, source_target_pairs={{0,8},{1,9},{2,3},{3,2},{4,12},{5,13},{6,7},{7,6},{8,0},{9,1},{10,... | collective-permute-start | bytes 221192 | tf_op jit(solution)/shard_map/ppermute | solution.py:351
  31.1 3.6 %inner_back_second.1 = (bf16[1536,256]{1,0:T(8,128)(2,1)}, f32[512,256]{1,0:T(8,128)S(1)}, f32[8,128]{1,0:T(8,128)S(1)}) custom-call(s32[3,12]{1,0:T(4,128)} %bitcast.7, s32[12]{0:T(128)} %cnt_ref.9, bf16[256,256]{1,0:T(8,128)(2,1)S(1)} %get-tuple-element.33.weight_ref, bf16[12,3,128,128]{3,2,1,0:T(8,128)(2,1)} %adj_hbm.5, ...), custom_call_target="tpu_custom_call" | custom-call | flops 180000000 | bytes 900000 | tf_op jit(solution)/shard_map/inner_back_second/pallas_call | solution.py:513
  34.7 0.0 collective-permute-done.2.first_ref
  34.7 0.0 collective-permute-done.3.second_ref
  34.7 0.8 %join_edges.1 = (bf16[1536,256]{1,0:T(8,128)(2,1)}, f32[8,128]{1,0:T(8,128)S(1)}) custom-call(f32[512,256]{1,0:T(8,128)S(1)} %get-tuple-element.49.edge_ref, bf16[256,256]{1,0:T(8,128)(2,1)S(1)} %collective-permute-done.2.first_ref, bf16[256,256]{1,0:T(8,128)(2,1)S(1)} %collective-permute-done.3.second_ref, ...), custom_call_target="tpu_custom_call", output_to_operand_aliasing={{0}: (3, {})} | custom-call | flops 60000000 | bytes 300000 | tf_op jit(solution)/shard_map/join_edges/pallas_call | solution.py:528
  35.5 0.0 collective-permute-done.10.refs_3_
  35.5 0.2 collective-permute-done.9.refs_2_
  35.7 0.0 collective-permute-done.8.refs_1_
  35.7 0.1 collective-permute-start.11
  35.8 1.4 %collective-permute-done.11.other_ref = f32[144,256]{1,0:T(8,128)S(1)} collective-permute-done((f32[144,256]{1,0:T(8,128)S(1)}, f32[144,256]{1,0:T(8,128)S(1)}, u32[]{:S(2)}, u32[]{:S(2)}) %collective-permute-start.11) | collective-permute-done | bytes 147488 | tf_op jit(solution)/shard_map/ppermute | solution.py:351
  37.2 0.7 %last_step.1 = (f32[256,256]{1,0:T(8,128)}, f32[1,256]{1,0:T(1,128)}) custom-call(f32[144,256]{1,0:T(8,128)S(1)} %add_halves.5.own_ref, f32[144,256]{1,0:T(8,128)S(1)} %collective-permute-done.11.other_ref), custom_call_target="tpu_custom_call" | custom-call | tf_op jit(solution)/shard_map/last_step/pallas_call | solution.py:546
  (3 shorter events, 0.1 us)
Async XLA Ops:
  1.6 8.1 %collective-permute-start = (bf16[256,256]{1,0:T(8,128)(2,1)S(1)}, bf16[256,256]{1,0:T(8,128)(2,1)S(1)}, u32[]{:S(2)}, u32[]{:S(2)}) collective-permute-start(bf16[256,256]{1,0:T(8,128)(2,1)S(1)} %get-tuple-element.37), channel_id=1, source_target_pairs={{0,1},{1,0},{2,3},{3,2},{4,5},{5,4},{6,7},{7,6},{8,9},{9,8},{10,11... | collective-permute-start | bytes 393224 | tf_op jit(solution)/shard_map/ppermute | solution.py:351
  4.7 5.1 %collective-permute-start.1 = (bf16[256,256]{1,0:T(8,128)(2,1)S(1)}, bf16[256,256]{1,0:T(8,128)(2,1)S(1)}, u32[]{:S(2)}, u32[]{:S(2)}) collective-permute-start(bf16[256,256]{1,0:T(8,128)(2,1)S(1)} %get-tuple-element.38), channel_id=1, source_target_pairs={{1,2},{2,1},{3,4},{4,3},{5,6},{6,5},{7,8},{8,7},{9,10},{10,9},{11,... | collective-permute-start | bytes 393224 | tf_op jit(solution)/shard_map/ppermute | solution.py:356
  11.5 3.7 %collective-permute-start.4 = (f32[144,256]{1,0:T(8,128)S(1)}, f32[144,256]{1,0:T(8,128)S(1)}, u32[]{:S(2)}, u32[]{:S(2)}) collective-permute-start(f32[144,256]{1,0:T(8,128)S(1)} %get-tuple-element.55), channel_id=1, source_target_pairs={{0,2},{1,3},{2,0},{3,1},{4,6},{5,7},{6,4},{7,5},{8,10},{9,11},{10,... | collective-permute-start | bytes 442376 | tf_op jit(solution)/shard_map/ppermute | solution.py:351
  15.3 9.7 %collective-permute-start.7 = (bf16[144,256]{1,0:T(8,128)(2,1)S(1)}, bf16[144,256]{1,0:T(8,128)(2,1)S(1)}, u32[]{:S(2)}, u32[]{:S(2)}) collective-permute-start(bf16[144,256]{1,0:T(8,128)(2,1)S(1)} %add_halves.3.refs_0_), channel_id=1, source_target_pairs={{0,5},{1,4},{2,26},{3,27},{4,1},{5,0},{6,30},{7,31},{8,13},{9,12},... | collective-permute-start | bytes 221192 | tf_op jit(solution)/shard_map/ppermute | solution.py:351
  19.2 5.8 %collective-permute-start.6 = (bf16[144,256]{1,0:T(8,128)(2,1)S(1)}, bf16[144,256]{1,0:T(8,128)(2,1)S(1)}, u32[]{:S(2)}, u32[]{:S(2)}) collective-permute-start(bf16[144,256]{1,0:T(8,128)(2,1)S(1)} %add_halves.3.refs_0_), channel_id=1, source_target_pairs={{0,4},{1,5},{2,18},{3,19},{4,0},{5,1},{6,22},{7,23},{8,12},{9,13},... | collective-permute-start | bytes 221192 | tf_op jit(solution)/shard_map/ppermute | solution.py:351
  19.7 5.3 %collective-permute-start.5 = (bf16[144,256]{1,0:T(8,128)(2,1)S(1)}, bf16[144,256]{1,0:T(8,128)(2,1)S(1)}, u32[]{:S(2)}, u32[]{:S(2)}) collective-permute-start(bf16[144,256]{1,0:T(8,128)(2,1)S(1)} %add_halves.3.refs_0_), channel_id=1, source_target_pairs={{0,1},{1,0},{2,10},{3,11},{4,5},{5,4},{6,14},{7,15},{8,9},{9,8},{1... | collective-permute-start | bytes 221192 | tf_op jit(solution)/shard_map/ppermute | solution.py:351
  19.9 14.8 %collective-permute-start.2 = (bf16[256,256]{1,0:T(8,128)(2,1)S(1)}, bf16[256,256]{1,0:T(8,128)(2,1)S(1)}, u32[]{:S(2)}, u32[]{:S(2)}) collective-permute-start(bf16[256,256]{1,0:T(8,128)(2,1)S(1)} %get-tuple-element.50), channel_id=1, source_target_pairs={{0,1},{1,0},{2,3},{3,2},{4,5},{5,4},{6,7},{7,6},{8,9},{9,8},{10,11... | collective-permute-start | bytes 393224 | tf_op jit(solution)/shard_map/ppermute | solution.py:351
  21.8 12.9 %collective-permute-start.3 = (bf16[256,256]{1,0:T(8,128)(2,1)S(1)}, bf16[256,256]{1,0:T(8,128)(2,1)S(1)}, u32[]{:S(2)}, u32[]{:S(2)}) collective-permute-start(bf16[256,256]{1,0:T(8,128)(2,1)S(1)} %get-tuple-element.51), channel_id=1, source_target_pairs={{1,2},{2,1},{3,4},{4,3},{5,6},{6,5},{7,8},{8,7},{9,10},{10,9},{11,... | collective-permute-start | bytes 393224 | tf_op jit(solution)/shard_map/ppermute | solution.py:356
  25.1 10.4 %collective-permute-start.10 = (bf16[144,256]{1,0:T(8,128)(2,1)S(1)}, bf16[144,256]{1,0:T(8,128)(2,1)S(1)}, u32[]{:S(2)}, u32[]{:S(2)}) collective-permute-start(bf16[144,256]{1,0:T(8,128)(2,1)S(1)} %add_halves.4.refs_0_), channel_id=1, source_target_pairs={{0,24},{1,25},{2,7},{3,6},{4,28},{5,29},{6,3},{7,2},{8,16},{9,17},... | collective-permute-start | bytes 221192 | tf_op jit(solution)/shard_map/ppermute | solution.py:351
  30.4 5.3 %collective-permute-start.9 = (bf16[144,256]{1,0:T(8,128)(2,1)S(1)}, bf16[144,256]{1,0:T(8,128)(2,1)S(1)}, u32[]{:S(2)}, u32[]{:S(2)}) collective-permute-start(bf16[144,256]{1,0:T(8,128)(2,1)S(1)} %add_halves.4.refs_0_), channel_id=1, source_target_pairs={{0,16},{1,17},{2,6},{3,7},{4,20},{5,21},{6,2},{7,3},{8,24},{9,25},... | collective-permute-start | bytes 221192 | tf_op jit(solution)/shard_map/ppermute | solution.py:351
  30.4 5.3 %collective-permute-start.8 = (bf16[144,256]{1,0:T(8,128)(2,1)S(1)}, bf16[144,256]{1,0:T(8,128)(2,1)S(1)}, u32[]{:S(2)}, u32[]{:S(2)}) collective-permute-start(bf16[144,256]{1,0:T(8,128)(2,1)S(1)} %add_halves.4.refs_0_), channel_id=1, source_target_pairs={{0,8},{1,9},{2,3},{3,2},{4,12},{5,13},{6,7},{7,6},{8,0},{9,1},{10,... | collective-permute-start | bytes 221192 | tf_op jit(solution)/shard_map/ppermute | solution.py:351
  35.7 1.4 %collective-permute-start.11 = (f32[144,256]{1,0:T(8,128)S(1)}, f32[144,256]{1,0:T(8,128)S(1)}, u32[]{:S(2)}, u32[]{:S(2)}) collective-permute-start(f32[144,256]{1,0:T(8,128)S(1)} %add_halves.5.own_ref), channel_id=1, source_target_pairs={{0,2},{1,3},{2,0},{3,1},{4,6},{5,7},{6,4},{7,5},{8,10},{9,11},{10,... | collective-permute-start | bytes 442376 | tf_op jit(solution)/shard_map/ppermute | solution.py:351

commit v5 on v4

--- a/solution.py
+++ b/solution.py
@@ -28,11 +28,26 @@
     )
 
 
-def places_of(off_ref, cnt_ref, block, shift, dump, slots):
-    return [
-        jnp.where(slot < cnt_ref[block], block + shift + off_ref[slot, block], dump)
-        for slot in range(slots)
-    ]
+def write_places(off_ref, cnt_ref, place_ref, blocks, slots):
+    for block in range(blocks):
+        if block < BAND:
+            shift, dump = BAND, 6 * BAND
+        elif block < blocks - BAND:
+            shift, dump = 0, blocks
+        else:
+            shift, dump = 5 * BAND - blocks, 6 * BAND
+        for slot in range(slots):
+            place_ref[block * slots + slot] = jnp.where(
+                slot < cnt_ref[block], block + shift + off_ref[slot, block], dump
+            )
+
+
+def places_of(place_ref, block, slots):
+    return [place_ref[block * slots + slot] for slot in range(slots)]
+
+
+def rim_block(step, blocks):
+    return step if step < BAND else blocks - 2 * BAND + step
 
 
 def place_in_mesh():
@@ -86,8 +101,9 @@
 
 def inner_kernel(
     off_ref, cnt_ref, weight_hbm, bias_hbm, feat_hbm, adj_hbm, cot_hbm,
-    act_hbm, grad_ref, partial_ref, sums_ref, weight_ref, bias_ref, feat_rim, adj_rim, cot_rim,
-    feat, adj, cot, act, agg_all, sems,
+    act_hbm, place_ref, grad_ref, partial_ref, sums_ref, weight_ref, bias_ref, feat_rim, adj_rim,
+    cot_rim, adj,
+    feat, cot, act, agg_all, sems,
 ):
     blocks, slots, block_rows, _ = adj_hbm.shape
     rows, width = feat_hbm.shape
@@ -117,6 +133,7 @@
     for copy in copies:
         copy.start()
     feat[rows:] = jnp.zeros((block_rows, width), jnp.bfloat16)
+    write_places(off_ref, cnt_ref, place_ref, blocks, slots)
     for copy in copies[:5]:
         copy.wait()
     weight = weight_ref[...]
@@ -124,7 +141,7 @@
     sums = jnp.zeros((8, width), jnp.float32)
     for step in range(0, count, 2):
         for block in (step, step + 1):
-            places = places_of(off_ref, cnt_ref, block + BAND, 0, blocks, slots)
+            places = places_of(place_ref, block + BAND, slots)
             agg_all[block * block_rows : (block + 1) * block_rows] = jnp.dot(
                 row_of(adj, block, slots), pick(feat, places, block_rows),
                 preferred_element_type=jnp.float32,
@@ -143,21 +160,14 @@
     act_out.wait()
 
 
-def rim_places(off_ref, cnt_ref, step, blocks, slots):
-    if step < BAND:
-        return places_of(off_ref, cnt_ref, step, BAND, 6 * BAND, slots)
-    block = blocks - 2 * BAND + step
-    return places_of(off_ref, cnt_ref, block, 5 * BAND - blocks, 6 * BAND, slots)
-
-
 def rim_kernel(
-    off_ref, cnt_ref, weight_ref, bias_ref, feat_ref, first_ref, second_ref, adj_ref,
-    cot_ref, partial_ref, sums_ref,
+    place_ref, weight_ref, bias_ref, feat_ref, first_ref, second_ref, adj_ref, cot_ref,
+    partial_ref, sums_ref,
     act_ref, grad_ref, send_ref, keep_ref,
     window, agg_all, payload,
 ):
-    blocks = off_ref.shape[1]
     steps, slots, block_rows, _ = adj_ref.shape
+    blocks = place_ref.shape[0] // slots
     width = feat_ref.shape[1]
     rim = BAND * block_rows
     odd = place_in_mesh() & 1
@@ -170,7 +180,7 @@
     sums = sums_ref[...]
     for step in range(0, steps, 2):
         for block in (step, step + 1):
-            places = rim_places(off_ref, cnt_ref, block, blocks, slots)
+            places = places_of(place_ref, rim_block(block, blocks), slots)
             agg_all[block * block_rows : (block + 1) * block_rows] = jnp.dot(
                 row_of(adj_ref, block, slots), pick(window, places, block_rows),
                 preferred_element_type=jnp.float32,
@@ -192,13 +202,26 @@
     send_ref[...] = payload[1 - side]
 
 
+def scatter_rows(places, weight_ref, adj_ref, grad_ref, spread):
+    _, slots, block_rows, _ = adj_ref.shape
+    upstream = to_upstream(weight_ref[...], grad_ref[...])
+    for step, targets in enumerate(places):
+        terms = jnp.dot(
+            upstream[:, step * block_rows : (step + 1) * block_rows],
+            row_of(adj_ref, step, slots),
+            preferred_element_type=jnp.float32,
+        )
+        for slot, target in enumerate(targets):
+            spread[target] += terms[:, slot * block_rows : (slot + 1) * block_rows]
+
+
 def rim_back_kernel(
-    off_ref, cnt_ref, weight_ref, adj_ref, grad_ref, act_ref, act_in,
+    place_ref, weight_ref, adj_ref, grad_ref, act_ref, act_in,
     act_hbm, spread, first_ref, second_ref, mark_ref,
     sems,
 ):
-    blocks = off_ref.shape[1]
     steps, slots, block_rows, _ = adj_ref.shape
+    blocks = place_ref.shape[0] // slots
     rim = BAND * block_rows
     rows = blocks * block_rows
     copies = [
@@ -210,16 +233,10 @@
     for copy in copies:
         copy.start()
     spread[...] = jnp.zeros_like(spread)
-    weight = weight_ref[...]
-    for step in range(steps):
-        here = pl.ds(step * block_rows, block_rows)
-        places = rim_places(off_ref, cnt_ref, step, blocks, slots)
-        terms = jnp.dot(
-            to_upstream(weight, grad_ref[here]), row_of(adj_ref, step, slots),
-            preferred_element_type=jnp.float32,
-        )
-        for slot, place in enumerate(places):
-            spread[place] += terms[:, slot * block_rows : (slot + 1) * block_rows]
+    scatter_rows(
+        [places_of(place_ref, rim_block(step, blocks), slots) for step in range(steps)],
+        weight_ref, adj_ref, grad_ref, spread,
+    )
     odd = place_in_mesh() & 1
     for block in range(BAND):
         here = pl.ds(block * block_rows, block_rows)
@@ -230,60 +247,26 @@
         copy.wait()
 
 
-def scatter_rows(off_ref, cnt_ref, weight, adj, grad_ref, spread, steps, blocks, slots):
-    block_rows = adj.shape[2]
-    for i, step in enumerate(steps):
-        here = pl.ds(step * block_rows, block_rows)
-        places = places_of(off_ref, cnt_ref, step + BAND, 0, blocks, slots)
-        terms = jnp.dot(
-            to_upstream(weight, grad_ref[here]), row_of(adj, i, slots),
-            preferred_element_type=jnp.float32,
-        )
-        for slot, place in enumerate(places):
-            spread[place] += terms[:, slot * block_rows : (slot + 1) * block_rows]
-
-
-def inner_back_first(
-    off_ref, cnt_ref, weight_ref, adj_hbm, grad_ref, rim_spread, spread, mark_ref, adj, sems
+def inner_back_kernel(
+    place_ref, weight_ref, adj_ref, grad_ref, rim_spread,
+    whole_hbm, edge_ref, mark_ref,
+    spread, out, sems,
 ):
-    blocks, slots, _, _ = adj_hbm.shape
-    count = adj.shape[0]
-    fetch = pltpu.make_async_copy(adj_hbm.at[pl.ds(BAND, count)], adj, sems.at[0])
-    fetch.start()
+    count, slots, block_rows, _ = adj_ref.shape
+    blocks = place_ref.shape[0] // slots
+    rim = BAND * block_rows
     spread[: 2 * BAND] = rim_spread[BAND : 3 * BAND]
     spread[2 * BAND :] = jnp.zeros_like(spread[2 * BAND :])
     spread[blocks - 2 * BAND : blocks] = rim_spread[3 * BAND : 5 * BAND]
     mark_ref[...] = jnp.zeros_like(mark_ref)
-    fetch.wait()
     scatter_rows(
-        off_ref, cnt_ref, weight_ref[...], adj, grad_ref, spread, range(count), blocks, slots
-    )
-
-
-def inner_back_second(
-    off_ref, cnt_ref, weight_ref, adj_hbm, grad_ref, half_spread,
-    whole_hbm, edge_ref, mark_ref,
-    adj, spread, out, sems,
-):
-    blocks, slots, block_rows, _ = adj_hbm.shape
-    count = blocks - 2 * BAND
-    first = count - adj.shape[0]
-    rim = BAND * block_rows
-    fetch = pltpu.make_async_copy(
-        adj_hbm.at[pl.ds(BAND + first, count - first)], adj, sems.at[0]
-    )
-    fetch.start()
-    spread[...] = half_spread[...]
-    mark_ref[...] = jnp.zeros_like(mark_ref)
-    fetch.wait()
-    scatter_rows(
-        off_ref, cnt_ref, weight_ref[...], adj, grad_ref, spread, range(first, count), blocks,
-        slots,
+        [places_of(place_ref, step + BAND, slots) for step in range(count)],
+        weight_ref, adj_ref, grad_ref, spread,
     )
     for step in range(count):
         here = pl.ds(step * block_rows, block_rows)
         out[here] = spread[BAND + step].T.astype(jnp.bfloat16)
-    finish = pltpu.make_async_copy(out, whole_hbm.at[pl.ds(rim, count * block_rows)], sems.at[1])
+    finish = pltpu.make_async_copy(out, whole_hbm.at[pl.ds(rim, count * block_rows)], sems.at[0])
     finish.start()
     for block in range(BAND):
         edge_ref[block * block_rows : (block + 1) * block_rows] = spread[block].T
@@ -292,7 +275,20 @@
     finish.wait()
 
 
-def edge_kernel(edge_ref, first_ref, second_ref, whole_in, whole_hbm, mark_ref, out, sems):
+def add_kernel(parts, *refs):
+    values = [ref[...].astype(jnp.float32) for ref in refs[:parts]]
+    total = values[0] + values[1]
+    if parts == 4:
+        total = total + (values[2] + values[3])
+    refs[-1][...] = total.astype(refs[-1].dtype)
+
+
+def last_kernel(
+    scale, own_ref, other_ref, edge_ref, first_ref, second_ref, whole_in,
+    weight_out, bias_out, whole_hbm,
+    out, sums, sems,
+):
+    half = sums.shape[0] // 2
     rim = first_ref.shape[0]
     rows = whole_hbm.shape[0]
     odd = place_in_mesh() & 1
@@ -304,31 +300,20 @@
         pltpu.make_async_copy(
             out.at[pl.ds(rim, rim)], whole_hbm.at[pl.ds(rows - rim, rim)], sems.at[1]
         ),
+        pltpu.make_async_copy(sums, weight_out, sems.at[2]),
     ]
-    for copy in copies:
+    for copy in copies[:2]:
         copy.start()
-    mark_ref[...] = jnp.zeros_like(mark_ref)
-    for copy in copies:
-        copy.wait()
-
-
-def add_kernel(parts, *refs):
-    values = [ref[...].astype(jnp.float32) for ref in refs[:parts]]
-    total = values[0] + values[1]
-    if parts == 4:
-        total = total + (values[2] + values[3])
-    refs[-1][...] = total.astype(refs[-1].dtype)
-
-
-def last_kernel(scale, own_ref, other_ref, weight_out, bias_out):
-    half = weight_out.shape[0] // 2
     side = core_side()
     own_rows = pl.ds(pl.multiple_of(side * half, half), half)
     other_rows = pl.ds(pl.multiple_of((1 - side) * half, half), half)
-    weight_out[own_rows] = own_ref[:half] * scale
-    weight_out[other_rows] = other_ref[:half] * scale
+    sums[own_rows] = own_ref[:half] * scale
+    sums[other_rows] = other_ref[:half] * scale
+    copies[2].start()
     first = jnp.where(side == 0, own_ref[half : half + 1], other_ref[half : half + 1])
     bias_out[...] = first * scale
+    for copy in copies:
+        copy.wait()
 
 
 def add(values, dtype, after=()):
@@ -421,11 +406,13 @@
     first_halo = swap(first_rim, [1] * count)
     second_halo = with_next(second_rim, count)
     (
-        activated, grad_inner, partial, sums, weight_near, bias_near, feat_rim, adj_rim, cot_rim,
+        activated, places, grad_inner, partial, sums, weight_near, bias_near, feat_rim, adj_rim,
+        cot_rim, adj_inner,
     ) = pl.pallas_call(
         inner_kernel,
         out_shape=(
             shape(rows, width),
+            shape(blocks * slots, dtype=jnp.int32),
             shape(inner, width),
             shape(width, width, dtype=jnp.float32),
             shape(8, width, dtype=jnp.float32),
@@ -434,12 +421,12 @@
             shape(4 * rim, width),
             shape(2 * BAND, slots, block_rows, block_rows),
             shape(2 * rim, width),
+            shape(blocks - 2 * BAND, slots, block_rows, block_rows),
         ),
         in_specs=[smem, smem] + [hbm] * 5,
-        out_specs=(hbm,) + (vmem,) * 8,
+        out_specs=(hbm, smem) + (vmem,) * 9,
         scratch_shapes=[
             pltpu.VMEM((rows + block_rows, width), jnp.bfloat16),
-            pltpu.VMEM((blocks - 2 * BAND, slots, block_rows, block_rows), jnp.bfloat16),
             pltpu.VMEM((inner, width), jnp.bfloat16),
             pltpu.VMEM((inner, width), jnp.bfloat16),
             pltpu.VMEM((inner, width), jnp.bfloat16),
@@ -461,7 +448,7 @@
             shape(*half_shape, dtype=jnp.float32),
             shape(*half_shape, dtype=jnp.float32),
         ),
-        in_specs=[smem] * 2 + [vmem] * 9,
+        in_specs=[smem] + [vmem] * 9,
         out_specs=(vmem,) * 4,
         scratch_shapes=[
             pltpu.VMEM((6 * rim + block_rows, width), jnp.bfloat16),
@@ -472,8 +459,8 @@
         cost_estimate=cost(0.2),
         name="rim_rows",
     )(
-        offsets, counts, weight_near, bias_near, feat_rim, first_halo, second_halo, adj_rim,
-        cot_rim, partial, sums,
+        places, weight_near, bias_near, feat_rim, first_halo, second_halo, adj_rim, cot_rim,
+        partial, sums,
     )
     mark = shape(8, 128, dtype=jnp.float32)
     activated, rim_spread, first_spill, second_spill, first_mark = pl.pallas_call(
@@ -485,75 +472,52 @@
             shape(rim, width),
             mark,
         ),
-        in_specs=[smem, smem] + [vmem] * 4 + [hbm],
+        in_specs=[smem] + [vmem] * 4 + [hbm],
         out_specs=(hbm,) + (vmem,) * 4,
         scratch_shapes=[pltpu.SemaphoreType.DMA((2,))],
-        input_output_aliases={6: 0},
+        input_output_aliases={5: 0},
         compiler_params=params(12),
         cost_estimate=cost(0.2),
         name="rim_rows_back",
-    )(offsets, counts, weight_near, adj_rim, grad_rim, act_rim, activated)
+    )(places, weight_near, adj_rim, grad_rim, act_rim, activated)
     first_part = swap(first_spill, [1] * count)
     second_part = with_next(second_spill, count)
-    spread_shape = (blocks + 1, width, block_rows)
-    steps = inner // block_rows
-    half_spread, second_mark = pl.pallas_call(
-        inner_back_first,
-        out_shape=(shape(*spread_shape, dtype=jnp.float32), mark),
-        in_specs=[smem, smem, vmem, hbm, vmem, vmem],
-        out_specs=(vmem, vmem),
+    grad_whole, edges, second_mark = pl.pallas_call(
+        inner_back_kernel,
+        out_shape=(shape(rows, width), shape(2 * rim, width, dtype=jnp.float32), mark),
+        in_specs=[smem] + [vmem] * 4,
+        out_specs=(hbm, vmem, vmem),
         scratch_shapes=[
-            pltpu.VMEM((steps // 2, slots, block_rows, block_rows), jnp.bfloat16),
+            pltpu.VMEM((blocks + 1, width, block_rows), jnp.float32),
+            pltpu.VMEM((inner, width), jnp.bfloat16),
             pltpu.SemaphoreType.DMA((1,)),
         ],
         compiler_params=params(12),
-        cost_estimate=cost(0.15),
-        name="inner_back_first",
-    )(offsets, counts, weight_near, in_hbm(adj_values), grad_inner, rim_spread)
-    grad_whole, edges, third_mark = pl.pallas_call(
-        inner_back_second,
-        out_shape=(shape(rows, width), shape(2 * rim, width, dtype=jnp.float32), mark),
-        in_specs=[smem, smem, vmem, hbm, vmem, vmem],
-        out_specs=(hbm, vmem, vmem),
-        scratch_shapes=[
-            pltpu.VMEM((steps - steps // 2, slots, block_rows, block_rows), jnp.bfloat16),
-            pltpu.VMEM(spread_shape, jnp.float32),
-            pltpu.VMEM((inner, width), jnp.bfloat16),
-            pltpu.SemaphoreType.DMA((2,)),
-        ],
-        compiler_params=params(12),
-        cost_estimate=cost(0.15),
-        name="inner_back_second",
-    )(offsets, counts, weight_near, in_hbm(adj_values), grad_inner, half_spread)
-    grad_features, last_mark = pl.pallas_call(
-        edge_kernel,
-        out_shape=(shape(rows, width), mark),
-        in_specs=[vmem] * 3 + [hbm],
-        out_specs=(hbm, vmem),
-        scratch_shapes=[
-            pltpu.VMEM((2 * rim, width), jnp.bfloat16),
-            pltpu.SemaphoreType.DMA((2,)),
-        ],
-        input_output_aliases={3: 0},
-        compiler_params=params(8),
-        cost_estimate=cost(0.05),
-        name="join_edges",
-    )(edges, first_part, second_part, grad_whole)
-    marks = {"core": (first_mark,), 0: (second_mark,), "last": (third_mark, last_mark)}
+        cost_estimate=cost(0.3),
+        name="inner_rows_back",
+    )(places, weight_near, adj_inner, grad_inner, rim_spread)
+    marks = {"core": (first_mark,), "last": (second_mark,)}
     own_half = sum_halves(send, keep, count, core_bit, marks)
     other_half = swap(own_half, [1 << core_bit] * count)
     norm_scale = 1.0 / math.sqrt(rows * count)
-    grad_weight, grad_bias = pl.pallas_call(
+    grad_weight, grad_bias, grad_features = pl.pallas_call(
         functools.partial(last_kernel, norm_scale),
         out_shape=(
             shape(width, width, dtype=jnp.float32),
             shape(1, width, dtype=jnp.float32),
-        ),
-        in_specs=[vmem, vmem],
-        out_specs=(vmem, vmem),
+            shape(rows, width),
+        ),
+        in_specs=[vmem] * 5 + [hbm],
+        out_specs=(hbm, vmem, hbm),
+        scratch_shapes=[
+            pltpu.VMEM((2 * rim, width), jnp.bfloat16),
+            pltpu.VMEM((width, width), jnp.float32),
+            pltpu.SemaphoreType.DMA((3,)),
+        ],
+        input_output_aliases={5: 2},
         compiler_params=params(8),
         name="last_step",
-    )(own_half, other_half)
+    )(own_half, other_half, edges, first_part, second_part, grad_whole)
     return (activated, grad_features, grad_weight, grad_bias.reshape(width))
 
 

time: 38.3 us -> 41.7 us (1.089)
  the two profiles are of different devices: /device:TPU:0 before, /device:TPU:7 now
where the time goes in v5:
time: 41.7 us; the launch traced here: 41.5 us
  starting transfers between devices  18.8 us (45%)
  Pallas kernels  13.5 us (32%)
  waiting for transfers between devices  8.49 us (20%)
  between operations  0.75 us (2%)
    ppermute x10, starting transfers between devices, swap(): return lax.ppermute(value, AXES, pairs)  11 us
    ppermute x2, starting transfers between devices, with_next(): return lax.ppermute(value, AXES, pairs)  7.86 us
    pallas_call x1, Pallas kernels, on_device(): pl.pallas_call(inner_kernel, out_shape=(shape(rows, width), shape(blocks...  5 us
    ppermute x10, waiting for transfers between devices, swap(): return lax.ppermute(value, AXES, pairs)  4.49 us
    ppermute x2, waiting for transfers between devices, with_next(): return lax.ppermute(value, AXES, pairs)  4 us
    pallas_call x1, Pallas kernels, on_device(): pl.pallas_call(inner_back_kernel, out_shape=(shape(rows, width), shape(2...  2.42 us
    pallas_call x1, Pallas kernels, on_device(): pl.pallas_call(rim_back_kernel, out_shape=(shape(rows, width), shape(6 *...  1.92 us
    pallas_call x1, Pallas kernels, on_device(): pl.pallas_call(rim_kernel, out_shape=(shape(2 * rim, width), shape(2 * ri...  1.59 us
  transfers between devices with their start and end apart: 12, of which 5 were waited for; matrix products, arithmetic and copies ran while one was open for 0% of the time, Pallas kernels for 22%

profile of v5, /device:TPU:7, one launch (start us, length us, event | category | flops | bytes accessed | tf_op | source)
XLA Modules:
  0.0 41.5 jit_solution(7907401691365345485)
XLA Ops:
  0.6 1.0 %halo_rows.1 = (bf16[256,256]{1,0:T(8,128)(2,1)S(1)}, bf16[256,256]{1,0:T(8,128)(2,1)S(1)}) custom-call(bf16[1536,256]{1,0:T(8,128)(2,1)} %feat_hbm.3), custom_call_target="tpu_custom_call" | custom-call | flops 60000000 | bytes 300000 | tf_op jit(solution)/shard_map/halo_rows/pallas_call | solution.py:396
  1.6 0.3 collective-permute-start
  1.9 5.0 %collective-permute-start.1 = (bf16[256,256]{1,0:T(8,128)(2,1)S(1)}, bf16[256,256]{1,0:T(8,128)(2,1)S(1)}, u32[]{:S(2)}, u32[]{:S(2)}) collective-permute-start(bf16[256,256]{1,0:T(8,128)(2,1)S(1)} %get-tuple-element.38), channel_id=1, source_target_pairs={{1,2},{2,1},{3,4},{4,3},{5,6},{6,5},{7,8},{8,7},{9,10},{10,9},{11,... | collective-permute-start | bytes 393224 | tf_op jit(solution)/shard_map/ppermute | solution.py:341
  6.9 5.0 %inner_rows.1 = (bf16[1536,256]{1,0:T(8,128)(2,1)}, s32[36]{0:T(128)S(1)}, bf16[1024,256]{1,0:T(8,128)(2,1)S(1)}, f32[256,256]{1,0:T(8,128)S(1)}, f32[8,256]{1,0...) custom-call(s32[3,12]{1,0:T(4,128)} %bitcast.3, ...), custom_call_target="tpu_custom_call" | custom-call | flops 600000000 | bytes 3000000 | tf_op jit(solution)/shard_map/inner_rows/pallas_call | solution.py:411
  11.9 0.0 collective-permute-done.first_ref
  11.9 0.0 collective-permute-done.1.second_ref
  11.9 1.6 %rim_rows.1 = (bf16[512,256]{1,0:T(8,128)(2,1)S(1)}, bf16[512,256]{1,0:T(8,128)(2,1)S(1)}, f32[144,256]{1,0:T(8,128)S(1)}, f32[144,256]{1,0:T(8,128)S(1)}) custom-call(s32[36]{0:T(128)S(1)} %get-tuple-element.32.place_ref, bf16[256,256]{1,0:T(8,128)(2,1)S(1)} %get-tuple-element.33.weight_ref, f32[1,256]{1,0:T(1,128)S(1)} %get-tuple-element.35.bias_ref, ...), custom_call_target="tpu_custom_call" | custom-call | flops 240000000 | bytes 1200000 | tf_op jit(solution)/shard_map/rim_rows/pallas_call | solution.py:443
  13.5 0.1 collective-permute-start.2
  13.6 1.9 %rim_rows_back.1 = (bf16[1536,256]{1,0:T(8,128)(2,1)}, f32[13,256,128]{2,1,0:T(8,128)S(1)}, bf16[256,256]{1,0:T(8,128)(2,1)S(1)}, bf16[256,256]{1,0:T(8,128)(2,1)S(1)}, f32[8,128]{1,0:T(8,128)S(1)}) custom-call(s32[36]{0:T(128)S(1)} %get-tuple-element.32.place_ref, ...), custom_call_target="tpu_custom_call", output_to_operand_aliasing={{0}: (5, {})} | custom-call | flops 240000000 | bytes 1200000 | tf_op jit(solution)/shard_map/rim_rows_back/pallas_call | solution.py:466
  15.5 0.0 collective-permute-done.2.refs_1_
  15.6 1.9 %collective-permute-start.5 = (bf16[144,256]{1,0:T(8,128)(2,1)S(1)}, bf16[144,256]{1,0:T(8,128)(2,1)S(1)}, u32[]{:S(2)}, u32[]{:S(2)}) collective-permute-start(bf16[144,256]{1,0:T(8,128)(2,1)S(1)} %add_halves.3.refs_0_), channel_id=1, source_target_pairs={{0,5},{1,4},{2,26},{3,27},{4,1},{5,0},{6,30},{7,31},{8,13},{9,12},... | collective-permute-start | bytes 221192 | tf_op jit(solution)/shard_map/ppermute | solution.py:336
  17.5 0.6 %collective-permute-start.4 = (bf16[144,256]{1,0:T(8,128)(2,1)S(1)}, bf16[144,256]{1,0:T(8,128)(2,1)S(1)}, u32[]{:S(2)}, u32[]{:S(2)}) collective-permute-start(bf16[144,256]{1,0:T(8,128)(2,1)S(1)} %add_halves.3.refs_0_), channel_id=1, source_target_pairs={{0,4},{1,5},{2,18},{3,19},{4,0},{5,1},{6,22},{7,23},{8,12},{9,13},... | collective-permute-start | bytes 221192 | tf_op jit(solution)/shard_map/ppermute | solution.py:336
  18.1 1.1 %collective-permute-start.3 = (bf16[144,256]{1,0:T(8,128)(2,1)S(1)}, bf16[144,256]{1,0:T(8,128)(2,1)S(1)}, u32[]{:S(2)}, u32[]{:S(2)}) collective-permute-start(bf16[144,256]{1,0:T(8,128)(2,1)S(1)} %add_halves.3.refs_0_), channel_id=1, source_target_pairs={{0,1},{1,0},{2,10},{3,11},{4,5},{5,4},{6,14},{7,15},{8,9},{9,8},{1... | collective-permute-start | bytes 221192 | tf_op jit(solution)/shard_map/ppermute | solution.py:336
  19.2 1.5 %collective-permute-done.5.refs_3_ = bf16[144,256]{1,0:T(8,128)(2,1)S(1)} collective-permute-done((bf16[144,256]{1,0:T(8,128)(2,1)S(1)}, bf16[144,256]{1,0:T(8,128)(2,1)S(1)}, u32[]{:S(2)}, u32[]{:S(2)}) %collective-permute-start.5) | collective-permute-done | bytes 73760 | tf_op jit(solution)/shard_map/ppermute | solution.py:336
  20.6 1.7 %collective-permute-done.4.refs_2_ = bf16[144,256]{1,0:T(8,128)(2,1)S(1)} collective-permute-done((bf16[144,256]{1,0:T(8,128)(2,1)S(1)}, bf16[144,256]{1,0:T(8,128)(2,1)S(1)}, u32[]{:S(2)}, u32[]{:S(2)}) %collective-permute-start.4) | collective-permute-done | bytes 73760 | tf_op jit(solution)/shard_map/ppermute | solution.py:336
  22.4 0.0 collective-permute-done.3.refs_1_
  22.4 0.9 %collective-permute-start.8 = (bf16[144,256]{1,0:T(8,128)(2,1)S(1)}, bf16[144,256]{1,0:T(8,128)(2,1)S(1)}, u32[]{:S(2)}, u32[]{:S(2)}) collective-permute-start(bf16[144,256]{1,0:T(8,128)(2,1)S(1)} %add_halves.4.refs_0_), channel_id=1, source_target_pairs={{0,24},{1,25},{2,7},{3,6},{4,28},{5,29},{6,3},{7,2},{8,16},{9,17},... | collective-permute-start | bytes 221192 | tf_op jit(solution)/shard_map/ppermute | solution.py:336
  23.4 0.4 %collective-permute-start.7 = (bf16[144,256]{1,0:T(8,128)(2,1)S(1)}, bf16[144,256]{1,0:T(8,128)(2,1)S(1)}, u32[]{:S(2)}, u32[]{:S(2)}) collective-permute-start(bf16[144,256]{1,0:T(8,128)(2,1)S(1)} %add_halves.4.refs_0_), channel_id=1, source_target_pairs={{0,16},{1,17},{2,6},{3,7},{4,20},{5,21},{6,2},{7,3},{8,24},{9,25},... | collective-permute-start | bytes 221192 | tf_op jit(solution)/shard_map/ppermute | solution.py:336
  23.8 1.3 %collective-permute-start.6 = (bf16[144,256]{1,0:T(8,128)(2,1)S(1)}, bf16[144,256]{1,0:T(8,128)(2,1)S(1)}, u32[]{:S(2)}, u32[]{:S(2)}) collective-permute-start(bf16[144,256]{1,0:T(8,128)(2,1)S(1)} %add_halves.4.refs_0_), channel_id=1, source_target_pairs={{0,8},{1,9},{2,3},{3,2},{4,12},{5,13},{6,7},{7,6},{8,0},{9,1},{10,... | collective-permute-start | bytes 221192 | tf_op jit(solution)/shard_map/ppermute | solution.py:336
  25.2 2.4 %inner_rows_back.1 = (bf16[1536,256]{1,0:T(8,128)(2,1)}, f32[512,256]{1,0:T(8,128)S(1)}, f32[8,128]{1,0:T(8,128)S(1)}) custom-call(s32[36]{0:T(128)S(1)} %get-tuple-element.32.place_ref, bf16[256,256]{1,0:T(8,128)(2,1)S(1)} %get-tuple-element.33.weight_ref, bf16[8,3,128,128]{3,2,1,0:T(8,128)(2,1)S(1)} %get-tuple-element.49.adj_ref, ...), custom_call_target="tpu_custom_call" | custom-call | flops 360000000 | bytes 1800000 | tf_op jit(solution)/shard_map/inner_rows_back/pallas_call | solution.py:485
  27.6 0.0 collective-permute-done.8.refs_3_
  27.6 0.0 collective-permute-done.7.refs_2_
  27.6 0.1 collective-permute-done.6.refs_1_
  27.7 3.3 %collective-permute-start.9 = (f32[144,256]{1,0:T(8,128)S(1)}, f32[144,256]{1,0:T(8,128)S(1)}, u32[]{:S(2)}, u32[]{:S(2)}) collective-permute-start(f32[144,256]{1,0:T(8,128)S(1)} %add_halves.5.own_ref), channel_id=1, source_target_pairs={{0,2},{1,3},{2,0},{3,1},{4,6},{5,7},{6,4},{7,5},{8,10},{9,11},{10,... | collective-permute-start | bytes 442376 | tf_op jit(solution)/shard_map/ppermute | solution.py:336
  31.0 1.0 %collective-permute-start.10 = (bf16[256,256]{1,0:T(8,128)(2,1)S(1)}, bf16[256,256]{1,0:T(8,128)(2,1)S(1)}, u32[]{:S(2)}, u32[]{:S(2)}) collective-permute-start(bf16[256,256]{1,0:T(8,128)(2,1)S(1)} %get-tuple-element.54), channel_id=1, source_target_pairs={{0,1},{1,0},{2,3},{3,2},{4,5},{5,4},{6,7},{7,6},{8,9},{9,8},{10,11... | collective-permute-start | bytes 393224 | tf_op jit(solution)/shard_map/ppermute | solution.py:336
  32.0 2.9 %collective-permute-start.11 = (bf16[256,256]{1,0:T(8,128)(2,1)S(1)}, bf16[256,256]{1,0:T(8,128)(2,1)S(1)}, u32[]{:S(2)}, u32[]{:S(2)}) collective-permute-start(bf16[256,256]{1,0:T(8,128)(2,1)S(1)} %get-tuple-element.55), channel_id=1, source_target_pairs={{1,2},{2,1},{3,4},{4,3},{5,6},{6,5},{7,8},{8,7},{9,10},{10,9},{11,... | collective-permute-start | bytes 393224 | tf_op jit(solution)/shard_map/ppermute | solution.py:341
  34.9 1.2 %collective-permute-done.10.first_ref = bf16[256,256]{1,0:T(8,128)(2,1)S(1)} collective-permute-done((bf16[256,256]{1,0:T(8,128)(2,1)S(1)}, bf16[256,256]{1,0:T(8,128)(2,1)S(1)}, u32[]{:S(2)}, u32[]{:S(2)}) %collective-permute-start.10) | collective-permute-done | bytes 131104 | tf_op jit(solution)/shard_map/ppermute | solution.py:336
  36.1 4.0 %collective-permute-done.11.second_ref = bf16[256,256]{1,0:T(8,128)(2,1)S(1)} collective-permute-done((bf16[256,256]{1,0:T(8,128)(2,1)S(1)}, bf16[256,256]{1,0:T(8,128)(2,1)S(1)}, u32[]{:S(2)}, u32[]{:S(2)}) %collective-permute-start.11) | collective-permute-done | bytes 131104 | tf_op jit(solution)/shard_map/ppermute | solution.py:341
  40.1 0.0 collective-permute-done.9.other_ref
  40.1 1.4 %last_step.1 = (f32[256,256]{1,0:T(8,128)}, f32[1,256]{1,0:T(1,128)}, bf16[1536,256]{1,0:T(8,128)(2,1)}) custom-call(f32[144,256]{1,0:T(8,128)S(1)} %add_halves.5.own_ref, f32[144,256]{1,0:T(8,128)S(1)} %collective-permute-done.9.other_ref, f32[512,256]{1,0:T(8,128)S(1)} %get-tuple-element.53.edge_ref, ...), custom_call_target="tpu_custom_call", output_to_operand_aliasing={{2}: (5, {})} | custom-call | tf_op jit(solution)/shard_map/last_step/pallas_call | solution.py:503
  (3 shorter events, 0.1 us)
Async XLA Ops:
  1.6 10.3 %collective-permute-start = (bf16[256,256]{1,0:T(8,128)(2,1)S(1)}, bf16[256,256]{1,0:T(8,128)(2,1)S(1)}, u32[]{:S(2)}, u32[]{:S(2)}) collective-permute-start(bf16[256,256]{1,0:T(8,128)(2,1)S(1)} %get-tuple-element.37), channel_id=1, source_target_pairs={{0,1},{1,0},{2,3},{3,2},{4,5},{5,4},{6,7},{7,6},{8,9},{9,8},{10,11... | collective-permute-start | bytes 393224 | tf_op jit(solution)/shard_map/ppermute | solution.py:336
  1.9 10.0 %collective-permute-start.1 = (bf16[256,256]{1,0:T(8,128)(2,1)S(1)}, bf16[256,256]{1,0:T(8,128)(2,1)S(1)}, u32[]{:S(2)}, u32[]{:S(2)}) collective-permute-start(bf16[256,256]{1,0:T(8,128)(2,1)S(1)} %get-tuple-element.38), channel_id=1, source_target_pairs={{1,2},{2,1},{3,4},{4,3},{5,6},{6,5},{7,8},{8,7},{9,10},{10,9},{11,... | collective-permute-start | bytes 393224 | tf_op jit(solution)/shard_map/ppermute | solution.py:341
  13.5 2.0 %collective-permute-start.2 = (f32[144,256]{1,0:T(8,128)S(1)}, f32[144,256]{1,0:T(8,128)S(1)}, u32[]{:S(2)}, u32[]{:S(2)}) collective-permute-start(f32[144,256]{1,0:T(8,128)S(1)} %get-tuple-element.47), channel_id=1, source_target_pairs={{0,2},{1,3},{2,0},{3,1},{4,6},{5,7},{6,4},{7,5},{8,10},{9,11},{10,... | collective-permute-start | bytes 442376 | tf_op jit(solution)/shard_map/ppermute | solution.py:336
  15.6 5.1 %collective-permute-start.5 = (bf16[144,256]{1,0:T(8,128)(2,1)S(1)}, bf16[144,256]{1,0:T(8,128)(2,1)S(1)}, u32[]{:S(2)}, u32[]{:S(2)}) collective-permute-start(bf16[144,256]{1,0:T(8,128)(2,1)S(1)} %add_halves.3.refs_0_), channel_id=1, source_target_pairs={{0,5},{1,4},{2,26},{3,27},{4,1},{5,0},{6,30},{7,31},{8,13},{9,12},... | collective-permute-start | bytes 221192 | tf_op jit(solution)/shard_map/ppermute | solution.py:336
  17.5 4.9 %collective-permute-start.4 = (bf16[144,256]{1,0:T(8,128)(2,1)S(1)}, bf16[144,256]{1,0:T(8,128)(2,1)S(1)}, u32[]{:S(2)}, u32[]{:S(2)}) collective-permute-start(bf16[144,256]{1,0:T(8,128)(2,1)S(1)} %add_halves.3.refs_0_), channel_id=1, source_target_pairs={{0,4},{1,5},{2,18},{3,19},{4,0},{5,1},{6,22},{7,23},{8,12},{9,13},... | collective-permute-start | bytes 221192 | tf_op jit(solution)/shard_map/ppermute | solution.py:336
  18.1 4.3 %collective-permute-start.3 = (bf16[144,256]{1,0:T(8,128)(2,1)S(1)}, bf16[144,256]{1,0:T(8,128)(2,1)S(1)}, u32[]{:S(2)}, u32[]{:S(2)}) collective-permute-start(bf16[144,256]{1,0:T(8,128)(2,1)S(1)} %add_halves.3.refs_0_), channel_id=1, source_target_pairs={{0,1},{1,0},{2,10},{3,11},{4,5},{5,4},{6,14},{7,15},{8,9},{9,8},{1... | collective-permute-start | bytes 221192 | tf_op jit(solution)/shard_map/ppermute | solution.py:336
  22.4 5.1 %collective-permute-start.8 = (bf16[144,256]{1,0:T(8,128)(2,1)S(1)}, bf16[144,256]{1,0:T(8,128)(2,1)S(1)}, u32[]{:S(2)}, u32[]{:S(2)}) collective-permute-start(bf16[144,256]{1,0:T(8,128)(2,1)S(1)} %add_halves.4.refs_0_), channel_id=1, source_target_pairs={{0,24},{1,25},{2,7},{3,6},{4,28},{5,29},{6,3},{7,2},{8,16},{9,17},... | collective-permute-start | bytes 221192 | tf_op jit(solution)/shard_map/ppermute | solution.py:336
  23.4 4.2 %collective-permute-start.7 = (bf16[144,256]{1,0:T(8,128)(2,1)S(1)}, bf16[144,256]{1,0:T(8,128)(2,1)S(1)}, u32[]{:S(2)}, u32[]{:S(2)}) collective-permute-start(bf16[144,256]{1,0:T(8,128)(2,1)S(1)} %add_halves.4.refs_0_), channel_id=1, source_target_pairs={{0,16},{1,17},{2,6},{3,7},{4,20},{5,21},{6,2},{7,3},{8,24},{9,25},... | collective-permute-start | bytes 221192 | tf_op jit(solution)/shard_map/ppermute | solution.py:336
  23.8 3.9 %collective-permute-start.6 = (bf16[144,256]{1,0:T(8,128)(2,1)S(1)}, bf16[144,256]{1,0:T(8,128)(2,1)S(1)}, u32[]{:S(2)}, u32[]{:S(2)}) collective-permute-start(bf16[144,256]{1,0:T(8,128)(2,1)S(1)} %add_halves.4.refs_0_), channel_id=1, source_target_pairs={{0,8},{1,9},{2,3},{3,2},{4,12},{5,13},{6,7},{7,6},{8,0},{9,1},{10,... | collective-permute-start | bytes 221192 | tf_op jit(solution)/shard_map/ppermute | solution.py:336
  27.7 12.4 %collective-permute-start.9 = (f32[144,256]{1,0:T(8,128)S(1)}, f32[144,256]{1,0:T(8,128)S(1)}, u32[]{:S(2)}, u32[]{:S(2)}) collective-permute-start(f32[144,256]{1,0:T(8,128)S(1)} %add_halves.5.own_ref), channel_id=1, source_target_pairs={{0,2},{1,3},{2,0},{3,1},{4,6},{5,7},{6,4},{7,5},{8,10},{9,11},{10,... | collective-permute-start | bytes 442376 | tf_op jit(solution)/shard_map/ppermute | solution.py:336
  31.0 5.1 %collective-permute-start.10 = (bf16[256,256]{1,0:T(8,128)(2,1)S(1)}, bf16[256,256]{1,0:T(8,128)(2,1)S(1)}, u32[]{:S(2)}, u32[]{:S(2)}) collective-permute-start(bf16[256,256]{1,0:T(8,128)(2,1)S(1)} %get-tuple-element.54), channel_id=1, source_target_pairs={{0,1},{1,0},{2,3},{3,2},{4,5},{5,4},{6,7},{7,6},{8,9},{9,8},{10,11... | collective-permute-start | bytes 393224 | tf_op jit(solution)/shard_map/ppermute | solution.py:336
  32.0 8.1 %collective-permute-start.11 = (bf16[256,256]{1,0:T(8,128)(2,1)S(1)}, bf16[256,256]{1,0:T(8,128)(2,1)S(1)}, u32[]{:S(2)}, u32[]{:S(2)}) collective-permute-start(bf16[256,256]{1,0:T(8,128)(2,1)S(1)} %get-tuple-element.55), channel_id=1, source_target_pairs={{1,2},{2,1},{3,4},{4,3},{5,6},{6,5},{7,8},{8,7},{9,10},{10,9},{11,... | collective-permute-start | bytes 393224 | tf_op jit(solution)/shard_map/ppermute | solution.py:341

commit v6 on v5

--- a/solution.py
+++ b/solution.py
@@ -496,7 +496,7 @@
         cost_estimate=cost(0.3),
         name="inner_rows_back",
     )(places, weight_near, adj_inner, grad_inner, rim_spread)
-    marks = {"core": (first_mark,), "last": (second_mark,)}
+    marks = {"core": (first_mark,), "last": (second_mark, first_part, second_part)}
     own_half = sum_halves(send, keep, count, core_bit, marks)
     other_half = swap(own_half, [1 << core_bit] * count)
     norm_scale = 1.0 / math.sqrt(rows * count)

time: 41.7 us -> 37 us (0.89)
  the two profiles are of different devices: /device:TPU:7 before, /device:TPU:0 now
where the time goes in v6:
time: 37 us; the launch traced here: 36.8 us
  starting transfers between devices  16.8 us (45%)
  Pallas kernels  13.4 us (36%)
  waiting for transfers between devices  5.83 us (16%)
  between operations  0.77 us (2%)
    ppermute x10, starting transfers between devices, swap(): return lax.ppermute(value, AXES, pairs)  15.5 us
    ppermute x10, waiting for transfers between devices, swap(): return lax.ppermute(value, AXES, pairs)  5.82 us
    pallas_call x1, Pallas kernels, on_device(): pl.pallas_call(inner_kernel, out_shape=(shape(rows, width), shape(blocks...  5 us
    pallas_call x1, Pallas kernels, on_device(): pl.pallas_call(inner_back_kernel, out_shape=(shape(rows, width), shape(2...  2.42 us
    pallas_call x1, Pallas kernels, on_device(): pl.pallas_call(rim_back_kernel, out_shape=(shape(rows, width), shape(6 *...  1.92 us
    pallas_call x1, Pallas kernels, on_device(): pl.pallas_call(rim_kernel, out_shape=(shape(2 * rim, width), shape(2 * ri...  1.59 us
    pallas_call x1, Pallas kernels, on_device(): pl.pallas_call(functools.partial(last_kernel, norm_scale), out_shape=(sha...  1.43 us
    ppermute x2, starting transfers between devices, with_next(): return lax.ppermute(value, AXES, pairs)  1.31 us
  transfers between devices with their start and end apart: 12, of which 4 were waited for; matrix products, arithmetic and copies ran while one was open for 0% of the time, Pallas kernels for 25%

profile of v6, /device:TPU:0, one launch (start us, length us, event | category | flops | bytes accessed | tf_op | source)
XLA Modules:
  0.0 36.8 jit_solution(11538918732922422343)
XLA Ops:
  0.6 1.0 %halo_rows.1 = (bf16[256,256]{1,0:T(8,128)(2,1)S(1)}, bf16[256,256]{1,0:T(8,128)(2,1)S(1)}) custom-call(bf16[1536,256]{1,0:T(8,128)(2,1)} %feat_hbm.3), custom_call_target="tpu_custom_call" | custom-call | flops 60000000 | bytes 300000 | tf_op jit(solution)/shard_map/halo_rows/pallas_call | solution.py:396
  1.6 3.0 %collective-permute-start = (bf16[256,256]{1,0:T(8,128)(2,1)S(1)}, bf16[256,256]{1,0:T(8,128)(2,1)S(1)}, u32[]{:S(2)}, u32[]{:S(2)}) collective-permute-start(bf16[256,256]{1,0:T(8,128)(2,1)S(1)} %get-tuple-element.37), channel_id=1, source_target_pairs={{0,1},{1,0},{2,3},{3,2},{4,5},{5,4},{6,7},{7,6},{8,9},{9,8},{10,11... | collective-permute-start | bytes 393224 | tf_op jit(solution)/shard_map/ppermute | solution.py:336
  4.7 0.7 %collective-permute-start.1 = (bf16[256,256]{1,0:T(8,128)(2,1)S(1)}, bf16[256,256]{1,0:T(8,128)(2,1)S(1)}, u32[]{:S(2)}, u32[]{:S(2)}) collective-permute-start(bf16[256,256]{1,0:T(8,128)(2,1)S(1)} %get-tuple-element.38), channel_id=1, source_target_pairs={{1,2},{2,1},{3,4},{4,3},{5,6},{6,5},{7,8},{8,7},{9,10},{10,9},{11,... | collective-permute-start | bytes 393224 | tf_op jit(solution)/shard_map/ppermute | solution.py:341
  5.3 5.0 %inner_rows.1 = (bf16[1536,256]{1,0:T(8,128)(2,1)}, s32[36]{0:T(128)S(1)}, bf16[1024,256]{1,0:T(8,128)(2,1)S(1)}, f32[256,256]{1,0:T(8,128)S(1)}, f32[8,256]{1,0...) custom-call(s32[3,12]{1,0:T(4,128)} %bitcast.3, ...), custom_call_target="tpu_custom_call" | custom-call | flops 600000000 | bytes 3000000 | tf_op jit(solution)/shard_map/inner_rows/pallas_call | solution.py:411
  10.3 0.0 collective-permute-done.first_ref
  10.4 0.0 collective-permute-done.1.second_ref
  10.4 1.6 %rim_rows.1 = (bf16[512,256]{1,0:T(8,128)(2,1)S(1)}, bf16[512,256]{1,0:T(8,128)(2,1)S(1)}, f32[144,256]{1,0:T(8,128)S(1)}, f32[144,256]{1,0:T(8,128)S(1)}) custom-call(s32[36]{0:T(128)S(1)} %get-tuple-element.32.place_ref, bf16[256,256]{1,0:T(8,128)(2,1)S(1)} %get-tuple-element.33.weight_ref, f32[1,256]{1,0:T(1,128)S(1)} %get-tuple-element.35.bias_ref, ...), custom_call_target="tpu_custom_call" | custom-call | flops 240000000 | bytes 1200000 | tf_op jit(solution)/shard_map/rim_rows/pallas_call | solution.py:443
  12.0 1.4 %collective-permute-start.2 = (f32[144,256]{1,0:T(8,128)S(1)}, f32[144,256]{1,0:T(8,128)S(1)}, u32[]{:S(2)}, u32[]{:S(2)}) collective-permute-start(f32[144,256]{1,0:T(8,128)S(1)} %get-tuple-element.47), channel_id=1, source_target_pairs={{0,2},{1,3},{2,0},{3,1},{4,6},{5,7},{6,4},{7,5},{8,10},{9,11},{10,... | collective-permute-start | bytes 442376 | tf_op jit(solution)/shard_map/ppermute | solution.py:336
  13.4 1.9 %rim_rows_back.1 = (bf16[1536,256]{1,0:T(8,128)(2,1)}, f32[13,256,128]{2,1,0:T(8,128)S(1)}, bf16[256,256]{1,0:T(8,128)(2,1)S(1)}, bf16[256,256]{1,0:T(8,128)(2,1)S(1)}, f32[8,128]{1,0:T(8,128)S(1)}) custom-call(s32[36]{0:T(128)S(1)} %get-tuple-element.32.place_ref, ...), custom_call_target="tpu_custom_call", output_to_operand_aliasing={{0}: (5, {})} | custom-call | flops 240000000 | bytes 1200000 | tf_op jit(solution)/shard_map/rim_rows_back/pallas_call | solution.py:466
  15.3 0.0 collective-permute-done.2.refs_1_
  15.4 4.0 %collective-permute-start.5 = (bf16[144,256]{1,0:T(8,128)(2,1)S(1)}, bf16[144,256]{1,0:T(8,128)(2,1)S(1)}, u32[]{:S(2)}, u32[]{:S(2)}) collective-permute-start(bf16[144,256]{1,0:T(8,128)(2,1)S(1)} %add_halves.3.refs_0_), channel_id=1, source_target_pairs={{0,5},{1,4},{2,26},{3,27},{4,1},{5,0},{6,30},{7,31},{8,13},{9,12},... | collective-permute-start | bytes 221192 | tf_op jit(solution)/shard_map/ppermute | solution.py:336
  19.3 0.5 %collective-permute-start.4 = (bf16[144,256]{1,0:T(8,128)(2,1)S(1)}, bf16[144,256]{1,0:T(8,128)(2,1)S(1)}, u32[]{:S(2)}, u32[]{:S(2)}) collective-permute-start(bf16[144,256]{1,0:T(8,128)(2,1)S(1)} %add_halves.3.refs_0_), channel_id=1, source_target_pairs={{0,4},{1,5},{2,18},{3,19},{4,0},{5,1},{6,22},{7,23},{8,12},{9,13},... | collective-permute-start | bytes 221192 | tf_op jit(solution)/shard_map/ppermute | solution.py:336
  19.8 0.2 collective-permute-start.3
  20.0 1.9 %collective-permute-start.9 = (bf16[256,256]{1,0:T(8,128)(2,1)S(1)}, bf16[256,256]{1,0:T(8,128)(2,1)S(1)}, u32[]{:S(2)}, u32[]{:S(2)}) collective-permute-start(bf16[256,256]{1,0:T(8,128)(2,1)S(1)} %get-tuple-element.53), channel_id=1, source_target_pairs={{0,1},{1,0},{2,3},{3,2},{4,5},{5,4},{6,7},{7,6},{8,9},{9,8},{10,11... | collective-permute-start | bytes 393224 | tf_op jit(solution)/shard_map/ppermute | solution.py:336
  21.8 0.7 %collective-permute-start.10 = (bf16[256,256]{1,0:T(8,128)(2,1)S(1)}, bf16[256,256]{1,0:T(8,128)(2,1)S(1)}, u32[]{:S(2)}, u32[]{:S(2)}) collective-permute-start(bf16[256,256]{1,0:T(8,128)(2,1)S(1)} %get-tuple-element.54), channel_id=1, source_target_pairs={{1,2},{2,1},{3,4},{4,3},{5,6},{6,5},{7,8},{8,7},{9,10},{10,9},{11,... | collective-permute-start | bytes 393224 | tf_op jit(solution)/shard_map/ppermute | solution.py:341
  22.5 0.0 collective-permute-done.5.refs_3_
  22.5 1.2 %collective-permute-done.4.refs_2_ = bf16[144,256]{1,0:T(8,128)(2,1)S(1)} collective-permute-done((bf16[144,256]{1,0:T(8,128)(2,1)S(1)}, bf16[144,256]{1,0:T(8,128)(2,1)S(1)}, u32[]{:S(2)}, u32[]{:S(2)}) %collective-permute-start.4) | collective-permute-done | bytes 73760 | tf_op jit(solution)/shard_map/ppermute | solution.py:336
  23.7 1.3 %collective-permute-done.3.refs_1_ = bf16[144,256]{1,0:T(8,128)(2,1)S(1)} collective-permute-done((bf16[144,256]{1,0:T(8,128)(2,1)S(1)}, bf16[144,256]{1,0:T(8,128)(2,1)S(1)}, u32[]{:S(2)}, u32[]{:S(2)}) %collective-permute-start.3) | collective-permute-done | bytes 73760 | tf_op jit(solution)/shard_map/ppermute | solution.py:336
  25.0 3.7 %collective-permute-start.8 = (bf16[144,256]{1,0:T(8,128)(2,1)S(1)}, bf16[144,256]{1,0:T(8,128)(2,1)S(1)}, u32[]{:S(2)}, u32[]{:S(2)}) collective-permute-start(bf16[144,256]{1,0:T(8,128)(2,1)S(1)} %add_halves.4.refs_0_), channel_id=1, source_target_pairs={{0,24},{1,25},{2,7},{3,6},{4,28},{5,29},{6,3},{7,2},{8,16},{9,17},... | collective-permute-start | bytes 221192 | tf_op jit(solution)/shard_map/ppermute | solution.py:336
  28.7 0.0 collective-permute-start.7
  28.7 0.8 %collective-permute-start.6 = (bf16[144,256]{1,0:T(8,128)(2,1)S(1)}, bf16[144,256]{1,0:T(8,128)(2,1)S(1)}, u32[]{:S(2)}, u32[]{:S(2)}) collective-permute-start(bf16[144,256]{1,0:T(8,128)(2,1)S(1)} %add_halves.4.refs_0_), channel_id=1, source_target_pairs={{0,8},{1,9},{2,3},{3,2},{4,12},{5,13},{6,7},{7,6},{8,0},{9,1},{10,... | collective-permute-start | bytes 221192 | tf_op jit(solution)/shard_map/ppermute | solution.py:336
  29.4 2.4 %inner_rows_back.1 = (bf16[1536,256]{1,0:T(8,128)(2,1)}, f32[512,256]{1,0:T(8,128)S(1)}, f32[8,128]{1,0:T(8,128)S(1)}) custom-call(s32[36]{0:T(128)S(1)} %get-tuple-element.32.place_ref, bf16[256,256]{1,0:T(8,128)(2,1)S(1)} %get-tuple-element.33.weight_ref, bf16[8,3,128,128]{3,2,1,0:T(8,128)(2,1)S(1)} %get-tuple-element.49.adj_ref, ...), custom_call_target="tpu_custom_call" | custom-call | flops 360000000 | bytes 1800000 | tf_op jit(solution)/shard_map/inner_rows_back/pallas_call | solution.py:485
  31.9 0.0 collective-permute-done.9.refs_5_.first_ref
  31.9 0.0 collective-permute-done.10.refs_6_.second_ref
  31.9 0.0 collective-permute-done.8.refs_3_
  31.9 2.0 %collective-permute-done.7.refs_2_ = bf16[144,256]{1,0:T(8,128)(2,1)S(1)} collective-permute-done((bf16[144,256]{1,0:T(8,128)(2,1)S(1)}, bf16[144,256]{1,0:T(8,128)(2,1)S(1)}, u32[]{:S(2)}, u32[]{:S(2)}) %collective-permute-start.7) | collective-permute-done | bytes 73760 | tf_op jit(solution)/shard_map/ppermute | solution.py:336
  33.9 0.0 collective-permute-done.6.refs_1_
  34.0 0.1 collective-permute-start.11
  34.0 1.4 %collective-permute-done.11.other_ref = f32[144,256]{1,0:T(8,128)S(1)} collective-permute-done((f32[144,256]{1,0:T(8,128)S(1)}, f32[144,256]{1,0:T(8,128)S(1)}, u32[]{:S(2)}, u32[]{:S(2)}) %collective-permute-start.11) | collective-permute-done | bytes 147488 | tf_op jit(solution)/shard_map/ppermute | solution.py:336
  35.4 1.4 %last_step.1 = (f32[256,256]{1,0:T(8,128)}, f32[1,256]{1,0:T(1,128)}, bf16[1536,256]{1,0:T(8,128)(2,1)}) custom-call(f32[144,256]{1,0:T(8,128)S(1)} %add_halves.5.own_ref, f32[144,256]{1,0:T(8,128)S(1)} %collective-permute-done.11.other_ref, f32[512,256]{1,0:T(8,128)S(1)} %get-tuple-element.55.edge_ref, ...), custom_call_target="tpu_custom_call", output_to_operand_aliasing={{2}: (5, {})} | custom-call | tf_op jit(solution)/shard_map/last_step/pallas_call | solution.py:503
  (3 shorter events, 0.1 us)
Async XLA Ops:
  1.6 8.7 %collective-permute-start = (bf16[256,256]{1,0:T(8,128)(2,1)S(1)}, bf16[256,256]{1,0:T(8,128)(2,1)S(1)}, u32[]{:S(2)}, u32[]{:S(2)}) collective-permute-start(bf16[256,256]{1,0:T(8,128)(2,1)S(1)} %get-tuple-element.37), channel_id=1, source_target_pairs={{0,1},{1,0},{2,3},{3,2},{4,5},{5,4},{6,7},{7,6},{8,9},{9,8},{10,11... | collective-permute-start | bytes 393224 | tf_op jit(solution)/shard_map/ppermute | solution.py:336
  4.7 5.7 %collective-permute-start.1 = (bf16[256,256]{1,0:T(8,128)(2,1)S(1)}, bf16[256,256]{1,0:T(8,128)(2,1)S(1)}, u32[]{:S(2)}, u32[]{:S(2)}) collective-permute-start(bf16[256,256]{1,0:T(8,128)(2,1)S(1)} %get-tuple-element.38), channel_id=1, source_target_pairs={{1,2},{2,1},{3,4},{4,3},{5,6},{6,5},{7,8},{8,7},{9,10},{10,9},{11,... | collective-permute-start | bytes 393224 | tf_op jit(solution)/shard_map/ppermute | solution.py:341
  12.0 3.4 %collective-permute-start.2 = (f32[144,256]{1,0:T(8,128)S(1)}, f32[144,256]{1,0:T(8,128)S(1)}, u32[]{:S(2)}, u32[]{:S(2)}) collective-permute-start(f32[144,256]{1,0:T(8,128)S(1)} %get-tuple-element.47), channel_id=1, source_target_pairs={{0,2},{1,3},{2,0},{3,1},{4,6},{5,7},{6,4},{7,5},{8,10},{9,11},{10,... | collective-permute-start | bytes 442376 | tf_op jit(solution)/shard_map/ppermute | solution.py:336
  15.4 7.2 %collective-permute-start.5 = (bf16[144,256]{1,0:T(8,128)(2,1)S(1)}, bf16[144,256]{1,0:T(8,128)(2,1)S(1)}, u32[]{:S(2)}, u32[]{:S(2)}) collective-permute-start(bf16[144,256]{1,0:T(8,128)(2,1)S(1)} %add_halves.3.refs_0_), channel_id=1, source_target_pairs={{0,5},{1,4},{2,26},{3,27},{4,1},{5,0},{6,30},{7,31},{8,13},{9,12},... | collective-permute-start | bytes 221192 | tf_op jit(solution)/shard_map/ppermute | solution.py:336
  19.3 4.4 %collective-permute-start.4 = (bf16[144,256]{1,0:T(8,128)(2,1)S(1)}, bf16[144,256]{1,0:T(8,128)(2,1)S(1)}, u32[]{:S(2)}, u32[]{:S(2)}) collective-permute-start(bf16[144,256]{1,0:T(8,128)(2,1)S(1)} %add_halves.3.refs_0_), channel_id=1, source_target_pairs={{0,4},{1,5},{2,18},{3,19},{4,0},{5,1},{6,22},{7,23},{8,12},{9,13},... | collective-permute-start | bytes 221192 | tf_op jit(solution)/shard_map/ppermute | solution.py:336
  19.8 5.1 %collective-permute-start.3 = (bf16[144,256]{1,0:T(8,128)(2,1)S(1)}, bf16[144,256]{1,0:T(8,128)(2,1)S(1)}, u32[]{:S(2)}, u32[]{:S(2)}) collective-permute-start(bf16[144,256]{1,0:T(8,128)(2,1)S(1)} %add_halves.3.refs_0_), channel_id=1, source_target_pairs={{0,1},{1,0},{2,10},{3,11},{4,5},{5,4},{6,14},{7,15},{8,9},{9,8},{1... | collective-permute-start | bytes 221192 | tf_op jit(solution)/shard_map/ppermute | solution.py:336
  20.0 11.9 %collective-permute-start.9 = (bf16[256,256]{1,0:T(8,128)(2,1)S(1)}, bf16[256,256]{1,0:T(8,128)(2,1)S(1)}, u32[]{:S(2)}, u32[]{:S(2)}) collective-permute-start(bf16[256,256]{1,0:T(8,128)(2,1)S(1)} %get-tuple-element.53), channel_id=1, source_target_pairs={{0,1},{1,0},{2,3},{3,2},{4,5},{5,4},{6,7},{7,6},{8,9},{9,8},{10,11... | collective-permute-start | bytes 393224 | tf_op jit(solution)/shard_map/ppermute | solution.py:336
  21.8 10.0 %collective-permute-start.10 = (bf16[256,256]{1,0:T(8,128)(2,1)S(1)}, bf16[256,256]{1,0:T(8,128)(2,1)S(1)}, u32[]{:S(2)}, u32[]{:S(2)}) collective-permute-start(bf16[256,256]{1,0:T(8,128)(2,1)S(1)} %get-tuple-element.54), channel_id=1, source_target_pairs={{1,2},{2,1},{3,4},{4,3},{5,6},{6,5},{7,8},{8,7},{9,10},{10,9},{11,... | collective-permute-start | bytes 393224 | tf_op jit(solution)/shard_map/ppermute | solution.py:341
  25.0 6.9 %collective-permute-start.8 = (bf16[144,256]{1,0:T(8,128)(2,1)S(1)}, bf16[144,256]{1,0:T(8,128)(2,1)S(1)}, u32[]{:S(2)}, u32[]{:S(2)}) collective-permute-start(bf16[144,256]{1,0:T(8,128)(2,1)S(1)} %add_halves.4.refs_0_), channel_id=1, source_target_pairs={{0,24},{1,25},{2,7},{3,6},{4,28},{5,29},{6,3},{7,2},{8,16},{9,17},... | collective-permute-start | bytes 221192 | tf_op jit(solution)/shard_map/ppermute | solution.py:336
  28.7 5.3 %collective-permute-start.7 = (bf16[144,256]{1,0:T(8,128)(2,1)S(1)}, bf16[144,256]{1,0:T(8,128)(2,1)S(1)}, u32[]{:S(2)}, u32[]{:S(2)}) collective-permute-start(bf16[144,256]{1,0:T(8,128)(2,1)S(1)} %add_halves.4.refs_0_), channel_id=1, source_target_pairs={{0,16},{1,17},{2,6},{3,7},{4,20},{5,21},{6,2},{7,3},{8,24},{9,25},... | collective-permute-start | bytes 221192 | tf_op jit(solution)/shard_map/ppermute | solution.py:336
  28.7 5.3 %collective-permute-start.6 = (bf16[144,256]{1,0:T(8,128)(2,1)S(1)}, bf16[144,256]{1,0:T(8,128)(2,1)S(1)}, u32[]{:S(2)}, u32[]{:S(2)}) collective-permute-start(bf16[144,256]{1,0:T(8,128)(2,1)S(1)} %add_halves.4.refs_0_), channel_id=1, source_target_pairs={{0,8},{1,9},{2,3},{3,2},{4,12},{5,13},{6,7},{7,6},{8,0},{9,1},{10,... | collective-permute-start | bytes 221192 | tf_op jit(solution)/shard_map/ppermute | solution.py:336
  34.0 1.4 %collective-permute-start.11 = (f32[144,256]{1,0:T(8,128)S(1)}, f32[144,256]{1,0:T(8,128)S(1)}, u32[]{:S(2)}, u32[]{:S(2)}) collective-permute-start(f32[144,256]{1,0:T(8,128)S(1)} %add_halves.5.own_ref), channel_id=1, source_target_pairs={{0,2},{1,3},{2,0},{3,1},{4,6},{5,7},{6,4},{7,5},{8,10},{9,11},{10,... | collective-permute-start | bytes 442376 | tf_op jit(solution)/shard_map/ppermute | solution.py:336

commit v7 on v6

--- a/solution.py
+++ b/solution.py
@@ -100,10 +100,10 @@
 
 
 def inner_kernel(
-    off_ref, cnt_ref, weight_hbm, bias_hbm, feat_hbm, adj_hbm, cot_hbm,
-    act_hbm, place_ref, grad_ref, partial_ref, sums_ref, weight_ref, bias_ref, feat_rim, adj_rim,
+    off_hbm, cnt_hbm, weight_hbm, bias_hbm, feat_hbm, adj_hbm, cot_hbm,
+    act_hbm, place_out, grad_ref, partial_ref, sums_ref, weight_ref, bias_ref, feat_rim, adj_rim,
     cot_rim, adj,
-    feat, cot, act, agg_all, sems,
+    off_ref, cnt_ref, place_ref, feat, cot, act, agg_all, sems,
 ):
     blocks, slots, block_rows, _ = adj_hbm.shape
     rows, width = feat_hbm.shape
@@ -111,6 +111,10 @@
     rim = BAND * block_rows
     half = 2 * rim
     inner = count * block_rows
+    scalars = [
+        pltpu.make_async_copy(off_hbm, off_ref, sems.at[12]),
+        pltpu.make_async_copy(cnt_hbm, cnt_ref, sems.at[13]),
+    ]
     copies = [
         pltpu.make_async_copy(feat_hbm, feat.at[pl.ds(0, rows)], sems.at[0]),
         pltpu.make_async_copy(adj_hbm.at[pl.ds(BAND, count)], adj, sems.at[1]),
@@ -130,10 +134,14 @@
             cot_hbm.at[pl.ds(rows - rim, rim)], cot_rim.at[pl.ds(rim, rim)], sems.at[10]
         ),
     ]
-    for copy in copies:
+    for copy in scalars + copies:
         copy.start()
     feat[rows:] = jnp.zeros((block_rows, width), jnp.bfloat16)
+    for copy in scalars:
+        copy.wait()
     write_places(off_ref, cnt_ref, place_ref, blocks, slots)
+    place_copy = pltpu.make_async_copy(place_ref, place_out, sems.at[14])
+    place_copy.start()
     for copy in copies[:5]:
         copy.wait()
     weight = weight_ref[...]
@@ -158,14 +166,17 @@
     for copy in copies[5:]:
         copy.wait()
     act_out.wait()
+    place_copy.wait()
 
 
 def rim_kernel(
-    place_ref, weight_ref, bias_ref, feat_ref, first_ref, second_ref, adj_ref, cot_ref,
+    place_in, weight_ref, bias_ref, feat_ref, first_ref, second_ref, adj_ref, cot_ref,
     partial_ref, sums_ref,
     act_ref, grad_ref, send_ref, keep_ref,
-    window, agg_all, payload,
+    place_ref, window, agg_all, payload, sems,
 ):
+    fetch = pltpu.make_async_copy(place_in, place_ref, sems.at[0])
+    fetch.start()
     steps, slots, block_rows, _ = adj_ref.shape
     blocks = place_ref.shape[0] // slots
     width = feat_ref.shape[1]
@@ -178,6 +189,7 @@
     weight = weight_ref[...]
     bias = bias_ref[...]
     sums = sums_ref[...]
+    fetch.wait()
     for step in range(0, steps, 2):
         for block in (step, step + 1):
             places = places_of(place_ref, rim_block(block, blocks), slots)
@@ -202,9 +214,8 @@
     send_ref[...] = payload[1 - side]
 
 
-def scatter_rows(places, weight_ref, adj_ref, grad_ref, spread):
+def scatter_rows(places, upstream, adj_ref, spread):
     _, slots, block_rows, _ = adj_ref.shape
-    upstream = to_upstream(weight_ref[...], grad_ref[...])
     for step, targets in enumerate(places):
         terms = jnp.dot(
             upstream[:, step * block_rows : (step + 1) * block_rows],
@@ -216,10 +227,12 @@
 
 
 def rim_back_kernel(
-    place_ref, weight_ref, adj_ref, grad_ref, act_ref, act_in,
+    place_in, weight_ref, adj_ref, grad_ref, act_ref, act_in,
     act_hbm, spread, first_ref, second_ref, mark_ref,
-    sems,
+    place_ref, sems,
 ):
+    fetch = pltpu.make_async_copy(place_in, place_ref, sems.at[2])
+    fetch.start()
     steps, slots, block_rows, _ = adj_ref.shape
     blocks = place_ref.shape[0] // slots
     rim = BAND * block_rows
@@ -233,9 +246,11 @@
     for copy in copies:
         copy.start()
     spread[...] = jnp.zeros_like(spread)
+    upstream = to_upstream(weight_ref[...], grad_ref[...])
+    fetch.wait()
     scatter_rows(
         [places_of(place_ref, rim_block(step, blocks), slots) for step in range(steps)],
-        weight_ref, adj_ref, grad_ref, spread,
+        upstream, adj_ref, spread,
     )
     odd = place_in_mesh() & 1
     for block in range(BAND):
@@ -248,20 +263,23 @@
 
 
 def inner_back_kernel(
-    place_ref, weight_ref, adj_ref, grad_ref, rim_spread,
-    whole_hbm, edge_ref, mark_ref,
-    spread, out, sems,
+    place_in, weight_ref, adj_ref, grad_ref, rim_spread,
+    whole_hbm, edge_ref,
+    place_ref, spread, out, sems,
 ):
+    fetch = pltpu.make_async_copy(place_in, place_ref, sems.at[1])
+    fetch.start()
     count, slots, block_rows, _ = adj_ref.shape
     blocks = place_ref.shape[0] // slots
     rim = BAND * block_rows
     spread[: 2 * BAND] = rim_spread[BAND : 3 * BAND]
     spread[2 * BAND :] = jnp.zeros_like(spread[2 * BAND :])
     spread[blocks - 2 * BAND : blocks] = rim_spread[3 * BAND : 5 * BAND]
-    mark_ref[...] = jnp.zeros_like(mark_ref)
+    upstream = to_upstream(weight_ref[...], grad_ref[...])
+    fetch.wait()
     scatter_rows(
         [places_of(place_ref, step + BAND, slots) for step in range(count)],
-        weight_ref, adj_ref, grad_ref, spread,
+        upstream, adj_ref, spread,
     )
     for step in range(count):
         here = pl.ds(step * block_rows, block_rows)
@@ -286,32 +304,34 @@
 def last_kernel(
     scale, own_ref, other_ref, edge_ref, first_ref, second_ref, whole_in,
     weight_out, bias_out, whole_hbm,
-    out, sums, sems,
+    out, sums, bias, sems,
 ):
     half = sums.shape[0] // 2
     rim = first_ref.shape[0]
     rows = whole_hbm.shape[0]
-    odd = place_in_mesh() & 1
-    for base, spill_ref in (((1 - odd) * rim, first_ref), (odd * rim, second_ref)):
-        here = pl.ds(pl.multiple_of(base, rim), rim)
-        out[here] = (edge_ref[here] + spill_ref[...].astype(jnp.float32)).astype(jnp.bfloat16)
     copies = [
-        pltpu.make_async_copy(out.at[pl.ds(0, rim)], whole_hbm.at[pl.ds(0, rim)], sems.at[0]),
+        pltpu.make_async_copy(sums, weight_out, sems.at[0]),
+        pltpu.make_async_copy(bias, bias_out, sems.at[1]),
+        pltpu.make_async_copy(out.at[pl.ds(0, rim)], whole_hbm.at[pl.ds(0, rim)], sems.at[2]),
         pltpu.make_async_copy(
-            out.at[pl.ds(rim, rim)], whole_hbm.at[pl.ds(rows - rim, rim)], sems.at[1]
-        ),
-        pltpu.make_async_copy(sums, weight_out, sems.at[2]),
+            out.at[pl.ds(rim, rim)], whole_hbm.at[pl.ds(rows - rim, rim)], sems.at[3]
+        ),
     ]
-    for copy in copies[:2]:
-        copy.start()
     side = core_side()
     own_rows = pl.ds(pl.multiple_of(side * half, half), half)
     other_rows = pl.ds(pl.multiple_of((1 - side) * half, half), half)
     sums[own_rows] = own_ref[:half] * scale
     sums[other_rows] = other_ref[:half] * scale
-    copies[2].start()
+    copies[0].start()
     first = jnp.where(side == 0, own_ref[half : half + 1], other_ref[half : half + 1])
-    bias_out[...] = first * scale
+    bias[...] = first * scale
+    copies[1].start()
+    odd = place_in_mesh() & 1
+    for base, spill_ref in (((1 - odd) * rim, first_ref), (odd * rim, second_ref)):
+        here = pl.ds(pl.multiple_of(base, rim), rim)
+        out[here] = (edge_ref[here] + spill_ref[...].astype(jnp.float32)).astype(jnp.bfloat16)
+    for copy in copies[2:]:
+        copy.start()
     for copy in copies:
         copy.wait()
 
@@ -370,9 +390,10 @@
     inner = rows - 2 * rim
     cols = lax.axis_size("cols")
     count = lax.axis_size("rows") * cols
-    smem = pl.BlockSpec(memory_space=pltpu.SMEM)
     vmem = pl.BlockSpec(memory_space=pltpu.VMEM)
     hbm = pl.BlockSpec(memory_space=pltpu.HBM)
+    anywhere = pl.BlockSpec(memory_space=pl.ANY)
+    place_scratch = pltpu.SMEM((blocks * slots,), jnp.int32)
     bias_row = bias_vector.reshape(1, width)
 
     def in_hbm(value):
@@ -423,14 +444,17 @@
             shape(2 * rim, width),
             shape(blocks - 2 * BAND, slots, block_rows, block_rows),
         ),
-        in_specs=[smem, smem] + [hbm] * 5,
-        out_specs=(hbm, smem) + (vmem,) * 9,
+        in_specs=[hbm] * 7,
+        out_specs=(hbm, anywhere) + (vmem,) * 9,
         scratch_shapes=[
+            pltpu.SMEM((slots, blocks), jnp.int32),
+            pltpu.SMEM((blocks,), jnp.int32),
+            place_scratch,
             pltpu.VMEM((rows + block_rows, width), jnp.bfloat16),
             pltpu.VMEM((inner, width), jnp.bfloat16),
             pltpu.VMEM((inner, width), jnp.bfloat16),
             pltpu.VMEM((inner, width), jnp.bfloat16),
-            pltpu.SemaphoreType.DMA((12,)),
+            pltpu.SemaphoreType.DMA((15,)),
         ],
         compiler_params=params(20),
         cost_estimate=cost(0.5),
@@ -448,12 +472,14 @@
             shape(*half_shape, dtype=jnp.float32),
             shape(*half_shape, dtype=jnp.float32),
         ),
-        in_specs=[smem] + [vmem] * 9,
+        in_specs=[anywhere] + [vmem] * 9,
         out_specs=(vmem,) * 4,
         scratch_shapes=[
+            place_scratch,
             pltpu.VMEM((6 * rim + block_rows, width), jnp.bfloat16),
             pltpu.VMEM((2 * rim, width), jnp.bfloat16),
             pltpu.VMEM((2,) + half_shape, jnp.float32),
+            pltpu.SemaphoreType.DMA((1,)),
         ],
         compiler_params=params(12),
         cost_estimate=cost(0.2),
@@ -472,9 +498,9 @@
             shape(rim, width),
             mark,
         ),
-        in_specs=[smem] + [vmem] * 4 + [hbm],
+        in_specs=[anywhere] + [vmem] * 4 + [hbm],
         out_specs=(hbm,) + (vmem,) * 4,
-        scratch_shapes=[pltpu.SemaphoreType.DMA((2,))],
+        scratch_shapes=[place_scratch, pltpu.SemaphoreType.DMA((3,))],
         input_output_aliases={5: 0},
         compiler_params=params(12),
         cost_estimate=cost(0.2),
@@ -482,21 +508,22 @@
     )(places, weight_near, adj_rim, grad_rim, act_rim, activated)
     first_part = swap(first_spill, [1] * count)
     second_part = with_next(second_spill, count)
-    grad_whole, edges, second_mark = pl.pallas_call(
+    grad_whole, edges = pl.pallas_call(
         inner_back_kernel,
-        out_shape=(shape(rows, width), shape(2 * rim, width, dtype=jnp.float32), mark),
-        in_specs=[smem] + [vmem] * 4,
-        out_specs=(hbm, vmem, vmem),
+        out_shape=(shape(rows, width), shape(2 * rim, width, dtype=jnp.float32)),
+        in_specs=[anywhere] + [vmem] * 4,
+        out_specs=(hbm, vmem),
         scratch_shapes=[
+            place_scratch,
             pltpu.VMEM((blocks + 1, width, block_rows), jnp.float32),
             pltpu.VMEM((inner, width), jnp.bfloat16),
-            pltpu.SemaphoreType.DMA((1,)),
+            pltpu.SemaphoreType.DMA((2,)),
         ],
         compiler_params=params(12),
-        cost_estimate=cost(0.3),
+        cost_estimate=cost(2.0),
         name="inner_rows_back",
     )(places, weight_near, adj_inner, grad_inner, rim_spread)
-    marks = {"core": (first_mark,), "last": (second_mark, first_part, second_part)}
+    marks = {0: (first_mark,)}
     own_half = sum_halves(send, keep, count, core_bit, marks)
     other_half = swap(own_half, [1 << core_bit] * count)
     norm_scale = 1.0 / math.sqrt(rows * count)
@@ -508,11 +535,12 @@
             shape(rows, width),
         ),
         in_specs=[vmem] * 5 + [hbm],
-        out_specs=(hbm, vmem, hbm),
+        out_specs=(hbm, hbm, hbm),
         scratch_shapes=[
             pltpu.VMEM((2 * rim, width), jnp.bfloat16),
             pltpu.VMEM((width, width), jnp.float32),
-            pltpu.SemaphoreType.DMA((3,)),
+            pltpu.VMEM((1, width), jnp.float32),
+            pltpu.SemaphoreType.DMA((4,)),
         ],
         input_output_aliases={5: 2},
         compiler_params=params(8),

time: 37 us -> 35.8 us (0.968)
  the two profiles are of different devices: /device:TPU:0 before, /device:TPU:24 now
where the time goes in v7:
time: 35.8 us; the launch traced here: 35.6 us
  starting transfers between devices  16.1 us (45%)
  Pallas kernels  10.6 us (30%)
  waiting for transfers between devices  8.18 us (23%)
  between operations  0.76 us (2%)
    ppermute x10, starting transfers between devices, swap(): return lax.ppermute(value, AXES, pairs)  11.8 us
    ppermute x2, waiting for transfers between devices, with_next(): return lax.ppermute(value, AXES, pairs)  5.28 us
    ppermute x2, starting transfers between devices, with_next(): return lax.ppermute(value, AXES, pairs)  4.28 us
    pallas_call x1, Pallas kernels, on_device(): pl.pallas_call(inner_kernel, out_shape=(shape(rows, width), shape(blocks...  3.74 us
    ppermute x10, waiting for transfers between devices, swap(): return lax.ppermute(value, AXES, pairs)  2.9 us
    pallas_call x1, Pallas kernels, on_device(): pl.pallas_call(inner_back_kernel, out_shape=(shape(rows, width), shape(2...  2.22 us
    pallas_call x1, Pallas kernels, on_device(): pl.pallas_call(rim_kernel, out_shape=(shape(2 * rim, width), shape(2 * ri...  1.53 us
    pallas_call x1, Pallas kernels, on_device(): pl.pallas_call(rim_back_kernel, out_shape=(shape(rows, width), shape(6 *...  1.11 us
  transfers between devices with their start and end apart: 12, of which 5 were waited for; matrix products, arithmetic and copies ran while one was open for 0% of the time, Pallas kernels for 20%

profile of v7, /device:TPU:24, one launch (start us, length us, event | category | flops | bytes accessed | tf_op | source)
XLA Modules:
  0.0 35.6 jit_solution(7176810192589398490)
XLA Ops:
  0.6 1.0 %halo_rows.1 = (bf16[256,256]{1,0:T(8,128)(2,1)S(1)}, bf16[256,256]{1,0:T(8,128)(2,1)S(1)}) custom-call(bf16[1536,256]{1,0:T(8,128)(2,1)} %feat_hbm.3), custom_call_target="tpu_custom_call" | custom-call | flops 60000000 | bytes 300000 | tf_op jit(solution)/shard_map/halo_rows/pallas_call | solution.py:417
  1.6 1.6 %collective-permute-start = (bf16[256,256]{1,0:T(8,128)(2,1)S(1)}, bf16[256,256]{1,0:T(8,128)(2,1)S(1)}, u32[]{:S(2)}, u32[]{:S(2)}) collective-permute-start(bf16[256,256]{1,0:T(8,128)(2,1)S(1)} %get-tuple-element.36), channel_id=1, source_target_pairs={{0,1},{1,0},{2,3},{3,2},{4,5},{5,4},{6,7},{7,6},{8,9},{9,8},{10,11... | collective-permute-start | bytes 393224 | tf_op jit(solution)/shard_map/ppermute | solution.py:356
  3.2 2.4 %collective-permute-start.1 = (bf16[256,256]{1,0:T(8,128)(2,1)S(1)}, bf16[256,256]{1,0:T(8,128)(2,1)S(1)}, u32[]{:S(2)}, u32[]{:S(2)}) collective-permute-start(bf16[256,256]{1,0:T(8,128)(2,1)S(1)} %get-tuple-element.37), channel_id=1, source_target_pairs={{1,2},{2,1},{3,4},{4,3},{5,6},{6,5},{7,8},{8,7},{9,10},{10,9},{11,... | collective-permute-start | bytes 393224 | tf_op jit(solution)/shard_map/ppermute | solution.py:361
  5.6 3.7 %inner_rows.1 = (bf16[1536,256]{1,0:T(8,128)(2,1)}, s32[36]{0:T(128)S(1)}, bf16[1024,256]{1,0:T(8,128)(2,1)S(1)}, f32[256,256]{1,0:T(8,128)S(1)}, f32[8,256]{1,0...) custom-call(s32[3,12]{1,0:T(4,128)} %bitcast.3, ...), custom_call_target="tpu_custom_call" | custom-call | flops 600000000 | bytes 3000000 | tf_op jit(solution)/shard_map/inner_rows/pallas_call | solution.py:432
  9.4 0.0 collective-permute-done.first_ref
  9.4 1.9 %collective-permute-done.1.second_ref = bf16[256,256]{1,0:T(8,128)(2,1)S(1)} collective-permute-done((bf16[256,256]{1,0:T(8,128)(2,1)S(1)}, bf16[256,256]{1,0:T(8,128)(2,1)S(1)}, u32[]{:S(2)}, u32[]{:S(2)}) %collective-permute-start.1) | collective-permute-done | bytes 131104 | tf_op jit(solution)/shard_map/ppermute | solution.py:361
  11.3 1.5 %rim_rows.1 = (bf16[512,256]{1,0:T(8,128)(2,1)S(1)}, bf16[512,256]{1,0:T(8,128)(2,1)S(1)}, f32[144,256]{1,0:T(8,128)S(1)}, f32[144,256]{1,0:T(8,128)S(1)}) custom-call(s32[36]{0:T(128)S(1)} %get-tuple-element.31.place_in, bf16[256,256]{1,0:T(8,128)(2,1)S(1)} %get-tuple-element.32.weight_ref, f32[1,256]{1,0:T(1,128)S(1)} %get-tuple-element.34.bias_ref, ...), custom_call_target="tpu_custom_call" | custom-call | flops 240000000 | bytes 1200000 | tf_op jit(solution)/shard_map/rim_rows/pallas_call | solution.py:467
  12.8 0.1 collective-permute-start.2
  12.9 1.4 %collective-permute-done.2.refs_1_ = f32[144,256]{1,0:T(8,128)S(1)} collective-permute-done((f32[144,256]{1,0:T(8,128)S(1)}, f32[144,256]{1,0:T(8,128)S(1)}, u32[]{:S(2)}, u32[]{:S(2)}) %collective-permute-start.2) | collective-permute-done | bytes 147488 | tf_op jit(solution)/shard_map/ppermute | solution.py:356
  14.3 0.1 collective-permute-start.5
  14.4 1.8 %collective-permute-start.4 = (bf16[144,256]{1,0:T(8,128)(2,1)S(1)}, bf16[144,256]{1,0:T(8,128)(2,1)S(1)}, u32[]{:S(2)}, u32[]{:S(2)}) collective-permute-start(bf16[144,256]{1,0:T(8,128)(2,1)S(1)} %add_halves.3.refs_0_), channel_id=1, source_target_pairs={{0,4},{1,5},{2,18},{3,19},{4,0},{5,1},{6,22},{7,23},{8,12},{9,13},... | collective-permute-start | bytes 221192 | tf_op jit(solution)/shard_map/ppermute | solution.py:356
  16.1 1.7 %collective-permute-start.3 = (bf16[144,256]{1,0:T(8,128)(2,1)S(1)}, bf16[144,256]{1,0:T(8,128)(2,1)S(1)}, u32[]{:S(2)}, u32[]{:S(2)}) collective-permute-start(bf16[144,256]{1,0:T(8,128)(2,1)S(1)} %add_halves.3.refs_0_), channel_id=1, source_target_pairs={{0,1},{1,0},{2,10},{3,11},{4,5},{5,4},{6,14},{7,15},{8,9},{9,8},{1... | collective-permute-start | bytes 221192 | tf_op jit(solution)/shard_map/ppermute | solution.py:356
  17.8 1.1 %rim_rows_back.1 = (bf16[1536,256]{1,0:T(8,128)(2,1)}, f32[13,256,128]{2,1,0:T(8,128)S(1)}, bf16[256,256]{1,0:T(8,128)(2,1)S(1)}, bf16[256,256]{1,0:T(8,128)(2,1)S(1)}, f32[8,128]{1,0:T(8,128)S(1)}) custom-call(s32[36]{0:T(128)S(1)} %get-tuple-element.31.place_in, ...), custom_call_target="tpu_custom_call", output_to_operand_aliasing={{0}: (5, {})} | custom-call | flops 240000000 | bytes 1200000 | tf_op jit(solution)/shard_map/rim_rows_back/pallas_call | solution.py:492
  19.0 0.6 %collective-permute-done.5.refs_3_ = bf16[144,256]{1,0:T(8,128)(2,1)S(1)} collective-permute-done((bf16[144,256]{1,0:T(8,128)(2,1)S(1)}, bf16[144,256]{1,0:T(8,128)(2,1)S(1)}, u32[]{:S(2)}, u32[]{:S(2)}) %collective-permute-start.5) | collective-permute-done | bytes 73760 | tf_op jit(solution)/shard_map/ppermute | solution.py:356
  19.6 0.0 collective-permute-done.4.refs_2_
  19.6 0.9 %collective-permute-done.3.refs_1_ = bf16[144,256]{1,0:T(8,128)(2,1)S(1)} collective-permute-done((bf16[144,256]{1,0:T(8,128)(2,1)S(1)}, bf16[144,256]{1,0:T(8,128)(2,1)S(1)}, u32[]{:S(2)}, u32[]{:S(2)}) %collective-permute-start.3) | collective-permute-done | bytes 73760 | tf_op jit(solution)/shard_map/ppermute | solution.py:356
  20.5 0.3 collective-permute-start.8
  20.8 1.7 %collective-permute-start.7 = (bf16[144,256]{1,0:T(8,128)(2,1)S(1)}, bf16[144,256]{1,0:T(8,128)(2,1)S(1)}, u32[]{:S(2)}, u32[]{:S(2)}) collective-permute-start(bf16[144,256]{1,0:T(8,128)(2,1)S(1)} %add_halves.4.refs_0_), channel_id=1, source_target_pairs={{0,16},{1,17},{2,6},{3,7},{4,20},{5,21},{6,2},{7,3},{8,24},{9,25},... | collective-permute-start | bytes 221192 | tf_op jit(solution)/shard_map/ppermute | solution.py:356
  22.5 2.5 %collective-permute-start.6 = (bf16[144,256]{1,0:T(8,128)(2,1)S(1)}, bf16[144,256]{1,0:T(8,128)(2,1)S(1)}, u32[]{:S(2)}, u32[]{:S(2)}) collective-permute-start(bf16[144,256]{1,0:T(8,128)(2,1)S(1)} %add_halves.4.refs_0_), channel_id=1, source_target_pairs={{0,8},{1,9},{2,3},{3,2},{4,12},{5,13},{6,7},{7,6},{8,0},{9,1},{10,... | collective-permute-start | bytes 221192 | tf_op jit(solution)/shard_map/ppermute | solution.py:356
  25.0 1.7 %collective-permute-start.10 = (bf16[256,256]{1,0:T(8,128)(2,1)S(1)}, bf16[256,256]{1,0:T(8,128)(2,1)S(1)}, u32[]{:S(2)}, u32[]{:S(2)}) collective-permute-start(bf16[256,256]{1,0:T(8,128)(2,1)S(1)} %get-tuple-element.52), channel_id=1, source_target_pairs={{0,1},{1,0},{2,3},{3,2},{4,5},{5,4},{6,7},{7,6},{8,9},{9,8},{10,11... | collective-permute-start | bytes 393224 | tf_op jit(solution)/shard_map/ppermute | solution.py:356
  26.7 1.9 %collective-permute-start.11 = (bf16[256,256]{1,0:T(8,128)(2,1)S(1)}, bf16[256,256]{1,0:T(8,128)(2,1)S(1)}, u32[]{:S(2)}, u32[]{:S(2)}) collective-permute-start(bf16[256,256]{1,0:T(8,128)(2,1)S(1)} %get-tuple-element.53), channel_id=1, source_target_pairs={{1,2},{2,1},{3,4},{4,3},{5,6},{6,5},{7,8},{8,7},{9,10},{10,9},{11,... | collective-permute-start | bytes 393224 | tf_op jit(solution)/shard_map/ppermute | solution.py:361
  28.6 0.0 collective-permute-done.8.refs_3_
  28.6 0.0 collective-permute-done.7.refs_2_
  28.6 0.0 collective-permute-done.6.refs_1_
  28.7 0.5 %collective-permute-start.9 = (f32[144,256]{1,0:T(8,128)S(1)}, f32[144,256]{1,0:T(8,128)S(1)}, u32[]{:S(2)}, u32[]{:S(2)}) collective-permute-start(f32[144,256]{1,0:T(8,128)S(1)} %add_halves.5.own_ref), channel_id=1, source_target_pairs={{0,2},{1,3},{2,0},{3,1},{4,6},{5,7},{6,4},{7,5},{8,10},{9,11},{10,... | collective-permute-start | bytes 442376 | tf_op jit(solution)/shard_map/ppermute | solution.py:356
  29.2 2.2 %inner_rows_back.1 = (bf16[1536,256]{1,0:T(8,128)(2,1)}, f32[512,256]{1,0:T(8,128)S(1)}) custom-call(s32[36]{0:T(128)S(1)} %get-tuple-element.31.place_in, bf16[256,256]{1,0:T(8,128)(2,1)S(1)} %get-tuple-element.32.weight_ref, bf16[8,3,128,128]{3,2,1,0:T(8,128)(2,1)S(1)} %get-tuple-element.48.adj_ref, bf16[1024,256]{1,0:T(8,128)(2,1)S(1)} %get-tuple-element.49.grad_ref, ...), custom_call_target="tpu_custom_call" | custom-call | flops 2400000000 | bytes 12000000 | tf_op jit(solution)/shard_map/inner_rows_back/pallas_call | solution.py:511
  31.4 0.0 collective-permute-done.10.first_ref
  31.4 3.4 %collective-permute-done.11.second_ref = bf16[256,256]{1,0:T(8,128)(2,1)S(1)} collective-permute-done((bf16[256,256]{1,0:T(8,128)(2,1)S(1)}, bf16[256,256]{1,0:T(8,128)(2,1)S(1)}, u32[]{:S(2)}, u32[]{:S(2)}) %collective-permute-start.11) | collective-permute-done | bytes 131104 | tf_op jit(solution)/shard_map/ppermute | solution.py:361
  34.8 0.0 collective-permute-done.9.other_ref
  34.8 0.9 %last_step.1 = (f32[256,256]{1,0:T(8,128)}, f32[1,256]{1,0:T(1,128)}, bf16[1536,256]{1,0:T(8,128)(2,1)}) custom-call(f32[144,256]{1,0:T(8,128)S(1)} %add_halves.5.own_ref, f32[144,256]{1,0:T(8,128)S(1)} %collective-permute-done.9.other_ref, f32[512,256]{1,0:T(8,128)S(1)} %get-tuple-element.51.edge_ref, ...), custom_call_target="tpu_custom_call", output_to_operand_aliasing={{2}: (5, {})} | custom-call | tf_op jit(solution)/shard_map/last_step/pallas_call | solution.py:530
  (3 shorter events, 0.1 us)
Async XLA Ops:
  1.6 7.7 %collective-permute-start = (bf16[256,256]{1,0:T(8,128)(2,1)S(1)}, bf16[256,256]{1,0:T(8,128)(2,1)S(1)}, u32[]{:S(2)}, u32[]{:S(2)}) collective-permute-start(bf16[256,256]{1,0:T(8,128)(2,1)S(1)} %get-tuple-element.36), channel_id=1, source_target_pairs={{0,1},{1,0},{2,3},{3,2},{4,5},{5,4},{6,7},{7,6},{8,9},{9,8},{10,11... | collective-permute-start | bytes 393224 | tf_op jit(solution)/shard_map/ppermute | solution.py:356
  3.2 8.1 %collective-permute-start.1 = (bf16[256,256]{1,0:T(8,128)(2,1)S(1)}, bf16[256,256]{1,0:T(8,128)(2,1)S(1)}, u32[]{:S(2)}, u32[]{:S(2)}) collective-permute-start(bf16[256,256]{1,0:T(8,128)(2,1)S(1)} %get-tuple-element.37), channel_id=1, source_target_pairs={{1,2},{2,1},{3,4},{4,3},{5,6},{6,5},{7,8},{8,7},{9,10},{10,9},{11,... | collective-permute-start | bytes 393224 | tf_op jit(solution)/shard_map/ppermute | solution.py:361
  12.8 1.4 %collective-permute-start.2 = (f32[144,256]{1,0:T(8,128)S(1)}, f32[144,256]{1,0:T(8,128)S(1)}, u32[]{:S(2)}, u32[]{:S(2)}) collective-permute-start(f32[144,256]{1,0:T(8,128)S(1)} %get-tuple-element.46), channel_id=1, source_target_pairs={{0,2},{1,3},{2,0},{3,1},{4,6},{5,7},{6,4},{7,5},{8,10},{9,11},{10,... | collective-permute-start | bytes 442376 | tf_op jit(solution)/shard_map/ppermute | solution.py:356
  14.3 5.3 %collective-permute-start.5 = (bf16[144,256]{1,0:T(8,128)(2,1)S(1)}, bf16[144,256]{1,0:T(8,128)(2,1)S(1)}, u32[]{:S(2)}, u32[]{:S(2)}) collective-permute-start(bf16[144,256]{1,0:T(8,128)(2,1)S(1)} %add_halves.3.refs_0_), channel_id=1, source_target_pairs={{0,5},{1,4},{2,26},{3,27},{4,1},{5,0},{6,30},{7,31},{8,13},{9,12},... | collective-permute-start | bytes 221192 | tf_op jit(solution)/shard_map/ppermute | solution.py:356
  14.4 5.2 %collective-permute-start.4 = (bf16[144,256]{1,0:T(8,128)(2,1)S(1)}, bf16[144,256]{1,0:T(8,128)(2,1)S(1)}, u32[]{:S(2)}, u32[]{:S(2)}) collective-permute-start(bf16[144,256]{1,0:T(8,128)(2,1)S(1)} %add_halves.3.refs_0_), channel_id=1, source_target_pairs={{0,4},{1,5},{2,18},{3,19},{4,0},{5,1},{6,22},{7,23},{8,12},{9,13},... | collective-permute-start | bytes 221192 | tf_op jit(solution)/shard_map/ppermute | solution.py:356
  16.1 4.4 %collective-permute-start.3 = (bf16[144,256]{1,0:T(8,128)(2,1)S(1)}, bf16[144,256]{1,0:T(8,128)(2,1)S(1)}, u32[]{:S(2)}, u32[]{:S(2)}) collective-permute-start(bf16[144,256]{1,0:T(8,128)(2,1)S(1)} %add_halves.3.refs_0_), channel_id=1, source_target_pairs={{0,1},{1,0},{2,10},{3,11},{4,5},{5,4},{6,14},{7,15},{8,9},{9,8},{1... | collective-permute-start | bytes 221192 | tf_op jit(solution)/shard_map/ppermute | solution.py:356
  20.5 8.1 %collective-permute-start.8 = (bf16[144,256]{1,0:T(8,128)(2,1)S(1)}, bf16[144,256]{1,0:T(8,128)(2,1)S(1)}, u32[]{:S(2)}, u32[]{:S(2)}) collective-permute-start(bf16[144,256]{1,0:T(8,128)(2,1)S(1)} %add_halves.4.refs_0_), channel_id=1, source_target_pairs={{0,24},{1,25},{2,7},{3,6},{4,28},{5,29},{6,3},{7,2},{8,16},{9,17},... | collective-permute-start | bytes 221192 | tf_op jit(solution)/shard_map/ppermute | solution.py:356
  20.8 7.8 %collective-permute-start.7 = (bf16[144,256]{1,0:T(8,128)(2,1)S(1)}, bf16[144,256]{1,0:T(8,128)(2,1)S(1)}, u32[]{:S(2)}, u32[]{:S(2)}) collective-permute-start(bf16[144,256]{1,0:T(8,128)(2,1)S(1)} %add_halves.4.refs_0_), channel_id=1, source_target_pairs={{0,16},{1,17},{2,6},{3,7},{4,20},{5,21},{6,2},{7,3},{8,24},{9,25},... | collective-permute-start | bytes 221192 | tf_op jit(solution)/shard_map/ppermute | solution.py:356
  22.5 6.1 %collective-permute-start.6 = (bf16[144,256]{1,0:T(8,128)(2,1)S(1)}, bf16[144,256]{1,0:T(8,128)(2,1)S(1)}, u32[]{:S(2)}, u32[]{:S(2)}) collective-permute-start(bf16[144,256]{1,0:T(8,128)(2,1)S(1)} %add_halves.4.refs_0_), channel_id=1, source_target_pairs={{0,8},{1,9},{2,3},{3,2},{4,12},{5,13},{6,7},{7,6},{8,0},{9,1},{10,... | collective-permute-start | bytes 221192 | tf_op jit(solution)/shard_map/ppermute | solution.py:356
  25.0 6.4 %collective-permute-start.10 = (bf16[256,256]{1,0:T(8,128)(2,1)S(1)}, bf16[256,256]{1,0:T(8,128)(2,1)S(1)}, u32[]{:S(2)}, u32[]{:S(2)}) collective-permute-start(bf16[256,256]{1,0:T(8,128)(2,1)S(1)} %get-tuple-element.52), channel_id=1, source_target_pairs={{0,1},{1,0},{2,3},{3,2},{4,5},{5,4},{6,7},{7,6},{8,9},{9,8},{10,11... | collective-permute-start | bytes 393224 | tf_op jit(solution)/shard_map/ppermute | solution.py:356
  26.7 8.1 %collective-permute-start.11 = (bf16[256,256]{1,0:T(8,128)(2,1)S(1)}, bf16[256,256]{1,0:T(8,128)(2,1)S(1)}, u32[]{:S(2)}, u32[]{:S(2)}) collective-permute-start(bf16[256,256]{1,0:T(8,128)(2,1)S(1)} %get-tuple-element.53), channel_id=1, source_target_pairs={{1,2},{2,1},{3,4},{4,3},{5,6},{6,5},{7,8},{8,7},{9,10},{10,9},{11,... | collective-permute-start | bytes 393224 | tf_op jit(solution)/shard_map/ppermute | solution.py:361
  28.7 6.1 %collective-permute-start.9 = (f32[144,256]{1,0:T(8,128)S(1)}, f32[144,256]{1,0:T(8,128)S(1)}, u32[]{:S(2)}, u32[]{:S(2)}) collective-permute-start(f32[144,256]{1,0:T(8,128)S(1)} %add_halves.5.own_ref), channel_id=1, source_target_pairs={{0,2},{1,3},{2,0},{3,1},{4,6},{5,7},{6,4},{7,5},{8,10},{9,11},{10,... | collective-permute-start | bytes 442376 | tf_op jit(solution)/shard_map/ppermute | solution.py:356

commit v8 on v7

--- a/solution.py
+++ b/solution.py
@@ -46,10 +46,6 @@
     return [place_ref[block * slots + slot] for slot in range(slots)]
 
 
-def rim_block(step, blocks):
-    return step if step < BAND else blocks - 2 * BAND + step
-
-
 def place_in_mesh():
     return lax.axis_index("rows") * lax.axis_size("cols") + lax.axis_index("cols")
 
@@ -58,22 +54,19 @@
     return lax.axis_index("rows") & 1
 
 
-def halo_kernel(feat_hbm, first_ref, second_ref, sems):
+def rim_start(rows, rim, order):
+    odd = place_in_mesh() & 1
+    return pl.multiple_of((odd if order else 1 - odd) * (rows - rim), rim)
+
+
+def halo_kernel(feat_hbm, first_ref, sems):
     rows = feat_hbm.shape[0]
     rim = first_ref.shape[0]
-    odd = place_in_mesh() & 1
-    last = rows - rim
-    starts = ((1 - odd) * last, odd * last)
-    copies = [
-        pltpu.make_async_copy(
-            feat_hbm.at[pl.ds(pl.multiple_of(start, rim), rim)], out_ref, sems.at[i]
-        )
-        for i, (start, out_ref) in enumerate(zip(starts, (first_ref, second_ref)))
-    ]
-    for copy in copies:
-        copy.start()
-    for copy in copies:
-        copy.wait()
+    copy = pltpu.make_async_copy(
+        feat_hbm.at[pl.ds(rim_start(rows, rim, 0), rim)], first_ref, sems.at[0]
+    )
+    copy.start()
+    copy.wait()
 
 
 def activate(preact, cotangent):
@@ -99,109 +92,130 @@
     )
 
 
-def inner_kernel(
+def forward_rows(place_ref, blocks, source, adj, weight, bias, cot, act, grad_ref, agg_all):
+    _, slots, block_rows, _ = adj.shape
+    sums = jnp.zeros((8, grad_ref.shape[1]), jnp.float32)
+    for step in range(0, len(blocks), 2):
+        for i in (step, step + 1):
+            agg_all[i * block_rows : (i + 1) * block_rows] = jnp.dot(
+                row_of(adj, blocks[i], slots),
+                pick(source, places_of(place_ref, blocks[i], slots), block_rows),
+                preferred_element_type=jnp.float32,
+            ).astype(jnp.bfloat16)
+        here = pl.ds(step * block_rows, 2 * block_rows)
+        there = pl.ds(blocks[step] * block_rows, 2 * block_rows)
+        preact = jnp.dot(agg_all[here], weight, preferred_element_type=jnp.float32) + bias
+        act[here], grad = activate(preact, cot[there])
+        grad_ref[here] = grad
+        sums = sums + column_sums(grad)
+    return sums
+
+
+def inner_first_kernel(
     off_hbm, cnt_hbm, weight_hbm, bias_hbm, feat_hbm, adj_hbm, cot_hbm,
-    act_hbm, place_out, grad_ref, partial_ref, sums_ref, weight_ref, bias_ref, feat_rim, adj_rim,
-    cot_rim, adj,
-    off_ref, cnt_ref, place_ref, feat, cot, act, agg_all, sems,
+    place_out, second_ref, weight_ref, bias_ref, feat, adj, cot, act_ref, grad_ref, agg_ref,
+    sums_ref,
+    off_ref, cnt_ref, place_ref, sems,
 ):
     blocks, slots, block_rows, _ = adj_hbm.shape
     rows, width = feat_hbm.shape
-    count = blocks - 2 * BAND
     rim = BAND * block_rows
-    half = 2 * rim
-    inner = count * block_rows
+    split = blocks // 2
+    cut = split * block_rows
     scalars = [
-        pltpu.make_async_copy(off_hbm, off_ref, sems.at[12]),
-        pltpu.make_async_copy(cnt_hbm, cnt_ref, sems.at[13]),
+        pltpu.make_async_copy(off_hbm, off_ref, sems.at[0]),
+        pltpu.make_async_copy(cnt_hbm, cnt_ref, sems.at[1]),
     ]
-    copies = [
-        pltpu.make_async_copy(feat_hbm, feat.at[pl.ds(0, rows)], sems.at[0]),
-        pltpu.make_async_copy(adj_hbm.at[pl.ds(BAND, count)], adj, sems.at[1]),
-        pltpu.make_async_copy(weight_hbm, weight_ref, sems.at[2]),
-        pltpu.make_async_copy(bias_hbm, bias_ref, sems.at[3]),
-        pltpu.make_async_copy(cot_hbm.at[pl.ds(rim, inner)], cot, sems.at[4]),
-        pltpu.make_async_copy(feat_hbm.at[pl.ds(0, half)], feat_rim.at[pl.ds(0, half)], sems.at[5]),
+    early = [
+        pltpu.make_async_copy(feat_hbm, feat.at[pl.ds(0, rows)], sems.at[2]),
         pltpu.make_async_copy(
-            feat_hbm.at[pl.ds(rows - half, half)], feat_rim.at[pl.ds(half, half)], sems.at[6]
-        ),
-        pltpu.make_async_copy(adj_hbm.at[pl.ds(0, BAND)], adj_rim.at[pl.ds(0, BAND)], sems.at[7]),
+            adj_hbm.at[pl.ds(0, split)], adj.at[pl.ds(0, split)], sems.at[3]
+        ),
+        pltpu.make_async_copy(weight_hbm, weight_ref, sems.at[4]),
+        pltpu.make_async_copy(bias_hbm, bias_ref, sems.at[5]),
+        pltpu.make_async_copy(cot_hbm.at[pl.ds(0, cut)], cot.at[pl.ds(0, cut)], sems.at[6]),
+    ]
+    late = [
         pltpu.make_async_copy(
-            adj_hbm.at[pl.ds(blocks - BAND, BAND)], adj_rim.at[pl.ds(BAND, BAND)], sems.at[8]
-        ),
-        pltpu.make_async_copy(cot_hbm.at[pl.ds(0, rim)], cot_rim.at[pl.ds(0, rim)], sems.at[9]),
+            adj_hbm.at[pl.ds(split, blocks - split)], adj.at[pl.ds(split, blocks - split)],
+            sems.at[7],
+        ),
         pltpu.make_async_copy(
-            cot_hbm.at[pl.ds(rows - rim, rim)], cot_rim.at[pl.ds(rim, rim)], sems.at[10]
+            cot_hbm.at[pl.ds(cut, rows - cut)], cot.at[pl.ds(cut, rows - cut)], sems.at[8]
         ),
     ]
-    for copy in scalars + copies:
+    for copy in scalars + early + late:
         copy.start()
     feat[rows:] = jnp.zeros((block_rows, width), jnp.bfloat16)
     for copy in scalars:
         copy.wait()
     write_places(off_ref, cnt_ref, place_ref, blocks, slots)
-    place_copy = pltpu.make_async_copy(place_ref, place_out, sems.at[14])
+    place_copy = pltpu.make_async_copy(place_ref, place_out, sems.at[9])
     place_copy.start()
-    for copy in copies[:5]:
+    for copy in early:
         copy.wait()
-    weight = weight_ref[...]
-    bias = bias_ref[...]
-    sums = jnp.zeros((8, width), jnp.float32)
-    for step in range(0, count, 2):
-        for block in (step, step + 1):
-            places = places_of(place_ref, block + BAND, slots)
-            agg_all[block * block_rows : (block + 1) * block_rows] = jnp.dot(
-                row_of(adj, block, slots), pick(feat, places, block_rows),
-                preferred_element_type=jnp.float32,
-            ).astype(jnp.bfloat16)
-        here = pl.ds(step * block_rows, 2 * block_rows)
-        preact = jnp.dot(agg_all[here], weight, preferred_element_type=jnp.float32) + bias
-        act[here], grad = activate(preact, cot[here])
-        grad_ref[here] = grad
-        sums = sums + column_sums(grad)
-    act_out = pltpu.make_async_copy(act, act_hbm.at[pl.ds(rim, inner)], sems.at[11])
-    act_out.start()
-    sums_ref[...] = sums
-    partial_ref[...] = weight_terms(agg_all[...], grad_ref[...])
-    for copy in copies[5:]:
+    second_ref[...] = feat[pl.ds(rim_start(rows, rim, 1), rim)]
+    sums_ref[...] = forward_rows(
+        place_ref, range(BAND, split), feat, adj, weight_ref[...], bias_ref[...], cot, act_ref,
+        grad_ref, agg_ref,
+    )
+    place_copy.wait()
+    for copy in late:
         copy.wait()
-    act_out.wait()
-    place_copy.wait()
+
+
+def inner_second_kernel(
+    place_in, weight_ref, bias_ref, feat, adj, cot, act_first, grad_first, agg_first, sums_first,
+    act_hbm, grad_ref, partial_ref, sums_ref,
+    place_ref, act, agg_all, sems,
+):
+    blocks, _, block_rows, _ = adj.shape
+    rim = BAND * block_rows
+    rows = blocks * block_rows
+    cut = blocks // 2 * block_rows
+    copies = [
+        pltpu.make_async_copy(act_first, act_hbm.at[pl.ds(rim, cut - rim)], sems.at[0]),
+        pltpu.make_async_copy(act, act_hbm.at[pl.ds(cut, rows - rim - cut)], sems.at[1]),
+    ]
+    fetch = pltpu.make_async_copy(place_in, place_ref, sems.at[2])
+    fetch.start()
+    copies[0].start()
+    partial = weight_terms(agg_first[...], grad_first[...])
+    fetch.wait()
+    sums = forward_rows(
+        place_ref, range(blocks // 2, blocks - BAND), feat, adj, weight_ref[...], bias_ref[...],
+        cot, act, grad_ref, agg_all,
+    )
+    copies[1].start()
+    sums_ref[...] = sums_first[...] + sums
+    partial_ref[...] = partial + weight_terms(agg_all[...], grad_ref[...])
+    for copy in copies:
+        copy.wait()
 
 
 def rim_kernel(
-    place_in, weight_ref, bias_ref, feat_ref, first_ref, second_ref, adj_ref, cot_ref,
-    partial_ref, sums_ref,
+    place_in, weight_ref, bias_ref, feat, first_ref, second_ref, adj, cot, partial_ref, sums_ref,
     act_ref, grad_ref, send_ref, keep_ref,
     place_ref, window, agg_all, payload, sems,
 ):
     fetch = pltpu.make_async_copy(place_in, place_ref, sems.at[0])
     fetch.start()
-    steps, slots, block_rows, _ = adj_ref.shape
-    blocks = place_ref.shape[0] // slots
-    width = feat_ref.shape[1]
+    blocks, _, block_rows, _ = adj.shape
+    width = feat.shape[1]
     rim = BAND * block_rows
+    rows = blocks * block_rows
     odd = place_in_mesh() & 1
     window[pl.ds(pl.multiple_of((1 - odd) * 5 * rim, rim), rim)] = first_ref[...]
     window[pl.ds(pl.multiple_of(odd * 5 * rim, rim), rim)] = second_ref[...]
-    window[rim : 5 * rim] = feat_ref[...]
+    window[rim : 3 * rim] = feat[: 2 * rim]
+    window[3 * rim : 5 * rim] = feat[rows - 2 * rim : rows]
     window[6 * rim :] = jnp.zeros((block_rows, width), jnp.bfloat16)
-    weight = weight_ref[...]
-    bias = bias_ref[...]
-    sums = sums_ref[...]
     fetch.wait()
-    for step in range(0, steps, 2):
-        for block in (step, step + 1):
-            places = places_of(place_ref, rim_block(block, blocks), slots)
-            agg_all[block * block_rows : (block + 1) * block_rows] = jnp.dot(
-                row_of(adj_ref, block, slots), pick(window, places, block_rows),
-                preferred_element_type=jnp.float32,
-            ).astype(jnp.bfloat16)
-        here = pl.ds(step * block_rows, 2 * block_rows)
-        preact = jnp.dot(agg_all[here], weight, preferred_element_type=jnp.float32) + bias
-        act_ref[here], grad = activate(preact, cot_ref[here])
-        grad_ref[here] = grad
-        sums = sums + column_sums(grad)
+    rim_blocks = [*range(BAND), *range(blocks - BAND, blocks)]
+    sums = sums_ref[...] + forward_rows(
+        place_ref, rim_blocks, window, adj, weight_ref[...], bias_ref[...], cot, act_ref,
+        grad_ref, agg_all,
+    )
     half = width // 2
     partial = partial_ref[...] + weight_terms(agg_all[...], grad_ref[...])
     payload[0, :half] = partial[:half]
@@ -214,27 +228,26 @@
     send_ref[...] = payload[1 - side]
 
 
-def scatter_rows(places, upstream, adj_ref, spread):
-    _, slots, block_rows, _ = adj_ref.shape
-    for step, targets in enumerate(places):
+def scatter_rows(place_ref, blocks, upstream, adj, spread):
+    _, slots, block_rows, _ = adj.shape
+    for step, block in enumerate(blocks):
         terms = jnp.dot(
             upstream[:, step * block_rows : (step + 1) * block_rows],
-            row_of(adj_ref, step, slots),
+            row_of(adj, block, slots),
             preferred_element_type=jnp.float32,
         )
-        for slot, target in enumerate(targets):
+        for slot, target in enumerate(places_of(place_ref, block, slots)):
             spread[target] += terms[:, slot * block_rows : (slot + 1) * block_rows]
 
 
 def rim_back_kernel(
-    place_in, weight_ref, adj_ref, grad_ref, act_ref, act_in,
+    place_in, weight_ref, adj, grad_ref, act_ref, act_in,
     act_hbm, spread, first_ref, second_ref, mark_ref,
     place_ref, sems,
 ):
     fetch = pltpu.make_async_copy(place_in, place_ref, sems.at[2])
     fetch.start()
-    steps, slots, block_rows, _ = adj_ref.shape
-    blocks = place_ref.shape[0] // slots
+    blocks, _, block_rows, _ = adj.shape
     rim = BAND * block_rows
     rows = blocks * block_rows
     copies = [
@@ -248,10 +261,8 @@
     spread[...] = jnp.zeros_like(spread)
     upstream = to_upstream(weight_ref[...], grad_ref[...])
     fetch.wait()
-    scatter_rows(
-        [places_of(place_ref, rim_block(step, blocks), slots) for step in range(steps)],
-        upstream, adj_ref, spread,
-    )
+    rim_blocks = [*range(BAND), *range(blocks - BAND, blocks)]
+    scatter_rows(place_ref, rim_blocks, upstream, adj, spread)
     odd = place_in_mesh() & 1
     for block in range(BAND):
         here = pl.ds(block * block_rows, block_rows)
@@ -263,24 +274,22 @@
 
 
 def inner_back_kernel(
-    place_in, weight_ref, adj_ref, grad_ref, rim_spread,
+    place_in, weight_ref, adj, grad_first, grad_second, rim_spread,
     whole_hbm, edge_ref,
     place_ref, spread, out, sems,
 ):
     fetch = pltpu.make_async_copy(place_in, place_ref, sems.at[1])
     fetch.start()
-    count, slots, block_rows, _ = adj_ref.shape
-    blocks = place_ref.shape[0] // slots
+    blocks, _, block_rows, _ = adj.shape
+    count = blocks - 2 * BAND
     rim = BAND * block_rows
     spread[: 2 * BAND] = rim_spread[BAND : 3 * BAND]
     spread[2 * BAND :] = jnp.zeros_like(spread[2 * BAND :])
     spread[blocks - 2 * BAND : blocks] = rim_spread[3 * BAND : 5 * BAND]
-    upstream = to_upstream(weight_ref[...], grad_ref[...])
+    grad = jnp.concatenate([grad_first[...], grad_second[...]], 0)
+    upstream = to_upstream(weight_ref[...], grad)
     fetch.wait()
-    scatter_rows(
-        [places_of(place_ref, step + BAND, slots) for step in range(count)],
-        upstream, adj_ref, spread,
-    )
+    scatter_rows(place_ref, range(BAND, blocks - BAND), upstream, adj, spread)
     for step in range(count):
         here = pl.ds(step * block_rows, block_rows)
         out[here] = spread[BAND + step].T.astype(jnp.bfloat16)
@@ -414,54 +423,74 @@
     offsets = in_hbm(adj_offset.T)
     counts = in_hbm(adj_count)
     core_bit = cols.bit_length() - 1
-    first_rim, second_rim = pl.pallas_call(
+    first_rim = pl.pallas_call(
         halo_kernel,
-        out_shape=(shape(rim, width), shape(rim, width)),
+        out_shape=shape(rim, width),
         in_specs=[hbm],
-        out_specs=(vmem, vmem),
-        scratch_shapes=[pltpu.SemaphoreType.DMA((2,))],
+        out_specs=vmem,
+        scratch_shapes=[pltpu.SemaphoreType.DMA((1,))],
         compiler_params=params(2),
         cost_estimate=cost(0.05),
         name="halo_rows",
     )(in_hbm(features))
     first_halo = swap(first_rim, [1] * count)
-    second_halo = with_next(second_rim, count)
+    cut = blocks // 2 * block_rows
     (
-        activated, places, grad_inner, partial, sums, weight_near, bias_near, feat_rim, adj_rim,
-        cot_rim, adj_inner,
+        places, second_rim, weight_near, bias_near, feat_near, adj_near, cot_near, act_first,
+        grad_first, agg_first, sums_first,
     ) = pl.pallas_call(
-        inner_kernel,
+        inner_first_kernel,
         out_shape=(
-            shape(rows, width),
             shape(blocks * slots, dtype=jnp.int32),
-            shape(inner, width),
-            shape(width, width, dtype=jnp.float32),
-            shape(8, width, dtype=jnp.float32),
+            shape(rim, width),
             shape(width, width),
             shape(1, width, dtype=jnp.float32),
-            shape(4 * rim, width),
-            shape(2 * BAND, slots, block_rows, block_rows),
-            shape(2 * rim, width),
-            shape(blocks - 2 * BAND, slots, block_rows, block_rows),
+            shape(rows + block_rows, width),
+            shape(*adj_values.shape),
+            shape(rows, width),
+            shape(cut - rim, width),
+            shape(cut - rim, width),
+            shape(cut - rim, width),
+            shape(8, width, dtype=jnp.float32),
         ),
         in_specs=[hbm] * 7,
-        out_specs=(hbm, anywhere) + (vmem,) * 9,
+        out_specs=(anywhere,) + (vmem,) * 10,
         scratch_shapes=[
             pltpu.SMEM((slots, blocks), jnp.int32),
             pltpu.SMEM((blocks,), jnp.int32),
             place_scratch,
-            pltpu.VMEM((rows + block_rows, width), jnp.bfloat16),
-            pltpu.VMEM((inner, width), jnp.bfloat16),
-            pltpu.VMEM((inner, width), jnp.bfloat16),
-            pltpu.VMEM((inner, width), jnp.bfloat16),
-            pltpu.SemaphoreType.DMA((15,)),
+            pltpu.SemaphoreType.DMA((10,)),
         ],
-        compiler_params=params(20),
-        cost_estimate=cost(0.5),
-        name="inner_rows",
+        compiler_params=params(12),
+        cost_estimate=cost(0.25),
+        name="inner_rows_first",
     )(
         offsets, counts,
         *(in_hbm(x) for x in (weight, bias_row, features, adj_values, cotangent)),
+    )
+    second_halo = with_next(second_rim, count)
+    activated, grad_second, partial, sums = pl.pallas_call(
+        inner_second_kernel,
+        out_shape=(
+            shape(rows, width),
+            shape(rows - rim - cut, width),
+            shape(width, width, dtype=jnp.float32),
+            shape(8, width, dtype=jnp.float32),
+        ),
+        in_specs=[anywhere] + [vmem] * 9,
+        out_specs=(hbm,) + (vmem,) * 3,
+        scratch_shapes=[
+            place_scratch,
+            pltpu.VMEM((rows - rim - cut, width), jnp.bfloat16),
+            pltpu.VMEM((rows - rim - cut, width), jnp.bfloat16),
+            pltpu.SemaphoreType.DMA((3,)),
+        ],
+        compiler_params=params(12),
+        cost_estimate=cost(0.25),
+        name="inner_rows_second",
+    )(
+        places, weight_near, bias_near, feat_near, adj_near, cot_near, act_first, grad_first,
+        agg_first, sums_first,
     )
     half_shape = (width // 2 + TAIL, width)
     act_rim, grad_rim, send, keep = pl.pallas_call(
@@ -485,7 +514,7 @@
         cost_estimate=cost(0.2),
         name="rim_rows",
     )(
-        places, weight_near, bias_near, feat_rim, first_halo, second_halo, adj_rim, cot_rim,
+        places, weight_near, bias_near, feat_near, first_halo, second_halo, adj_near, cot_near,
         partial, sums,
     )
     mark = shape(8, 128, dtype=jnp.float32)
@@ -505,13 +534,13 @@
         compiler_params=params(12),
         cost_estimate=cost(0.2),
         name="rim_rows_back",
-    )(places, weight_near, adj_rim, grad_rim, act_rim, activated)
+    )(places, weight_near, adj_near, grad_rim, act_rim, activated)
     first_part = swap(first_spill, [1] * count)
     second_part = with_next(second_spill, count)
     grad_whole, edges = pl.pallas_call(
         inner_back_kernel,
         out_shape=(shape(rows, width), shape(2 * rim, width, dtype=jnp.float32)),
-        in_specs=[anywhere] + [vmem] * 4,
+        in_specs=[anywhere] + [vmem] * 5,
         out_specs=(hbm, vmem),
         scratch_shapes=[
             place_scratch,
@@ -522,8 +551,8 @@
         compiler_params=params(12),
         cost_estimate=cost(2.0),
         name="inner_rows_back",
-    )(places, weight_near, adj_inner, grad_inner, rim_spread)
-    marks = {0: (first_mark,)}
+    )(places, weight_near, adj_near, grad_first, grad_second, rim_spread)
+    marks = {0: (first_mark,), "last": (first_part,)}
     own_half = sum_halves(send, keep, count, core_bit, marks)
     other_half = swap(own_half, [1 << core_bit] * count)
     norm_scale = 1.0 / math.sqrt(rows * count)

time: 35.8 us -> 36.5 us (1.020)
  the two profiles are of different devices: /device:TPU:24 before, /device:TPU:0 now
where the time goes in v8:
time: 36.5 us; the launch traced here: 36.2 us
  starting transfers between devices  18.4 us (50%)
  Pallas kernels  11 us (30%)
  waiting for transfers between devices  6.1 us (17%)
  between operations  0.76 us (2%)
    ppermute x10, starting transfers between devices, swap(): return lax.ppermute(value, AXES, pairs)  17 us
    ppermute x10, waiting for transfers between devices, swap(): return lax.ppermute(value, AXES, pairs)  6.1 us
    pallas_call x1, Pallas kernels, on_device(): pl.pallas_call(inner_first_kernel, out_shape=(shape(blocks * slots, dtype...  2.24 us
    pallas_call x1, Pallas kernels, on_device(): pl.pallas_call(inner_back_kernel, out_shape=(shape(rows, width), shape(2...  2.22 us
    pallas_call x1, Pallas kernels, on_device(): pl.pallas_call(inner_second_kernel, out_shape=(shape(rows, width), shape(...  2.02 us
    pallas_call x1, Pallas kernels, on_device(): pl.pallas_call(rim_kernel, out_shape=(shape(2 * rim, width), shape(2 * ri...  1.54 us
    ppermute x2, starting transfers between devices, with_next(): return lax.ppermute(value, AXES, pairs)  1.33 us
    pallas_call x1, Pallas kernels, on_device(): pl.pallas_call(rim_back_kernel, out_shape=(shape(rows, width), shape(6 *...  1.11 us
  transfers between devices with their start and end apart: 12, of which 5 were waited for; matrix products, arithmetic and copies ran while one was open for 0% of the time, Pallas kernels for 21%

profile of v8, /device:TPU:0, one launch (start us, length us, event | category | flops | bytes accessed | tf_op | source)
XLA Modules:
  0.0 36.2 jit_solution(4752252012204154189)
XLA Ops:
  0.6 0.9 %halo_rows.1 = bf16[256,256]{1,0:T(8,128)(2,1)S(1)} custom-call(bf16[1536,256]{1,0:T(8,128)(2,1)} %feat_hbm.3), custom_call_target="tpu_custom_call" | custom-call | flops 60000000 | bytes 300000 | tf_op jit(solution)/shard_map/halo_rows/pallas_call | solution.py:426
  1.6 3.0 %collective-permute-start = (bf16[256,256]{1,0:T(8,128)(2,1)S(1)}, bf16[256,256]{1,0:T(8,128)(2,1)S(1)}, u32[]{:S(2)}, u32[]{:S(2)}) collective-permute-start(bf16[256,256]{1,0:T(8,128)(2,1)S(1)} %halo_rows.1), channel_id=1, source_target_pairs={{0,1},{1,0},{2,3},{3,2},{4,5},{5,4},{6,7},{7,6},{8,9},{9,8},{10,11... | collective-permute-start | bytes 393224 | tf_op jit(solution)/shard_map/ppermute | solution.py:365
  4.6 2.2 %inner_rows_first.1 = (s32[36]{0:T(128)S(1)}, bf16[256,256]{1,0:T(8,128)(2,1)S(1)}, bf16[256,256]{1,0:T(8,128)(2,1)S(1)}, f32[1,256]{1,0:T(1,128)S(1)}, bf16[166...) custom-call(s32[3,12]{1,0:T(4,128)} %bitcast.3, ...), custom_call_target="tpu_custom_call" | custom-call | flops 300000000 | bytes 1500000 | tf_op jit(solution)/shard_map/inner_rows_first/pallas_call | solution.py:441
  6.8 0.7 %collective-permute-start.1 = (bf16[256,256]{1,0:T(8,128)(2,1)S(1)}, bf16[256,256]{1,0:T(8,128)(2,1)S(1)}, u32[]{:S(2)}, u32[]{:S(2)}) collective-permute-start(bf16[256,256]{1,0:T(8,128)(2,1)S(1)} %get-tuple-element.38), channel_id=1, source_target_pairs={{1,2},{2,1},{3,4},{4,3},{5,6},{6,5},{7,8},{8,7},{9,10},{10,9},{11,... | collective-permute-start | bytes 393224 | tf_op jit(solution)/shard_map/ppermute | solution.py:370
  7.5 2.0 %inner_rows_second.1 = (bf16[1536,256]{1,0:T(8,128)(2,1)}, bf16[512,256]{1,0:T(8,128)(2,1)S(1)}, f32[256,256]{1,0:T(8,128)S(1)}, f32[8,256]{1,0:T(8,128)S(1)}) custom-call(s32[36]{0:T(128)S(1)} %get-tuple-element.33.place_in, bf16[256,256]{1,0:T(8,128)(2,1)S(1)} %get-tuple-element.34.weight_ref, f32[1,256]{1,0:T(1,128)S(1)} %get-tuple-element.36.bias_ref, ...), custom_call_target="tpu_custom_call" | custom-call | flops 300000000 | bytes 1500000 | tf_op jit(solution)/shard_map/inner_rows_second/pallas_call | solution.py:472
  9.5 0.0 collective-permute-done.first_ref
  9.6 0.0 collective-permute-done.1.second_ref
  9.6 1.5 %rim_rows.1 = (bf16[512,256]{1,0:T(8,128)(2,1)S(1)}, bf16[512,256]{1,0:T(8,128)(2,1)S(1)}, f32[144,256]{1,0:T(8,128)S(1)}, f32[144,256]{1,0:T(8,128)S(1)}) custom-call(s32[36]{0:T(128)S(1)} %get-tuple-element.33.place_in, bf16[256,256]{1,0:T(8,128)(2,1)S(1)} %get-tuple-element.34.weight_ref, f32[1,256]{1,0:T(1,128)S(1)} %get-tuple-element.36.bias_ref, ...), custom_call_target="tpu_custom_call" | custom-call | flops 240000000 | bytes 1200000 | tf_op jit(solution)/shard_map/rim_rows/pallas_call | solution.py:496
  11.1 3.2 %collective-permute-start.2 = (f32[144,256]{1,0:T(8,128)S(1)}, f32[144,256]{1,0:T(8,128)S(1)}, u32[]{:S(2)}, u32[]{:S(2)}) collective-permute-start(f32[144,256]{1,0:T(8,128)S(1)} %get-tuple-element.51), channel_id=1, source_target_pairs={{0,2},{1,3},{2,0},{3,1},{4,6},{5,7},{6,4},{7,5},{8,10},{9,11},{10,... | collective-permute-start | bytes 442376 | tf_op jit(solution)/shard_map/ppermute | solution.py:365
  14.3 1.0 %collective-permute-done.2.refs_1_ = f32[144,256]{1,0:T(8,128)S(1)} collective-permute-done((f32[144,256]{1,0:T(8,128)S(1)}, f32[144,256]{1,0:T(8,128)S(1)}, u32[]{:S(2)}, u32[]{:S(2)}) %collective-permute-start.2) | collective-permute-done | bytes 147488 | tf_op jit(solution)/shard_map/ppermute | solution.py:365
  15.3 3.3 %collective-permute-start.5 = (bf16[144,256]{1,0:T(8,128)(2,1)S(1)}, bf16[144,256]{1,0:T(8,128)(2,1)S(1)}, u32[]{:S(2)}, u32[]{:S(2)}) collective-permute-start(bf16[144,256]{1,0:T(8,128)(2,1)S(1)} %add_halves.3.refs_0_), channel_id=1, source_target_pairs={{0,5},{1,4},{2,26},{3,27},{4,1},{5,0},{6,30},{7,31},{8,13},{9,12},... | collective-permute-start | bytes 221192 | tf_op jit(solution)/shard_map/ppermute | solution.py:365
  18.6 0.1 collective-permute-start.4
  18.8 1.4 %collective-permute-start.3 = (bf16[144,256]{1,0:T(8,128)(2,1)S(1)}, bf16[144,256]{1,0:T(8,128)(2,1)S(1)}, u32[]{:S(2)}, u32[]{:S(2)}) collective-permute-start(bf16[144,256]{1,0:T(8,128)(2,1)S(1)} %add_halves.3.refs_0_), channel_id=1, source_target_pairs={{0,1},{1,0},{2,10},{3,11},{4,5},{5,4},{6,14},{7,15},{8,9},{9,8},{1... | collective-permute-start | bytes 221192 | tf_op jit(solution)/shard_map/ppermute | solution.py:365
  20.2 1.1 %rim_rows_back.1 = (bf16[1536,256]{1,0:T(8,128)(2,1)}, f32[13,256,128]{2,1,0:T(8,128)S(1)}, bf16[256,256]{1,0:T(8,128)(2,1)S(1)}, bf16[256,256]{1,0:T(8,128)(2,1)S(1)}, f32[8,128]{1,0:T(8,128)S(1)}) custom-call(s32[36]{0:T(128)S(1)} %get-tuple-element.33.place_in, ...), custom_call_target="tpu_custom_call", output_to_operand_aliasing={{0}: (5, {})} | custom-call | flops 240000000 | bytes 1200000 | tf_op jit(solution)/shard_map/rim_rows_back/pallas_call | solution.py:521
  21.3 0.7 %collective-permute-start.9 = (bf16[256,256]{1,0:T(8,128)(2,1)S(1)}, bf16[256,256]{1,0:T(8,128)(2,1)S(1)}, u32[]{:S(2)}, u32[]{:S(2)}) collective-permute-start(bf16[256,256]{1,0:T(8,128)(2,1)S(1)} %get-tuple-element.53), channel_id=1, source_target_pairs={{0,1},{1,0},{2,3},{3,2},{4,5},{5,4},{6,7},{7,6},{8,9},{9,8},{10,11... | collective-permute-start | bytes 393224 | tf_op jit(solution)/shard_map/ppermute | solution.py:365
  22.0 0.0 collective-permute-done.5.refs_3_
  22.0 1.0 %collective-permute-done.4.refs_2_ = bf16[144,256]{1,0:T(8,128)(2,1)S(1)} collective-permute-done((bf16[144,256]{1,0:T(8,128)(2,1)S(1)}, bf16[144,256]{1,0:T(8,128)(2,1)S(1)}, u32[]{:S(2)}, u32[]{:S(2)}) %collective-permute-start.4) | collective-permute-done | bytes 73760 | tf_op jit(solution)/shard_map/ppermute | solution.py:365
  23.0 0.1 collective-permute-done.3.refs_1_
  23.2 4.6 %collective-permute-start.8 = (bf16[144,256]{1,0:T(8,128)(2,1)S(1)}, bf16[144,256]{1,0:T(8,128)(2,1)S(1)}, u32[]{:S(2)}, u32[]{:S(2)}) collective-permute-start(bf16[144,256]{1,0:T(8,128)(2,1)S(1)} %add_halves.4.refs_0_), channel_id=1, source_target_pairs={{0,24},{1,25},{2,7},{3,6},{4,28},{5,29},{6,3},{7,2},{8,16},{9,17},... | collective-permute-start | bytes 221192 | tf_op jit(solution)/shard_map/ppermute | solution.py:365
  27.8 0.0 collective-permute-start.7
  27.8 0.6 %collective-permute-start.6 = (bf16[144,256]{1,0:T(8,128)(2,1)S(1)}, bf16[144,256]{1,0:T(8,128)(2,1)S(1)}, u32[]{:S(2)}, u32[]{:S(2)}) collective-permute-start(bf16[144,256]{1,0:T(8,128)(2,1)S(1)} %add_halves.4.refs_0_), channel_id=1, source_target_pairs={{0,8},{1,9},{2,3},{3,2},{4,12},{5,13},{6,7},{7,6},{8,0},{9,1},{10,... | collective-permute-start | bytes 221192 | tf_op jit(solution)/shard_map/ppermute | solution.py:365
  28.4 0.7 %collective-permute-start.11 = (bf16[256,256]{1,0:T(8,128)(2,1)S(1)}, bf16[256,256]{1,0:T(8,128)(2,1)S(1)}, u32[]{:S(2)}, u32[]{:S(2)}) collective-permute-start(bf16[256,256]{1,0:T(8,128)(2,1)S(1)} %get-tuple-element.57), channel_id=1, source_target_pairs={{1,2},{2,1},{3,4},{4,3},{5,6},{6,5},{7,8},{8,7},{9,10},{10,9},{11,... | collective-permute-start | bytes 393224 | tf_op jit(solution)/shard_map/ppermute | solution.py:370
  29.1 0.0 collective-permute-done.9.refs_4_.first_ref
  29.1 1.1 %collective-permute-done.8.refs_3_ = bf16[144,256]{1,0:T(8,128)(2,1)S(1)} collective-permute-done((bf16[144,256]{1,0:T(8,128)(2,1)S(1)}, bf16[144,256]{1,0:T(8,128)(2,1)S(1)}, u32[]{:S(2)}, u32[]{:S(2)}) %collective-permute-start.8) | collective-permute-done | bytes 73760 | tf_op jit(solution)/shard_map/ppermute | solution.py:365
  30.2 2.8 %collective-permute-done.7.refs_2_ = bf16[144,256]{1,0:T(8,128)(2,1)S(1)} collective-permute-done((bf16[144,256]{1,0:T(8,128)(2,1)S(1)}, bf16[144,256]{1,0:T(8,128)(2,1)S(1)}, u32[]{:S(2)}, u32[]{:S(2)}) %collective-permute-start.7) | collective-permute-done | bytes 73760 | tf_op jit(solution)/shard_map/ppermute | solution.py:365
  33.0 0.0 collective-permute-done.6.refs_1_
  33.0 0.1 collective-permute-start.10
  33.1 2.2 %inner_rows_back.1 = (bf16[1536,256]{1,0:T(8,128)(2,1)}, f32[512,256]{1,0:T(8,128)S(1)}) custom-call(s32[36]{0:T(128)S(1)} %get-tuple-element.33.place_in, bf16[256,256]{1,0:T(8,128)(2,1)S(1)} %get-tuple-element.34.weight_ref, bf16[12,3,128,128]{3,2,1,0:T(8,128)(2,1)S(1)} %get-tuple-element.35.adj, bf16[512,256]{1,0:T(8,128)(2,1)S(1)} %get-tuple-element.41.grad_first, ...), custom_call_target="tpu_custom_call" | custom-call | flops 2400000000 | bytes 12000000 | tf_op jit(solution)/shard_map/inner_rows_back/pallas_call | solution.py:540
  35.4 0.0 collective-permute-done.11.second_ref
  35.4 0.0 collective-permute-done.10.other_ref
  35.4 0.9 %last_step.1 = (f32[256,256]{1,0:T(8,128)}, f32[1,256]{1,0:T(1,128)}, bf16[1536,256]{1,0:T(8,128)(2,1)}) custom-call(f32[144,256]{1,0:T(8,128)S(1)} %add_halves.5.own_ref, f32[144,256]{1,0:T(8,128)S(1)} %collective-permute-done.10.other_ref, f32[512,256]{1,0:T(8,128)S(1)} %get-tuple-element.56.edge_ref, ...), custom_call_target="tpu_custom_call", output_to_operand_aliasing={{2}: (5, {})} | custom-call | tf_op jit(solution)/shard_map/last_step/pallas_call | solution.py:559
  (3 shorter events, 0.1 us)
Async XLA Ops:
  1.6 8.0 %collective-permute-start = (bf16[256,256]{1,0:T(8,128)(2,1)S(1)}, bf16[256,256]{1,0:T(8,128)(2,1)S(1)}, u32[]{:S(2)}, u32[]{:S(2)}) collective-permute-start(bf16[256,256]{1,0:T(8,128)(2,1)S(1)} %halo_rows.1), channel_id=1, source_target_pairs={{0,1},{1,0},{2,3},{3,2},{4,5},{5,4},{6,7},{7,6},{8,9},{9,8},{10,11... | collective-permute-start | bytes 393224 | tf_op jit(solution)/shard_map/ppermute | solution.py:365
  6.8 2.7 %collective-permute-start.1 = (bf16[256,256]{1,0:T(8,128)(2,1)S(1)}, bf16[256,256]{1,0:T(8,128)(2,1)S(1)}, u32[]{:S(2)}, u32[]{:S(2)}) collective-permute-start(bf16[256,256]{1,0:T(8,128)(2,1)S(1)} %get-tuple-element.38), channel_id=1, source_target_pairs={{1,2},{2,1},{3,4},{4,3},{5,6},{6,5},{7,8},{8,7},{9,10},{10,9},{11,... | collective-permute-start | bytes 393224 | tf_op jit(solution)/shard_map/ppermute | solution.py:370
  11.1 4.2 %collective-permute-start.2 = (f32[144,256]{1,0:T(8,128)S(1)}, f32[144,256]{1,0:T(8,128)S(1)}, u32[]{:S(2)}, u32[]{:S(2)}) collective-permute-start(f32[144,256]{1,0:T(8,128)S(1)} %get-tuple-element.51), channel_id=1, source_target_pairs={{0,2},{1,3},{2,0},{3,1},{4,6},{5,7},{6,4},{7,5},{8,10},{9,11},{10,... | collective-permute-start | bytes 442376 | tf_op jit(solution)/shard_map/ppermute | solution.py:365
  15.3 6.7 %collective-permute-start.5 = (bf16[144,256]{1,0:T(8,128)(2,1)S(1)}, bf16[144,256]{1,0:T(8,128)(2,1)S(1)}, u32[]{:S(2)}, u32[]{:S(2)}) collective-permute-start(bf16[144,256]{1,0:T(8,128)(2,1)S(1)} %add_halves.3.refs_0_), channel_id=1, source_target_pairs={{0,5},{1,4},{2,26},{3,27},{4,1},{5,0},{6,30},{7,31},{8,13},{9,12},... | collective-permute-start | bytes 221192 | tf_op jit(solution)/shard_map/ppermute | solution.py:365
  18.6 4.4 %collective-permute-start.4 = (bf16[144,256]{1,0:T(8,128)(2,1)S(1)}, bf16[144,256]{1,0:T(8,128)(2,1)S(1)}, u32[]{:S(2)}, u32[]{:S(2)}) collective-permute-start(bf16[144,256]{1,0:T(8,128)(2,1)S(1)} %add_halves.3.refs_0_), channel_id=1, source_target_pairs={{0,4},{1,5},{2,18},{3,19},{4,0},{5,1},{6,22},{7,23},{8,12},{9,13},... | collective-permute-start | bytes 221192 | tf_op jit(solution)/shard_map/ppermute | solution.py:365
  18.8 4.4 %collective-permute-start.3 = (bf16[144,256]{1,0:T(8,128)(2,1)S(1)}, bf16[144,256]{1,0:T(8,128)(2,1)S(1)}, u32[]{:S(2)}, u32[]{:S(2)}) collective-permute-start(bf16[144,256]{1,0:T(8,128)(2,1)S(1)} %add_halves.3.refs_0_), channel_id=1, source_target_pairs={{0,1},{1,0},{2,10},{3,11},{4,5},{5,4},{6,14},{7,15},{8,9},{9,8},{1... | collective-permute-start | bytes 221192 | tf_op jit(solution)/shard_map/ppermute | solution.py:365
  21.3 7.8 %collective-permute-start.9 = (bf16[256,256]{1,0:T(8,128)(2,1)S(1)}, bf16[256,256]{1,0:T(8,128)(2,1)S(1)}, u32[]{:S(2)}, u32[]{:S(2)}) collective-permute-start(bf16[256,256]{1,0:T(8,128)(2,1)S(1)} %get-tuple-element.53), channel_id=1, source_target_pairs={{0,1},{1,0},{2,3},{3,2},{4,5},{5,4},{6,7},{7,6},{8,9},{9,8},{10,11... | collective-permute-start | bytes 393224 | tf_op jit(solution)/shard_map/ppermute | solution.py:365
  23.2 7.0 %collective-permute-start.8 = (bf16[144,256]{1,0:T(8,128)(2,1)S(1)}, bf16[144,256]{1,0:T(8,128)(2,1)S(1)}, u32[]{:S(2)}, u32[]{:S(2)}) collective-permute-start(bf16[144,256]{1,0:T(8,128)(2,1)S(1)} %add_halves.4.refs_0_), channel_id=1, source_target_pairs={{0,24},{1,25},{2,7},{3,6},{4,28},{5,29},{6,3},{7,2},{8,16},{9,17},... | collective-permute-start | bytes 221192 | tf_op jit(solution)/shard_map/ppermute | solution.py:365
  27.8 5.3 %collective-permute-start.7 = (bf16[144,256]{1,0:T(8,128)(2,1)S(1)}, bf16[144,256]{1,0:T(8,128)(2,1)S(1)}, u32[]{:S(2)}, u32[]{:S(2)}) collective-permute-start(bf16[144,256]{1,0:T(8,128)(2,1)S(1)} %add_halves.4.refs_0_), channel_id=1, source_target_pairs={{0,16},{1,17},{2,6},{3,7},{4,20},{5,21},{6,2},{7,3},{8,24},{9,25},... | collective-permute-start | bytes 221192 | tf_op jit(solution)/shard_map/ppermute | solution.py:365
  27.8 5.3 %collective-permute-start.6 = (bf16[144,256]{1,0:T(8,128)(2,1)S(1)}, bf16[144,256]{1,0:T(8,128)(2,1)S(1)}, u32[]{:S(2)}, u32[]{:S(2)}) collective-permute-start(bf16[144,256]{1,0:T(8,128)(2,1)S(1)} %add_halves.4.refs_0_), channel_id=1, source_target_pairs={{0,8},{1,9},{2,3},{3,2},{4,12},{5,13},{6,7},{7,6},{8,0},{9,1},{10,... | collective-permute-start | bytes 221192 | tf_op jit(solution)/shard_map/ppermute | solution.py:365
  28.4 7.0 %collective-permute-start.11 = (bf16[256,256]{1,0:T(8,128)(2,1)S(1)}, bf16[256,256]{1,0:T(8,128)(2,1)S(1)}, u32[]{:S(2)}, u32[]{:S(2)}) collective-permute-start(bf16[256,256]{1,0:T(8,128)(2,1)S(1)} %get-tuple-element.57), channel_id=1, source_target_pairs={{1,2},{2,1},{3,4},{4,3},{5,6},{6,5},{7,8},{8,7},{9,10},{10,9},{11,... | collective-permute-start | bytes 393224 | tf_op jit(solution)/shard_map/ppermute | solution.py:370
  33.0 2.3 %collective-permute-start.10 = (f32[144,256]{1,0:T(8,128)S(1)}, f32[144,256]{1,0:T(8,128)S(1)}, u32[]{:S(2)}, u32[]{:S(2)}) collective-permute-start(f32[144,256]{1,0:T(8,128)S(1)} %add_halves.5.own_ref), channel_id=1, source_target_pairs={{0,2},{1,3},{2,0},{3,1},{4,6},{5,7},{6,4},{7,5},{8,10},{9,11},{10,... | collective-permute-start | bytes 442376 | tf_op jit(solution)/shard_map/ppermute | solution.py:365

commit v9 on v7

--- a/solution.py
+++ b/solution.py
@@ -357,7 +357,7 @@
 
 
 def with_next(value, count):
-    pairs = [(i, i + 1 if i & 1 else i - 1) for i in range(1, count - 1)]
+    pairs = [(i, (i + 1 if i & 1 else i - 1) % count) for i in range(count)]
     return lax.ppermute(value, AXES, pairs)
 
 

time: 35.8 us -> 37.1 us (1.036)
  the two profiles are of different devices: /device:TPU:24 before, /device:TPU:0 now
where the time goes in v9:
time: 37.1 us; the launch traced here: 36.9 us
  starting transfers between devices  16.8 us (45%)
  Pallas kernels  10.5 us (28%)
  waiting for transfers between devices  8.86 us (24%)
  between operations  0.72 us (2%)
    ppermute x10, starting transfers between devices, swap(): return lax.ppermute(value, AXES, pairs)  13 us
    ppermute x10, waiting for transfers between devices, swap(): return lax.ppermute(value, AXES, pairs)  5.22 us
    ppermute x2, starting transfers between devices, with_next(): return lax.ppermute(value, AXES, pairs)  3.81 us
    pallas_call x1, Pallas kernels, on_device(): pl.pallas_call(inner_kernel, out_shape=(shape(rows, width), shape(blocks...  3.73 us
    ppermute x2, waiting for transfers between devices, with_next(): return lax.ppermute(value, AXES, pairs)  3.64 us
    pallas_call x1, Pallas kernels, on_device(): pl.pallas_call(inner_back_kernel, out_shape=(shape(rows, width), shape(2...  2.22 us
    pallas_call x1, Pallas kernels, on_device(): pl.pallas_call(rim_kernel, out_shape=(shape(2 * rim, width), shape(2 * ri...  1.53 us
    pallas_call x1, Pallas kernels, on_device(): pl.pallas_call(rim_back_kernel, out_shape=(shape(rows, width), shape(6 *...  1.11 us
  transfers between devices with their start and end apart: 12, of which 7 were waited for; matrix products, arithmetic and copies ran while one was open for 0% of the time, Pallas kernels for 19%

profile of v9, /device:TPU:0, one launch (start us, length us, event | category | flops | bytes accessed | tf_op | source)
XLA Modules:
  0.0 36.9 jit_solution(6952291625315272105)
XLA Ops:
  0.6 1.0 %halo_rows.1 = (bf16[256,256]{1,0:T(8,128)(2,1)S(1)}, bf16[256,256]{1,0:T(8,128)(2,1)S(1)}) custom-call(bf16[1536,256]{1,0:T(8,128)(2,1)} %feat_hbm.3), custom_call_target="tpu_custom_call" | custom-call | flops 60000000 | bytes 300000 | tf_op jit(solution)/shard_map/halo_rows/pallas_call | solution.py:417
  1.6 3.0 %collective-permute-start = (bf16[256,256]{1,0:T(8,128)(2,1)S(1)}, bf16[256,256]{1,0:T(8,128)(2,1)S(1)}, u32[]{:S(2)}, u32[]{:S(2)}) collective-permute-start(bf16[256,256]{1,0:T(8,128)(2,1)S(1)} %get-tuple-element.36), channel_id=1, source_target_pairs={{0,1},{1,0},{2,3},{3,2},{4,5},{5,4},{6,7},{7,6},{8,9},{9,8},{10,11... | collective-permute-start | bytes 393224 | tf_op jit(solution)/shard_map/ppermute | solution.py:356
  4.7 3.6 %collective-permute-start.1 = (bf16[256,256]{1,0:T(8,128)(2,1)S(1)}, bf16[256,256]{1,0:T(8,128)(2,1)S(1)}, u32[]{:S(2)}, u32[]{:S(2)}) collective-permute-start(bf16[256,256]{1,0:T(8,128)(2,1)S(1)} %get-tuple-element.37), channel_id=1, source_target_pairs={{0,31},{1,2},{2,1},{3,4},{4,3},{5,6},{6,5},{7,8},{8,7},{9,10},{10,... | collective-permute-start | bytes 393224 | tf_op jit(solution)/shard_map/ppermute | solution.py:361
  8.3 3.7 %inner_rows.1 = (bf16[1536,256]{1,0:T(8,128)(2,1)}, s32[36]{0:T(128)S(1)}, bf16[1024,256]{1,0:T(8,128)(2,1)S(1)}, f32[256,256]{1,0:T(8,128)S(1)}, f32[8,256]{1,0...) custom-call(s32[3,12]{1,0:T(4,128)} %bitcast.3, ...), custom_call_target="tpu_custom_call" | custom-call | flops 600000000 | bytes 3000000 | tf_op jit(solution)/shard_map/inner_rows/pallas_call | solution.py:432
  12.0 0.0 collective-permute-done.first_ref
  12.0 0.6 %collective-permute-done.1.second_ref = bf16[256,256]{1,0:T(8,128)(2,1)S(1)} collective-permute-done((bf16[256,256]{1,0:T(8,128)(2,1)S(1)}, bf16[256,256]{1,0:T(8,128)(2,1)S(1)}, u32[]{:S(2)}, u32[]{:S(2)}) %collective-permute-start.1) | collective-permute-done | bytes 131104 | tf_op jit(solution)/shard_map/ppermute | solution.py:361
  12.7 1.5 %rim_rows.1 = (bf16[512,256]{1,0:T(8,128)(2,1)S(1)}, bf16[512,256]{1,0:T(8,128)(2,1)S(1)}, f32[144,256]{1,0:T(8,128)S(1)}, f32[144,256]{1,0:T(8,128)S(1)}) custom-call(s32[36]{0:T(128)S(1)} %get-tuple-element.31.place_in, bf16[256,256]{1,0:T(8,128)(2,1)S(1)} %get-tuple-element.32.weight_ref, f32[1,256]{1,0:T(1,128)S(1)} %get-tuple-element.34.bias_ref, ...), custom_call_target="tpu_custom_call" | custom-call | flops 240000000 | bytes 1200000 | tf_op jit(solution)/shard_map/rim_rows/pallas_call | solution.py:467
  14.2 0.1 collective-permute-start.2
  14.3 1.4 %collective-permute-done.2.refs_1_ = f32[144,256]{1,0:T(8,128)S(1)} collective-permute-done((f32[144,256]{1,0:T(8,128)S(1)}, f32[144,256]{1,0:T(8,128)S(1)}, u32[]{:S(2)}, u32[]{:S(2)}) %collective-permute-start.2) | collective-permute-done | bytes 147488 | tf_op jit(solution)/shard_map/ppermute | solution.py:356
  15.7 1.0 %collective-permute-start.5 = (bf16[144,256]{1,0:T(8,128)(2,1)S(1)}, bf16[144,256]{1,0:T(8,128)(2,1)S(1)}, u32[]{:S(2)}, u32[]{:S(2)}) collective-permute-start(bf16[144,256]{1,0:T(8,128)(2,1)S(1)} %add_halves.3.refs_0_), channel_id=1, source_target_pairs={{0,5},{1,4},{2,26},{3,27},{4,1},{5,0},{6,30},{7,31},{8,13},{9,12},... | collective-permute-start | bytes 221192 | tf_op jit(solution)/shard_map/ppermute | solution.py:356
  16.7 0.5 %collective-permute-start.4 = (bf16[144,256]{1,0:T(8,128)(2,1)S(1)}, bf16[144,256]{1,0:T(8,128)(2,1)S(1)}, u32[]{:S(2)}, u32[]{:S(2)}) collective-permute-start(bf16[144,256]{1,0:T(8,128)(2,1)S(1)} %add_halves.3.refs_0_), channel_id=1, source_target_pairs={{0,4},{1,5},{2,18},{3,19},{4,0},{5,1},{6,22},{7,23},{8,12},{9,13},... | collective-permute-start | bytes 221192 | tf_op jit(solution)/shard_map/ppermute | solution.py:356
  17.2 2.0 %collective-permute-start.3 = (bf16[144,256]{1,0:T(8,128)(2,1)S(1)}, bf16[144,256]{1,0:T(8,128)(2,1)S(1)}, u32[]{:S(2)}, u32[]{:S(2)}) collective-permute-start(bf16[144,256]{1,0:T(8,128)(2,1)S(1)} %add_halves.3.refs_0_), channel_id=1, source_target_pairs={{0,1},{1,0},{2,10},{3,11},{4,5},{5,4},{6,14},{7,15},{8,9},{9,8},{1... | collective-permute-start | bytes 221192 | tf_op jit(solution)/shard_map/ppermute | solution.py:356
  19.2 1.1 %rim_rows_back.1 = (bf16[1536,256]{1,0:T(8,128)(2,1)}, f32[13,256,128]{2,1,0:T(8,128)S(1)}, bf16[256,256]{1,0:T(8,128)(2,1)S(1)}, bf16[256,256]{1,0:T(8,128)(2,1)S(1)}, f32[8,128]{1,0:T(8,128)S(1)}) custom-call(s32[36]{0:T(128)S(1)} %get-tuple-element.31.place_in, ...), custom_call_target="tpu_custom_call", output_to_operand_aliasing={{0}: (5, {})} | custom-call | flops 240000000 | bytes 1200000 | tf_op jit(solution)/shard_map/rim_rows_back/pallas_call | solution.py:492
  20.3 0.7 %collective-permute-done.5.refs_3_ = bf16[144,256]{1,0:T(8,128)(2,1)S(1)} collective-permute-done((bf16[144,256]{1,0:T(8,128)(2,1)S(1)}, bf16[144,256]{1,0:T(8,128)(2,1)S(1)}, u32[]{:S(2)}, u32[]{:S(2)}) %collective-permute-start.5) | collective-permute-done | bytes 73760 | tf_op jit(solution)/shard_map/ppermute | solution.py:356
  21.0 0.1 collective-permute-done.4.refs_2_
  21.1 0.7 %collective-permute-done.3.refs_1_ = bf16[144,256]{1,0:T(8,128)(2,1)S(1)} collective-permute-done((bf16[144,256]{1,0:T(8,128)(2,1)S(1)}, bf16[144,256]{1,0:T(8,128)(2,1)S(1)}, u32[]{:S(2)}, u32[]{:S(2)}) %collective-permute-start.3) | collective-permute-done | bytes 73760 | tf_op jit(solution)/shard_map/ppermute | solution.py:356
  21.8 3.5 %collective-permute-start.8 = (bf16[144,256]{1,0:T(8,128)(2,1)S(1)}, bf16[144,256]{1,0:T(8,128)(2,1)S(1)}, u32[]{:S(2)}, u32[]{:S(2)}) collective-permute-start(bf16[144,256]{1,0:T(8,128)(2,1)S(1)} %add_halves.4.refs_0_), channel_id=1, source_target_pairs={{0,24},{1,25},{2,7},{3,6},{4,28},{5,29},{6,3},{7,2},{8,16},{9,17},... | collective-permute-start | bytes 221192 | tf_op jit(solution)/shard_map/ppermute | solution.py:356
  25.3 0.0 collective-permute-start.7
  25.3 1.0 %collective-permute-start.6 = (bf16[144,256]{1,0:T(8,128)(2,1)S(1)}, bf16[144,256]{1,0:T(8,128)(2,1)S(1)}, u32[]{:S(2)}, u32[]{:S(2)}) collective-permute-start(bf16[144,256]{1,0:T(8,128)(2,1)S(1)} %add_halves.4.refs_0_), channel_id=1, source_target_pairs={{0,8},{1,9},{2,3},{3,2},{4,12},{5,13},{6,7},{7,6},{8,0},{9,1},{10,... | collective-permute-start | bytes 221192 | tf_op jit(solution)/shard_map/ppermute | solution.py:356
  26.3 1.8 %collective-permute-start.10 = (bf16[256,256]{1,0:T(8,128)(2,1)S(1)}, bf16[256,256]{1,0:T(8,128)(2,1)S(1)}, u32[]{:S(2)}, u32[]{:S(2)}) collective-permute-start(bf16[256,256]{1,0:T(8,128)(2,1)S(1)} %get-tuple-element.52), channel_id=1, source_target_pairs={{0,1},{1,0},{2,3},{3,2},{4,5},{5,4},{6,7},{7,6},{8,9},{9,8},{10,11... | collective-permute-start | bytes 393224 | tf_op jit(solution)/shard_map/ppermute | solution.py:356
  28.1 0.2 collective-permute-start.11
  28.2 0.0 collective-permute-done.8.refs_3_
  28.2 2.4 %collective-permute-done.7.refs_2_ = bf16[144,256]{1,0:T(8,128)(2,1)S(1)} collective-permute-done((bf16[144,256]{1,0:T(8,128)(2,1)S(1)}, bf16[144,256]{1,0:T(8,128)(2,1)S(1)}, u32[]{:S(2)}, u32[]{:S(2)}) %collective-permute-start.7) | collective-permute-done | bytes 73760 | tf_op jit(solution)/shard_map/ppermute | solution.py:356
  30.7 0.0 collective-permute-done.6.refs_1_
  30.7 0.1 collective-permute-start.9
  30.8 2.2 %inner_rows_back.1 = (bf16[1536,256]{1,0:T(8,128)(2,1)}, f32[512,256]{1,0:T(8,128)S(1)}) custom-call(s32[36]{0:T(128)S(1)} %get-tuple-element.31.place_in, bf16[256,256]{1,0:T(8,128)(2,1)S(1)} %get-tuple-element.32.weight_ref, bf16[8,3,128,128]{3,2,1,0:T(8,128)(2,1)S(1)} %get-tuple-element.48.adj_ref, bf16[1024,256]{1,0:T(8,128)(2,1)S(1)} %get-tuple-element.49.grad_ref, ...), custom_call_target="tpu_custom_call" | custom-call | flops 2400000000 | bytes 12000000 | tf_op jit(solution)/shard_map/inner_rows_back/pallas_call | solution.py:511
  33.0 0.0 collective-permute-done.10.first_ref
  33.0 3.0 %collective-permute-done.11.second_ref = bf16[256,256]{1,0:T(8,128)(2,1)S(1)} collective-permute-done((bf16[256,256]{1,0:T(8,128)(2,1)S(1)}, bf16[256,256]{1,0:T(8,128)(2,1)S(1)}, u32[]{:S(2)}, u32[]{:S(2)}) %collective-permute-start.11) | collective-permute-done | bytes 131104 | tf_op jit(solution)/shard_map/ppermute | solution.py:361
  36.1 0.0 collective-permute-done.9.other_ref
  36.1 0.9 %last_step.1 = (f32[256,256]{1,0:T(8,128)}, f32[1,256]{1,0:T(1,128)}, bf16[1536,256]{1,0:T(8,128)(2,1)}) custom-call(f32[144,256]{1,0:T(8,128)S(1)} %add_halves.5.own_ref, f32[144,256]{1,0:T(8,128)S(1)} %collective-permute-done.9.other_ref, f32[512,256]{1,0:T(8,128)S(1)} %get-tuple-element.51.edge_ref, ...), custom_call_target="tpu_custom_call", output_to_operand_aliasing={{2}: (5, {})} | custom-call | tf_op jit(solution)/shard_map/last_step/pallas_call | solution.py:530
  (3 shorter events, 0.1 us)
Async XLA Ops:
  1.6 10.4 %collective-permute-start = (bf16[256,256]{1,0:T(8,128)(2,1)S(1)}, bf16[256,256]{1,0:T(8,128)(2,1)S(1)}, u32[]{:S(2)}, u32[]{:S(2)}) collective-permute-start(bf16[256,256]{1,0:T(8,128)(2,1)S(1)} %get-tuple-element.36), channel_id=1, source_target_pairs={{0,1},{1,0},{2,3},{3,2},{4,5},{5,4},{6,7},{7,6},{8,9},{9,8},{10,11... | collective-permute-start | bytes 393224 | tf_op jit(solution)/shard_map/ppermute | solution.py:356
  4.7 8.0 %collective-permute-start.1 = (bf16[256,256]{1,0:T(8,128)(2,1)S(1)}, bf16[256,256]{1,0:T(8,128)(2,1)S(1)}, u32[]{:S(2)}, u32[]{:S(2)}) collective-permute-start(bf16[256,256]{1,0:T(8,128)(2,1)S(1)} %get-tuple-element.37), channel_id=1, source_target_pairs={{0,31},{1,2},{2,1},{3,4},{4,3},{5,6},{6,5},{7,8},{8,7},{9,10},{10,... | collective-permute-start | bytes 393224 | tf_op jit(solution)/shard_map/ppermute | solution.py:361
  14.2 1.4 %collective-permute-start.2 = (f32[144,256]{1,0:T(8,128)S(1)}, f32[144,256]{1,0:T(8,128)S(1)}, u32[]{:S(2)}, u32[]{:S(2)}) collective-permute-start(f32[144,256]{1,0:T(8,128)S(1)} %get-tuple-element.46), channel_id=1, source_target_pairs={{0,2},{1,3},{2,0},{3,1},{4,6},{5,7},{6,4},{7,5},{8,10},{9,11},{10,... | collective-permute-start | bytes 442376 | tf_op jit(solution)/shard_map/ppermute | solution.py:356
  15.7 5.3 %collective-permute-start.5 = (bf16[144,256]{1,0:T(8,128)(2,1)S(1)}, bf16[144,256]{1,0:T(8,128)(2,1)S(1)}, u32[]{:S(2)}, u32[]{:S(2)}) collective-permute-start(bf16[144,256]{1,0:T(8,128)(2,1)S(1)} %add_halves.3.refs_0_), channel_id=1, source_target_pairs={{0,5},{1,4},{2,26},{3,27},{4,1},{5,0},{6,30},{7,31},{8,13},{9,12},... | collective-permute-start | bytes 221192 | tf_op jit(solution)/shard_map/ppermute | solution.py:356
  16.7 4.4 %collective-permute-start.4 = (bf16[144,256]{1,0:T(8,128)(2,1)S(1)}, bf16[144,256]{1,0:T(8,128)(2,1)S(1)}, u32[]{:S(2)}, u32[]{:S(2)}) collective-permute-start(bf16[144,256]{1,0:T(8,128)(2,1)S(1)} %add_halves.3.refs_0_), channel_id=1, source_target_pairs={{0,4},{1,5},{2,18},{3,19},{4,0},{5,1},{6,22},{7,23},{8,12},{9,13},... | collective-permute-start | bytes 221192 | tf_op jit(solution)/shard_map/ppermute | solution.py:356
  17.2 4.5 %collective-permute-start.3 = (bf16[144,256]{1,0:T(8,128)(2,1)S(1)}, bf16[144,256]{1,0:T(8,128)(2,1)S(1)}, u32[]{:S(2)}, u32[]{:S(2)}) collective-permute-start(bf16[144,256]{1,0:T(8,128)(2,1)S(1)} %add_halves.3.refs_0_), channel_id=1, source_target_pairs={{0,1},{1,0},{2,10},{3,11},{4,5},{5,4},{6,14},{7,15},{8,9},{9,8},{1... | collective-permute-start | bytes 221192 | tf_op jit(solution)/shard_map/ppermute | solution.py:356
  21.8 6.4 %collective-permute-start.8 = (bf16[144,256]{1,0:T(8,128)(2,1)S(1)}, bf16[144,256]{1,0:T(8,128)(2,1)S(1)}, u32[]{:S(2)}, u32[]{:S(2)}) collective-permute-start(bf16[144,256]{1,0:T(8,128)(2,1)S(1)} %add_halves.4.refs_0_), channel_id=1, source_target_pairs={{0,24},{1,25},{2,7},{3,6},{4,28},{5,29},{6,3},{7,2},{8,16},{9,17},... | collective-permute-start | bytes 221192 | tf_op jit(solution)/shard_map/ppermute | solution.py:356
  25.3 5.4 %collective-permute-start.7 = (bf16[144,256]{1,0:T(8,128)(2,1)S(1)}, bf16[144,256]{1,0:T(8,128)(2,1)S(1)}, u32[]{:S(2)}, u32[]{:S(2)}) collective-permute-start(bf16[144,256]{1,0:T(8,128)(2,1)S(1)} %add_halves.4.refs_0_), channel_id=1, source_target_pairs={{0,16},{1,17},{2,6},{3,7},{4,20},{5,21},{6,2},{7,3},{8,24},{9,25},... | collective-permute-start | bytes 221192 | tf_op jit(solution)/shard_map/ppermute | solution.py:356
  25.3 5.4 %collective-permute-start.6 = (bf16[144,256]{1,0:T(8,128)(2,1)S(1)}, bf16[144,256]{1,0:T(8,128)(2,1)S(1)}, u32[]{:S(2)}, u32[]{:S(2)}) collective-permute-start(bf16[144,256]{1,0:T(8,128)(2,1)S(1)} %add_halves.4.refs_0_), channel_id=1, source_target_pairs={{0,8},{1,9},{2,3},{3,2},{4,12},{5,13},{6,7},{7,6},{8,0},{9,1},{10,... | collective-permute-start | bytes 221192 | tf_op jit(solution)/shard_map/ppermute | solution.py:356
  26.3 6.8 %collective-permute-start.10 = (bf16[256,256]{1,0:T(8,128)(2,1)S(1)}, bf16[256,256]{1,0:T(8,128)(2,1)S(1)}, u32[]{:S(2)}, u32[]{:S(2)}) collective-permute-start(bf16[256,256]{1,0:T(8,128)(2,1)S(1)} %get-tuple-element.52), channel_id=1, source_target_pairs={{0,1},{1,0},{2,3},{3,2},{4,5},{5,4},{6,7},{7,6},{8,9},{9,8},{10,11... | collective-permute-start | bytes 393224 | tf_op jit(solution)/shard_map/ppermute | solution.py:356
  28.1 8.0 %collective-permute-start.11 = (bf16[256,256]{1,0:T(8,128)(2,1)S(1)}, bf16[256,256]{1,0:T(8,128)(2,1)S(1)}, u32[]{:S(2)}, u32[]{:S(2)}) collective-permute-start(bf16[256,256]{1,0:T(8,128)(2,1)S(1)} %get-tuple-element.53), channel_id=1, source_target_pairs={{0,31},{1,2},{2,1},{3,4},{4,3},{5,6},{6,5},{7,8},{8,7},{9,10},{10,... | collective-permute-start | bytes 393224 | tf_op jit(solution)/shard_map/ppermute | solution.py:361
  30.7 5.3 %collective-permute-start.9 = (f32[144,256]{1,0:T(8,128)S(1)}, f32[144,256]{1,0:T(8,128)S(1)}, u32[]{:S(2)}, u32[]{:S(2)}) collective-permute-start(f32[144,256]{1,0:T(8,128)S(1)} %add_halves.5.own_ref), channel_id=1, source_target_pairs={{0,2},{1,3},{2,0},{3,1},{4,6},{5,7},{6,4},{7,5},{8,10},{9,11},{10,... | collective-permute-start | bytes 442376 | tf_op jit(solution)/shard_map/ppermute | solution.py:356

commit v10 on v9

--- a/solution.py
+++ b/solution.py
@@ -264,7 +264,7 @@
 
 def inner_back_kernel(
     place_in, weight_ref, adj_ref, grad_ref, rim_spread,
-    whole_hbm, edge_ref,
+    whole_hbm, edge_ref, mark_ref,
     place_ref, spread, out, sems,
 ):
     fetch = pltpu.make_async_copy(place_in, place_ref, sems.at[1])
@@ -286,6 +286,7 @@
         out[here] = spread[BAND + step].T.astype(jnp.bfloat16)
     finish = pltpu.make_async_copy(out, whole_hbm.at[pl.ds(rim, count * block_rows)], sems.at[0])
     finish.start()
+    mark_ref[...] = jnp.zeros_like(mark_ref)
     for block in range(BAND):
         edge_ref[block * block_rows : (block + 1) * block_rows] = spread[block].T
         after = BAND + block
@@ -357,7 +358,8 @@
 
 
 def with_next(value, count):
-    pairs = [(i, (i + 1 if i & 1 else i - 1) % count) for i in range(count)]
+    pairs = [(0, 0), (count - 1, count - 1)]
+    pairs += [(i, i + 1 if i & 1 else i - 1) for i in range(1, count - 1)]
     return lax.ppermute(value, AXES, pairs)
 
 
@@ -508,11 +510,11 @@
     )(places, weight_near, adj_rim, grad_rim, act_rim, activated)
     first_part = swap(first_spill, [1] * count)
     second_part = with_next(second_spill, count)
-    grad_whole, edges = pl.pallas_call(
+    grad_whole, edges, second_mark = pl.pallas_call(
         inner_back_kernel,
-        out_shape=(shape(rows, width), shape(2 * rim, width, dtype=jnp.float32)),
+        out_shape=(shape(rows, width), shape(2 * rim, width, dtype=jnp.float32), mark),
         in_specs=[anywhere] + [vmem] * 4,
-        out_specs=(hbm, vmem),
+        out_specs=(hbm, vmem, vmem),
         scratch_shapes=[
             place_scratch,
             pltpu.VMEM((blocks + 1, width, block_rows), jnp.float32),
@@ -520,10 +522,10 @@
             pltpu.SemaphoreType.DMA((2,)),
         ],
         compiler_params=params(12),
-        cost_estimate=cost(2.0),
+        cost_estimate=cost(0.3),
         name="inner_rows_back",
     )(places, weight_near, adj_inner, grad_inner, rim_spread)
-    marks = {0: (first_mark,)}
+    marks = {"core": (first_mark,), "last": (second_mark, first_part, second_part)}
     own_half = sum_halves(send, keep, count, core_bit, marks)
     other_half = swap(own_half, [1 << core_bit] * count)
     norm_scale = 1.0 / math.sqrt(rows * count)

time: 37.1 us -> 34.2 us (0.922)
  waiting for transfers between devices: 8.86 us -> 5.39 us
  starting transfers between devices: 16.8 us -> 17.4 us
    ppermute x2, waiting for transfers between devices: 3.64 us -> 0.01 us  [with_next(): return lax.ppermute(value, AXES, pairs)]
    ppermute x10, starting transfers between devices: 13 us -> 16 us  [swap(): return lax.ppermute(value, AXES, pairs)]
    ppermute x2, starting transfers between devices: 3.81 us -> 1.31 us  [with_next(): return lax.ppermute(value, AXES, pairs)]
  transfers between devices with their start and end apart: 12 -> 12, of which waited for: 7 -> 5; matrix products, arithmetic and copies ran while one was open for 0% -> 0% of each run, Pallas kernels for 19% -> 21%
where the time goes in v10:
time: 34.2 us; the launch traced here: 34.1 us
  starting transfers between devices  17.4 us (51%)
  Pallas kernels  10.6 us (31%)
  waiting for transfers between devices  5.39 us (16%)
  between operations  0.76 us (2%)
    ppermute x10, starting transfers between devices, swap(): return lax.ppermute(value, AXES, pairs)  16 us
    ppermute x10, waiting for transfers between devices, swap(): return lax.ppermute(value, AXES, pairs)  5.38 us
    pallas_call x1, Pallas kernels, on_device(): pl.pallas_call(inner_kernel, out_shape=(shape(rows, width), shape(blocks...  3.75 us
    pallas_call x1, Pallas kernels, on_device(): pl.pallas_call(inner_back_kernel, out_shape=(shape(rows, width), shape(2...  2.22 us
    pallas_call x1, Pallas kernels, on_device(): pl.pallas_call(rim_kernel, out_shape=(shape(2 * rim, width), shape(2 * ri...  1.53 us
    ppermute x2, starting transfers between devices, with_next(): return lax.ppermute(value, AXES, pairs)  1.31 us
    pallas_call x1, Pallas kernels, on_device(): pl.pallas_call(rim_back_kernel, out_shape=(shape(rows, width), shape(6 *...  1.11 us
    pallas_call x1, Pallas kernels, on_device(): pl.pallas_call(halo_kernel, out_shape=(shape(rim, width), shape(rim, widt...  1 us
  transfers between devices with their start and end apart: 12, of which 5 were waited for; matrix products, arithmetic and copies ran while one was open for 0% of the time, Pallas kernels for 21%

profile of v10, /device:TPU:0, one launch (start us, length us, event | category | flops | bytes accessed | tf_op | source)
XLA Modules:
  0.0 34.1 jit_solution(8079704336632097824)
XLA Ops:
  0.6 1.0 %halo_rows.1 = (bf16[256,256]{1,0:T(8,128)(2,1)S(1)}, bf16[256,256]{1,0:T(8,128)(2,1)S(1)}) custom-call(bf16[1536,256]{1,0:T(8,128)(2,1)} %feat_hbm.3), custom_call_target="tpu_custom_call" | custom-call | flops 60000000 | bytes 300000 | tf_op jit(solution)/shard_map/halo_rows/pallas_call | solution.py:419
  1.6 3.0 %collective-permute-start = (bf16[256,256]{1,0:T(8,128)(2,1)S(1)}, bf16[256,256]{1,0:T(8,128)(2,1)S(1)}, u32[]{:S(2)}, u32[]{:S(2)}) collective-permute-start(bf16[256,256]{1,0:T(8,128)(2,1)S(1)} %get-tuple-element.37), channel_id=1, source_target_pairs={{0,1},{1,0},{2,3},{3,2},{4,5},{5,4},{6,7},{7,6},{8,9},{9,8},{10,11... | collective-permute-start | bytes 393224 | tf_op jit(solution)/shard_map/ppermute | solution.py:357
  4.7 0.7 %collective-permute-start.1 = (bf16[256,256]{1,0:T(8,128)(2,1)S(1)}, bf16[256,256]{1,0:T(8,128)(2,1)S(1)}, u32[]{:S(2)}, u32[]{:S(2)}) collective-permute-start(bf16[256,256]{1,0:T(8,128)(2,1)S(1)} %get-tuple-element.38), channel_id=1, source_target_pairs={{0,0},{31,31},{1,2},{2,1},{3,4},{4,3},{5,6},{6,5},{7,8},{8,7},{9,1... | collective-permute-start | bytes 393224 | tf_op jit(solution)/shard_map/ppermute | solution.py:363
  5.3 3.7 %inner_rows.1 = (bf16[1536,256]{1,0:T(8,128)(2,1)}, s32[36]{0:T(128)S(1)}, bf16[1024,256]{1,0:T(8,128)(2,1)S(1)}, f32[256,256]{1,0:T(8,128)S(1)}, f32[8,256]{1,0...) custom-call(s32[3,12]{1,0:T(4,128)} %bitcast.3, ...), custom_call_target="tpu_custom_call" | custom-call | flops 600000000 | bytes 3000000 | tf_op jit(solution)/shard_map/inner_rows/pallas_call | solution.py:434
  9.1 0.0 collective-permute-done.first_ref
  9.1 0.0 collective-permute-done.1.second_ref
  9.1 1.5 %rim_rows.1 = (bf16[512,256]{1,0:T(8,128)(2,1)S(1)}, bf16[512,256]{1,0:T(8,128)(2,1)S(1)}, f32[144,256]{1,0:T(8,128)S(1)}, f32[144,256]{1,0:T(8,128)S(1)}) custom-call(s32[36]{0:T(128)S(1)} %get-tuple-element.32.place_in, bf16[256,256]{1,0:T(8,128)(2,1)S(1)} %get-tuple-element.33.weight_ref, f32[1,256]{1,0:T(1,128)S(1)} %get-tuple-element.35.bias_ref, ...), custom_call_target="tpu_custom_call" | custom-call | flops 240000000 | bytes 1200000 | tf_op jit(solution)/shard_map/rim_rows/pallas_call | solution.py:469
  10.7 1.5 %collective-permute-start.2 = (f32[144,256]{1,0:T(8,128)S(1)}, f32[144,256]{1,0:T(8,128)S(1)}, u32[]{:S(2)}, u32[]{:S(2)}) collective-permute-start(f32[144,256]{1,0:T(8,128)S(1)} %get-tuple-element.47), channel_id=1, source_target_pairs={{0,2},{1,3},{2,0},{3,1},{4,6},{5,7},{6,4},{7,5},{8,10},{9,11},{10,... | collective-permute-start | bytes 442376 | tf_op jit(solution)/shard_map/ppermute | solution.py:357
  12.1 1.1 %rim_rows_back.1 = (bf16[1536,256]{1,0:T(8,128)(2,1)}, f32[13,256,128]{2,1,0:T(8,128)S(1)}, bf16[256,256]{1,0:T(8,128)(2,1)S(1)}, bf16[256,256]{1,0:T(8,128)(2,1)S(1)}, f32[8,128]{1,0:T(8,128)S(1)}) custom-call(s32[36]{0:T(128)S(1)} %get-tuple-element.32.place_in, ...), custom_call_target="tpu_custom_call", output_to_operand_aliasing={{0}: (5, {})} | custom-call | flops 240000000 | bytes 1200000 | tf_op jit(solution)/shard_map/rim_rows_back/pallas_call | solution.py:494
  13.2 0.0 collective-permute-done.2.refs_1_
  13.3 4.0 %collective-permute-start.5 = (bf16[144,256]{1,0:T(8,128)(2,1)S(1)}, bf16[144,256]{1,0:T(8,128)(2,1)S(1)}, u32[]{:S(2)}, u32[]{:S(2)}) collective-permute-start(bf16[144,256]{1,0:T(8,128)(2,1)S(1)} %add_halves.3.refs_0_), channel_id=1, source_target_pairs={{0,5},{1,4},{2,26},{3,27},{4,1},{5,0},{6,30},{7,31},{8,13},{9,12},... | collective-permute-start | bytes 221192 | tf_op jit(solution)/shard_map/ppermute | solution.py:357
  17.2 0.5 %collective-permute-start.4 = (bf16[144,256]{1,0:T(8,128)(2,1)S(1)}, bf16[144,256]{1,0:T(8,128)(2,1)S(1)}, u32[]{:S(2)}, u32[]{:S(2)}) collective-permute-start(bf16[144,256]{1,0:T(8,128)(2,1)S(1)} %add_halves.3.refs_0_), channel_id=1, source_target_pairs={{0,4},{1,5},{2,18},{3,19},{4,0},{5,1},{6,22},{7,23},{8,12},{9,13},... | collective-permute-start | bytes 221192 | tf_op jit(solution)/shard_map/ppermute | solution.py:357
  17.7 0.3 collective-permute-start.3
  18.0 1.8 %collective-permute-start.9 = (bf16[256,256]{1,0:T(8,128)(2,1)S(1)}, bf16[256,256]{1,0:T(8,128)(2,1)S(1)}, u32[]{:S(2)}, u32[]{:S(2)}) collective-permute-start(bf16[256,256]{1,0:T(8,128)(2,1)S(1)} %get-tuple-element.53), channel_id=1, source_target_pairs={{0,1},{1,0},{2,3},{3,2},{4,5},{5,4},{6,7},{7,6},{8,9},{9,8},{10,11... | collective-permute-start | bytes 393224 | tf_op jit(solution)/shard_map/ppermute | solution.py:357
  19.7 0.7 %collective-permute-start.10 = (bf16[256,256]{1,0:T(8,128)(2,1)S(1)}, bf16[256,256]{1,0:T(8,128)(2,1)S(1)}, u32[]{:S(2)}, u32[]{:S(2)}) collective-permute-start(bf16[256,256]{1,0:T(8,128)(2,1)S(1)} %get-tuple-element.54), channel_id=1, source_target_pairs={{0,0},{31,31},{1,2},{2,1},{3,4},{4,3},{5,6},{6,5},{7,8},{8,7},{9,1... | collective-permute-start | bytes 393224 | tf_op jit(solution)/shard_map/ppermute | solution.py:363
  20.4 0.0 collective-permute-done.5.refs_3_
  20.4 1.2 %collective-permute-done.4.refs_2_ = bf16[144,256]{1,0:T(8,128)(2,1)S(1)} collective-permute-done((bf16[144,256]{1,0:T(8,128)(2,1)S(1)}, bf16[144,256]{1,0:T(8,128)(2,1)S(1)}, u32[]{:S(2)}, u32[]{:S(2)}) %collective-permute-start.4) | collective-permute-done | bytes 73760 | tf_op jit(solution)/shard_map/ppermute | solution.py:357
  21.6 0.5 %collective-permute-done.3.refs_1_ = bf16[144,256]{1,0:T(8,128)(2,1)S(1)} collective-permute-done((bf16[144,256]{1,0:T(8,128)(2,1)S(1)}, bf16[144,256]{1,0:T(8,128)(2,1)S(1)}, u32[]{:S(2)}, u32[]{:S(2)}) %collective-permute-start.3) | collective-permute-done | bytes 73760 | tf_op jit(solution)/shard_map/ppermute | solution.py:357
  22.1 4.4 %collective-permute-start.8 = (bf16[144,256]{1,0:T(8,128)(2,1)S(1)}, bf16[144,256]{1,0:T(8,128)(2,1)S(1)}, u32[]{:S(2)}, u32[]{:S(2)}) collective-permute-start(bf16[144,256]{1,0:T(8,128)(2,1)S(1)} %add_halves.4.refs_0_), channel_id=1, source_target_pairs={{0,24},{1,25},{2,7},{3,6},{4,28},{5,29},{6,3},{7,2},{8,16},{9,17},... | collective-permute-start | bytes 221192 | tf_op jit(solution)/shard_map/ppermute | solution.py:357
  26.5 0.0 collective-permute-start.7
  26.5 0.6 %collective-permute-start.6 = (bf16[144,256]{1,0:T(8,128)(2,1)S(1)}, bf16[144,256]{1,0:T(8,128)(2,1)S(1)}, u32[]{:S(2)}, u32[]{:S(2)}) collective-permute-start(bf16[144,256]{1,0:T(8,128)(2,1)S(1)} %add_halves.4.refs_0_), channel_id=1, source_target_pairs={{0,8},{1,9},{2,3},{3,2},{4,12},{5,13},{6,7},{7,6},{8,0},{9,1},{10,... | collective-permute-start | bytes 221192 | tf_op jit(solution)/shard_map/ppermute | solution.py:357
  27.1 2.2 %inner_rows_back.1 = (bf16[1536,256]{1,0:T(8,128)(2,1)}, f32[512,256]{1,0:T(8,128)S(1)}, f32[8,128]{1,0:T(8,128)S(1)}) custom-call(s32[36]{0:T(128)S(1)} %get-tuple-element.32.place_in, bf16[256,256]{1,0:T(8,128)(2,1)S(1)} %get-tuple-element.33.weight_ref, bf16[8,3,128,128]{3,2,1,0:T(8,128)(2,1)S(1)} %get-tuple-element.49.adj_ref, ...), custom_call_target="tpu_custom_call" | custom-call | flops 360000000 | bytes 1800000 | tf_op jit(solution)/shard_map/inner_rows_back/pallas_call | solution.py:513
  29.4 0.0 collective-permute-done.9.refs_5_.first_ref
  29.4 0.0 collective-permute-done.10.refs_6_.second_ref
  29.4 0.7 %collective-permute-done.8.refs_3_ = bf16[144,256]{1,0:T(8,128)(2,1)S(1)} collective-permute-done((bf16[144,256]{1,0:T(8,128)(2,1)S(1)}, bf16[144,256]{1,0:T(8,128)(2,1)S(1)}, u32[]{:S(2)}, u32[]{:S(2)}) %collective-permute-start.8) | collective-permute-done | bytes 73760 | tf_op jit(solution)/shard_map/ppermute | solution.py:357
  30.0 1.7 %collective-permute-done.7.refs_2_ = bf16[144,256]{1,0:T(8,128)(2,1)S(1)} collective-permute-done((bf16[144,256]{1,0:T(8,128)(2,1)S(1)}, bf16[144,256]{1,0:T(8,128)(2,1)S(1)}, u32[]{:S(2)}, u32[]{:S(2)}) %collective-permute-start.7) | collective-permute-done | bytes 73760 | tf_op jit(solution)/shard_map/ppermute | solution.py:357
  31.7 0.0 collective-permute-done.6.refs_1_
  31.8 0.1 collective-permute-start.11
  31.9 1.4 %collective-permute-done.11.other_ref = f32[144,256]{1,0:T(8,128)S(1)} collective-permute-done((f32[144,256]{1,0:T(8,128)S(1)}, f32[144,256]{1,0:T(8,128)S(1)}, u32[]{:S(2)}, u32[]{:S(2)}) %collective-permute-start.11) | collective-permute-done | bytes 147488 | tf_op jit(solution)/shard_map/ppermute | solution.py:357
  33.2 0.9 %last_step.1 = (f32[256,256]{1,0:T(8,128)}, f32[1,256]{1,0:T(1,128)}, bf16[1536,256]{1,0:T(8,128)(2,1)}) custom-call(f32[144,256]{1,0:T(8,128)S(1)} %add_halves.5.own_ref, f32[144,256]{1,0:T(8,128)S(1)} %collective-permute-done.11.other_ref, f32[512,256]{1,0:T(8,128)S(1)} %get-tuple-element.55.edge_ref, ...), custom_call_target="tpu_custom_call", output_to_operand_aliasing={{2}: (5, {})} | custom-call | tf_op jit(solution)/shard_map/last_step/pallas_call | solution.py:532
  (3 shorter events, 0.1 us)
Async XLA Ops:
  1.6 7.5 %collective-permute-start = (bf16[256,256]{1,0:T(8,128)(2,1)S(1)}, bf16[256,256]{1,0:T(8,128)(2,1)S(1)}, u32[]{:S(2)}, u32[]{:S(2)}) collective-permute-start(bf16[256,256]{1,0:T(8,128)(2,1)S(1)} %get-tuple-element.37), channel_id=1, source_target_pairs={{0,1},{1,0},{2,3},{3,2},{4,5},{5,4},{6,7},{7,6},{8,9},{9,8},{10,11... | collective-permute-start | bytes 393224 | tf_op jit(solution)/shard_map/ppermute | solution.py:357
  4.7 4.4 %collective-permute-start.1 = (bf16[256,256]{1,0:T(8,128)(2,1)S(1)}, bf16[256,256]{1,0:T(8,128)(2,1)S(1)}, u32[]{:S(2)}, u32[]{:S(2)}) collective-permute-start(bf16[256,256]{1,0:T(8,128)(2,1)S(1)} %get-tuple-element.38), channel_id=1, source_target_pairs={{0,0},{31,31},{1,2},{2,1},{3,4},{4,3},{5,6},{6,5},{7,8},{8,7},{9,1... | collective-permute-start | bytes 393224 | tf_op jit(solution)/shard_map/ppermute | solution.py:363
  10.7 2.6 %collective-permute-start.2 = (f32[144,256]{1,0:T(8,128)S(1)}, f32[144,256]{1,0:T(8,128)S(1)}, u32[]{:S(2)}, u32[]{:S(2)}) collective-permute-start(f32[144,256]{1,0:T(8,128)S(1)} %get-tuple-element.47), channel_id=1, source_target_pairs={{0,2},{1,3},{2,0},{3,1},{4,6},{5,7},{6,4},{7,5},{8,10},{9,11},{10,... | collective-permute-start | bytes 442376 | tf_op jit(solution)/shard_map/ppermute | solution.py:357
  13.3 7.1 %collective-permute-start.5 = (bf16[144,256]{1,0:T(8,128)(2,1)S(1)}, bf16[144,256]{1,0:T(8,128)(2,1)S(1)}, u32[]{:S(2)}, u32[]{:S(2)}) collective-permute-start(bf16[144,256]{1,0:T(8,128)(2,1)S(1)} %add_halves.3.refs_0_), channel_id=1, source_target_pairs={{0,5},{1,4},{2,26},{3,27},{4,1},{5,0},{6,30},{7,31},{8,13},{9,12},... | collective-permute-start | bytes 221192 | tf_op jit(solution)/shard_map/ppermute | solution.py:357
  17.2 4.4 %collective-permute-start.4 = (bf16[144,256]{1,0:T(8,128)(2,1)S(1)}, bf16[144,256]{1,0:T(8,128)(2,1)S(1)}, u32[]{:S(2)}, u32[]{:S(2)}) collective-permute-start(bf16[144,256]{1,0:T(8,128)(2,1)S(1)} %add_halves.3.refs_0_), channel_id=1, source_target_pairs={{0,4},{1,5},{2,18},{3,19},{4,0},{5,1},{6,22},{7,23},{8,12},{9,13},... | collective-permute-start | bytes 221192 | tf_op jit(solution)/shard_map/ppermute | solution.py:357
  17.7 4.4 %collective-permute-start.3 = (bf16[144,256]{1,0:T(8,128)(2,1)S(1)}, bf16[144,256]{1,0:T(8,128)(2,1)S(1)}, u32[]{:S(2)}, u32[]{:S(2)}) collective-permute-start(bf16[144,256]{1,0:T(8,128)(2,1)S(1)} %add_halves.3.refs_0_), channel_id=1, source_target_pairs={{0,1},{1,0},{2,10},{3,11},{4,5},{5,4},{6,14},{7,15},{8,9},{9,8},{1... | collective-permute-start | bytes 221192 | tf_op jit(solution)/shard_map/ppermute | solution.py:357
  18.0 11.4 %collective-permute-start.9 = (bf16[256,256]{1,0:T(8,128)(2,1)S(1)}, bf16[256,256]{1,0:T(8,128)(2,1)S(1)}, u32[]{:S(2)}, u32[]{:S(2)}) collective-permute-start(bf16[256,256]{1,0:T(8,128)(2,1)S(1)} %get-tuple-element.53), channel_id=1, source_target_pairs={{0,1},{1,0},{2,3},{3,2},{4,5},{5,4},{6,7},{7,6},{8,9},{9,8},{10,11... | collective-permute-start | bytes 393224 | tf_op jit(solution)/shard_map/ppermute | solution.py:357
  19.7 9.6 %collective-permute-start.10 = (bf16[256,256]{1,0:T(8,128)(2,1)S(1)}, bf16[256,256]{1,0:T(8,128)(2,1)S(1)}, u32[]{:S(2)}, u32[]{:S(2)}) collective-permute-start(bf16[256,256]{1,0:T(8,128)(2,1)S(1)} %get-tuple-element.54), channel_id=1, source_target_pairs={{0,0},{31,31},{1,2},{2,1},{3,4},{4,3},{5,6},{6,5},{7,8},{8,7},{9,1... | collective-permute-start | bytes 393224 | tf_op jit(solution)/shard_map/ppermute | solution.py:363
  22.1 7.9 %collective-permute-start.8 = (bf16[144,256]{1,0:T(8,128)(2,1)S(1)}, bf16[144,256]{1,0:T(8,128)(2,1)S(1)}, u32[]{:S(2)}, u32[]{:S(2)}) collective-permute-start(bf16[144,256]{1,0:T(8,128)(2,1)S(1)} %add_halves.4.refs_0_), channel_id=1, source_target_pairs={{0,24},{1,25},{2,7},{3,6},{4,28},{5,29},{6,3},{7,2},{8,16},{9,17},... | collective-permute-start | bytes 221192 | tf_op jit(solution)/shard_map/ppermute | solution.py:357
  26.5 5.3 %collective-permute-start.7 = (bf16[144,256]{1,0:T(8,128)(2,1)S(1)}, bf16[144,256]{1,0:T(8,128)(2,1)S(1)}, u32[]{:S(2)}, u32[]{:S(2)}) collective-permute-start(bf16[144,256]{1,0:T(8,128)(2,1)S(1)} %add_halves.4.refs_0_), channel_id=1, source_target_pairs={{0,16},{1,17},{2,6},{3,7},{4,20},{5,21},{6,2},{7,3},{8,24},{9,25},... | collective-permute-start | bytes 221192 | tf_op jit(solution)/shard_map/ppermute | solution.py:357
  26.5 5.3 %collective-permute-start.6 = (bf16[144,256]{1,0:T(8,128)(2,1)S(1)}, bf16[144,256]{1,0:T(8,128)(2,1)S(1)}, u32[]{:S(2)}, u32[]{:S(2)}) collective-permute-start(bf16[144,256]{1,0:T(8,128)(2,1)S(1)} %add_halves.4.refs_0_), channel_id=1, source_target_pairs={{0,8},{1,9},{2,3},{3,2},{4,12},{5,13},{6,7},{7,6},{8,0},{9,1},{10,... | collective-permute-start | bytes 221192 | tf_op jit(solution)/shard_map/ppermute | solution.py:357
  31.8 1.4 %collective-permute-start.11 = (f32[144,256]{1,0:T(8,128)S(1)}, f32[144,256]{1,0:T(8,128)S(1)}, u32[]{:S(2)}, u32[]{:S(2)}) collective-permute-start(f32[144,256]{1,0:T(8,128)S(1)} %add_halves.5.own_ref), channel_id=1, source_target_pairs={{0,2},{1,3},{2,0},{3,1},{4,6},{5,7},{6,4},{7,5},{8,10},{9,11},{10,... | collective-permute-start | bytes 442376 | tf_op jit(solution)/shard_map/ppermute | solution.py:357

commit v11 on v10

--- a/solution.py
+++ b/solution.py
@@ -358,8 +358,7 @@
 
 
 def with_next(value, count):
-    pairs = [(0, 0), (count - 1, count - 1)]
-    pairs += [(i, i + 1 if i & 1 else i - 1) for i in range(1, count - 1)]
+    pairs = [(i, (i + 1 if i & 1 else i - 1) % count) for i in range(count)]
     return lax.ppermute(value, AXES, pairs)
 
 

time: 34.2 us -> 33.7 us (0.985)
  waiting for transfers between devices: 5.39 us -> 3.75 us
  starting transfers between devices: 17.4 us -> 18.5 us
    ppermute x2, starting transfers between devices: 1.31 us -> 7.31 us  [with_next(): return lax.ppermute(value, AXES, pairs)]
    ppermute x10, starting transfers between devices: 16 us -> 11.2 us  [swap(): return lax.ppermute(value, AXES, pairs)]
    ppermute x10, waiting for transfers between devices: 5.38 us -> 3.14 us  [swap(): return lax.ppermute(value, AXES, pairs)]
    ppermute x2, waiting for transfers between devices: 0.01 us -> 0.61 us  [with_next(): return lax.ppermute(value, AXES, pairs)]
  transfers between devices with their start and end apart: 12 -> 12, of which waited for: 5 -> 4; matrix products, arithmetic and copies ran while one was open for 0% -> 0% of each run, Pallas kernels for 21% -> 21%
where the time goes in v11:
time: 33.7 us; the launch traced here: 33.6 us
  starting transfers between devices  18.5 us (55%)
  Pallas kernels  10.5 us (31%)
  waiting for transfers between devices  3.75 us (11%)
  between operations  0.74 us (2%)
    ppermute x10, starting transfers between devices, swap(): return lax.ppermute(value, AXES, pairs)  11.2 us
    ppermute x2, starting transfers between devices, with_next(): return lax.ppermute(value, AXES, pairs)  7.31 us
    pallas_call x1, Pallas kernels, on_device(): pl.pallas_call(inner_kernel, out_shape=(shape(rows, width), shape(blocks...  3.73 us
    ppermute x10, waiting for transfers between devices, swap(): return lax.ppermute(value, AXES, pairs)  3.14 us
    pallas_call x1, Pallas kernels, on_device(): pl.pallas_call(inner_back_kernel, out_shape=(shape(rows, width), shape(2...  2.22 us
    pallas_call x1, Pallas kernels, on_device(): pl.pallas_call(rim_kernel, out_shape=(shape(2 * rim, width), shape(2 * ri...  1.53 us
    pallas_call x1, Pallas kernels, on_device(): pl.pallas_call(rim_back_kernel, out_shape=(shape(rows, width), shape(6 *...  1.12 us
    pallas_call x1, Pallas kernels, on_device(): pl.pallas_call(halo_kernel, out_shape=(shape(rim, width), shape(rim, widt...  1 us
  transfers between devices with their start and end apart: 12, of which 4 were waited for; matrix products, arithmetic and copies ran while one was open for 0% of the time, Pallas kernels for 21%

profile of v11, /device:TPU:0, one launch (start us, length us, event | category | flops | bytes accessed | tf_op | source)
XLA Modules:
  0.0 33.6 jit_solution(12665401472809858272)
XLA Ops:
  0.6 1.0 %halo_rows.1 = (bf16[256,256]{1,0:T(8,128)(2,1)S(1)}, bf16[256,256]{1,0:T(8,128)(2,1)S(1)}) custom-call(bf16[1536,256]{1,0:T(8,128)(2,1)} %feat_hbm.3), custom_call_target="tpu_custom_call" | custom-call | flops 60000000 | bytes 300000 | tf_op jit(solution)/shard_map/halo_rows/pallas_call | solution.py:418
  1.6 3.0 %collective-permute-start = (bf16[256,256]{1,0:T(8,128)(2,1)S(1)}, bf16[256,256]{1,0:T(8,128)(2,1)S(1)}, u32[]{:S(2)}, u32[]{:S(2)}) collective-permute-start(bf16[256,256]{1,0:T(8,128)(2,1)S(1)} %get-tuple-element.37), channel_id=1, source_target_pairs={{0,1},{1,0},{2,3},{3,2},{4,5},{5,4},{6,7},{7,6},{8,9},{9,8},{10,11... | collective-permute-start | bytes 393224 | tf_op jit(solution)/shard_map/ppermute | solution.py:357
  4.7 3.6 %collective-permute-start.1 = (bf16[256,256]{1,0:T(8,128)(2,1)S(1)}, bf16[256,256]{1,0:T(8,128)(2,1)S(1)}, u32[]{:S(2)}, u32[]{:S(2)}) collective-permute-start(bf16[256,256]{1,0:T(8,128)(2,1)S(1)} %get-tuple-element.38), channel_id=1, source_target_pairs={{0,31},{1,2},{2,1},{3,4},{4,3},{5,6},{6,5},{7,8},{8,7},{9,10},{10,... | collective-permute-start | bytes 393224 | tf_op jit(solution)/shard_map/ppermute | solution.py:362
  8.3 3.7 %inner_rows.1 = (bf16[1536,256]{1,0:T(8,128)(2,1)}, s32[36]{0:T(128)S(1)}, bf16[1024,256]{1,0:T(8,128)(2,1)S(1)}, f32[256,256]{1,0:T(8,128)S(1)}, f32[8,256]{1,0...) custom-call(s32[3,12]{1,0:T(4,128)} %bitcast.3, ...), custom_call_target="tpu_custom_call" | custom-call | flops 600000000 | bytes 3000000 | tf_op jit(solution)/shard_map/inner_rows/pallas_call | solution.py:433
  12.0 0.0 collective-permute-done.first_ref
  12.0 0.6 %collective-permute-done.1.second_ref = bf16[256,256]{1,0:T(8,128)(2,1)S(1)} collective-permute-done((bf16[256,256]{1,0:T(8,128)(2,1)S(1)}, bf16[256,256]{1,0:T(8,128)(2,1)S(1)}, u32[]{:S(2)}, u32[]{:S(2)}) %collective-permute-start.1) | collective-permute-done | bytes 131104 | tf_op jit(solution)/shard_map/ppermute | solution.py:362
  12.7 1.5 %rim_rows.1 = (bf16[512,256]{1,0:T(8,128)(2,1)S(1)}, bf16[512,256]{1,0:T(8,128)(2,1)S(1)}, f32[144,256]{1,0:T(8,128)S(1)}, f32[144,256]{1,0:T(8,128)S(1)}) custom-call(s32[36]{0:T(128)S(1)} %get-tuple-element.32.place_in, bf16[256,256]{1,0:T(8,128)(2,1)S(1)} %get-tuple-element.33.weight_ref, f32[1,256]{1,0:T(1,128)S(1)} %get-tuple-element.35.bias_ref, ...), custom_call_target="tpu_custom_call" | custom-call | flops 240000000 | bytes 1200000 | tf_op jit(solution)/shard_map/rim_rows/pallas_call | solution.py:468
  14.2 0.1 collective-permute-start.2
  14.3 1.1 %rim_rows_back.1 = (bf16[1536,256]{1,0:T(8,128)(2,1)}, f32[13,256,128]{2,1,0:T(8,128)S(1)}, bf16[256,256]{1,0:T(8,128)(2,1)S(1)}, bf16[256,256]{1,0:T(8,128)(2,1)S(1)}, f32[8,128]{1,0:T(8,128)S(1)}) custom-call(s32[36]{0:T(128)S(1)} %get-tuple-element.32.place_in, ...), custom_call_target="tpu_custom_call", output_to_operand_aliasing={{0}: (5, {})} | custom-call | flops 240000000 | bytes 1200000 | tf_op jit(solution)/shard_map/rim_rows_back/pallas_call | solution.py:493
  15.4 0.2 collective-permute-done.2.refs_1_
  15.7 1.1 %collective-permute-start.5 = (bf16[144,256]{1,0:T(8,128)(2,1)S(1)}, bf16[144,256]{1,0:T(8,128)(2,1)S(1)}, u32[]{:S(2)}, u32[]{:S(2)}) collective-permute-start(bf16[144,256]{1,0:T(8,128)(2,1)S(1)} %add_halves.3.refs_0_), channel_id=1, source_target_pairs={{0,5},{1,4},{2,26},{3,27},{4,1},{5,0},{6,30},{7,31},{8,13},{9,12},... | collective-permute-start | bytes 221192 | tf_op jit(solution)/shard_map/ppermute | solution.py:357
  16.7 0.5 %collective-permute-start.4 = (bf16[144,256]{1,0:T(8,128)(2,1)S(1)}, bf16[144,256]{1,0:T(8,128)(2,1)S(1)}, u32[]{:S(2)}, u32[]{:S(2)}) collective-permute-start(bf16[144,256]{1,0:T(8,128)(2,1)S(1)} %add_halves.3.refs_0_), channel_id=1, source_target_pairs={{0,4},{1,5},{2,18},{3,19},{4,0},{5,1},{6,22},{7,23},{8,12},{9,13},... | collective-permute-start | bytes 221192 | tf_op jit(solution)/shard_map/ppermute | solution.py:357
  17.2 2.0 %collective-permute-start.3 = (bf16[144,256]{1,0:T(8,128)(2,1)S(1)}, bf16[144,256]{1,0:T(8,128)(2,1)S(1)}, u32[]{:S(2)}, u32[]{:S(2)}) collective-permute-start(bf16[144,256]{1,0:T(8,128)(2,1)S(1)} %add_halves.3.refs_0_), channel_id=1, source_target_pairs={{0,1},{1,0},{2,10},{3,11},{4,5},{5,4},{6,14},{7,15},{8,9},{9,8},{1... | collective-permute-start | bytes 221192 | tf_op jit(solution)/shard_map/ppermute | solution.py:357
  19.2 0.1 collective-permute-start.9
  19.3 3.7 %collective-permute-start.10 = (bf16[256,256]{1,0:T(8,128)(2,1)S(1)}, bf16[256,256]{1,0:T(8,128)(2,1)S(1)}, u32[]{:S(2)}, u32[]{:S(2)}) collective-permute-start(bf16[256,256]{1,0:T(8,128)(2,1)S(1)} %get-tuple-element.54), channel_id=1, source_target_pairs={{0,31},{1,2},{2,1},{3,4},{4,3},{5,6},{6,5},{7,8},{8,7},{9,10},{10,... | collective-permute-start | bytes 393224 | tf_op jit(solution)/shard_map/ppermute | solution.py:362
  22.9 0.0 collective-permute-done.5.refs_3_
  22.9 0.0 collective-permute-done.4.refs_2_
  22.9 0.0 collective-permute-done.3.refs_1_
  23.0 3.0 %collective-permute-start.8 = (bf16[144,256]{1,0:T(8,128)(2,1)S(1)}, bf16[144,256]{1,0:T(8,128)(2,1)S(1)}, u32[]{:S(2)}, u32[]{:S(2)}) collective-permute-start(bf16[144,256]{1,0:T(8,128)(2,1)S(1)} %add_halves.4.refs_0_), channel_id=1, source_target_pairs={{0,24},{1,25},{2,7},{3,6},{4,28},{5,29},{6,3},{7,2},{8,16},{9,17},... | collective-permute-start | bytes 221192 | tf_op jit(solution)/shard_map/ppermute | solution.py:357
  26.0 0.0 collective-permute-start.7
  26.0 1.5 %collective-permute-start.6 = (bf16[144,256]{1,0:T(8,128)(2,1)S(1)}, bf16[144,256]{1,0:T(8,128)(2,1)S(1)}, u32[]{:S(2)}, u32[]{:S(2)}) collective-permute-start(bf16[144,256]{1,0:T(8,128)(2,1)S(1)} %add_halves.4.refs_0_), channel_id=1, source_target_pairs={{0,8},{1,9},{2,3},{3,2},{4,12},{5,13},{6,7},{7,6},{8,0},{9,1},{10,... | collective-permute-start | bytes 221192 | tf_op jit(solution)/shard_map/ppermute | solution.py:357
  27.5 2.2 %inner_rows_back.1 = (bf16[1536,256]{1,0:T(8,128)(2,1)}, f32[512,256]{1,0:T(8,128)S(1)}, f32[8,128]{1,0:T(8,128)S(1)}) custom-call(s32[36]{0:T(128)S(1)} %get-tuple-element.32.place_in, bf16[256,256]{1,0:T(8,128)(2,1)S(1)} %get-tuple-element.33.weight_ref, bf16[8,3,128,128]{3,2,1,0:T(8,128)(2,1)S(1)} %get-tuple-element.49.adj_ref, ...), custom_call_target="tpu_custom_call" | custom-call | flops 360000000 | bytes 1800000 | tf_op jit(solution)/shard_map/inner_rows_back/pallas_call | solution.py:512
  29.7 0.0 collective-permute-done.9.refs_5_.first_ref
  29.7 0.0 collective-permute-done.10.refs_6_.second_ref
  29.7 0.0 collective-permute-done.8.refs_3_
  29.7 1.5 %collective-permute-done.7.refs_2_ = bf16[144,256]{1,0:T(8,128)(2,1)S(1)} collective-permute-done((bf16[144,256]{1,0:T(8,128)(2,1)S(1)}, bf16[144,256]{1,0:T(8,128)(2,1)S(1)}, u32[]{:S(2)}, u32[]{:S(2)}) %collective-permute-start.7) | collective-permute-done | bytes 73760 | tf_op jit(solution)/shard_map/ppermute | solution.py:357
  31.3 0.0 collective-permute-done.6.refs_1_
  31.3 0.1 collective-permute-start.11
  31.4 1.4 %collective-permute-done.11.other_ref = f32[144,256]{1,0:T(8,128)S(1)} collective-permute-done((f32[144,256]{1,0:T(8,128)S(1)}, f32[144,256]{1,0:T(8,128)S(1)}, u32[]{:S(2)}, u32[]{:S(2)}) %collective-permute-start.11) | collective-permute-done | bytes 147488 | tf_op jit(solution)/shard_map/ppermute | solution.py:357
  32.7 0.9 %last_step.1 = (f32[256,256]{1,0:T(8,128)}, f32[1,256]{1,0:T(1,128)}, bf16[1536,256]{1,0:T(8,128)(2,1)}) custom-call(f32[144,256]{1,0:T(8,128)S(1)} %add_halves.5.own_ref, f32[144,256]{1,0:T(8,128)S(1)} %collective-permute-done.11.other_ref, f32[512,256]{1,0:T(8,128)S(1)} %get-tuple-element.55.edge_ref, ...), custom_call_target="tpu_custom_call", output_to_operand_aliasing={{2}: (5, {})} | custom-call | tf_op jit(solution)/shard_map/last_step/pallas_call | solution.py:531
  (3 shorter events, 0.1 us)
Async XLA Ops:
  1.6 10.4 %collective-permute-start = (bf16[256,256]{1,0:T(8,128)(2,1)S(1)}, bf16[256,256]{1,0:T(8,128)(2,1)S(1)}, u32[]{:S(2)}, u32[]{:S(2)}) collective-permute-start(bf16[256,256]{1,0:T(8,128)(2,1)S(1)} %get-tuple-element.37), channel_id=1, source_target_pairs={{0,1},{1,0},{2,3},{3,2},{4,5},{5,4},{6,7},{7,6},{8,9},{9,8},{10,11... | collective-permute-start | bytes 393224 | tf_op jit(solution)/shard_map/ppermute | solution.py:357
  4.7 8.0 %collective-permute-start.1 = (bf16[256,256]{1,0:T(8,128)(2,1)S(1)}, bf16[256,256]{1,0:T(8,128)(2,1)S(1)}, u32[]{:S(2)}, u32[]{:S(2)}) collective-permute-start(bf16[256,256]{1,0:T(8,128)(2,1)S(1)} %get-tuple-element.38), channel_id=1, source_target_pairs={{0,31},{1,2},{2,1},{3,4},{4,3},{5,6},{6,5},{7,8},{8,7},{9,10},{10,... | collective-permute-start | bytes 393224 | tf_op jit(solution)/shard_map/ppermute | solution.py:362
  14.2 1.4 %collective-permute-start.2 = (f32[144,256]{1,0:T(8,128)S(1)}, f32[144,256]{1,0:T(8,128)S(1)}, u32[]{:S(2)}, u32[]{:S(2)}) collective-permute-start(f32[144,256]{1,0:T(8,128)S(1)} %get-tuple-element.47), channel_id=1, source_target_pairs={{0,2},{1,3},{2,0},{3,1},{4,6},{5,7},{6,4},{7,5},{8,10},{9,11},{10,... | collective-permute-start | bytes 442376 | tf_op jit(solution)/shard_map/ppermute | solution.py:357
  15.7 7.3 %collective-permute-start.5 = (bf16[144,256]{1,0:T(8,128)(2,1)S(1)}, bf16[144,256]{1,0:T(8,128)(2,1)S(1)}, u32[]{:S(2)}, u32[]{:S(2)}) collective-permute-start(bf16[144,256]{1,0:T(8,128)(2,1)S(1)} %add_halves.3.refs_0_), channel_id=1, source_target_pairs={{0,5},{1,4},{2,26},{3,27},{4,1},{5,0},{6,30},{7,31},{8,13},{9,12},... | collective-permute-start | bytes 221192 | tf_op jit(solution)/shard_map/ppermute | solution.py:357
  16.7 6.2 %collective-permute-start.4 = (bf16[144,256]{1,0:T(8,128)(2,1)S(1)}, bf16[144,256]{1,0:T(8,128)(2,1)S(1)}, u32[]{:S(2)}, u32[]{:S(2)}) collective-permute-start(bf16[144,256]{1,0:T(8,128)(2,1)S(1)} %add_halves.3.refs_0_), channel_id=1, source_target_pairs={{0,4},{1,5},{2,18},{3,19},{4,0},{5,1},{6,22},{7,23},{8,12},{9,13},... | collective-permute-start | bytes 221192 | tf_op jit(solution)/shard_map/ppermute | solution.py:357
  17.2 5.7 %collective-permute-start.3 = (bf16[144,256]{1,0:T(8,128)(2,1)S(1)}, bf16[144,256]{1,0:T(8,128)(2,1)S(1)}, u32[]{:S(2)}, u32[]{:S(2)}) collective-permute-start(bf16[144,256]{1,0:T(8,128)(2,1)S(1)} %add_halves.3.refs_0_), channel_id=1, source_target_pairs={{0,1},{1,0},{2,10},{3,11},{4,5},{5,4},{6,14},{7,15},{8,9},{9,8},{1... | collective-permute-start | bytes 221192 | tf_op jit(solution)/shard_map/ppermute | solution.py:357
  19.2 10.5 %collective-permute-start.9 = (bf16[256,256]{1,0:T(8,128)(2,1)S(1)}, bf16[256,256]{1,0:T(8,128)(2,1)S(1)}, u32[]{:S(2)}, u32[]{:S(2)}) collective-permute-start(bf16[256,256]{1,0:T(8,128)(2,1)S(1)} %get-tuple-element.53), channel_id=1, source_target_pairs={{0,1},{1,0},{2,3},{3,2},{4,5},{5,4},{6,7},{7,6},{8,9},{9,8},{10,11... | collective-permute-start | bytes 393224 | tf_op jit(solution)/shard_map/ppermute | solution.py:357
  19.3 10.4 %collective-permute-start.10 = (bf16[256,256]{1,0:T(8,128)(2,1)S(1)}, bf16[256,256]{1,0:T(8,128)(2,1)S(1)}, u32[]{:S(2)}, u32[]{:S(2)}) collective-permute-start(bf16[256,256]{1,0:T(8,128)(2,1)S(1)} %get-tuple-element.54), channel_id=1, source_target_pairs={{0,31},{1,2},{2,1},{3,4},{4,3},{5,6},{6,5},{7,8},{8,7},{9,10},{10,... | collective-permute-start | bytes 393224 | tf_op jit(solution)/shard_map/ppermute | solution.py:362
  23.0 6.7 %collective-permute-start.8 = (bf16[144,256]{1,0:T(8,128)(2,1)S(1)}, bf16[144,256]{1,0:T(8,128)(2,1)S(1)}, u32[]{:S(2)}, u32[]{:S(2)}) collective-permute-start(bf16[144,256]{1,0:T(8,128)(2,1)S(1)} %add_halves.4.refs_0_), channel_id=1, source_target_pairs={{0,24},{1,25},{2,7},{3,6},{4,28},{5,29},{6,3},{7,2},{8,16},{9,17},... | collective-permute-start | bytes 221192 | tf_op jit(solution)/shard_map/ppermute | solution.py:357
  26.0 5.3 %collective-permute-start.7 = (bf16[144,256]{1,0:T(8,128)(2,1)S(1)}, bf16[144,256]{1,0:T(8,128)(2,1)S(1)}, u32[]{:S(2)}, u32[]{:S(2)}) collective-permute-start(bf16[144,256]{1,0:T(8,128)(2,1)S(1)} %add_halves.4.refs_0_), channel_id=1, source_target_pairs={{0,16},{1,17},{2,6},{3,7},{4,20},{5,21},{6,2},{7,3},{8,24},{9,25},... | collective-permute-start | bytes 221192 | tf_op jit(solution)/shard_map/ppermute | solution.py:357
  26.0 5.3 %collective-permute-start.6 = (bf16[144,256]{1,0:T(8,128)(2,1)S(1)}, bf16[144,256]{1,0:T(8,128)(2,1)S(1)}, u32[]{:S(2)}, u32[]{:S(2)}) collective-permute-start(bf16[144,256]{1,0:T(8,128)(2,1)S(1)} %add_halves.4.refs_0_), channel_id=1, source_target_pairs={{0,8},{1,9},{2,3},{3,2},{4,12},{5,13},{6,7},{7,6},{8,0},{9,1},{10,... | collective-permute-start | bytes 221192 | tf_op jit(solution)/shard_map/ppermute | solution.py:357
  31.3 1.4 %collective-permute-start.11 = (f32[144,256]{1,0:T(8,128)S(1)}, f32[144,256]{1,0:T(8,128)S(1)}, u32[]{:S(2)}, u32[]{:S(2)}) collective-permute-start(f32[144,256]{1,0:T(8,128)S(1)} %add_halves.5.own_ref), channel_id=1, source_target_pairs={{0,2},{1,3},{2,0},{3,1},{4,6},{5,7},{6,4},{7,5},{8,10},{9,11},{10,... | collective-permute-start | bytes 442376 | tf_op jit(solution)/shard_map/ppermute | solution.py:357

commit v12 on v11

--- a/solution.py
+++ b/solution.py
@@ -9,7 +9,7 @@
 from jax.sharding import PartitionSpec as P
 
 BAND = 2
-TAIL = 16
+TAIL = 8
 AXES = ("rows", "cols")
 MIB = 1024 * 1024
 
@@ -365,6 +365,7 @@
 def sum_halves(send, keep, count, core_bit, marks):
     others = [bit for bit in range(count.bit_length() - 1) if bit != core_bit]
     groups = [others[i : i + 2] for i in range(0, len(others), 2)]
+    groups[0] = groups[0][::-1]
     total = add([keep, swap(send, [1 << core_bit] * count)], jnp.bfloat16, marks.get("core", ()))
     for step in range(len(groups)):
         masks = []

time: 33.7 us -> 33.1 us (0.982)
  waiting for transfers between devices: 3.75 us -> 3.15 us
    ppermute x10, waiting for transfers between devices: 3.14 us -> 2.54 us  [swap(): return lax.ppermute(value, AXES, pairs)]
  transfers between devices with their start and end apart: 12 -> 12, of which waited for: 4 -> 4; matrix products, arithmetic and copies ran while one was open for 0% -> 0% of each run, Pallas kernels for 21% -> 22%
where the time goes in v12:
time: 33.1 us; the launch traced here: 33 us
  starting transfers between devices  18.5 us (56%)
  Pallas kernels  10.5 us (32%)
  waiting for transfers between devices  3.15 us (10%)
  between operations  0.74 us (2%)
    ppermute x10, starting transfers between devices, swap(): return lax.ppermute(value, AXES, pairs)  11.2 us
    ppermute x2, starting transfers between devices, with_next(): return lax.ppermute(value, AXES, pairs)  7.31 us
    pallas_call x1, Pallas kernels, on_device(): pl.pallas_call(inner_kernel, out_shape=(shape(rows, width), shape(blocks...  3.73 us
    ppermute x10, waiting for transfers between devices, swap(): return lax.ppermute(value, AXES, pairs)  2.54 us
    pallas_call x1, Pallas kernels, on_device(): pl.pallas_call(inner_back_kernel, out_shape=(shape(rows, width), shape(2...  2.21 us
    pallas_call x1, Pallas kernels, on_device(): pl.pallas_call(rim_kernel, out_shape=(shape(2 * rim, width), shape(2 * ri...  1.53 us
    pallas_call x1, Pallas kernels, on_device(): pl.pallas_call(rim_back_kernel, out_shape=(shape(rows, width), shape(6 *...  1.12 us
    pallas_call x1, Pallas kernels, on_device(): pl.pallas_call(halo_kernel, out_shape=(shape(rim, width), shape(rim, widt...  1 us
  transfers between devices with their start and end apart: 12, of which 4 were waited for; matrix products, arithmetic and copies ran while one was open for 0% of the time, Pallas kernels for 22%

profile of v12, /device:TPU:0, one launch (start us, length us, event | category | flops | bytes accessed | tf_op | source)
XLA Modules:
  0.0 33.0 jit_solution(14032050998582571238)
XLA Ops:
  0.6 1.0 %halo_rows.1 = (bf16[256,256]{1,0:T(8,128)(2,1)S(1)}, bf16[256,256]{1,0:T(8,128)(2,1)S(1)}) custom-call(bf16[1536,256]{1,0:T(8,128)(2,1)} %feat_hbm.3), custom_call_target="tpu_custom_call" | custom-call | flops 60000000 | bytes 300000 | tf_op jit(solution)/shard_map/halo_rows/pallas_call | solution.py:419
  1.6 3.0 %collective-permute-start = (bf16[256,256]{1,0:T(8,128)(2,1)S(1)}, bf16[256,256]{1,0:T(8,128)(2,1)S(1)}, u32[]{:S(2)}, u32[]{:S(2)}) collective-permute-start(bf16[256,256]{1,0:T(8,128)(2,1)S(1)} %get-tuple-element.37), channel_id=1, source_target_pairs={{0,1},{1,0},{2,3},{3,2},{4,5},{5,4},{6,7},{7,6},{8,9},{9,8},{10,11... | collective-permute-start | bytes 393224 | tf_op jit(solution)/shard_map/ppermute | solution.py:357
  4.7 3.6 %collective-permute-start.1 = (bf16[256,256]{1,0:T(8,128)(2,1)S(1)}, bf16[256,256]{1,0:T(8,128)(2,1)S(1)}, u32[]{:S(2)}, u32[]{:S(2)}) collective-permute-start(bf16[256,256]{1,0:T(8,128)(2,1)S(1)} %get-tuple-element.38), channel_id=1, source_target_pairs={{0,31},{1,2},{2,1},{3,4},{4,3},{5,6},{6,5},{7,8},{8,7},{9,10},{10,... | collective-permute-start | bytes 393224 | tf_op jit(solution)/shard_map/ppermute | solution.py:362
  8.3 3.7 %inner_rows.1 = (bf16[1536,256]{1,0:T(8,128)(2,1)}, s32[36]{0:T(128)S(1)}, bf16[1024,256]{1,0:T(8,128)(2,1)S(1)}, f32[256,256]{1,0:T(8,128)S(1)}, f32[8,256]{1,0...) custom-call(s32[3,12]{1,0:T(4,128)} %bitcast.3, ...), custom_call_target="tpu_custom_call" | custom-call | flops 600000000 | bytes 3000000 | tf_op jit(solution)/shard_map/inner_rows/pallas_call | solution.py:434
  12.0 0.0 collective-permute-done.first_ref
  12.0 0.6 %collective-permute-done.1.second_ref = bf16[256,256]{1,0:T(8,128)(2,1)S(1)} collective-permute-done((bf16[256,256]{1,0:T(8,128)(2,1)S(1)}, bf16[256,256]{1,0:T(8,128)(2,1)S(1)}, u32[]{:S(2)}, u32[]{:S(2)}) %collective-permute-start.1) | collective-permute-done | bytes 131104 | tf_op jit(solution)/shard_map/ppermute | solution.py:362
  12.7 1.5 %rim_rows.1 = (bf16[512,256]{1,0:T(8,128)(2,1)S(1)}, bf16[512,256]{1,0:T(8,128)(2,1)S(1)}, f32[136,256]{1,0:T(8,128)S(1)}, f32[136,256]{1,0:T(8,128)S(1)}) custom-call(s32[36]{0:T(128)S(1)} %get-tuple-element.32.place_in, bf16[256,256]{1,0:T(8,128)(2,1)S(1)} %get-tuple-element.33.weight_ref, f32[1,256]{1,0:T(1,128)S(1)} %get-tuple-element.35.bias_ref, ...), custom_call_target="tpu_custom_call" | custom-call | flops 240000000 | bytes 1200000 | tf_op jit(solution)/shard_map/rim_rows/pallas_call | solution.py:469
  14.2 0.1 collective-permute-start.2
  14.3 1.1 %rim_rows_back.1 = (bf16[1536,256]{1,0:T(8,128)(2,1)}, f32[13,256,128]{2,1,0:T(8,128)S(1)}, bf16[256,256]{1,0:T(8,128)(2,1)S(1)}, bf16[256,256]{1,0:T(8,128)(2,1)S(1)}, f32[8,128]{1,0:T(8,128)S(1)}) custom-call(s32[36]{0:T(128)S(1)} %get-tuple-element.32.place_in, ...), custom_call_target="tpu_custom_call", output_to_operand_aliasing={{0}: (5, {})} | custom-call | flops 240000000 | bytes 1200000 | tf_op jit(solution)/shard_map/rim_rows_back/pallas_call | solution.py:494
  15.4 0.2 collective-permute-done.2.refs_1_
  15.6 1.0 %collective-permute-start.5 = (bf16[136,256]{1,0:T(8,128)(2,1)S(1)}, bf16[136,256]{1,0:T(8,128)(2,1)S(1)}, u32[]{:S(2)}, u32[]{:S(2)}) collective-permute-start(bf16[136,256]{1,0:T(8,128)(2,1)S(1)} %add_halves.3.refs_0_), channel_id=1, source_target_pairs={{0,5},{1,4},{2,26},{3,27},{4,1},{5,0},{6,30},{7,31},{8,13},{9,12},... | collective-permute-start | bytes 208904 | tf_op jit(solution)/shard_map/ppermute | solution.py:357
  16.7 0.1 collective-permute-start.4
  16.8 2.4 %collective-permute-start.3 = (bf16[136,256]{1,0:T(8,128)(2,1)S(1)}, bf16[136,256]{1,0:T(8,128)(2,1)S(1)}, u32[]{:S(2)}, u32[]{:S(2)}) collective-permute-start(bf16[136,256]{1,0:T(8,128)(2,1)S(1)} %add_halves.3.refs_0_), channel_id=1, source_target_pairs={{0,4},{1,5},{2,10},{3,11},{4,0},{5,1},{6,14},{7,15},{8,12},{9,13},... | collective-permute-start | bytes 208904 | tf_op jit(solution)/shard_map/ppermute | solution.py:357
  19.2 0.1 collective-permute-start.9
  19.3 3.7 %collective-permute-start.10 = (bf16[256,256]{1,0:T(8,128)(2,1)S(1)}, bf16[256,256]{1,0:T(8,128)(2,1)S(1)}, u32[]{:S(2)}, u32[]{:S(2)}) collective-permute-start(bf16[256,256]{1,0:T(8,128)(2,1)S(1)} %get-tuple-element.54), channel_id=1, source_target_pairs={{0,31},{1,2},{2,1},{3,4},{4,3},{5,6},{6,5},{7,8},{8,7},{9,10},{10,... | collective-permute-start | bytes 393224 | tf_op jit(solution)/shard_map/ppermute | solution.py:362
  22.9 0.0 collective-permute-done.5.refs_3_
  22.9 0.0 collective-permute-done.4.refs_2_
  22.9 0.0 collective-permute-done.3.refs_1_
  23.0 1.9 %collective-permute-start.8 = (bf16[136,256]{1,0:T(8,128)(2,1)S(1)}, bf16[136,256]{1,0:T(8,128)(2,1)S(1)}, u32[]{:S(2)}, u32[]{:S(2)}) collective-permute-start(bf16[136,256]{1,0:T(8,128)(2,1)S(1)} %add_halves.4.refs_0_), channel_id=1, source_target_pairs={{0,24},{1,25},{2,7},{3,6},{4,28},{5,29},{6,3},{7,2},{8,16},{9,17},... | collective-permute-start | bytes 208904 | tf_op jit(solution)/shard_map/ppermute | solution.py:357
  24.9 0.0 collective-permute-start.7
  24.9 2.5 %collective-permute-start.6 = (bf16[136,256]{1,0:T(8,128)(2,1)S(1)}, bf16[136,256]{1,0:T(8,128)(2,1)S(1)}, u32[]{:S(2)}, u32[]{:S(2)}) collective-permute-start(bf16[136,256]{1,0:T(8,128)(2,1)S(1)} %add_halves.4.refs_0_), channel_id=1, source_target_pairs={{0,8},{1,9},{2,6},{3,7},{4,12},{5,13},{6,2},{7,3},{8,0},{9,1},{10,... | collective-permute-start | bytes 208904 | tf_op jit(solution)/shard_map/ppermute | solution.py:357
  27.4 2.2 %inner_rows_back.1 = (bf16[1536,256]{1,0:T(8,128)(2,1)}, f32[512,256]{1,0:T(8,128)S(1)}, f32[8,128]{1,0:T(8,128)S(1)}) custom-call(s32[36]{0:T(128)S(1)} %get-tuple-element.32.place_in, bf16[256,256]{1,0:T(8,128)(2,1)S(1)} %get-tuple-element.33.weight_ref, bf16[8,3,128,128]{3,2,1,0:T(8,128)(2,1)S(1)} %get-tuple-element.49.adj_ref, ...), custom_call_target="tpu_custom_call" | custom-call | flops 360000000 | bytes 1800000 | tf_op jit(solution)/shard_map/inner_rows_back/pallas_call | solution.py:513
  29.7 0.0 collective-permute-done.9.refs_5_.first_ref
  29.7 0.0 collective-permute-done.10.refs_6_.second_ref
  29.7 0.0 collective-permute-done.8.refs_3_
  29.7 1.0 %collective-permute-done.7.refs_2_ = bf16[136,256]{1,0:T(8,128)(2,1)S(1)} collective-permute-done((bf16[136,256]{1,0:T(8,128)(2,1)S(1)}, bf16[136,256]{1,0:T(8,128)(2,1)S(1)}, u32[]{:S(2)}, u32[]{:S(2)}) %collective-permute-start.7) | collective-permute-done | bytes 69664 | tf_op jit(solution)/shard_map/ppermute | solution.py:357
  30.7 0.0 collective-permute-done.6.refs_1_
  30.7 0.1 collective-permute-start.11
  30.8 1.3 %collective-permute-done.11.other_ref = f32[136,256]{1,0:T(8,128)S(1)} collective-permute-done((f32[136,256]{1,0:T(8,128)S(1)}, f32[136,256]{1,0:T(8,128)S(1)}, u32[]{:S(2)}, u32[]{:S(2)}) %collective-permute-start.11) | collective-permute-done | bytes 139296 | tf_op jit(solution)/shard_map/ppermute | solution.py:357
  32.1 0.9 %last_step.1 = (f32[256,256]{1,0:T(8,128)}, f32[1,256]{1,0:T(1,128)}, bf16[1536,256]{1,0:T(8,128)(2,1)}) custom-call(f32[136,256]{1,0:T(8,128)S(1)} %add_halves.5.own_ref, f32[136,256]{1,0:T(8,128)S(1)} %collective-permute-done.11.other_ref, f32[512,256]{1,0:T(8,128)S(1)} %get-tuple-element.55.edge_ref, ...), custom_call_target="tpu_custom_call", output_to_operand_aliasing={{2}: (5, {})} | custom-call | tf_op jit(solution)/shard_map/last_step/pallas_call | solution.py:532
  (3 shorter events, 0.1 us)
Async XLA Ops:
  1.6 10.4 %collective-permute-start = (bf16[256,256]{1,0:T(8,128)(2,1)S(1)}, bf16[256,256]{1,0:T(8,128)(2,1)S(1)}, u32[]{:S(2)}, u32[]{:S(2)}) collective-permute-start(bf16[256,256]{1,0:T(8,128)(2,1)S(1)} %get-tuple-element.37), channel_id=1, source_target_pairs={{0,1},{1,0},{2,3},{3,2},{4,5},{5,4},{6,7},{7,6},{8,9},{9,8},{10,11... | collective-permute-start | bytes 393224 | tf_op jit(solution)/shard_map/ppermute | solution.py:357
  4.7 8.0 %collective-permute-start.1 = (bf16[256,256]{1,0:T(8,128)(2,1)S(1)}, bf16[256,256]{1,0:T(8,128)(2,1)S(1)}, u32[]{:S(2)}, u32[]{:S(2)}) collective-permute-start(bf16[256,256]{1,0:T(8,128)(2,1)S(1)} %get-tuple-element.38), channel_id=1, source_target_pairs={{0,31},{1,2},{2,1},{3,4},{4,3},{5,6},{6,5},{7,8},{8,7},{9,10},{10,... | collective-permute-start | bytes 393224 | tf_op jit(solution)/shard_map/ppermute | solution.py:362
  14.2 1.4 %collective-permute-start.2 = (f32[136,256]{1,0:T(8,128)S(1)}, f32[136,256]{1,0:T(8,128)S(1)}, u32[]{:S(2)}, u32[]{:S(2)}) collective-permute-start(f32[136,256]{1,0:T(8,128)S(1)} %get-tuple-element.47), channel_id=1, source_target_pairs={{0,2},{1,3},{2,0},{3,1},{4,6},{5,7},{6,4},{7,5},{8,10},{9,11},{10,... | collective-permute-start | bytes 417800 | tf_op jit(solution)/shard_map/ppermute | solution.py:357
  15.6 7.3 %collective-permute-start.5 = (bf16[136,256]{1,0:T(8,128)(2,1)S(1)}, bf16[136,256]{1,0:T(8,128)(2,1)S(1)}, u32[]{:S(2)}, u32[]{:S(2)}) collective-permute-start(bf16[136,256]{1,0:T(8,128)(2,1)S(1)} %add_halves.3.refs_0_), channel_id=1, source_target_pairs={{0,5},{1,4},{2,26},{3,27},{4,1},{5,0},{6,30},{7,31},{8,13},{9,12},... | collective-permute-start | bytes 208904 | tf_op jit(solution)/shard_map/ppermute | solution.py:357
  16.7 6.2 %collective-permute-start.4 = (bf16[136,256]{1,0:T(8,128)(2,1)S(1)}, bf16[136,256]{1,0:T(8,128)(2,1)S(1)}, u32[]{:S(2)}, u32[]{:S(2)}) collective-permute-start(bf16[136,256]{1,0:T(8,128)(2,1)S(1)} %add_halves.3.refs_0_), channel_id=1, source_target_pairs={{0,1},{1,0},{2,18},{3,19},{4,5},{5,4},{6,22},{7,23},{8,9},{9,8},{1... | collective-permute-start | bytes 208904 | tf_op jit(solution)/shard_map/ppermute | solution.py:357
  16.8 6.1 %collective-permute-start.3 = (bf16[136,256]{1,0:T(8,128)(2,1)S(1)}, bf16[136,256]{1,0:T(8,128)(2,1)S(1)}, u32[]{:S(2)}, u32[]{:S(2)}) collective-permute-start(bf16[136,256]{1,0:T(8,128)(2,1)S(1)} %add_halves.3.refs_0_), channel_id=1, source_target_pairs={{0,4},{1,5},{2,10},{3,11},{4,0},{5,1},{6,14},{7,15},{8,12},{9,13},... | collective-permute-start | bytes 208904 | tf_op jit(solution)/shard_map/ppermute | solution.py:357
  19.2 10.5 %collective-permute-start.9 = (bf16[256,256]{1,0:T(8,128)(2,1)S(1)}, bf16[256,256]{1,0:T(8,128)(2,1)S(1)}, u32[]{:S(2)}, u32[]{:S(2)}) collective-permute-start(bf16[256,256]{1,0:T(8,128)(2,1)S(1)} %get-tuple-element.53), channel_id=1, source_target_pairs={{0,1},{1,0},{2,3},{3,2},{4,5},{5,4},{6,7},{7,6},{8,9},{9,8},{10,11... | collective-permute-start | bytes 393224 | tf_op jit(solution)/shard_map/ppermute | solution.py:357
  19.3 10.4 %collective-permute-start.10 = (bf16[256,256]{1,0:T(8,128)(2,1)S(1)}, bf16[256,256]{1,0:T(8,128)(2,1)S(1)}, u32[]{:S(2)}, u32[]{:S(2)}) collective-permute-start(bf16[256,256]{1,0:T(8,128)(2,1)S(1)} %get-tuple-element.54), channel_id=1, source_target_pairs={{0,31},{1,2},{2,1},{3,4},{4,3},{5,6},{6,5},{7,8},{8,7},{9,10},{10,... | collective-permute-start | bytes 393224 | tf_op jit(solution)/shard_map/ppermute | solution.py:362
  23.0 6.7 %collective-permute-start.8 = (bf16[136,256]{1,0:T(8,128)(2,1)S(1)}, bf16[136,256]{1,0:T(8,128)(2,1)S(1)}, u32[]{:S(2)}, u32[]{:S(2)}) collective-permute-start(bf16[136,256]{1,0:T(8,128)(2,1)S(1)} %add_halves.4.refs_0_), channel_id=1, source_target_pairs={{0,24},{1,25},{2,7},{3,6},{4,28},{5,29},{6,3},{7,2},{8,16},{9,17},... | collective-permute-start | bytes 208904 | tf_op jit(solution)/shard_map/ppermute | solution.py:357
  24.9 5.8 %collective-permute-start.7 = (bf16[136,256]{1,0:T(8,128)(2,1)S(1)}, bf16[136,256]{1,0:T(8,128)(2,1)S(1)}, u32[]{:S(2)}, u32[]{:S(2)}) collective-permute-start(bf16[136,256]{1,0:T(8,128)(2,1)S(1)} %add_halves.4.refs_0_), channel_id=1, source_target_pairs={{0,16},{1,17},{2,3},{3,2},{4,20},{5,21},{6,7},{7,6},{8,24},{9,25},... | collective-permute-start | bytes 208904 | tf_op jit(solution)/shard_map/ppermute | solution.py:357
  24.9 5.8 %collective-permute-start.6 = (bf16[136,256]{1,0:T(8,128)(2,1)S(1)}, bf16[136,256]{1,0:T(8,128)(2,1)S(1)}, u32[]{:S(2)}, u32[]{:S(2)}) collective-permute-start(bf16[136,256]{1,0:T(8,128)(2,1)S(1)} %add_halves.4.refs_0_), channel_id=1, source_target_pairs={{0,8},{1,9},{2,6},{3,7},{4,12},{5,13},{6,2},{7,3},{8,0},{9,1},{10,... | collective-permute-start | bytes 208904 | tf_op jit(solution)/shard_map/ppermute | solution.py:357
  30.7 1.4 %collective-permute-start.11 = (f32[136,256]{1,0:T(8,128)S(1)}, f32[136,256]{1,0:T(8,128)S(1)}, u32[]{:S(2)}, u32[]{:S(2)}) collective-permute-start(f32[136,256]{1,0:T(8,128)S(1)} %add_halves.5.own_ref), channel_id=1, source_target_pairs={{0,2},{1,3},{2,0},{3,1},{4,6},{5,7},{6,4},{7,5},{8,10},{9,11},{10,... | collective-permute-start | bytes 417800 | tf_op jit(solution)/shard_map/ppermute | solution.py:357

commit v13 on v12

--- a/solution.py
+++ b/solution.py
@@ -525,7 +525,7 @@
         cost_estimate=cost(0.3),
         name="inner_rows_back",
     )(places, weight_near, adj_inner, grad_inner, rim_spread)
-    marks = {"core": (first_mark,), "last": (second_mark, first_part, second_part)}
+    marks = {0: (first_mark,), "last": (second_mark, first_part, second_part)}
     own_half = sum_halves(send, keep, count, core_bit, marks)
     other_half = swap(own_half, [1 << core_bit] * count)
     norm_scale = 1.0 / math.sqrt(rows * count)

time: 33.1 us -> 33.9 us (1.024)
  waiting for transfers between devices: 3.15 us -> 3.77 us
    ppermute x10, waiting for transfers between devices: 2.54 us -> 3.16 us  [swap(): return lax.ppermute(value, AXES, pairs)]
  transfers between devices with their start and end apart: 12 -> 12, of which waited for: 4 -> 4; matrix products, arithmetic and copies ran while one was open for 0% -> 0% of each run, Pallas kernels for 22% -> 21%
where the time goes in v13:
time: 33.9 us; the launch traced here: 33.7 us
  starting transfers between devices  18.7 us (55%)
  Pallas kernels  10.5 us (31%)
  waiting for transfers between devices  3.77 us (11%)
  between operations  0.74 us (2%)
    ppermute x10, starting transfers between devices, swap(): return lax.ppermute(value, AXES, pairs)  11.3 us
    ppermute x2, starting transfers between devices, with_next(): return lax.ppermute(value, AXES, pairs)  7.35 us
    pallas_call x1, Pallas kernels, on_device(): pl.pallas_call(inner_kernel, out_shape=(shape(rows, width), shape(blocks...  3.73 us
    ppermute x10, waiting for transfers between devices, swap(): return lax.ppermute(value, AXES, pairs)  3.16 us
    pallas_call x1, Pallas kernels, on_device(): pl.pallas_call(inner_back_kernel, out_shape=(shape(rows, width), shape(2...  2.22 us
    pallas_call x1, Pallas kernels, on_device(): pl.pallas_call(rim_kernel, out_shape=(shape(2 * rim, width), shape(2 * ri...  1.53 us
    pallas_call x1, Pallas kernels, on_device(): pl.pallas_call(rim_back_kernel, out_shape=(shape(rows, width), shape(6 *...  1.11 us
    pallas_call x1, Pallas kernels, on_device(): pl.pallas_call(halo_kernel, out_shape=(shape(rim, width), shape(rim, widt...  1 us
  transfers between devices with their start and end apart: 12, of which 4 were waited for; matrix products, arithmetic and copies ran while one was open for 0% of the time, Pallas kernels for 21%

profile of v13, /device:TPU:0, one launch (start us, length us, event | category | flops | bytes accessed | tf_op | source)
XLA Modules:
  0.0 33.7 jit_solution(14139595708605457531)
XLA Ops:
  0.6 1.0 %halo_rows.1 = (bf16[256,256]{1,0:T(8,128)(2,1)S(1)}, bf16[256,256]{1,0:T(8,128)(2,1)S(1)}) custom-call(bf16[1536,256]{1,0:T(8,128)(2,1)} %feat_hbm.3), custom_call_target="tpu_custom_call" | custom-call | flops 60000000 | bytes 300000 | tf_op jit(solution)/shard_map/halo_rows/pallas_call | solution.py:419
  1.6 3.0 %collective-permute-start = (bf16[256,256]{1,0:T(8,128)(2,1)S(1)}, bf16[256,256]{1,0:T(8,128)(2,1)S(1)}, u32[]{:S(2)}, u32[]{:S(2)}) collective-permute-start(bf16[256,256]{1,0:T(8,128)(2,1)S(1)} %get-tuple-element.37), channel_id=1, source_target_pairs={{0,1},{1,0},{2,3},{3,2},{4,5},{5,4},{6,7},{7,6},{8,9},{9,8},{10,11... | collective-permute-start | bytes 393224 | tf_op jit(solution)/shard_map/ppermute | solution.py:357
  4.7 3.6 %collective-permute-start.1 = (bf16[256,256]{1,0:T(8,128)(2,1)S(1)}, bf16[256,256]{1,0:T(8,128)(2,1)S(1)}, u32[]{:S(2)}, u32[]{:S(2)}) collective-permute-start(bf16[256,256]{1,0:T(8,128)(2,1)S(1)} %get-tuple-element.38), channel_id=1, source_target_pairs={{0,31},{1,2},{2,1},{3,4},{4,3},{5,6},{6,5},{7,8},{8,7},{9,10},{10,... | collective-permute-start | bytes 393224 | tf_op jit(solution)/shard_map/ppermute | solution.py:362
  8.3 3.7 %inner_rows.1 = (bf16[1536,256]{1,0:T(8,128)(2,1)}, s32[36]{0:T(128)S(1)}, bf16[1024,256]{1,0:T(8,128)(2,1)S(1)}, f32[256,256]{1,0:T(8,128)S(1)}, f32[8,256]{1,0...) custom-call(s32[3,12]{1,0:T(4,128)} %bitcast.3, ...), custom_call_target="tpu_custom_call" | custom-call | flops 600000000 | bytes 3000000 | tf_op jit(solution)/shard_map/inner_rows/pallas_call | solution.py:434
  12.0 0.0 collective-permute-done.first_ref
  12.0 0.6 %collective-permute-done.1.second_ref = bf16[256,256]{1,0:T(8,128)(2,1)S(1)} collective-permute-done((bf16[256,256]{1,0:T(8,128)(2,1)S(1)}, bf16[256,256]{1,0:T(8,128)(2,1)S(1)}, u32[]{:S(2)}, u32[]{:S(2)}) %collective-permute-start.1) | collective-permute-done | bytes 131104 | tf_op jit(solution)/shard_map/ppermute | solution.py:362
  12.7 1.5 %rim_rows.1 = (bf16[512,256]{1,0:T(8,128)(2,1)S(1)}, bf16[512,256]{1,0:T(8,128)(2,1)S(1)}, f32[136,256]{1,0:T(8,128)S(1)}, f32[136,256]{1,0:T(8,128)S(1)}) custom-call(s32[36]{0:T(128)S(1)} %get-tuple-element.32.place_in, bf16[256,256]{1,0:T(8,128)(2,1)S(1)} %get-tuple-element.33.weight_ref, f32[1,256]{1,0:T(1,128)S(1)} %get-tuple-element.35.bias_ref, ...), custom_call_target="tpu_custom_call" | custom-call | flops 240000000 | bytes 1200000 | tf_op jit(solution)/shard_map/rim_rows/pallas_call | solution.py:469
  14.2 0.1 collective-permute-start.2
  14.3 1.3 %collective-permute-done.2.refs_1_ = f32[136,256]{1,0:T(8,128)S(1)} collective-permute-done((f32[136,256]{1,0:T(8,128)S(1)}, f32[136,256]{1,0:T(8,128)S(1)}, u32[]{:S(2)}, u32[]{:S(2)}) %collective-permute-start.2) | collective-permute-done | bytes 139296 | tf_op jit(solution)/shard_map/ppermute | solution.py:357
  15.6 1.1 %collective-permute-start.5 = (bf16[136,256]{1,0:T(8,128)(2,1)S(1)}, bf16[136,256]{1,0:T(8,128)(2,1)S(1)}, u32[]{:S(2)}, u32[]{:S(2)}) collective-permute-start(bf16[136,256]{1,0:T(8,128)(2,1)S(1)} %add_halves.3.refs_0_), channel_id=1, source_target_pairs={{0,5},{1,4},{2,26},{3,27},{4,1},{5,0},{6,30},{7,31},{8,13},{9,12},... | collective-permute-start | bytes 208904 | tf_op jit(solution)/shard_map/ppermute | solution.py:357
  16.7 0.0 collective-permute-start.4
  16.7 2.5 %collective-permute-start.3 = (bf16[136,256]{1,0:T(8,128)(2,1)S(1)}, bf16[136,256]{1,0:T(8,128)(2,1)S(1)}, u32[]{:S(2)}, u32[]{:S(2)}) collective-permute-start(bf16[136,256]{1,0:T(8,128)(2,1)S(1)} %add_halves.3.refs_0_), channel_id=1, source_target_pairs={{0,4},{1,5},{2,10},{3,11},{4,0},{5,1},{6,14},{7,15},{8,12},{9,13},... | collective-permute-start | bytes 208904 | tf_op jit(solution)/shard_map/ppermute | solution.py:357
  19.2 1.1 %rim_rows_back.1 = (bf16[1536,256]{1,0:T(8,128)(2,1)}, f32[13,256,128]{2,1,0:T(8,128)S(1)}, bf16[256,256]{1,0:T(8,128)(2,1)S(1)}, bf16[256,256]{1,0:T(8,128)(2,1)S(1)}, f32[8,128]{1,0:T(8,128)S(1)}) custom-call(s32[36]{0:T(128)S(1)} %get-tuple-element.32.place_in, ...), custom_call_target="tpu_custom_call", output_to_operand_aliasing={{0}: (5, {})} | custom-call | flops 240000000 | bytes 1200000 | tf_op jit(solution)/shard_map/rim_rows_back/pallas_call | solution.py:494
  20.3 0.1 collective-permute-start.9
  20.4 3.7 %collective-permute-start.10 = (bf16[256,256]{1,0:T(8,128)(2,1)S(1)}, bf16[256,256]{1,0:T(8,128)(2,1)S(1)}, u32[]{:S(2)}, u32[]{:S(2)}) collective-permute-start(bf16[256,256]{1,0:T(8,128)(2,1)S(1)} %get-tuple-element.54), channel_id=1, source_target_pairs={{0,31},{1,2},{2,1},{3,4},{4,3},{5,6},{6,5},{7,8},{8,7},{9,10},{10,... | collective-permute-start | bytes 393224 | tf_op jit(solution)/shard_map/ppermute | solution.py:362
  24.2 0.0 collective-permute-done.5.refs_3_
  24.2 0.0 collective-permute-done.4.refs_2_
  24.2 0.0 collective-permute-done.3.refs_1_
  24.2 0.5 %collective-permute-start.8 = (bf16[136,256]{1,0:T(8,128)(2,1)S(1)}, bf16[136,256]{1,0:T(8,128)(2,1)S(1)}, u32[]{:S(2)}, u32[]{:S(2)}) collective-permute-start(bf16[136,256]{1,0:T(8,128)(2,1)S(1)} %add_halves.4.refs_0_), channel_id=1, source_target_pairs={{0,24},{1,25},{2,7},{3,6},{4,28},{5,29},{6,3},{7,2},{8,16},{9,17},... | collective-permute-start | bytes 208904 | tf_op jit(solution)/shard_map/ppermute | solution.py:357
  24.7 0.0 collective-permute-start.7
  24.7 4.0 %collective-permute-start.6 = (bf16[136,256]{1,0:T(8,128)(2,1)S(1)}, bf16[136,256]{1,0:T(8,128)(2,1)S(1)}, u32[]{:S(2)}, u32[]{:S(2)}) collective-permute-start(bf16[136,256]{1,0:T(8,128)(2,1)S(1)} %add_halves.4.refs_0_), channel_id=1, source_target_pairs={{0,8},{1,9},{2,6},{3,7},{4,12},{5,13},{6,2},{7,3},{8,0},{9,1},{10,... | collective-permute-start | bytes 208904 | tf_op jit(solution)/shard_map/ppermute | solution.py:357
  28.7 2.2 %inner_rows_back.1 = (bf16[1536,256]{1,0:T(8,128)(2,1)}, f32[512,256]{1,0:T(8,128)S(1)}, f32[8,128]{1,0:T(8,128)S(1)}) custom-call(s32[36]{0:T(128)S(1)} %get-tuple-element.32.place_in, bf16[256,256]{1,0:T(8,128)(2,1)S(1)} %get-tuple-element.33.weight_ref, bf16[8,3,128,128]{3,2,1,0:T(8,128)(2,1)S(1)} %get-tuple-element.49.adj_ref, ...), custom_call_target="tpu_custom_call" | custom-call | flops 360000000 | bytes 1800000 | tf_op jit(solution)/shard_map/inner_rows_back/pallas_call | solution.py:513
  30.9 0.0 collective-permute-done.9.refs_5_.first_ref
  30.9 0.0 collective-permute-done.10.refs_6_.second_ref
  30.9 0.0 collective-permute-done.8.refs_3_
  30.9 0.4 %collective-permute-done.7.refs_2_ = bf16[136,256]{1,0:T(8,128)(2,1)S(1)} collective-permute-done((bf16[136,256]{1,0:T(8,128)(2,1)S(1)}, bf16[136,256]{1,0:T(8,128)(2,1)S(1)}, u32[]{:S(2)}, u32[]{:S(2)}) %collective-permute-start.7) | collective-permute-done | bytes 69664 | tf_op jit(solution)/shard_map/ppermute | solution.py:357
  31.4 0.0 collective-permute-done.6.refs_1_
  31.4 0.1 collective-permute-start.11
  31.5 1.3 %collective-permute-done.11.other_ref = f32[136,256]{1,0:T(8,128)S(1)} collective-permute-done((f32[136,256]{1,0:T(8,128)S(1)}, f32[136,256]{1,0:T(8,128)S(1)}, u32[]{:S(2)}, u32[]{:S(2)}) %collective-permute-start.11) | collective-permute-done | bytes 139296 | tf_op jit(solution)/shard_map/ppermute | solution.py:357
  32.8 0.9 %last_step.1 = (f32[256,256]{1,0:T(8,128)}, f32[1,256]{1,0:T(1,128)}, bf16[1536,256]{1,0:T(8,128)(2,1)}) custom-call(f32[136,256]{1,0:T(8,128)S(1)} %add_halves.5.own_ref, f32[136,256]{1,0:T(8,128)S(1)} %collective-permute-done.11.other_ref, f32[512,256]{1,0:T(8,128)S(1)} %get-tuple-element.55.edge_ref, ...), custom_call_target="tpu_custom_call", output_to_operand_aliasing={{2}: (5, {})} | custom-call | tf_op jit(solution)/shard_map/last_step/pallas_call | solution.py:532
  (3 shorter events, 0.1 us)
Async XLA Ops:
  1.6 10.4 %collective-permute-start = (bf16[256,256]{1,0:T(8,128)(2,1)S(1)}, bf16[256,256]{1,0:T(8,128)(2,1)S(1)}, u32[]{:S(2)}, u32[]{:S(2)}) collective-permute-start(bf16[256,256]{1,0:T(8,128)(2,1)S(1)} %get-tuple-element.37), channel_id=1, source_target_pairs={{0,1},{1,0},{2,3},{3,2},{4,5},{5,4},{6,7},{7,6},{8,9},{9,8},{10,11... | collective-permute-start | bytes 393224 | tf_op jit(solution)/shard_map/ppermute | solution.py:357
  4.7 8.0 %collective-permute-start.1 = (bf16[256,256]{1,0:T(8,128)(2,1)S(1)}, bf16[256,256]{1,0:T(8,128)(2,1)S(1)}, u32[]{:S(2)}, u32[]{:S(2)}) collective-permute-start(bf16[256,256]{1,0:T(8,128)(2,1)S(1)} %get-tuple-element.38), channel_id=1, source_target_pairs={{0,31},{1,2},{2,1},{3,4},{4,3},{5,6},{6,5},{7,8},{8,7},{9,10},{10,... | collective-permute-start | bytes 393224 | tf_op jit(solution)/shard_map/ppermute | solution.py:362
  14.2 1.4 %collective-permute-start.2 = (f32[136,256]{1,0:T(8,128)S(1)}, f32[136,256]{1,0:T(8,128)S(1)}, u32[]{:S(2)}, u32[]{:S(2)}) collective-permute-start(f32[136,256]{1,0:T(8,128)S(1)} %get-tuple-element.47), channel_id=1, source_target_pairs={{0,2},{1,3},{2,0},{3,1},{4,6},{5,7},{6,4},{7,5},{8,10},{9,11},{10,... | collective-permute-start | bytes 417800 | tf_op jit(solution)/shard_map/ppermute | solution.py:357
  15.6 8.5 %collective-permute-start.5 = (bf16[136,256]{1,0:T(8,128)(2,1)S(1)}, bf16[136,256]{1,0:T(8,128)(2,1)S(1)}, u32[]{:S(2)}, u32[]{:S(2)}) collective-permute-start(bf16[136,256]{1,0:T(8,128)(2,1)S(1)} %add_halves.3.refs_0_), channel_id=1, source_target_pairs={{0,5},{1,4},{2,26},{3,27},{4,1},{5,0},{6,30},{7,31},{8,13},{9,12},... | collective-permute-start | bytes 208904 | tf_op jit(solution)/shard_map/ppermute | solution.py:357
  16.7 7.5 %collective-permute-start.4 = (bf16[136,256]{1,0:T(8,128)(2,1)S(1)}, bf16[136,256]{1,0:T(8,128)(2,1)S(1)}, u32[]{:S(2)}, u32[]{:S(2)}) collective-permute-start(bf16[136,256]{1,0:T(8,128)(2,1)S(1)} %add_halves.3.refs_0_), channel_id=1, source_target_pairs={{0,1},{1,0},{2,18},{3,19},{4,5},{5,4},{6,22},{7,23},{8,9},{9,8},{1... | collective-permute-start | bytes 208904 | tf_op jit(solution)/shard_map/ppermute | solution.py:357
  16.7 7.5 %collective-permute-start.3 = (bf16[136,256]{1,0:T(8,128)(2,1)S(1)}, bf16[136,256]{1,0:T(8,128)(2,1)S(1)}, u32[]{:S(2)}, u32[]{:S(2)}) collective-permute-start(bf16[136,256]{1,0:T(8,128)(2,1)S(1)} %add_halves.3.refs_0_), channel_id=1, source_target_pairs={{0,4},{1,5},{2,10},{3,11},{4,0},{5,1},{6,14},{7,15},{8,12},{9,13},... | collective-permute-start | bytes 208904 | tf_op jit(solution)/shard_map/ppermute | solution.py:357
  20.3 10.6 %collective-permute-start.9 = (bf16[256,256]{1,0:T(8,128)(2,1)S(1)}, bf16[256,256]{1,0:T(8,128)(2,1)S(1)}, u32[]{:S(2)}, u32[]{:S(2)}) collective-permute-start(bf16[256,256]{1,0:T(8,128)(2,1)S(1)} %get-tuple-element.53), channel_id=1, source_target_pairs={{0,1},{1,0},{2,3},{3,2},{4,5},{5,4},{6,7},{7,6},{8,9},{9,8},{10,11... | collective-permute-start | bytes 393224 | tf_op jit(solution)/shard_map/ppermute | solution.py:357
  20.4 10.5 %collective-permute-start.10 = (bf16[256,256]{1,0:T(8,128)(2,1)S(1)}, bf16[256,256]{1,0:T(8,128)(2,1)S(1)}, u32[]{:S(2)}, u32[]{:S(2)}) collective-permute-start(bf16[256,256]{1,0:T(8,128)(2,1)S(1)} %get-tuple-element.54), channel_id=1, source_target_pairs={{0,31},{1,2},{2,1},{3,4},{4,3},{5,6},{6,5},{7,8},{8,7},{9,10},{10,... | collective-permute-start | bytes 393224 | tf_op jit(solution)/shard_map/ppermute | solution.py:362
  24.2 6.7 %collective-permute-start.8 = (bf16[136,256]{1,0:T(8,128)(2,1)S(1)}, bf16[136,256]{1,0:T(8,128)(2,1)S(1)}, u32[]{:S(2)}, u32[]{:S(2)}) collective-permute-start(bf16[136,256]{1,0:T(8,128)(2,1)S(1)} %add_halves.4.refs_0_), channel_id=1, source_target_pairs={{0,24},{1,25},{2,7},{3,6},{4,28},{5,29},{6,3},{7,2},{8,16},{9,17},... | collective-permute-start | bytes 208904 | tf_op jit(solution)/shard_map/ppermute | solution.py:357
  24.7 6.7 %collective-permute-start.7 = (bf16[136,256]{1,0:T(8,128)(2,1)S(1)}, bf16[136,256]{1,0:T(8,128)(2,1)S(1)}, u32[]{:S(2)}, u32[]{:S(2)}) collective-permute-start(bf16[136,256]{1,0:T(8,128)(2,1)S(1)} %add_halves.4.refs_0_), channel_id=1, source_target_pairs={{0,16},{1,17},{2,3},{3,2},{4,20},{5,21},{6,7},{7,6},{8,24},{9,25},... | collective-permute-start | bytes 208904 | tf_op jit(solution)/shard_map/ppermute | solution.py:357
  24.7 6.7 %collective-permute-start.6 = (bf16[136,256]{1,0:T(8,128)(2,1)S(1)}, bf16[136,256]{1,0:T(8,128)(2,1)S(1)}, u32[]{:S(2)}, u32[]{:S(2)}) collective-permute-start(bf16[136,256]{1,0:T(8,128)(2,1)S(1)} %add_halves.4.refs_0_), channel_id=1, source_target_pairs={{0,8},{1,9},{2,6},{3,7},{4,12},{5,13},{6,2},{7,3},{8,0},{9,1},{10,... | collective-permute-start | bytes 208904 | tf_op jit(solution)/shard_map/ppermute | solution.py:357
  31.4 1.4 %collective-permute-start.11 = (f32[136,256]{1,0:T(8,128)S(1)}, f32[136,256]{1,0:T(8,128)S(1)}, u32[]{:S(2)}, u32[]{:S(2)}) collective-permute-start(f32[136,256]{1,0:T(8,128)S(1)} %add_halves.5.own_ref), channel_id=1, source_target_pairs={{0,2},{1,3},{2,0},{3,1},{4,6},{5,7},{6,4},{7,5},{8,10},{9,11},{10,... | collective-permute-start | bytes 417800 | tf_op jit(solution)/shard_map/ppermute | solution.py:357

commit v14 on v12

--- a/solution.py
+++ b/solution.py
@@ -31,11 +31,11 @@
 def write_places(off_ref, cnt_ref, place_ref, blocks, slots):
     for block in range(blocks):
         if block < BAND:
-            shift, dump = BAND, 6 * BAND
+            shift, dump = BAND, 3 * BAND
         elif block < blocks - BAND:
             shift, dump = 0, blocks
         else:
-            shift, dump = 5 * BAND - blocks, 6 * BAND
+            shift, dump = 2 * BAND - blocks, 3 * BAND
         for slot in range(slots):
             place_ref[block * slots + slot] = jnp.where(
                 slot < cnt_ref[block], block + shift + off_ref[slot, block], dump
@@ -46,8 +46,8 @@
     return [place_ref[block * slots + slot] for slot in range(slots)]
 
 
-def rim_block(step, blocks):
-    return step if step < BAND else blocks - 2 * BAND + step
+def side_by_side(dense, side, first, last):
+    return jnp.concatenate([dense[side, place] for place in range(first, last)], 1)
 
 
 def place_in_mesh():
@@ -101,15 +101,14 @@
 
 def inner_kernel(
     off_hbm, cnt_hbm, weight_hbm, bias_hbm, feat_hbm, adj_hbm, cot_hbm,
-    act_hbm, place_out, grad_ref, partial_ref, sums_ref, weight_ref, bias_ref, feat_rim, adj_rim,
+    act_hbm, place_out, grad_ref, partial_ref, sums_ref, weight_ref, bias_ref, dense, own_ref,
     cot_rim, adj,
-    off_ref, cnt_ref, place_ref, feat, cot, act, agg_all, sems,
+    off_ref, cnt_ref, place_ref, feat, adj_rim, cot, act, agg_all, sems,
 ):
     blocks, slots, block_rows, _ = adj_hbm.shape
     rows, width = feat_hbm.shape
     count = blocks - 2 * BAND
     rim = BAND * block_rows
-    half = 2 * rim
     inner = count * block_rows
     scalars = [
         pltpu.make_async_copy(off_hbm, off_ref, sems.at[12]),
@@ -121,22 +120,19 @@
         pltpu.make_async_copy(weight_hbm, weight_ref, sems.at[2]),
         pltpu.make_async_copy(bias_hbm, bias_ref, sems.at[3]),
         pltpu.make_async_copy(cot_hbm.at[pl.ds(rim, inner)], cot, sems.at[4]),
-        pltpu.make_async_copy(feat_hbm.at[pl.ds(0, half)], feat_rim.at[pl.ds(0, half)], sems.at[5]),
+        pltpu.make_async_copy(adj_hbm.at[pl.ds(0, BAND)], adj_rim.at[pl.ds(0, BAND)], sems.at[5]),
         pltpu.make_async_copy(
-            feat_hbm.at[pl.ds(rows - half, half)], feat_rim.at[pl.ds(half, half)], sems.at[6]
-        ),
-        pltpu.make_async_copy(adj_hbm.at[pl.ds(0, BAND)], adj_rim.at[pl.ds(0, BAND)], sems.at[7]),
+            adj_hbm.at[pl.ds(blocks - BAND, BAND)], adj_rim.at[pl.ds(BAND, BAND)], sems.at[6]
+        ),
+        pltpu.make_async_copy(cot_hbm.at[pl.ds(0, rim)], cot_rim.at[pl.ds(0, rim)], sems.at[7]),
         pltpu.make_async_copy(
-            adj_hbm.at[pl.ds(blocks - BAND, BAND)], adj_rim.at[pl.ds(BAND, BAND)], sems.at[8]
-        ),
-        pltpu.make_async_copy(cot_hbm.at[pl.ds(0, rim)], cot_rim.at[pl.ds(0, rim)], sems.at[9]),
-        pltpu.make_async_copy(
-            cot_hbm.at[pl.ds(rows - rim, rim)], cot_rim.at[pl.ds(rim, rim)], sems.at[10]
+            cot_hbm.at[pl.ds(rows - rim, rim)], cot_rim.at[pl.ds(rim, rim)], sems.at[8]
         ),
     ]
     for copy in scalars + copies:
         copy.start()
     feat[rows:] = jnp.zeros((block_rows, width), jnp.bfloat16)
+    dense[...] = jnp.zeros_like(dense)
     for copy in scalars:
         copy.wait()
     write_places(off_ref, cnt_ref, place_ref, blocks, slots)
@@ -165,40 +161,44 @@
     partial_ref[...] = weight_terms(agg_all[...], grad_ref[...])
     for copy in copies[5:]:
         copy.wait()
+    for side, first in enumerate((0, blocks - BAND)):
+        for row in range(BAND):
+            here = pl.ds(row * block_rows, block_rows)
+            for slot, place in enumerate(places_of(place_ref, first + row, slots)):
+                dense[side, place, here] = adj_rim[side * BAND + row, slot]
+    own_ref[:rim] = jnp.dot(
+        side_by_side(dense, 0, BAND, 3 * BAND), feat[: 2 * rim],
+        preferred_element_type=jnp.float32,
+    )
+    own_ref[rim:] = jnp.dot(
+        side_by_side(dense, 1, 0, 2 * BAND), feat[rows - 2 * rim : rows],
+        preferred_element_type=jnp.float32,
+    )
     act_out.wait()
     place_copy.wait()
 
 
 def rim_kernel(
-    place_in, weight_ref, bias_ref, feat_ref, first_ref, second_ref, adj_ref, cot_ref,
-    partial_ref, sums_ref,
+    weight_ref, bias_ref, own_ref, first_ref, second_ref, dense, cot_ref, partial_ref, sums_ref,
     act_ref, grad_ref, send_ref, keep_ref,
-    place_ref, window, agg_all, payload, sems,
+    halo, agg_all, payload,
 ):
-    fetch = pltpu.make_async_copy(place_in, place_ref, sems.at[0])
-    fetch.start()
-    steps, slots, block_rows, _ = adj_ref.shape
-    blocks = place_ref.shape[0] // slots
-    width = feat_ref.shape[1]
-    rim = BAND * block_rows
+    rim, width = first_ref.shape
     odd = place_in_mesh() & 1
-    window[pl.ds(pl.multiple_of((1 - odd) * 5 * rim, rim), rim)] = first_ref[...]
-    window[pl.ds(pl.multiple_of(odd * 5 * rim, rim), rim)] = second_ref[...]
-    window[rim : 5 * rim] = feat_ref[...]
-    window[6 * rim :] = jnp.zeros((block_rows, width), jnp.bfloat16)
+    halo[pl.ds(pl.multiple_of((1 - odd) * rim, rim), rim)] = first_ref[...]
+    halo[pl.ds(pl.multiple_of(odd * rim, rim), rim)] = second_ref[...]
     weight = weight_ref[...]
     bias = bias_ref[...]
     sums = sums_ref[...]
-    fetch.wait()
-    for step in range(0, steps, 2):
-        for block in (step, step + 1):
-            places = places_of(place_ref, rim_block(block, blocks), slots)
-            agg_all[block * block_rows : (block + 1) * block_rows] = jnp.dot(
-                row_of(adj_ref, block, slots), pick(window, places, block_rows),
-                preferred_element_type=jnp.float32,
-            ).astype(jnp.bfloat16)
-        here = pl.ds(step * block_rows, 2 * block_rows)
-        preact = jnp.dot(agg_all[here], weight, preferred_element_type=jnp.float32) + bias
+    for side, first in enumerate((0, 2 * BAND)):
+        here = pl.ds(side * rim, rim)
+        agg = own_ref[here] + jnp.dot(
+            side_by_side(dense, side, first, first + BAND), halo[here],
+            preferred_element_type=jnp.float32,
+        )
+        agg = agg.astype(jnp.bfloat16)
+        agg_all[here] = agg
+        preact = jnp.dot(agg, weight, preferred_element_type=jnp.float32) + bias
         act_ref[here], grad = activate(preact, cot_ref[here])
         grad_ref[here] = grad
         sums = sums + column_sums(grad)
@@ -227,16 +227,13 @@
 
 
 def rim_back_kernel(
-    place_in, weight_ref, adj_ref, grad_ref, act_ref, act_in,
+    weight_ref, dense, grad_ref, act_ref, act_in,
     act_hbm, spread, first_ref, second_ref, mark_ref,
-    place_ref, sems,
+    spill, sems,
 ):
-    fetch = pltpu.make_async_copy(place_in, place_ref, sems.at[2])
-    fetch.start()
-    steps, slots, block_rows, _ = adj_ref.shape
-    blocks = place_ref.shape[0] // slots
+    block_rows = dense.shape[3]
     rim = BAND * block_rows
-    rows = blocks * block_rows
+    rows = act_hbm.shape[0]
     copies = [
         pltpu.make_async_copy(act_ref.at[pl.ds(0, rim)], act_hbm.at[pl.ds(0, rim)], sems.at[0]),
         pltpu.make_async_copy(
@@ -245,18 +242,23 @@
     ]
     for copy in copies:
         copy.start()
-    spread[...] = jnp.zeros_like(spread)
-    upstream = to_upstream(weight_ref[...], grad_ref[...])
-    fetch.wait()
-    scatter_rows(
-        [places_of(place_ref, rim_block(step, blocks), slots) for step in range(steps)],
-        upstream, adj_ref, spread,
-    )
+    weight = weight_ref[...]
+    for side, (inside, outside) in enumerate(((BAND, 0), (0, 2 * BAND))):
+        terms = jnp.dot(
+            to_upstream(weight, grad_ref[side * rim : (side + 1) * rim]),
+            side_by_side(dense, side, 0, 3 * BAND),
+            preferred_element_type=jnp.float32,
+        )
+        for block in range(2 * BAND):
+            lane = (inside + block) * block_rows
+            spread[side * 2 * BAND + block] = terms[:, lane : lane + block_rows]
+        for block in range(BAND):
+            lane = (outside + block) * block_rows
+            here = pl.ds(side * rim + block * block_rows, block_rows)
+            spill[here] = terms[:, lane : lane + block_rows].T.astype(jnp.bfloat16)
     odd = place_in_mesh() & 1
-    for block in range(BAND):
-        here = pl.ds(block * block_rows, block_rows)
-        first_ref[here] = spread[(1 - odd) * 5 * BAND + block].T.astype(jnp.bfloat16)
-        second_ref[here] = spread[odd * 5 * BAND + block].T.astype(jnp.bfloat16)
+    first_ref[...] = spill[pl.ds(pl.multiple_of((1 - odd) * rim, rim), rim)]
+    second_ref[...] = spill[pl.ds(pl.multiple_of(odd * rim, rim), rim)]
     mark_ref[...] = jnp.zeros_like(mark_ref)
     for copy in copies:
         copy.wait()
@@ -272,9 +274,9 @@
     count, slots, block_rows, _ = adj_ref.shape
     blocks = place_ref.shape[0] // slots
     rim = BAND * block_rows
-    spread[: 2 * BAND] = rim_spread[BAND : 3 * BAND]
+    spread[: 2 * BAND] = rim_spread[: 2 * BAND]
     spread[2 * BAND :] = jnp.zeros_like(spread[2 * BAND :])
-    spread[blocks - 2 * BAND : blocks] = rim_spread[3 * BAND : 5 * BAND]
+    spread[blocks - 2 * BAND : blocks] = rim_spread[2 * BAND :]
     upstream = to_upstream(weight_ref[...], grad_ref[...])
     fetch.wait()
     scatter_rows(
@@ -429,7 +431,7 @@
     first_halo = swap(first_rim, [1] * count)
     second_halo = with_next(second_rim, count)
     (
-        activated, places, grad_inner, partial, sums, weight_near, bias_near, feat_rim, adj_rim,
+        activated, places, grad_inner, partial, sums, weight_near, bias_near, dense, own_part,
         cot_rim, adj_inner,
     ) = pl.pallas_call(
         inner_kernel,
@@ -441,8 +443,8 @@
             shape(8, width, dtype=jnp.float32),
             shape(width, width),
             shape(1, width, dtype=jnp.float32),
-            shape(4 * rim, width),
-            shape(2 * BAND, slots, block_rows, block_rows),
+            shape(2, 3 * BAND + 1, rim, block_rows),
+            shape(2 * rim, width, dtype=jnp.float32),
             shape(2 * rim, width),
             shape(blocks - 2 * BAND, slots, block_rows, block_rows),
         ),
@@ -453,6 +455,7 @@
             pltpu.SMEM((blocks,), jnp.int32),
             place_scratch,
             pltpu.VMEM((rows + block_rows, width), jnp.bfloat16),
+            pltpu.VMEM((2 * BAND, slots, block_rows, block_rows), jnp.bfloat16),
             pltpu.VMEM((inner, width), jnp.bfloat16),
             pltpu.VMEM((inner, width), jnp.bfloat16),
             pltpu.VMEM((inner, width), jnp.bfloat16),
@@ -474,40 +477,40 @@
             shape(*half_shape, dtype=jnp.float32),
             shape(*half_shape, dtype=jnp.float32),
         ),
-        in_specs=[anywhere] + [vmem] * 9,
+        in_specs=[vmem] * 9,
         out_specs=(vmem,) * 4,
         scratch_shapes=[
-            place_scratch,
-            pltpu.VMEM((6 * rim + block_rows, width), jnp.bfloat16),
+            pltpu.VMEM((2 * rim, width), jnp.bfloat16),
             pltpu.VMEM((2 * rim, width), jnp.bfloat16),
             pltpu.VMEM((2,) + half_shape, jnp.float32),
-            pltpu.SemaphoreType.DMA((1,)),
         ],
         compiler_params=params(12),
         cost_estimate=cost(0.2),
         name="rim_rows",
     )(
-        places, weight_near, bias_near, feat_rim, first_halo, second_halo, adj_rim, cot_rim,
-        partial, sums,
+        weight_near, bias_near, own_part, first_halo, second_halo, dense, cot_rim, partial, sums,
     )
     mark = shape(8, 128, dtype=jnp.float32)
     activated, rim_spread, first_spill, second_spill, first_mark = pl.pallas_call(
         rim_back_kernel,
         out_shape=(
             shape(rows, width),
-            shape(6 * BAND + 1, width, block_rows, dtype=jnp.float32),
+            shape(4 * BAND, width, block_rows, dtype=jnp.float32),
             shape(rim, width),
             shape(rim, width),
             mark,
         ),
-        in_specs=[anywhere] + [vmem] * 4 + [hbm],
+        in_specs=[vmem] * 4 + [hbm],
         out_specs=(hbm,) + (vmem,) * 4,
-        scratch_shapes=[place_scratch, pltpu.SemaphoreType.DMA((3,))],
-        input_output_aliases={5: 0},
+        scratch_shapes=[
+            pltpu.VMEM((2 * rim, width), jnp.bfloat16),
+            pltpu.SemaphoreType.DMA((2,)),
+        ],
+        input_output_aliases={4: 0},
         compiler_params=params(12),
         cost_estimate=cost(0.2),
         name="rim_rows_back",
-    )(places, weight_near, adj_rim, grad_rim, act_rim, activated)
+    )(weight_near, dense, grad_rim, act_rim, activated)
     first_part = swap(first_spill, [1] * count)
     second_part = with_next(second_spill, count)
     grad_whole, edges, second_mark = pl.pallas_call(

time: 33.1 us -> 32.5 us (0.982)
  Pallas kernels: 10.5 us -> 9.44 us
  waiting for transfers between devices: 3.15 us -> 3.57 us
    pallas_call x1, Pallas kernels: 1.53 us -> 0.84 us  [on_device(): pl.pallas_call(rim_kernel, out_shape=(shape(2 * rim, width), shape(2 * ri...]
  transfers between devices with their start and end apart: 12 -> 12, of which waited for: 4 -> 4; matrix products, arithmetic and copies ran while one was open for 0% -> 0% of each run, Pallas kernels for 22% -> 21%
where the time goes in v14:
time: 32.5 us; the launch traced here: 32.3 us
  starting transfers between devices  18.6 us (57%)
  Pallas kernels  9.44 us (29%)
  waiting for transfers between devices  3.57 us (11%)
  between operations  0.74 us (2%)
    ppermute x10, starting transfers between devices, swap(): return lax.ppermute(value, AXES, pairs)  11.2 us
    ppermute x2, starting transfers between devices, with_next(): return lax.ppermute(value, AXES, pairs)  7.32 us
    pallas_call x1, Pallas kernels, on_device(): pl.pallas_call(inner_kernel, out_shape=(shape(rows, width), shape(blocks...  3.54 us
    ppermute x10, waiting for transfers between devices, swap(): return lax.ppermute(value, AXES, pairs)  2.77 us
    pallas_call x1, Pallas kernels, on_device(): pl.pallas_call(inner_back_kernel, out_shape=(shape(rows, width), shape(2...  2.22 us
    pallas_call x1, Pallas kernels, on_device(): pl.pallas_call(halo_kernel, out_shape=(shape(rim, width), shape(rim, widt...  1 us
    pallas_call x1, Pallas kernels, on_device(): pl.pallas_call(rim_back_kernel, out_shape=(shape(rows, width), shape(4 *...  0.88 us
    pallas_call x1, Pallas kernels, on_device(): pl.pallas_call(functools.partial(last_kernel, norm_scale), out_shape=(sha...  0.85 us
  transfers between devices with their start and end apart: 12, of which 4 were waited for; matrix products, arithmetic and copies ran while one was open for 0% of the time, Pallas kernels for 21%

profile of v14, /device:TPU:0, one launch (start us, length us, event | category | flops | bytes accessed | tf_op | source)
XLA Modules:
  0.0 32.3 jit_solution(8157385462207071535)
XLA Ops:
  0.6 1.0 %halo_rows.1 = (bf16[256,256]{1,0:T(8,128)(2,1)S(1)}, bf16[256,256]{1,0:T(8,128)(2,1)S(1)}) custom-call(bf16[1536,256]{1,0:T(8,128)(2,1)} %feat_hbm.3), custom_call_target="tpu_custom_call" | custom-call | flops 60000000 | bytes 300000 | tf_op jit(solution)/shard_map/halo_rows/pallas_call | solution.py:421
  1.6 3.0 %collective-permute-start = (bf16[256,256]{1,0:T(8,128)(2,1)S(1)}, bf16[256,256]{1,0:T(8,128)(2,1)S(1)}, u32[]{:S(2)}, u32[]{:S(2)}) collective-permute-start(bf16[256,256]{1,0:T(8,128)(2,1)S(1)} %get-tuple-element.36), channel_id=1, source_target_pairs={{0,1},{1,0},{2,3},{3,2},{4,5},{5,4},{6,7},{7,6},{8,9},{9,8},{10,11... | collective-permute-start | bytes 393224 | tf_op jit(solution)/shard_map/ppermute | solution.py:359
  4.7 3.6 %collective-permute-start.1 = (bf16[256,256]{1,0:T(8,128)(2,1)S(1)}, bf16[256,256]{1,0:T(8,128)(2,1)S(1)}, u32[]{:S(2)}, u32[]{:S(2)}) collective-permute-start(bf16[256,256]{1,0:T(8,128)(2,1)S(1)} %get-tuple-element.37), channel_id=1, source_target_pairs={{0,31},{1,2},{2,1},{3,4},{4,3},{5,6},{6,5},{7,8},{8,7},{9,10},{10,... | collective-permute-start | bytes 393224 | tf_op jit(solution)/shard_map/ppermute | solution.py:364
  8.3 3.5 %inner_rows.1 = (bf16[1536,256]{1,0:T(8,128)(2,1)}, s32[36]{0:T(128)S(1)}, bf16[1024,256]{1,0:T(8,128)(2,1)S(1)}, f32[256,256]{1,0:T(8,128)S(1)}, f32[8,256]{1,0...) custom-call(s32[3,12]{1,0:T(4,128)} %bitcast.3, ...), custom_call_target="tpu_custom_call" | custom-call | flops 600000000 | bytes 3000000 | tf_op jit(solution)/shard_map/inner_rows/pallas_call | solution.py:436
  11.9 0.0 collective-permute-done.first_ref
  11.9 0.8 %collective-permute-done.1.second_ref = bf16[256,256]{1,0:T(8,128)(2,1)S(1)} collective-permute-done((bf16[256,256]{1,0:T(8,128)(2,1)S(1)}, bf16[256,256]{1,0:T(8,128)(2,1)S(1)}, u32[]{:S(2)}, u32[]{:S(2)}) %collective-permute-start.1) | collective-permute-done | bytes 131104 | tf_op jit(solution)/shard_map/ppermute | solution.py:364
  12.7 0.8 %rim_rows.1 = (bf16[512,256]{1,0:T(8,128)(2,1)S(1)}, bf16[512,256]{1,0:T(8,128)(2,1)S(1)}, f32[136,256]{1,0:T(8,128)S(1)}, f32[136,256]{1,0:T(8,128)S(1)}) custom-call(bf16[256,256]{1,0:T(8,128)(2,1)S(1)} %get-tuple-element.32.weight_ref, f32[1,256]{1,0:T(1,128)S(1)} %get-tuple-element.34.bias_ref, f32[512,256]{1,0:T(8,128)S(1)} %get-tuple-element.35.own_ref, ...), custom_call_target="tpu_custom_call" | custom-call | flops 240000000 | bytes 1200000 | tf_op jit(solution)/shard_map/rim_rows/pallas_call | solution.py:472
  13.5 0.1 collective-permute-start.2
  13.6 0.9 %rim_rows_back.1 = (bf16[1536,256]{1,0:T(8,128)(2,1)}, f32[8,256,128]{2,1,0:T(8,128)S(1)}, bf16[256,256]{1,0:T(8,128)(2,1)S(1)}, bf16[256,256]{1,0:T(8,128)(2,1)S(1)}, f32[8,128]{1,0:T(8,128)S(1)}) custom-call(bf16[256,256]{1,0:T(8,128)(2,1)S(1)} %get-tuple-element.32.weight_ref, ...), custom_call_target="tpu_custom_call", output_to_operand_aliasing={{0}: (4, {})} | custom-call | flops 240000000 | bytes 1200000 | tf_op jit(solution)/shard_map/rim_rows_back/pallas_call | solution.py:494
  14.5 0.5 %collective-permute-done.2.refs_1_ = f32[136,256]{1,0:T(8,128)S(1)} collective-permute-done((f32[136,256]{1,0:T(8,128)S(1)}, f32[136,256]{1,0:T(8,128)S(1)}, u32[]{:S(2)}, u32[]{:S(2)}) %collective-permute-start.2) | collective-permute-done | bytes 139296 | tf_op jit(solution)/shard_map/ppermute | solution.py:359
  15.0 1.0 %collective-permute-start.5 = (bf16[136,256]{1,0:T(8,128)(2,1)S(1)}, bf16[136,256]{1,0:T(8,128)(2,1)S(1)}, u32[]{:S(2)}, u32[]{:S(2)}) collective-permute-start(bf16[136,256]{1,0:T(8,128)(2,1)S(1)} %add_halves.3.refs_0_), channel_id=1, source_target_pairs={{0,5},{1,4},{2,26},{3,27},{4,1},{5,0},{6,30},{7,31},{8,13},{9,12},... | collective-permute-start | bytes 208904 | tf_op jit(solution)/shard_map/ppermute | solution.py:359
  16.0 0.0 collective-permute-start.4
  16.0 2.5 %collective-permute-start.3 = (bf16[136,256]{1,0:T(8,128)(2,1)S(1)}, bf16[136,256]{1,0:T(8,128)(2,1)S(1)}, u32[]{:S(2)}, u32[]{:S(2)}) collective-permute-start(bf16[136,256]{1,0:T(8,128)(2,1)S(1)} %add_halves.3.refs_0_), channel_id=1, source_target_pairs={{0,4},{1,5},{2,10},{3,11},{4,0},{5,1},{6,14},{7,15},{8,12},{9,13},... | collective-permute-start | bytes 208904 | tf_op jit(solution)/shard_map/ppermute | solution.py:359
  18.5 0.1 collective-permute-start.9
  18.6 3.7 %collective-permute-start.10 = (bf16[256,256]{1,0:T(8,128)(2,1)S(1)}, bf16[256,256]{1,0:T(8,128)(2,1)S(1)}, u32[]{:S(2)}, u32[]{:S(2)}) collective-permute-start(bf16[256,256]{1,0:T(8,128)(2,1)S(1)} %get-tuple-element.54), channel_id=1, source_target_pairs={{0,31},{1,2},{2,1},{3,4},{4,3},{5,6},{6,5},{7,8},{8,7},{9,10},{10,... | collective-permute-start | bytes 393224 | tf_op jit(solution)/shard_map/ppermute | solution.py:364
  22.3 0.0 collective-permute-done.5.refs_3_
  22.3 0.0 collective-permute-done.4.refs_2_
  22.3 0.0 collective-permute-done.3.refs_1_
  22.3 1.8 %collective-permute-start.8 = (bf16[136,256]{1,0:T(8,128)(2,1)S(1)}, bf16[136,256]{1,0:T(8,128)(2,1)S(1)}, u32[]{:S(2)}, u32[]{:S(2)}) collective-permute-start(bf16[136,256]{1,0:T(8,128)(2,1)S(1)} %add_halves.4.refs_0_), channel_id=1, source_target_pairs={{0,24},{1,25},{2,7},{3,6},{4,28},{5,29},{6,3},{7,2},{8,16},{9,17},... | collective-permute-start | bytes 208904 | tf_op jit(solution)/shard_map/ppermute | solution.py:359
  24.1 0.0 collective-permute-start.7
  24.1 2.7 %collective-permute-start.6 = (bf16[136,256]{1,0:T(8,128)(2,1)S(1)}, bf16[136,256]{1,0:T(8,128)(2,1)S(1)}, u32[]{:S(2)}, u32[]{:S(2)}) collective-permute-start(bf16[136,256]{1,0:T(8,128)(2,1)S(1)} %add_halves.4.refs_0_), channel_id=1, source_target_pairs={{0,8},{1,9},{2,6},{3,7},{4,12},{5,13},{6,2},{7,3},{8,0},{9,1},{10,... | collective-permute-start | bytes 208904 | tf_op jit(solution)/shard_map/ppermute | solution.py:359
  26.8 2.2 %inner_rows_back.1 = (bf16[1536,256]{1,0:T(8,128)(2,1)}, f32[512,256]{1,0:T(8,128)S(1)}, f32[8,128]{1,0:T(8,128)S(1)}) custom-call(s32[36]{0:T(128)S(1)} %get-tuple-element.48.place_in, bf16[256,256]{1,0:T(8,128)(2,1)S(1)} %get-tuple-element.32.weight_ref, bf16[8,3,128,128]{3,2,1,0:T(8,128)(2,1)S(1)} %get-tuple-element.49.adj_ref, ...), custom_call_target="tpu_custom_call" | custom-call | flops 360000000 | bytes 1800000 | tf_op jit(solution)/shard_map/inner_rows_back/pallas_call | solution.py:516
  29.0 0.0 collective-permute-done.9.refs_5_.first_ref
  29.0 0.0 collective-permute-done.10.refs_6_.second_ref
  29.0 0.0 collective-permute-done.8.refs_3_
  29.0 1.0 %collective-permute-done.7.refs_2_ = bf16[136,256]{1,0:T(8,128)(2,1)S(1)} collective-permute-done((bf16[136,256]{1,0:T(8,128)(2,1)S(1)}, bf16[136,256]{1,0:T(8,128)(2,1)S(1)}, u32[]{:S(2)}, u32[]{:S(2)}) %collective-permute-start.7) | collective-permute-done | bytes 69664 | tf_op jit(solution)/shard_map/ppermute | solution.py:359
  30.0 0.0 collective-permute-done.6.refs_1_
  30.0 0.1 collective-permute-start.11
  30.1 1.3 %collective-permute-done.11.other_ref = f32[136,256]{1,0:T(8,128)S(1)} collective-permute-done((f32[136,256]{1,0:T(8,128)S(1)}, f32[136,256]{1,0:T(8,128)S(1)}, u32[]{:S(2)}, u32[]{:S(2)}) %collective-permute-start.11) | collective-permute-done | bytes 139296 | tf_op jit(solution)/shard_map/ppermute | solution.py:359
  31.4 0.9 %last_step.1 = (f32[256,256]{1,0:T(8,128)}, f32[1,256]{1,0:T(1,128)}, bf16[1536,256]{1,0:T(8,128)(2,1)}) custom-call(f32[136,256]{1,0:T(8,128)S(1)} %add_halves.5.own_ref, f32[136,256]{1,0:T(8,128)S(1)} %collective-permute-done.11.other_ref, f32[512,256]{1,0:T(8,128)S(1)} %get-tuple-element.55.edge_ref, ...), custom_call_target="tpu_custom_call", output_to_operand_aliasing={{2}: (5, {})} | custom-call | tf_op jit(solution)/shard_map/last_step/pallas_call | solution.py:535
  (3 shorter events, 0.1 us)
Async XLA Ops:
  1.6 10.2 %collective-permute-start = (bf16[256,256]{1,0:T(8,128)(2,1)S(1)}, bf16[256,256]{1,0:T(8,128)(2,1)S(1)}, u32[]{:S(2)}, u32[]{:S(2)}) collective-permute-start(bf16[256,256]{1,0:T(8,128)(2,1)S(1)} %get-tuple-element.36), channel_id=1, source_target_pairs={{0,1},{1,0},{2,3},{3,2},{4,5},{5,4},{6,7},{7,6},{8,9},{9,8},{10,11... | collective-permute-start | bytes 393224 | tf_op jit(solution)/shard_map/ppermute | solution.py:359
  4.7 8.0 %collective-permute-start.1 = (bf16[256,256]{1,0:T(8,128)(2,1)S(1)}, bf16[256,256]{1,0:T(8,128)(2,1)S(1)}, u32[]{:S(2)}, u32[]{:S(2)}) collective-permute-start(bf16[256,256]{1,0:T(8,128)(2,1)S(1)} %get-tuple-element.37), channel_id=1, source_target_pairs={{0,31},{1,2},{2,1},{3,4},{4,3},{5,6},{6,5},{7,8},{8,7},{9,10},{10,... | collective-permute-start | bytes 393224 | tf_op jit(solution)/shard_map/ppermute | solution.py:364
  13.5 1.4 %collective-permute-start.2 = (f32[136,256]{1,0:T(8,128)S(1)}, f32[136,256]{1,0:T(8,128)S(1)}, u32[]{:S(2)}, u32[]{:S(2)}) collective-permute-start(f32[136,256]{1,0:T(8,128)S(1)} %get-tuple-element.46), channel_id=1, source_target_pairs={{0,2},{1,3},{2,0},{3,1},{4,6},{5,7},{6,4},{7,5},{8,10},{9,11},{10,... | collective-permute-start | bytes 417800 | tf_op jit(solution)/shard_map/ppermute | solution.py:359
  15.0 7.3 %collective-permute-start.5 = (bf16[136,256]{1,0:T(8,128)(2,1)S(1)}, bf16[136,256]{1,0:T(8,128)(2,1)S(1)}, u32[]{:S(2)}, u32[]{:S(2)}) collective-permute-start(bf16[136,256]{1,0:T(8,128)(2,1)S(1)} %add_halves.3.refs_0_), channel_id=1, source_target_pairs={{0,5},{1,4},{2,26},{3,27},{4,1},{5,0},{6,30},{7,31},{8,13},{9,12},... | collective-permute-start | bytes 208904 | tf_op jit(solution)/shard_map/ppermute | solution.py:359
  16.0 6.3 %collective-permute-start.4 = (bf16[136,256]{1,0:T(8,128)(2,1)S(1)}, bf16[136,256]{1,0:T(8,128)(2,1)S(1)}, u32[]{:S(2)}, u32[]{:S(2)}) collective-permute-start(bf16[136,256]{1,0:T(8,128)(2,1)S(1)} %add_halves.3.refs_0_), channel_id=1, source_target_pairs={{0,1},{1,0},{2,18},{3,19},{4,5},{5,4},{6,22},{7,23},{8,9},{9,8},{1... | collective-permute-start | bytes 208904 | tf_op jit(solution)/shard_map/ppermute | solution.py:359
  16.0 6.3 %collective-permute-start.3 = (bf16[136,256]{1,0:T(8,128)(2,1)S(1)}, bf16[136,256]{1,0:T(8,128)(2,1)S(1)}, u32[]{:S(2)}, u32[]{:S(2)}) collective-permute-start(bf16[136,256]{1,0:T(8,128)(2,1)S(1)} %add_halves.3.refs_0_), channel_id=1, source_target_pairs={{0,4},{1,5},{2,10},{3,11},{4,0},{5,1},{6,14},{7,15},{8,12},{9,13},... | collective-permute-start | bytes 208904 | tf_op jit(solution)/shard_map/ppermute | solution.py:359
  18.5 10.5 %collective-permute-start.9 = (bf16[256,256]{1,0:T(8,128)(2,1)S(1)}, bf16[256,256]{1,0:T(8,128)(2,1)S(1)}, u32[]{:S(2)}, u32[]{:S(2)}) collective-permute-start(bf16[256,256]{1,0:T(8,128)(2,1)S(1)} %get-tuple-element.53), channel_id=1, source_target_pairs={{0,1},{1,0},{2,3},{3,2},{4,5},{5,4},{6,7},{7,6},{8,9},{9,8},{10,11... | collective-permute-start | bytes 393224 | tf_op jit(solution)/shard_map/ppermute | solution.py:359
  18.6 10.4 %collective-permute-start.10 = (bf16[256,256]{1,0:T(8,128)(2,1)S(1)}, bf16[256,256]{1,0:T(8,128)(2,1)S(1)}, u32[]{:S(2)}, u32[]{:S(2)}) collective-permute-start(bf16[256,256]{1,0:T(8,128)(2,1)S(1)} %get-tuple-element.54), channel_id=1, source_target_pairs={{0,31},{1,2},{2,1},{3,4},{4,3},{5,6},{6,5},{7,8},{8,7},{9,10},{10,... | collective-permute-start | bytes 393224 | tf_op jit(solution)/shard_map/ppermute | solution.py:364
  22.3 6.7 %collective-permute-start.8 = (bf16[136,256]{1,0:T(8,128)(2,1)S(1)}, bf16[136,256]{1,0:T(8,128)(2,1)S(1)}, u32[]{:S(2)}, u32[]{:S(2)}) collective-permute-start(bf16[136,256]{1,0:T(8,128)(2,1)S(1)} %add_halves.4.refs_0_), channel_id=1, source_target_pairs={{0,24},{1,25},{2,7},{3,6},{4,28},{5,29},{6,3},{7,2},{8,16},{9,17},... | collective-permute-start | bytes 208904 | tf_op jit(solution)/shard_map/ppermute | solution.py:359
  24.1 5.9 %collective-permute-start.7 = (bf16[136,256]{1,0:T(8,128)(2,1)S(1)}, bf16[136,256]{1,0:T(8,128)(2,1)S(1)}, u32[]{:S(2)}, u32[]{:S(2)}) collective-permute-start(bf16[136,256]{1,0:T(8,128)(2,1)S(1)} %add_halves.4.refs_0_), channel_id=1, source_target_pairs={{0,16},{1,17},{2,3},{3,2},{4,20},{5,21},{6,7},{7,6},{8,24},{9,25},... | collective-permute-start | bytes 208904 | tf_op jit(solution)/shard_map/ppermute | solution.py:359
  24.1 5.9 %collective-permute-start.6 = (bf16[136,256]{1,0:T(8,128)(2,1)S(1)}, bf16[136,256]{1,0:T(8,128)(2,1)S(1)}, u32[]{:S(2)}, u32[]{:S(2)}) collective-permute-start(bf16[136,256]{1,0:T(8,128)(2,1)S(1)} %add_halves.4.refs_0_), channel_id=1, source_target_pairs={{0,8},{1,9},{2,6},{3,7},{4,12},{5,13},{6,2},{7,3},{8,0},{9,1},{10,... | collective-permute-start | bytes 208904 | tf_op jit(solution)/shard_map/ppermute | solution.py:359
  30.0 1.4 %collective-permute-start.11 = (f32[136,256]{1,0:T(8,128)S(1)}, f32[136,256]{1,0:T(8,128)S(1)}, u32[]{:S(2)}, u32[]{:S(2)}) collective-permute-start(f32[136,256]{1,0:T(8,128)S(1)} %add_halves.5.own_ref), channel_id=1, source_target_pairs={{0,2},{1,3},{2,0},{3,1},{4,6},{5,7},{6,4},{7,5},{8,10},{9,11},{10,... | collective-permute-start | bytes 417800 | tf_op jit(solution)/shard_map/ppermute | solution.py:359

commit v15 on v14

--- a/solution.py
+++ b/solution.py
@@ -211,7 +211,7 @@
     payload[1, half:] = tail
     side = core_side()
     keep_ref[...] = payload[side]
-    send_ref[...] = payload[1 - side]
+    send_ref[...] = payload[1 - side].astype(send_ref.dtype)
 
 
 def scatter_rows(places, upstream, adj_ref, spread):
@@ -323,11 +323,12 @@
     side = core_side()
     own_rows = pl.ds(pl.multiple_of(side * half, half), half)
     other_rows = pl.ds(pl.multiple_of((1 - side) * half, half), half)
-    sums[own_rows] = own_ref[:half] * scale
-    sums[other_rows] = other_ref[:half] * scale
+    own = own_ref[...].astype(jnp.float32) * scale
+    other = other_ref[...].astype(jnp.float32) * scale
+    sums[own_rows] = own[:half]
+    sums[other_rows] = other[:half]
     copies[0].start()
-    first = jnp.where(side == 0, own_ref[half : half + 1], other_ref[half : half + 1])
-    bias[...] = first * scale
+    bias[...] = jnp.where(side == 0, own[half : half + 1], other[half : half + 1])
     copies[1].start()
     odd = place_in_mesh() & 1
     for base, spill_ref in (((1 - odd) * rim, first_ref), (odd * rim, second_ref)):
@@ -382,7 +383,7 @@
         ]
         last = step == len(groups) - 1
         name = "last" if last else step
-        total = add(parts, jnp.float32 if last else jnp.bfloat16, marks.get(name, ()))
+        total = add(parts, jnp.bfloat16, marks.get(name, ()))
     return total
 
 
@@ -474,7 +475,7 @@
         out_shape=(
             shape(2 * rim, width),
             shape(2 * rim, width),
-            shape(*half_shape, dtype=jnp.float32),
+            shape(*half_shape),
             shape(*half_shape, dtype=jnp.float32),
         ),
         in_specs=[vmem] * 9,

time: 32.5 us -> 32.3 us (level)
  no operation moved by 1% of the time
where the time goes in v15:
time: 32.3 us; the launch traced here: 32.1 us
  starting transfers between devices  18.6 us (58%)
  Pallas kernels  9.44 us (29%)
  waiting for transfers between devices  3.38 us (10%)
  between operations  0.73 us (2%)
    ppermute x10, starting transfers between devices, swap(): return lax.ppermute(value, AXES, pairs)  11.2 us
    ppermute x2, starting transfers between devices, with_next(): return lax.ppermute(value, AXES, pairs)  7.32 us
    pallas_call x1, Pallas kernels, on_device(): pl.pallas_call(inner_kernel, out_shape=(shape(rows, width), shape(blocks...  3.54 us
    ppermute x10, waiting for transfers between devices, swap(): return lax.ppermute(value, AXES, pairs)  2.58 us
    pallas_call x1, Pallas kernels, on_device(): pl.pallas_call(inner_back_kernel, out_shape=(shape(rows, width), shape(2...  2.22 us
    pallas_call x1, Pallas kernels, on_device(): pl.pallas_call(halo_kernel, out_shape=(shape(rim, width), shape(rim, widt...  1 us
    pallas_call x1, Pallas kernels, on_device(): pl.pallas_call(rim_back_kernel, out_shape=(shape(rows, width), shape(4 *...  0.88 us
    pallas_call x1, Pallas kernels, on_device(): pl.pallas_call(functools.partial(last_kernel, norm_scale), out_shape=(sha...  0.85 us
  transfers between devices with their start and end apart: 12, of which 4 were waited for; matrix products, arithmetic and copies ran while one was open for 0% of the time, Pallas kernels for 21%

profile of v15, /device:TPU:0, one launch (start us, length us, event | category | flops | bytes accessed | tf_op | source)
XLA Modules:
  0.0 32.1 jit_solution(16188088249095780220)
XLA Ops:
  0.6 1.0 %halo_rows.1 = (bf16[256,256]{1,0:T(8,128)(2,1)S(1)}, bf16[256,256]{1,0:T(8,128)(2,1)S(1)}) custom-call(bf16[1536,256]{1,0:T(8,128)(2,1)} %feat_hbm.3), custom_call_target="tpu_custom_call" | custom-call | flops 60000000 | bytes 300000 | tf_op jit(solution)/shard_map/halo_rows/pallas_call | solution.py:422
  1.6 3.0 %collective-permute-start = (bf16[256,256]{1,0:T(8,128)(2,1)S(1)}, bf16[256,256]{1,0:T(8,128)(2,1)S(1)}, u32[]{:S(2)}, u32[]{:S(2)}) collective-permute-start(bf16[256,256]{1,0:T(8,128)(2,1)S(1)} %get-tuple-element.36), channel_id=1, source_target_pairs={{0,1},{1,0},{2,3},{3,2},{4,5},{5,4},{6,7},{7,6},{8,9},{9,8},{10,11... | collective-permute-start | bytes 393224 | tf_op jit(solution)/shard_map/ppermute | solution.py:360
  4.7 3.6 %collective-permute-start.1 = (bf16[256,256]{1,0:T(8,128)(2,1)S(1)}, bf16[256,256]{1,0:T(8,128)(2,1)S(1)}, u32[]{:S(2)}, u32[]{:S(2)}) collective-permute-start(bf16[256,256]{1,0:T(8,128)(2,1)S(1)} %get-tuple-element.37), channel_id=1, source_target_pairs={{0,31},{1,2},{2,1},{3,4},{4,3},{5,6},{6,5},{7,8},{8,7},{9,10},{10,... | collective-permute-start | bytes 393224 | tf_op jit(solution)/shard_map/ppermute | solution.py:365
  8.3 3.5 %inner_rows.1 = (bf16[1536,256]{1,0:T(8,128)(2,1)}, s32[36]{0:T(128)S(1)}, bf16[1024,256]{1,0:T(8,128)(2,1)S(1)}, f32[256,256]{1,0:T(8,128)S(1)}, f32[8,256]{1,0...) custom-call(s32[3,12]{1,0:T(4,128)} %bitcast.3, ...), custom_call_target="tpu_custom_call" | custom-call | flops 600000000 | bytes 3000000 | tf_op jit(solution)/shard_map/inner_rows/pallas_call | solution.py:437
  11.9 0.0 collective-permute-done.first_ref
  11.9 0.8 %collective-permute-done.1.second_ref = bf16[256,256]{1,0:T(8,128)(2,1)S(1)} collective-permute-done((bf16[256,256]{1,0:T(8,128)(2,1)S(1)}, bf16[256,256]{1,0:T(8,128)(2,1)S(1)}, u32[]{:S(2)}, u32[]{:S(2)}) %collective-permute-start.1) | collective-permute-done | bytes 131104 | tf_op jit(solution)/shard_map/ppermute | solution.py:365
  12.7 0.8 %rim_rows.1 = (bf16[512,256]{1,0:T(8,128)(2,1)S(1)}, bf16[512,256]{1,0:T(8,128)(2,1)S(1)}, bf16[136,256]{1,0:T(8,128)(2,1)S(1)}, f32[136,256]{1,0:T(8,128)S(1)}) custom-call(bf16[256,256]{1,0:T(8,128)(2,1)S(1)} %get-tuple-element.32.weight_ref, f32[1,256]{1,0:T(1,128)S(1)} %get-tuple-element.34.bias_ref, f32[512,256]{1,0:T(8,128)S(1)} %get-tuple-element.35.own_ref, ...), custom_call_target="tpu_custom_call" | custom-call | flops 240000000 | bytes 1200000 | tf_op jit(solution)/shard_map/rim_rows/pallas_call | solution.py:473
  13.5 0.1 collective-permute-start.2
  13.6 0.9 %rim_rows_back.1 = (bf16[1536,256]{1,0:T(8,128)(2,1)}, f32[8,256,128]{2,1,0:T(8,128)S(1)}, bf16[256,256]{1,0:T(8,128)(2,1)S(1)}, bf16[256,256]{1,0:T(8,128)(2,1)S(1)}, f32[8,128]{1,0:T(8,128)S(1)}) custom-call(bf16[256,256]{1,0:T(8,128)(2,1)S(1)} %get-tuple-element.32.weight_ref, ...), custom_call_target="tpu_custom_call", output_to_operand_aliasing={{0}: (4, {})} | custom-call | flops 240000000 | bytes 1200000 | tf_op jit(solution)/shard_map/rim_rows_back/pallas_call | solution.py:495
  14.5 0.4 %collective-permute-done.2.refs_1_ = bf16[136,256]{1,0:T(8,128)(2,1)S(1)} collective-permute-done((bf16[136,256]{1,0:T(8,128)(2,1)S(1)}, bf16[136,256]{1,0:T(8,128)(2,1)S(1)}, u32[]{:S(2)}, u32[]{:S(2)}) %collective-permute-start.2) | collective-permute-done | bytes 69664 | tf_op jit(solution)/shard_map/ppermute | solution.py:360
  14.9 1.0 %collective-permute-start.5 = (bf16[136,256]{1,0:T(8,128)(2,1)S(1)}, bf16[136,256]{1,0:T(8,128)(2,1)S(1)}, u32[]{:S(2)}, u32[]{:S(2)}) collective-permute-start(bf16[136,256]{1,0:T(8,128)(2,1)S(1)} %add_halves.3.refs_0_), channel_id=1, source_target_pairs={{0,5},{1,4},{2,26},{3,27},{4,1},{5,0},{6,30},{7,31},{8,13},{9,12},... | collective-permute-start | bytes 208904 | tf_op jit(solution)/shard_map/ppermute | solution.py:360
  15.9 0.0 collective-permute-start.4
  15.9 2.5 %collective-permute-start.3 = (bf16[136,256]{1,0:T(8,128)(2,1)S(1)}, bf16[136,256]{1,0:T(8,128)(2,1)S(1)}, u32[]{:S(2)}, u32[]{:S(2)}) collective-permute-start(bf16[136,256]{1,0:T(8,128)(2,1)S(1)} %add_halves.3.refs_0_), channel_id=1, source_target_pairs={{0,4},{1,5},{2,10},{3,11},{4,0},{5,1},{6,14},{7,15},{8,12},{9,13},... | collective-permute-start | bytes 208904 | tf_op jit(solution)/shard_map/ppermute | solution.py:360
  18.4 0.1 collective-permute-start.9
  18.5 3.7 %collective-permute-start.10 = (bf16[256,256]{1,0:T(8,128)(2,1)S(1)}, bf16[256,256]{1,0:T(8,128)(2,1)S(1)}, u32[]{:S(2)}, u32[]{:S(2)}) collective-permute-start(bf16[256,256]{1,0:T(8,128)(2,1)S(1)} %get-tuple-element.54), channel_id=1, source_target_pairs={{0,31},{1,2},{2,1},{3,4},{4,3},{5,6},{6,5},{7,8},{8,7},{9,10},{10,... | collective-permute-start | bytes 393224 | tf_op jit(solution)/shard_map/ppermute | solution.py:365
  22.2 0.0 collective-permute-done.5.refs_3_
  22.2 0.0 collective-permute-done.4.refs_2_
  22.2 0.0 collective-permute-done.3.refs_1_
  22.2 1.8 %collective-permute-start.8 = (bf16[136,256]{1,0:T(8,128)(2,1)S(1)}, bf16[136,256]{1,0:T(8,128)(2,1)S(1)}, u32[]{:S(2)}, u32[]{:S(2)}) collective-permute-start(bf16[136,256]{1,0:T(8,128)(2,1)S(1)} %add_halves.4.refs_0_), channel_id=1, source_target_pairs={{0,24},{1,25},{2,7},{3,6},{4,28},{5,29},{6,3},{7,2},{8,16},{9,17},... | collective-permute-start | bytes 208904 | tf_op jit(solution)/shard_map/ppermute | solution.py:360
  24.0 0.0 collective-permute-start.7
  24.0 2.7 %collective-permute-start.6 = (bf16[136,256]{1,0:T(8,128)(2,1)S(1)}, bf16[136,256]{1,0:T(8,128)(2,1)S(1)}, u32[]{:S(2)}, u32[]{:S(2)}) collective-permute-start(bf16[136,256]{1,0:T(8,128)(2,1)S(1)} %add_halves.4.refs_0_), channel_id=1, source_target_pairs={{0,8},{1,9},{2,6},{3,7},{4,12},{5,13},{6,2},{7,3},{8,0},{9,1},{10,... | collective-permute-start | bytes 208904 | tf_op jit(solution)/shard_map/ppermute | solution.py:360
  26.7 2.2 %inner_rows_back.1 = (bf16[1536,256]{1,0:T(8,128)(2,1)}, f32[512,256]{1,0:T(8,128)S(1)}, f32[8,128]{1,0:T(8,128)S(1)}) custom-call(s32[36]{0:T(128)S(1)} %get-tuple-element.48.place_in, bf16[256,256]{1,0:T(8,128)(2,1)S(1)} %get-tuple-element.32.weight_ref, bf16[8,3,128,128]{3,2,1,0:T(8,128)(2,1)S(1)} %get-tuple-element.49.adj_ref, ...), custom_call_target="tpu_custom_call" | custom-call | flops 360000000 | bytes 1800000 | tf_op jit(solution)/shard_map/inner_rows_back/pallas_call | solution.py:517
  28.9 0.0 collective-permute-done.9.refs_5_.first_ref
  28.9 0.0 collective-permute-done.10.refs_6_.second_ref
  28.9 0.0 collective-permute-done.8.refs_3_
  28.9 1.0 %collective-permute-done.7.refs_2_ = bf16[136,256]{1,0:T(8,128)(2,1)S(1)} collective-permute-done((bf16[136,256]{1,0:T(8,128)(2,1)S(1)}, bf16[136,256]{1,0:T(8,128)(2,1)S(1)}, u32[]{:S(2)}, u32[]{:S(2)}) %collective-permute-start.7) | collective-permute-done | bytes 69664 | tf_op jit(solution)/shard_map/ppermute | solution.py:360
  29.9 0.0 collective-permute-done.6.refs_1_
  29.9 0.1 collective-permute-start.11
  30.0 1.2 %collective-permute-done.11.other_ref = bf16[136,256]{1,0:T(8,128)(2,1)S(1)} collective-permute-done((bf16[136,256]{1,0:T(8,128)(2,1)S(1)}, bf16[136,256]{1,0:T(8,128)(2,1)S(1)}, u32[]{:S(2)}, u32[]{:S(2)}) %collective-permute-start.11) | collective-permute-done | bytes 69664 | tf_op jit(solution)/shard_map/ppermute | solution.py:360
  31.3 0.9 %last_step.1 = (f32[256,256]{1,0:T(8,128)}, f32[1,256]{1,0:T(1,128)}, bf16[1536,256]{1,0:T(8,128)(2,1)}) custom-call(bf16[136,256]{1,0:T(8,128)(2,1)S(1)} %add_halves.5.own_ref, bf16[136,256]{1,0:T(8,128)(2,1)S(1)} %collective-permute-done.11.other_ref, f32[512,256]{1,0:T(8,128)S(1)} %get-tuple-element.55.edge_ref, ...), custom_call_target="tpu_custom_call", output_to_operand_aliasing={{2}: (5, {})} | custom-call | tf_op jit(solution)/shard_map/last_step/pallas_call | solution.py:536
  (3 shorter events, 0.1 us)
Async XLA Ops:
  1.6 10.2 %collective-permute-start = (bf16[256,256]{1,0:T(8,128)(2,1)S(1)}, bf16[256,256]{1,0:T(8,128)(2,1)S(1)}, u32[]{:S(2)}, u32[]{:S(2)}) collective-permute-start(bf16[256,256]{1,0:T(8,128)(2,1)S(1)} %get-tuple-element.36), channel_id=1, source_target_pairs={{0,1},{1,0},{2,3},{3,2},{4,5},{5,4},{6,7},{7,6},{8,9},{9,8},{10,11... | collective-permute-start | bytes 393224 | tf_op jit(solution)/shard_map/ppermute | solution.py:360
  4.7 8.0 %collective-permute-start.1 = (bf16[256,256]{1,0:T(8,128)(2,1)S(1)}, bf16[256,256]{1,0:T(8,128)(2,1)S(1)}, u32[]{:S(2)}, u32[]{:S(2)}) collective-permute-start(bf16[256,256]{1,0:T(8,128)(2,1)S(1)} %get-tuple-element.37), channel_id=1, source_target_pairs={{0,31},{1,2},{2,1},{3,4},{4,3},{5,6},{6,5},{7,8},{8,7},{9,10},{10,... | collective-permute-start | bytes 393224 | tf_op jit(solution)/shard_map/ppermute | solution.py:365
  13.5 1.3 %collective-permute-start.2 = (bf16[136,256]{1,0:T(8,128)(2,1)S(1)}, bf16[136,256]{1,0:T(8,128)(2,1)S(1)}, u32[]{:S(2)}, u32[]{:S(2)}) collective-permute-start(bf16[136,256]{1,0:T(8,128)(2,1)S(1)} %get-tuple-element.46), channel_id=1, source_target_pairs={{0,2},{1,3},{2,0},{3,1},{4,6},{5,7},{6,4},{7,5},{8,10},{9,11},{10,... | collective-permute-start | bytes 208904 | tf_op jit(solution)/shard_map/ppermute | solution.py:360
  14.9 7.3 %collective-permute-start.5 = (bf16[136,256]{1,0:T(8,128)(2,1)S(1)}, bf16[136,256]{1,0:T(8,128)(2,1)S(1)}, u32[]{:S(2)}, u32[]{:S(2)}) collective-permute-start(bf16[136,256]{1,0:T(8,128)(2,1)S(1)} %add_halves.3.refs_0_), channel_id=1, source_target_pairs={{0,5},{1,4},{2,26},{3,27},{4,1},{5,0},{6,30},{7,31},{8,13},{9,12},... | collective-permute-start | bytes 208904 | tf_op jit(solution)/shard_map/ppermute | solution.py:360
  15.9 6.3 %collective-permute-start.4 = (bf16[136,256]{1,0:T(8,128)(2,1)S(1)}, bf16[136,256]{1,0:T(8,128)(2,1)S(1)}, u32[]{:S(2)}, u32[]{:S(2)}) collective-permute-start(bf16[136,256]{1,0:T(8,128)(2,1)S(1)} %add_halves.3.refs_0_), channel_id=1, source_target_pairs={{0,1},{1,0},{2,18},{3,19},{4,5},{5,4},{6,22},{7,23},{8,9},{9,8},{1... | collective-permute-start | bytes 208904 | tf_op jit(solution)/shard_map/ppermute | solution.py:360
  15.9 6.3 %collective-permute-start.3 = (bf16[136,256]{1,0:T(8,128)(2,1)S(1)}, bf16[136,256]{1,0:T(8,128)(2,1)S(1)}, u32[]{:S(2)}, u32[]{:S(2)}) collective-permute-start(bf16[136,256]{1,0:T(8,128)(2,1)S(1)} %add_halves.3.refs_0_), channel_id=1, source_target_pairs={{0,4},{1,5},{2,10},{3,11},{4,0},{5,1},{6,14},{7,15},{8,12},{9,13},... | collective-permute-start | bytes 208904 | tf_op jit(solution)/shard_map/ppermute | solution.py:360
  18.4 10.5 %collective-permute-start.9 = (bf16[256,256]{1,0:T(8,128)(2,1)S(1)}, bf16[256,256]{1,0:T(8,128)(2,1)S(1)}, u32[]{:S(2)}, u32[]{:S(2)}) collective-permute-start(bf16[256,256]{1,0:T(8,128)(2,1)S(1)} %get-tuple-element.53), channel_id=1, source_target_pairs={{0,1},{1,0},{2,3},{3,2},{4,5},{5,4},{6,7},{7,6},{8,9},{9,8},{10,11... | collective-permute-start | bytes 393224 | tf_op jit(solution)/shard_map/ppermute | solution.py:360
  18.5 10.4 %collective-permute-start.10 = (bf16[256,256]{1,0:T(8,128)(2,1)S(1)}, bf16[256,256]{1,0:T(8,128)(2,1)S(1)}, u32[]{:S(2)}, u32[]{:S(2)}) collective-permute-start(bf16[256,256]{1,0:T(8,128)(2,1)S(1)} %get-tuple-element.54), channel_id=1, source_target_pairs={{0,31},{1,2},{2,1},{3,4},{4,3},{5,6},{6,5},{7,8},{8,7},{9,10},{10,... | collective-permute-start | bytes 393224 | tf_op jit(solution)/shard_map/ppermute | solution.py:365
  22.2 6.7 %collective-permute-start.8 = (bf16[136,256]{1,0:T(8,128)(2,1)S(1)}, bf16[136,256]{1,0:T(8,128)(2,1)S(1)}, u32[]{:S(2)}, u32[]{:S(2)}) collective-permute-start(bf16[136,256]{1,0:T(8,128)(2,1)S(1)} %add_halves.4.refs_0_), channel_id=1, source_target_pairs={{0,24},{1,25},{2,7},{3,6},{4,28},{5,29},{6,3},{7,2},{8,16},{9,17},... | collective-permute-start | bytes 208904 | tf_op jit(solution)/shard_map/ppermute | solution.py:360
  24.0 5.9 %collective-permute-start.7 = (bf16[136,256]{1,0:T(8,128)(2,1)S(1)}, bf16[136,256]{1,0:T(8,128)(2,1)S(1)}, u32[]{:S(2)}, u32[]{:S(2)}) collective-permute-start(bf16[136,256]{1,0:T(8,128)(2,1)S(1)} %add_halves.4.refs_0_), channel_id=1, source_target_pairs={{0,16},{1,17},{2,3},{3,2},{4,20},{5,21},{6,7},{7,6},{8,24},{9,25},... | collective-permute-start | bytes 208904 | tf_op jit(solution)/shard_map/ppermute | solution.py:360
  24.0 5.9 %collective-permute-start.6 = (bf16[136,256]{1,0:T(8,128)(2,1)S(1)}, bf16[136,256]{1,0:T(8,128)(2,1)S(1)}, u32[]{:S(2)}, u32[]{:S(2)}) collective-permute-start(bf16[136,256]{1,0:T(8,128)(2,1)S(1)} %add_halves.4.refs_0_), channel_id=1, source_target_pairs={{0,8},{1,9},{2,6},{3,7},{4,12},{5,13},{6,2},{7,3},{8,0},{9,1},{10,... | collective-permute-start | bytes 208904 | tf_op jit(solution)/shard_map/ppermute | solution.py:360
  29.9 1.3 %collective-permute-start.11 = (bf16[136,256]{1,0:T(8,128)(2,1)S(1)}, bf16[136,256]{1,0:T(8,128)(2,1)S(1)}, u32[]{:S(2)}, u32[]{:S(2)}) collective-permute-start(bf16[136,256]{1,0:T(8,128)(2,1)S(1)} %add_halves.5.own_ref), channel_id=1, source_target_pairs={{0,2},{1,3},{2,0},{3,1},{4,6},{5,7},{6,4},{7,5},{8,10},{9,11},{10,... | collective-permute-start | bytes 208904 | tf_op jit(solution)/shard_map/ppermute | solution.py:360

commit v16 on v15

--- a/solution.py
+++ b/solution.py
@@ -375,8 +375,12 @@
         for group in (groups[step], groups[len(groups) - 1 - step]):
             if len(groups[0]) != len(groups[-1]):
                 group = groups[step]
-            low = 1 << group[0]
-            masks.append((low, 1 << group[1], low | 1 << group[1]) if group[1:] else (low,))
+            bits = [1 << bit for bit in group]
+            if group[1:]:
+                both = bits[0] | bits[1]
+                near = group is groups[0]
+                bits = [bits[0], both, bits[1]] if near else [*bits, both]
+            masks.append(bits)
         parts = [total] + [
             swap(total, [masks[(i >> core_bit) & 1][k] for i in range(count)])
             for k in range(len(masks[0]))

time: 32.3 us -> 32.3 us (level)
  no operation moved by 1% of the time
where the time goes in v16:
time: 32.3 us; the launch traced here: 32.1 us
  starting transfers between devices  18.6 us (58%)
  Pallas kernels  9.44 us (29%)
  waiting for transfers between devices  3.38 us (10%)
  between operations  0.73 us (2%)
    ppermute x10, starting transfers between devices, swap(): return lax.ppermute(value, AXES, pairs)  11.3 us
    ppermute x2, starting transfers between devices, with_next(): return lax.ppermute(value, AXES, pairs)  7.3 us
    pallas_call x1, Pallas kernels, on_device(): pl.pallas_call(inner_kernel, out_shape=(shape(rows, width), shape(blocks...  3.54 us
    ppermute x10, waiting for transfers between devices, swap(): return lax.ppermute(value, AXES, pairs)  2.58 us
    pallas_call x1, Pallas kernels, on_device(): pl.pallas_call(inner_back_kernel, out_shape=(shape(rows, width), shape(2...  2.22 us
    pallas_call x1, Pallas kernels, on_device(): pl.pallas_call(halo_kernel, out_shape=(shape(rim, width), shape(rim, widt...  1 us
    pallas_call x1, Pallas kernels, on_device(): pl.pallas_call(rim_back_kernel, out_shape=(shape(rows, width), shape(4 *...  0.88 us
    pallas_call x1, Pallas kernels, on_device(): pl.pallas_call(functools.partial(last_kernel, norm_scale), out_shape=(sha...  0.85 us
  transfers between devices with their start and end apart: 12, of which 4 were waited for; matrix products, arithmetic and copies ran while one was open for 0% of the time, Pallas kernels for 21%

profile of v16, /device:TPU:0, one launch (start us, length us, event | category | flops | bytes accessed | tf_op | source)
XLA Modules:
  0.0 32.1 jit_solution(11788317315231548199)
XLA Ops:
  0.6 1.0 %halo_rows.1 = (bf16[256,256]{1,0:T(8,128)(2,1)S(1)}, bf16[256,256]{1,0:T(8,128)(2,1)S(1)}) custom-call(bf16[1536,256]{1,0:T(8,128)(2,1)} %feat_hbm.3), custom_call_target="tpu_custom_call" | custom-call | flops 60000000 | bytes 300000 | tf_op jit(solution)/shard_map/halo_rows/pallas_call | solution.py:426
  1.6 3.0 %collective-permute-start = (bf16[256,256]{1,0:T(8,128)(2,1)S(1)}, bf16[256,256]{1,0:T(8,128)(2,1)S(1)}, u32[]{:S(2)}, u32[]{:S(2)}) collective-permute-start(bf16[256,256]{1,0:T(8,128)(2,1)S(1)} %get-tuple-element.36), channel_id=1, source_target_pairs={{0,1},{1,0},{2,3},{3,2},{4,5},{5,4},{6,7},{7,6},{8,9},{9,8},{10,11... | collective-permute-start | bytes 393224 | tf_op jit(solution)/shard_map/ppermute | solution.py:360
  4.7 3.6 %collective-permute-start.1 = (bf16[256,256]{1,0:T(8,128)(2,1)S(1)}, bf16[256,256]{1,0:T(8,128)(2,1)S(1)}, u32[]{:S(2)}, u32[]{:S(2)}) collective-permute-start(bf16[256,256]{1,0:T(8,128)(2,1)S(1)} %get-tuple-element.37), channel_id=1, source_target_pairs={{0,31},{1,2},{2,1},{3,4},{4,3},{5,6},{6,5},{7,8},{8,7},{9,10},{10,... | collective-permute-start | bytes 393224 | tf_op jit(solution)/shard_map/ppermute | solution.py:365
  8.3 3.5 %inner_rows.1 = (bf16[1536,256]{1,0:T(8,128)(2,1)}, s32[36]{0:T(128)S(1)}, bf16[1024,256]{1,0:T(8,128)(2,1)S(1)}, f32[256,256]{1,0:T(8,128)S(1)}, f32[8,256]{1,0...) custom-call(s32[3,12]{1,0:T(4,128)} %bitcast.3, ...), custom_call_target="tpu_custom_call" | custom-call | flops 600000000 | bytes 3000000 | tf_op jit(solution)/shard_map/inner_rows/pallas_call | solution.py:441
  11.9 0.0 collective-permute-done.first_ref
  11.9 0.8 %collective-permute-done.1.second_ref = bf16[256,256]{1,0:T(8,128)(2,1)S(1)} collective-permute-done((bf16[256,256]{1,0:T(8,128)(2,1)S(1)}, bf16[256,256]{1,0:T(8,128)(2,1)S(1)}, u32[]{:S(2)}, u32[]{:S(2)}) %collective-permute-start.1) | collective-permute-done | bytes 131104 | tf_op jit(solution)/shard_map/ppermute | solution.py:365
  12.7 0.8 %rim_rows.1 = (bf16[512,256]{1,0:T(8,128)(2,1)S(1)}, bf16[512,256]{1,0:T(8,128)(2,1)S(1)}, bf16[136,256]{1,0:T(8,128)(2,1)S(1)}, f32[136,256]{1,0:T(8,128)S(1)}) custom-call(bf16[256,256]{1,0:T(8,128)(2,1)S(1)} %get-tuple-element.32.weight_ref, f32[1,256]{1,0:T(1,128)S(1)} %get-tuple-element.34.bias_ref, f32[512,256]{1,0:T(8,128)S(1)} %get-tuple-element.35.own_ref, ...), custom_call_target="tpu_custom_call" | custom-call | flops 240000000 | bytes 1200000 | tf_op jit(solution)/shard_map/rim_rows/pallas_call | solution.py:477
  13.5 0.1 collective-permute-start.2
  13.6 0.9 %rim_rows_back.1 = (bf16[1536,256]{1,0:T(8,128)(2,1)}, f32[8,256,128]{2,1,0:T(8,128)S(1)}, bf16[256,256]{1,0:T(8,128)(2,1)S(1)}, bf16[256,256]{1,0:T(8,128)(2,1)S(1)}, f32[8,128]{1,0:T(8,128)S(1)}) custom-call(bf16[256,256]{1,0:T(8,128)(2,1)S(1)} %get-tuple-element.32.weight_ref, ...), custom_call_target="tpu_custom_call", output_to_operand_aliasing={{0}: (4, {})} | custom-call | flops 240000000 | bytes 1200000 | tf_op jit(solution)/shard_map/rim_rows_back/pallas_call | solution.py:499
  14.5 0.4 %collective-permute-done.2.refs_1_ = bf16[136,256]{1,0:T(8,128)(2,1)S(1)} collective-permute-done((bf16[136,256]{1,0:T(8,128)(2,1)S(1)}, bf16[136,256]{1,0:T(8,128)(2,1)S(1)}, u32[]{:S(2)}, u32[]{:S(2)}) %collective-permute-start.2) | collective-permute-done | bytes 69664 | tf_op jit(solution)/shard_map/ppermute | solution.py:360
  14.9 0.1 collective-permute-start.5
  15.0 1.0 %collective-permute-start.4 = (bf16[136,256]{1,0:T(8,128)(2,1)S(1)}, bf16[136,256]{1,0:T(8,128)(2,1)S(1)}, u32[]{:S(2)}, u32[]{:S(2)}) collective-permute-start(bf16[136,256]{1,0:T(8,128)(2,1)S(1)} %add_halves.3.refs_0_), channel_id=1, source_target_pairs={{0,5},{1,4},{2,18},{3,19},{4,1},{5,0},{6,22},{7,23},{8,13},{9,12},... | collective-permute-start | bytes 208904 | tf_op jit(solution)/shard_map/ppermute | solution.py:360
  16.0 2.4 %collective-permute-start.3 = (bf16[136,256]{1,0:T(8,128)(2,1)S(1)}, bf16[136,256]{1,0:T(8,128)(2,1)S(1)}, u32[]{:S(2)}, u32[]{:S(2)}) collective-permute-start(bf16[136,256]{1,0:T(8,128)(2,1)S(1)} %add_halves.3.refs_0_), channel_id=1, source_target_pairs={{0,4},{1,5},{2,10},{3,11},{4,0},{5,1},{6,14},{7,15},{8,12},{9,13},... | collective-permute-start | bytes 208904 | tf_op jit(solution)/shard_map/ppermute | solution.py:360
  18.4 0.1 collective-permute-start.9
  18.5 3.7 %collective-permute-start.10 = (bf16[256,256]{1,0:T(8,128)(2,1)S(1)}, bf16[256,256]{1,0:T(8,128)(2,1)S(1)}, u32[]{:S(2)}, u32[]{:S(2)}) collective-permute-start(bf16[256,256]{1,0:T(8,128)(2,1)S(1)} %get-tuple-element.54), channel_id=1, source_target_pairs={{0,31},{1,2},{2,1},{3,4},{4,3},{5,6},{6,5},{7,8},{8,7},{9,10},{10,... | collective-permute-start | bytes 393224 | tf_op jit(solution)/shard_map/ppermute | solution.py:365
  22.2 0.0 collective-permute-done.5.refs_3_
  22.2 0.0 collective-permute-done.4.refs_2_
  22.2 0.0 collective-permute-done.3.refs_1_
  22.2 1.8 %collective-permute-start.8 = (bf16[136,256]{1,0:T(8,128)(2,1)S(1)}, bf16[136,256]{1,0:T(8,128)(2,1)S(1)}, u32[]{:S(2)}, u32[]{:S(2)}) collective-permute-start(bf16[136,256]{1,0:T(8,128)(2,1)S(1)} %add_halves.4.refs_0_), channel_id=1, source_target_pairs={{0,24},{1,25},{2,3},{3,2},{4,28},{5,29},{6,7},{7,6},{8,16},{9,17},... | collective-permute-start | bytes 208904 | tf_op jit(solution)/shard_map/ppermute | solution.py:360
  24.0 0.0 collective-permute-start.7
  24.0 2.7 %collective-permute-start.6 = (bf16[136,256]{1,0:T(8,128)(2,1)S(1)}, bf16[136,256]{1,0:T(8,128)(2,1)S(1)}, u32[]{:S(2)}, u32[]{:S(2)}) collective-permute-start(bf16[136,256]{1,0:T(8,128)(2,1)S(1)} %add_halves.4.refs_0_), channel_id=1, source_target_pairs={{0,8},{1,9},{2,6},{3,7},{4,12},{5,13},{6,2},{7,3},{8,0},{9,1},{10,... | collective-permute-start | bytes 208904 | tf_op jit(solution)/shard_map/ppermute | solution.py:360
  26.7 2.2 %inner_rows_back.1 = (bf16[1536,256]{1,0:T(8,128)(2,1)}, f32[512,256]{1,0:T(8,128)S(1)}, f32[8,128]{1,0:T(8,128)S(1)}) custom-call(s32[36]{0:T(128)S(1)} %get-tuple-element.48.place_in, bf16[256,256]{1,0:T(8,128)(2,1)S(1)} %get-tuple-element.32.weight_ref, bf16[8,3,128,128]{3,2,1,0:T(8,128)(2,1)S(1)} %get-tuple-element.49.adj_ref, ...), custom_call_target="tpu_custom_call" | custom-call | flops 360000000 | bytes 1800000 | tf_op jit(solution)/shard_map/inner_rows_back/pallas_call | solution.py:521
  28.9 0.0 collective-permute-done.9.refs_5_.first_ref
  28.9 0.0 collective-permute-done.10.refs_6_.second_ref
  28.9 0.0 collective-permute-done.8.refs_3_
  28.9 1.0 %collective-permute-done.7.refs_2_ = bf16[136,256]{1,0:T(8,128)(2,1)S(1)} collective-permute-done((bf16[136,256]{1,0:T(8,128)(2,1)S(1)}, bf16[136,256]{1,0:T(8,128)(2,1)S(1)}, u32[]{:S(2)}, u32[]{:S(2)}) %collective-permute-start.7) | collective-permute-done | bytes 69664 | tf_op jit(solution)/shard_map/ppermute | solution.py:360
  29.9 0.0 collective-permute-done.6.refs_1_
  29.9 0.1 collective-permute-start.11
  30.0 1.2 %collective-permute-done.11.other_ref = bf16[136,256]{1,0:T(8,128)(2,1)S(1)} collective-permute-done((bf16[136,256]{1,0:T(8,128)(2,1)S(1)}, bf16[136,256]{1,0:T(8,128)(2,1)S(1)}, u32[]{:S(2)}, u32[]{:S(2)}) %collective-permute-start.11) | collective-permute-done | bytes 69664 | tf_op jit(solution)/shard_map/ppermute | solution.py:360
  31.3 0.9 %last_step.1 = (f32[256,256]{1,0:T(8,128)}, f32[1,256]{1,0:T(1,128)}, bf16[1536,256]{1,0:T(8,128)(2,1)}) custom-call(bf16[136,256]{1,0:T(8,128)(2,1)S(1)} %add_halves.5.own_ref, bf16[136,256]{1,0:T(8,128)(2,1)S(1)} %collective-permute-done.11.other_ref, f32[512,256]{1,0:T(8,128)S(1)} %get-tuple-element.55.edge_ref, ...), custom_call_target="tpu_custom_call", output_to_operand_aliasing={{2}: (5, {})} | custom-call | tf_op jit(solution)/shard_map/last_step/pallas_call | solution.py:540
  (3 shorter events, 0.1 us)
Async XLA Ops:
  1.6 10.2 %collective-permute-start = (bf16[256,256]{1,0:T(8,128)(2,1)S(1)}, bf16[256,256]{1,0:T(8,128)(2,1)S(1)}, u32[]{:S(2)}, u32[]{:S(2)}) collective-permute-start(bf16[256,256]{1,0:T(8,128)(2,1)S(1)} %get-tuple-element.36), channel_id=1, source_target_pairs={{0,1},{1,0},{2,3},{3,2},{4,5},{5,4},{6,7},{7,6},{8,9},{9,8},{10,11... | collective-permute-start | bytes 393224 | tf_op jit(solution)/shard_map/ppermute | solution.py:360
  4.7 8.0 %collective-permute-start.1 = (bf16[256,256]{1,0:T(8,128)(2,1)S(1)}, bf16[256,256]{1,0:T(8,128)(2,1)S(1)}, u32[]{:S(2)}, u32[]{:S(2)}) collective-permute-start(bf16[256,256]{1,0:T(8,128)(2,1)S(1)} %get-tuple-element.37), channel_id=1, source_target_pairs={{0,31},{1,2},{2,1},{3,4},{4,3},{5,6},{6,5},{7,8},{8,7},{9,10},{10,... | collective-permute-start | bytes 393224 | tf_op jit(solution)/shard_map/ppermute | solution.py:365
  13.5 1.3 %collective-permute-start.2 = (bf16[136,256]{1,0:T(8,128)(2,1)S(1)}, bf16[136,256]{1,0:T(8,128)(2,1)S(1)}, u32[]{:S(2)}, u32[]{:S(2)}) collective-permute-start(bf16[136,256]{1,0:T(8,128)(2,1)S(1)} %get-tuple-element.46), channel_id=1, source_target_pairs={{0,2},{1,3},{2,0},{3,1},{4,6},{5,7},{6,4},{7,5},{8,10},{9,11},{10,... | collective-permute-start | bytes 208904 | tf_op jit(solution)/shard_map/ppermute | solution.py:360
  14.9 7.3 %collective-permute-start.5 = (bf16[136,256]{1,0:T(8,128)(2,1)S(1)}, bf16[136,256]{1,0:T(8,128)(2,1)S(1)}, u32[]{:S(2)}, u32[]{:S(2)}) collective-permute-start(bf16[136,256]{1,0:T(8,128)(2,1)S(1)} %add_halves.3.refs_0_), channel_id=1, source_target_pairs={{0,1},{1,0},{2,26},{3,27},{4,5},{5,4},{6,30},{7,31},{8,9},{9,8},{1... | collective-permute-start | bytes 208904 | tf_op jit(solution)/shard_map/ppermute | solution.py:360
  15.0 7.2 %collective-permute-start.4 = (bf16[136,256]{1,0:T(8,128)(2,1)S(1)}, bf16[136,256]{1,0:T(8,128)(2,1)S(1)}, u32[]{:S(2)}, u32[]{:S(2)}) collective-permute-start(bf16[136,256]{1,0:T(8,128)(2,1)S(1)} %add_halves.3.refs_0_), channel_id=1, source_target_pairs={{0,5},{1,4},{2,18},{3,19},{4,1},{5,0},{6,22},{7,23},{8,13},{9,12},... | collective-permute-start | bytes 208904 | tf_op jit(solution)/shard_map/ppermute | solution.py:360
  16.0 6.2 %collective-permute-start.3 = (bf16[136,256]{1,0:T(8,128)(2,1)S(1)}, bf16[136,256]{1,0:T(8,128)(2,1)S(1)}, u32[]{:S(2)}, u32[]{:S(2)}) collective-permute-start(bf16[136,256]{1,0:T(8,128)(2,1)S(1)} %add_halves.3.refs_0_), channel_id=1, source_target_pairs={{0,4},{1,5},{2,10},{3,11},{4,0},{5,1},{6,14},{7,15},{8,12},{9,13},... | collective-permute-start | bytes 208904 | tf_op jit(solution)/shard_map/ppermute | solution.py:360
  18.4 10.5 %collective-permute-start.9 = (bf16[256,256]{1,0:T(8,128)(2,1)S(1)}, bf16[256,256]{1,0:T(8,128)(2,1)S(1)}, u32[]{:S(2)}, u32[]{:S(2)}) collective-permute-start(bf16[256,256]{1,0:T(8,128)(2,1)S(1)} %get-tuple-element.53), channel_id=1, source_target_pairs={{0,1},{1,0},{2,3},{3,2},{4,5},{5,4},{6,7},{7,6},{8,9},{9,8},{10,11... | collective-permute-start | bytes 393224 | tf_op jit(solution)/shard_map/ppermute | solution.py:360
  18.5 10.4 %collective-permute-start.10 = (bf16[256,256]{1,0:T(8,128)(2,1)S(1)}, bf16[256,256]{1,0:T(8,128)(2,1)S(1)}, u32[]{:S(2)}, u32[]{:S(2)}) collective-permute-start(bf16[256,256]{1,0:T(8,128)(2,1)S(1)} %get-tuple-element.54), channel_id=1, source_target_pairs={{0,31},{1,2},{2,1},{3,4},{4,3},{5,6},{6,5},{7,8},{8,7},{9,10},{10,... | collective-permute-start | bytes 393224 | tf_op jit(solution)/shard_map/ppermute | solution.py:365
  22.2 6.7 %collective-permute-start.8 = (bf16[136,256]{1,0:T(8,128)(2,1)S(1)}, bf16[136,256]{1,0:T(8,128)(2,1)S(1)}, u32[]{:S(2)}, u32[]{:S(2)}) collective-permute-start(bf16[136,256]{1,0:T(8,128)(2,1)S(1)} %add_halves.4.refs_0_), channel_id=1, source_target_pairs={{0,24},{1,25},{2,3},{3,2},{4,28},{5,29},{6,7},{7,6},{8,16},{9,17},... | collective-permute-start | bytes 208904 | tf_op jit(solution)/shard_map/ppermute | solution.py:360
  24.0 5.9 %collective-permute-start.7 = (bf16[136,256]{1,0:T(8,128)(2,1)S(1)}, bf16[136,256]{1,0:T(8,128)(2,1)S(1)}, u32[]{:S(2)}, u32[]{:S(2)}) collective-permute-start(bf16[136,256]{1,0:T(8,128)(2,1)S(1)} %add_halves.4.refs_0_), channel_id=1, source_target_pairs={{0,16},{1,17},{2,7},{3,6},{4,20},{5,21},{6,3},{7,2},{8,24},{9,25},... | collective-permute-start | bytes 208904 | tf_op jit(solution)/shard_map/ppermute | solution.py:360
  24.0 5.9 %collective-permute-start.6 = (bf16[136,256]{1,0:T(8,128)(2,1)S(1)}, bf16[136,256]{1,0:T(8,128)(2,1)S(1)}, u32[]{:S(2)}, u32[]{:S(2)}) collective-permute-start(bf16[136,256]{1,0:T(8,128)(2,1)S(1)} %add_halves.4.refs_0_), channel_id=1, source_target_pairs={{0,8},{1,9},{2,6},{3,7},{4,12},{5,13},{6,2},{7,3},{8,0},{9,1},{10,... | collective-permute-start | bytes 208904 | tf_op jit(solution)/shard_map/ppermute | solution.py:360
  29.9 1.3 %collective-permute-start.11 = (bf16[136,256]{1,0:T(8,128)(2,1)S(1)}, bf16[136,256]{1,0:T(8,128)(2,1)S(1)}, u32[]{:S(2)}, u32[]{:S(2)}) collective-permute-start(bf16[136,256]{1,0:T(8,128)(2,1)S(1)} %add_halves.5.own_ref), channel_id=1, source_target_pairs={{0,2},{1,3},{2,0},{3,1},{4,6},{5,7},{6,4},{7,5},{8,10},{9,11},{10,... | collective-permute-start | bytes 208904 | tf_op jit(solution)/shard_map/ppermute | solution.py:360

commit v17 on v16

--- a/solution.py
+++ b/solution.py
@@ -533,7 +533,7 @@
         cost_estimate=cost(0.3),
         name="inner_rows_back",
     )(places, weight_near, adj_inner, grad_inner, rim_spread)
-    marks = {"core": (first_mark,), "last": (second_mark, first_part, second_part)}
+    marks = {"core": (first_mark,), "last": (second_mark, first_part)}
     own_half = sum_halves(send, keep, count, core_bit, marks)
     other_half = swap(own_half, [1 << core_bit] * count)
     norm_scale = 1.0 / math.sqrt(rows * count)

time: 32.3 us -> 34.9 us (1.080)
  waiting for transfers between devices: 3.38 us -> 8.34 us
  starting transfers between devices: 18.6 us -> 16.3 us
    ppermute x2, waiting for transfers between devices: 0.8 us -> 5.02 us  [with_next(): return lax.ppermute(value, AXES, pairs)]
    ppermute x2, starting transfers between devices: 7.3 us -> 5 us  [with_next(): return lax.ppermute(value, AXES, pairs)]
    ppermute x10, waiting for transfers between devices: 2.58 us -> 3.32 us  [swap(): return lax.ppermute(value, AXES, pairs)]
  transfers between devices with their start and end apart: 12 -> 12, of which waited for: 4 -> 6; matrix products, arithmetic and copies ran while one was open for 0% -> 0% of each run, Pallas kernels for 21% -> 19%
where the time goes in v17:
time: 34.9 us; the launch traced here: 34.8 us
  starting transfers between devices  16.3 us (47%)
  Pallas kernels  9.44 us (27%)
  waiting for transfers between devices  8.34 us (24%)
  between operations  0.74 us (2%)
    ppermute x10, starting transfers between devices, swap(): return lax.ppermute(value, AXES, pairs)  11.3 us
    ppermute x2, waiting for transfers between devices, with_next(): return lax.ppermute(value, AXES, pairs)  5.02 us
    ppermute x2, starting transfers between devices, with_next(): return lax.ppermute(value, AXES, pairs)  5 us
    pallas_call x1, Pallas kernels, on_device(): pl.pallas_call(inner_kernel, out_shape=(shape(rows, width), shape(blocks...  3.54 us
    ppermute x10, waiting for transfers between devices, swap(): return lax.ppermute(value, AXES, pairs)  3.32 us
    pallas_call x1, Pallas kernels, on_device(): pl.pallas_call(inner_back_kernel, out_shape=(shape(rows, width), shape(2...  2.22 us
    pallas_call x1, Pallas kernels, on_device(): pl.pallas_call(halo_kernel, out_shape=(shape(rim, width), shape(rim, widt...  1 us
    pallas_call x1, Pallas kernels, on_device(): pl.pallas_call(rim_back_kernel, out_shape=(shape(rows, width), shape(4 *...  0.88 us
  transfers between devices with their start and end apart: 12, of which 6 were waited for; matrix products, arithmetic and copies ran while one was open for 0% of the time, Pallas kernels for 19%

profile of v17, /device:TPU:0, one launch (start us, length us, event | category | flops | bytes accessed | tf_op | source)
XLA Modules:
  0.0 34.8 jit_solution(12868397210018385603)
XLA Ops:
  0.6 1.0 %halo_rows.1 = (bf16[256,256]{1,0:T(8,128)(2,1)S(1)}, bf16[256,256]{1,0:T(8,128)(2,1)S(1)}) custom-call(bf16[1536,256]{1,0:T(8,128)(2,1)} %feat_hbm.3), custom_call_target="tpu_custom_call" | custom-call | flops 60000000 | bytes 300000 | tf_op jit(solution)/shard_map/halo_rows/pallas_call | solution.py:426
  1.6 3.0 %collective-permute-start = (bf16[256,256]{1,0:T(8,128)(2,1)S(1)}, bf16[256,256]{1,0:T(8,128)(2,1)S(1)}, u32[]{:S(2)}, u32[]{:S(2)}) collective-permute-start(bf16[256,256]{1,0:T(8,128)(2,1)S(1)} %get-tuple-element.36), channel_id=1, source_target_pairs={{0,1},{1,0},{2,3},{3,2},{4,5},{5,4},{6,7},{7,6},{8,9},{9,8},{10,11... | collective-permute-start | bytes 393224 | tf_op jit(solution)/shard_map/ppermute | solution.py:360
  4.7 3.6 %collective-permute-start.1 = (bf16[256,256]{1,0:T(8,128)(2,1)S(1)}, bf16[256,256]{1,0:T(8,128)(2,1)S(1)}, u32[]{:S(2)}, u32[]{:S(2)}) collective-permute-start(bf16[256,256]{1,0:T(8,128)(2,1)S(1)} %get-tuple-element.37), channel_id=1, source_target_pairs={{0,31},{1,2},{2,1},{3,4},{4,3},{5,6},{6,5},{7,8},{8,7},{9,10},{10,... | collective-permute-start | bytes 393224 | tf_op jit(solution)/shard_map/ppermute | solution.py:365
  8.3 3.5 %inner_rows.1 = (bf16[1536,256]{1,0:T(8,128)(2,1)}, s32[36]{0:T(128)S(1)}, bf16[1024,256]{1,0:T(8,128)(2,1)S(1)}, f32[256,256]{1,0:T(8,128)S(1)}, f32[8,256]{1,0...) custom-call(s32[3,12]{1,0:T(4,128)} %bitcast.3, ...), custom_call_target="tpu_custom_call" | custom-call | flops 600000000 | bytes 3000000 | tf_op jit(solution)/shard_map/inner_rows/pallas_call | solution.py:441
  11.9 0.0 collective-permute-done.first_ref
  11.9 0.8 %collective-permute-done.1.second_ref = bf16[256,256]{1,0:T(8,128)(2,1)S(1)} collective-permute-done((bf16[256,256]{1,0:T(8,128)(2,1)S(1)}, bf16[256,256]{1,0:T(8,128)(2,1)S(1)}, u32[]{:S(2)}, u32[]{:S(2)}) %collective-permute-start.1) | collective-permute-done | bytes 131104 | tf_op jit(solution)/shard_map/ppermute | solution.py:365
  12.7 0.8 %rim_rows.1 = (bf16[512,256]{1,0:T(8,128)(2,1)S(1)}, bf16[512,256]{1,0:T(8,128)(2,1)S(1)}, bf16[136,256]{1,0:T(8,128)(2,1)S(1)}, f32[136,256]{1,0:T(8,128)S(1)}) custom-call(bf16[256,256]{1,0:T(8,128)(2,1)S(1)} %get-tuple-element.32.weight_ref, f32[1,256]{1,0:T(1,128)S(1)} %get-tuple-element.34.bias_ref, f32[512,256]{1,0:T(8,128)S(1)} %get-tuple-element.35.own_ref, ...), custom_call_target="tpu_custom_call" | custom-call | flops 240000000 | bytes 1200000 | tf_op jit(solution)/shard_map/rim_rows/pallas_call | solution.py:477
  13.5 0.1 collective-permute-start.2
  13.6 0.9 %rim_rows_back.1 = (bf16[1536,256]{1,0:T(8,128)(2,1)}, f32[8,256,128]{2,1,0:T(8,128)S(1)}, bf16[256,256]{1,0:T(8,128)(2,1)S(1)}, bf16[256,256]{1,0:T(8,128)(2,1)S(1)}, f32[8,128]{1,0:T(8,128)S(1)}) custom-call(bf16[256,256]{1,0:T(8,128)(2,1)S(1)} %get-tuple-element.32.weight_ref, ...), custom_call_target="tpu_custom_call", output_to_operand_aliasing={{0}: (4, {})} | custom-call | flops 240000000 | bytes 1200000 | tf_op jit(solution)/shard_map/rim_rows_back/pallas_call | solution.py:499
  14.5 0.4 %collective-permute-done.2.refs_1_ = bf16[136,256]{1,0:T(8,128)(2,1)S(1)} collective-permute-done((bf16[136,256]{1,0:T(8,128)(2,1)S(1)}, bf16[136,256]{1,0:T(8,128)(2,1)S(1)}, u32[]{:S(2)}, u32[]{:S(2)}) %collective-permute-start.2) | collective-permute-done | bytes 69664 | tf_op jit(solution)/shard_map/ppermute | solution.py:360
  14.9 0.1 collective-permute-start.5
  15.0 1.0 %collective-permute-start.4 = (bf16[136,256]{1,0:T(8,128)(2,1)S(1)}, bf16[136,256]{1,0:T(8,128)(2,1)S(1)}, u32[]{:S(2)}, u32[]{:S(2)}) collective-permute-start(bf16[136,256]{1,0:T(8,128)(2,1)S(1)} %add_halves.3.refs_0_), channel_id=1, source_target_pairs={{0,5},{1,4},{2,18},{3,19},{4,1},{5,0},{6,22},{7,23},{8,13},{9,12},... | collective-permute-start | bytes 208904 | tf_op jit(solution)/shard_map/ppermute | solution.py:360
  16.0 2.4 %collective-permute-start.3 = (bf16[136,256]{1,0:T(8,128)(2,1)S(1)}, bf16[136,256]{1,0:T(8,128)(2,1)S(1)}, u32[]{:S(2)}, u32[]{:S(2)}) collective-permute-start(bf16[136,256]{1,0:T(8,128)(2,1)S(1)} %add_halves.3.refs_0_), channel_id=1, source_target_pairs={{0,4},{1,5},{2,10},{3,11},{4,0},{5,1},{6,14},{7,15},{8,12},{9,13},... | collective-permute-start | bytes 208904 | tf_op jit(solution)/shard_map/ppermute | solution.py:360
  18.4 0.1 collective-permute-start.9
  18.5 0.7 %collective-permute-done.5.refs_3_ = bf16[136,256]{1,0:T(8,128)(2,1)S(1)} collective-permute-done((bf16[136,256]{1,0:T(8,128)(2,1)S(1)}, bf16[136,256]{1,0:T(8,128)(2,1)S(1)}, u32[]{:S(2)}, u32[]{:S(2)}) %collective-permute-start.5) | collective-permute-done | bytes 69664 | tf_op jit(solution)/shard_map/ppermute | solution.py:360
  19.2 1.0 %collective-permute-done.4.refs_2_ = bf16[136,256]{1,0:T(8,128)(2,1)S(1)} collective-permute-done((bf16[136,256]{1,0:T(8,128)(2,1)S(1)}, bf16[136,256]{1,0:T(8,128)(2,1)S(1)}, u32[]{:S(2)}, u32[]{:S(2)}) %collective-permute-start.4) | collective-permute-done | bytes 69664 | tf_op jit(solution)/shard_map/ppermute | solution.py:360
  20.2 1.2 %collective-permute-done.3.refs_1_ = bf16[136,256]{1,0:T(8,128)(2,1)S(1)} collective-permute-done((bf16[136,256]{1,0:T(8,128)(2,1)S(1)}, bf16[136,256]{1,0:T(8,128)(2,1)S(1)}, u32[]{:S(2)}, u32[]{:S(2)}) %collective-permute-start.3) | collective-permute-done | bytes 69664 | tf_op jit(solution)/shard_map/ppermute | solution.py:360
  21.5 2.5 %collective-permute-start.8 = (bf16[136,256]{1,0:T(8,128)(2,1)S(1)}, bf16[136,256]{1,0:T(8,128)(2,1)S(1)}, u32[]{:S(2)}, u32[]{:S(2)}) collective-permute-start(bf16[136,256]{1,0:T(8,128)(2,1)S(1)} %add_halves.4.refs_0_), channel_id=1, source_target_pairs={{0,24},{1,25},{2,3},{3,2},{4,28},{5,29},{6,7},{7,6},{8,16},{9,17},... | collective-permute-start | bytes 208904 | tf_op jit(solution)/shard_map/ppermute | solution.py:360
  24.0 0.0 collective-permute-start.7
  24.0 2.0 %collective-permute-start.6 = (bf16[136,256]{1,0:T(8,128)(2,1)S(1)}, bf16[136,256]{1,0:T(8,128)(2,1)S(1)}, u32[]{:S(2)}, u32[]{:S(2)}) collective-permute-start(bf16[136,256]{1,0:T(8,128)(2,1)S(1)} %add_halves.4.refs_0_), channel_id=1, source_target_pairs={{0,8},{1,9},{2,6},{3,7},{4,12},{5,13},{6,2},{7,3},{8,0},{9,1},{10,... | collective-permute-start | bytes 208904 | tf_op jit(solution)/shard_map/ppermute | solution.py:360
  25.9 1.4 %collective-permute-start.11 = (bf16[256,256]{1,0:T(8,128)(2,1)S(1)}, bf16[256,256]{1,0:T(8,128)(2,1)S(1)}, u32[]{:S(2)}, u32[]{:S(2)}) collective-permute-start(bf16[256,256]{1,0:T(8,128)(2,1)S(1)} %get-tuple-element.55), channel_id=1, source_target_pairs={{0,31},{1,2},{2,1},{3,4},{4,3},{5,6},{6,5},{7,8},{8,7},{9,10},{10,... | collective-permute-start | bytes 393224 | tf_op jit(solution)/shard_map/ppermute | solution.py:365
  27.3 2.2 %inner_rows_back.1 = (bf16[1536,256]{1,0:T(8,128)(2,1)}, f32[512,256]{1,0:T(8,128)S(1)}, f32[8,128]{1,0:T(8,128)S(1)}) custom-call(s32[36]{0:T(128)S(1)} %get-tuple-element.48.place_in, bf16[256,256]{1,0:T(8,128)(2,1)S(1)} %get-tuple-element.32.weight_ref, bf16[8,3,128,128]{3,2,1,0:T(8,128)(2,1)S(1)} %get-tuple-element.49.adj_ref, ...), custom_call_target="tpu_custom_call" | custom-call | flops 360000000 | bytes 1800000 | tf_op jit(solution)/shard_map/inner_rows_back/pallas_call | solution.py:521
  29.5 0.0 collective-permute-done.9.refs_5_.first_ref
  29.5 0.0 collective-permute-done.8.refs_3_
  29.6 0.0 collective-permute-done.7.refs_2_
  29.6 0.0 collective-permute-done.6.refs_1_
  29.6 0.1 collective-permute-start.10
  29.7 4.2 %collective-permute-done.11.second_ref = bf16[256,256]{1,0:T(8,128)(2,1)S(1)} collective-permute-done((bf16[256,256]{1,0:T(8,128)(2,1)S(1)}, bf16[256,256]{1,0:T(8,128)(2,1)S(1)}, u32[]{:S(2)}, u32[]{:S(2)}) %collective-permute-start.11) | collective-permute-done | bytes 131104 | tf_op jit(solution)/shard_map/ppermute | solution.py:365
  33.9 0.0 collective-permute-done.10.other_ref
  33.9 0.9 %last_step.1 = (f32[256,256]{1,0:T(8,128)}, f32[1,256]{1,0:T(1,128)}, bf16[1536,256]{1,0:T(8,128)(2,1)}) custom-call(bf16[136,256]{1,0:T(8,128)(2,1)S(1)} %add_halves.5.own_ref, bf16[136,256]{1,0:T(8,128)(2,1)S(1)} %collective-permute-done.10.other_ref, f32[512,256]{1,0:T(8,128)S(1)} %get-tuple-element.54.edge_ref, ...), custom_call_target="tpu_custom_call", output_to_operand_aliasing={{2}: (5, {})} | custom-call | tf_op jit(solution)/shard_map/last_step/pallas_call | solution.py:540
  (3 shorter events, 0.1 us)
Async XLA Ops:
  1.6 10.2 %collective-permute-start = (bf16[256,256]{1,0:T(8,128)(2,1)S(1)}, bf16[256,256]{1,0:T(8,128)(2,1)S(1)}, u32[]{:S(2)}, u32[]{:S(2)}) collective-permute-start(bf16[256,256]{1,0:T(8,128)(2,1)S(1)} %get-tuple-element.36), channel_id=1, source_target_pairs={{0,1},{1,0},{2,3},{3,2},{4,5},{5,4},{6,7},{7,6},{8,9},{9,8},{10,11... | collective-permute-start | bytes 393224 | tf_op jit(solution)/shard_map/ppermute | solution.py:360
  4.7 8.0 %collective-permute-start.1 = (bf16[256,256]{1,0:T(8,128)(2,1)S(1)}, bf16[256,256]{1,0:T(8,128)(2,1)S(1)}, u32[]{:S(2)}, u32[]{:S(2)}) collective-permute-start(bf16[256,256]{1,0:T(8,128)(2,1)S(1)} %get-tuple-element.37), channel_id=1, source_target_pairs={{0,31},{1,2},{2,1},{3,4},{4,3},{5,6},{6,5},{7,8},{8,7},{9,10},{10,... | collective-permute-start | bytes 393224 | tf_op jit(solution)/shard_map/ppermute | solution.py:365
  13.5 1.3 %collective-permute-start.2 = (bf16[136,256]{1,0:T(8,128)(2,1)S(1)}, bf16[136,256]{1,0:T(8,128)(2,1)S(1)}, u32[]{:S(2)}, u32[]{:S(2)}) collective-permute-start(bf16[136,256]{1,0:T(8,128)(2,1)S(1)} %get-tuple-element.46), channel_id=1, source_target_pairs={{0,2},{1,3},{2,0},{3,1},{4,6},{5,7},{6,4},{7,5},{8,10},{9,11},{10,... | collective-permute-start | bytes 208904 | tf_op jit(solution)/shard_map/ppermute | solution.py:360
  14.9 4.4 %collective-permute-start.5 = (bf16[136,256]{1,0:T(8,128)(2,1)S(1)}, bf16[136,256]{1,0:T(8,128)(2,1)S(1)}, u32[]{:S(2)}, u32[]{:S(2)}) collective-permute-start(bf16[136,256]{1,0:T(8,128)(2,1)S(1)} %add_halves.3.refs_0_), channel_id=1, source_target_pairs={{0,1},{1,0},{2,26},{3,27},{4,5},{5,4},{6,30},{7,31},{8,9},{9,8},{1... | collective-permute-start | bytes 208904 | tf_op jit(solution)/shard_map/ppermute | solution.py:360
  15.0 5.2 %collective-permute-start.4 = (bf16[136,256]{1,0:T(8,128)(2,1)S(1)}, bf16[136,256]{1,0:T(8,128)(2,1)S(1)}, u32[]{:S(2)}, u32[]{:S(2)}) collective-permute-start(bf16[136,256]{1,0:T(8,128)(2,1)S(1)} %add_halves.3.refs_0_), channel_id=1, source_target_pairs={{0,5},{1,4},{2,18},{3,19},{4,1},{5,0},{6,22},{7,23},{8,13},{9,12},... | collective-permute-start | bytes 208904 | tf_op jit(solution)/shard_map/ppermute | solution.py:360
  16.0 5.5 %collective-permute-start.3 = (bf16[136,256]{1,0:T(8,128)(2,1)S(1)}, bf16[136,256]{1,0:T(8,128)(2,1)S(1)}, u32[]{:S(2)}, u32[]{:S(2)}) collective-permute-start(bf16[136,256]{1,0:T(8,128)(2,1)S(1)} %add_halves.3.refs_0_), channel_id=1, source_target_pairs={{0,4},{1,5},{2,10},{3,11},{4,0},{5,1},{6,14},{7,15},{8,12},{9,13},... | collective-permute-start | bytes 208904 | tf_op jit(solution)/shard_map/ppermute | solution.py:360
  18.4 11.1 %collective-permute-start.9 = (bf16[256,256]{1,0:T(8,128)(2,1)S(1)}, bf16[256,256]{1,0:T(8,128)(2,1)S(1)}, u32[]{:S(2)}, u32[]{:S(2)}) collective-permute-start(bf16[256,256]{1,0:T(8,128)(2,1)S(1)} %get-tuple-element.53), channel_id=1, source_target_pairs={{0,1},{1,0},{2,3},{3,2},{4,5},{5,4},{6,7},{7,6},{8,9},{9,8},{10,11... | collective-permute-start | bytes 393224 | tf_op jit(solution)/shard_map/ppermute | solution.py:360
  21.5 8.1 %collective-permute-start.8 = (bf16[136,256]{1,0:T(8,128)(2,1)S(1)}, bf16[136,256]{1,0:T(8,128)(2,1)S(1)}, u32[]{:S(2)}, u32[]{:S(2)}) collective-permute-start(bf16[136,256]{1,0:T(8,128)(2,1)S(1)} %add_halves.4.refs_0_), channel_id=1, source_target_pairs={{0,24},{1,25},{2,3},{3,2},{4,28},{5,29},{6,7},{7,6},{8,16},{9,17},... | collective-permute-start | bytes 208904 | tf_op jit(solution)/shard_map/ppermute | solution.py:360
  24.0 5.6 %collective-permute-start.7 = (bf16[136,256]{1,0:T(8,128)(2,1)S(1)}, bf16[136,256]{1,0:T(8,128)(2,1)S(1)}, u32[]{:S(2)}, u32[]{:S(2)}) collective-permute-start(bf16[136,256]{1,0:T(8,128)(2,1)S(1)} %add_halves.4.refs_0_), channel_id=1, source_target_pairs={{0,16},{1,17},{2,7},{3,6},{4,20},{5,21},{6,3},{7,2},{8,24},{9,25},... | collective-permute-start | bytes 208904 | tf_op jit(solution)/shard_map/ppermute | solution.py:360
  24.0 5.6 %collective-permute-start.6 = (bf16[136,256]{1,0:T(8,128)(2,1)S(1)}, bf16[136,256]{1,0:T(8,128)(2,1)S(1)}, u32[]{:S(2)}, u32[]{:S(2)}) collective-permute-start(bf16[136,256]{1,0:T(8,128)(2,1)S(1)} %add_halves.4.refs_0_), channel_id=1, source_target_pairs={{0,8},{1,9},{2,6},{3,7},{4,12},{5,13},{6,2},{7,3},{8,0},{9,1},{10,... | collective-permute-start | bytes 208904 | tf_op jit(solution)/shard_map/ppermute | solution.py:360
  25.9 8.0 %collective-permute-start.11 = (bf16[256,256]{1,0:T(8,128)(2,1)S(1)}, bf16[256,256]{1,0:T(8,128)(2,1)S(1)}, u32[]{:S(2)}, u32[]{:S(2)}) collective-permute-start(bf16[256,256]{1,0:T(8,128)(2,1)S(1)} %get-tuple-element.55), channel_id=1, source_target_pairs={{0,31},{1,2},{2,1},{3,4},{4,3},{5,6},{6,5},{7,8},{8,7},{9,10},{10,... | collective-permute-start | bytes 393224 | tf_op jit(solution)/shard_map/ppermute | solution.py:365
  29.6 4.3 %collective-permute-start.10 = (bf16[136,256]{1,0:T(8,128)(2,1)S(1)}, bf16[136,256]{1,0:T(8,128)(2,1)S(1)}, u32[]{:S(2)}, u32[]{:S(2)}) collective-permute-start(bf16[136,256]{1,0:T(8,128)(2,1)S(1)} %add_halves.5.own_ref), channel_id=1, source_target_pairs={{0,2},{1,3},{2,0},{3,1},{4,6},{5,7},{6,4},{7,5},{8,10},{9,11},{10,... | collective-permute-start | bytes 208904 | tf_op jit(solution)/shard_map/ppermute | solution.py:360

commit v18 on v17

--- a/solution.py
+++ b/solution.py
@@ -360,9 +360,9 @@
     return lax.ppermute(value, AXES, pairs)
 
 
-def with_next(value, count):
+def with_next(value, count, closed):
     pairs = [(i, (i + 1 if i & 1 else i - 1) % count) for i in range(count)]
-    return lax.ppermute(value, AXES, pairs)
+    return lax.ppermute(value, AXES, pairs if closed else pairs[1:-1])
 
 
 def sum_halves(send, keep, count, core_bit, marks):
@@ -434,7 +434,7 @@
         name="halo_rows",
     )(in_hbm(features))
     first_halo = swap(first_rim, [1] * count)
-    second_halo = with_next(second_rim, count)
+    second_halo = with_next(second_rim, count, True)
     (
         activated, places, grad_inner, partial, sums, weight_near, bias_near, dense, own_part,
         cot_rim, adj_inner,
@@ -517,7 +517,7 @@
         name="rim_rows_back",
     )(weight_near, dense, grad_rim, act_rim, activated)
     first_part = swap(first_spill, [1] * count)
-    second_part = with_next(second_spill, count)
+    second_part = with_next(second_spill, count, False)
     grad_whole, edges, second_mark = pl.pallas_call(
         inner_back_kernel,
         out_shape=(shape(rows, width), shape(2 * rim, width, dtype=jnp.float32), mark),
@@ -533,7 +533,7 @@
         cost_estimate=cost(0.3),
         name="inner_rows_back",
     )(places, weight_near, adj_inner, grad_inner, rim_spread)
-    marks = {"core": (first_mark,), "last": (second_mark, first_part)}
+    marks = {"core": (first_mark,), "last": (second_mark, second_part)}
     own_half = sum_halves(send, keep, count, core_bit, marks)
     other_half = swap(own_half, [1 << core_bit] * count)
     norm_scale = 1.0 / math.sqrt(rows * count)

time: 34.9 us -> 32 us (0.917)
  waiting for transfers between devices: 8.34 us -> 5.43 us
    ppermute x2, waiting for transfers between devices: 5.02 us -> 0.8 us  [with_next(): return lax.ppermute(value, AXES, pairs if closed else pairs[1:-1])]
    ppermute x10, waiting for transfers between devices: 3.32 us -> 4.63 us  [swap(): return lax.ppermute(value, AXES, pairs)]
    ppermute x10, starting transfers between devices: 11.3 us -> 12 us  [swap(): return lax.ppermute(value, AXES, pairs)]
    ppermute x2, starting transfers between devices: 5 us -> 4.29 us  [with_next(): return lax.ppermute(value, AXES, pairs if closed else pairs[1:-1])]
  transfers between devices with their start and end apart: 12 -> 12, of which waited for: 6 -> 8; matrix products, arithmetic and copies ran while one was open for 0% -> 0% of each run, Pallas kernels for 19% -> 21%
where the time goes in v18:
time: 32 us; the launch traced here: 31.9 us
  starting transfers between devices  16.3 us (51%)
  Pallas kernels  9.44 us (30%)
  waiting for transfers between devices  5.43 us (17%)
  between operations  0.73 us (2%)
    ppermute x10, starting transfers between devices, swap(): return lax.ppermute(value, AXES, pairs)  12 us
    ppermute x10, waiting for transfers between devices, swap(): return lax.ppermute(value, AXES, pairs)  4.63 us
    ppermute x2, starting transfers between devices, with_next(): return lax.ppermute(value, AXES, pairs if closed else pairs[1:-1])  4.29 us
    pallas_call x1, Pallas kernels, on_device(): pl.pallas_call(inner_kernel, out_shape=(shape(rows, width), shape(blocks...  3.54 us
    pallas_call x1, Pallas kernels, on_device(): pl.pallas_call(inner_back_kernel, out_shape=(shape(rows, width), shape(2...  2.22 us
    pallas_call x1, Pallas kernels, on_device(): pl.pallas_call(halo_kernel, out_shape=(shape(rim, width), shape(rim, widt...  1 us
    pallas_call x1, Pallas kernels, on_device(): pl.pallas_call(rim_back_kernel, out_shape=(shape(rows, width), shape(4 *...  0.88 us
    pallas_call x1, Pallas kernels, on_device(): pl.pallas_call(functools.partial(last_kernel, norm_scale), out_shape=(sha...  0.85 us
  transfers between devices with their start and end apart: 12, of which 8 were waited for; matrix products, arithmetic and copies ran while one was open for 0% of the time, Pallas kernels for 21%

profile of v18, /device:TPU:0, one launch (start us, length us, event | category | flops | bytes accessed | tf_op | source)
XLA Modules:
  0.0 31.9 jit_solution(12505800973311064807)
XLA Ops:
  0.6 1.0 %halo_rows.1 = (bf16[256,256]{1,0:T(8,128)(2,1)S(1)}, bf16[256,256]{1,0:T(8,128)(2,1)S(1)}) custom-call(bf16[1536,256]{1,0:T(8,128)(2,1)} %feat_hbm.3), custom_call_target="tpu_custom_call" | custom-call | flops 60000000 | bytes 300000 | tf_op jit(solution)/shard_map/halo_rows/pallas_call | solution.py:426
  1.6 3.0 %collective-permute-start = (bf16[256,256]{1,0:T(8,128)(2,1)S(1)}, bf16[256,256]{1,0:T(8,128)(2,1)S(1)}, u32[]{:S(2)}, u32[]{:S(2)}) collective-permute-start(bf16[256,256]{1,0:T(8,128)(2,1)S(1)} %get-tuple-element.36), channel_id=1, source_target_pairs={{0,1},{1,0},{2,3},{3,2},{4,5},{5,4},{6,7},{7,6},{8,9},{9,8},{10,11... | collective-permute-start | bytes 393224 | tf_op jit(solution)/shard_map/ppermute | solution.py:360
  4.7 3.6 %collective-permute-start.1 = (bf16[256,256]{1,0:T(8,128)(2,1)S(1)}, bf16[256,256]{1,0:T(8,128)(2,1)S(1)}, u32[]{:S(2)}, u32[]{:S(2)}) collective-permute-start(bf16[256,256]{1,0:T(8,128)(2,1)S(1)} %get-tuple-element.37), channel_id=1, source_target_pairs={{0,31},{1,2},{2,1},{3,4},{4,3},{5,6},{6,5},{7,8},{8,7},{9,10},{10,... | collective-permute-start | bytes 393224 | tf_op jit(solution)/shard_map/ppermute | solution.py:365
  8.3 3.5 %inner_rows.1 = (bf16[1536,256]{1,0:T(8,128)(2,1)}, s32[36]{0:T(128)S(1)}, bf16[1024,256]{1,0:T(8,128)(2,1)S(1)}, f32[256,256]{1,0:T(8,128)S(1)}, f32[8,256]{1,0...) custom-call(s32[3,12]{1,0:T(4,128)} %bitcast.3, ...), custom_call_target="tpu_custom_call" | custom-call | flops 600000000 | bytes 3000000 | tf_op jit(solution)/shard_map/inner_rows/pallas_call | solution.py:441
  11.9 0.0 collective-permute-done.first_ref
  11.9 0.8 %collective-permute-done.1.second_ref = bf16[256,256]{1,0:T(8,128)(2,1)S(1)} collective-permute-done((bf16[256,256]{1,0:T(8,128)(2,1)S(1)}, bf16[256,256]{1,0:T(8,128)(2,1)S(1)}, u32[]{:S(2)}, u32[]{:S(2)}) %collective-permute-start.1) | collective-permute-done | bytes 131104 | tf_op jit(solution)/shard_map/ppermute | solution.py:365
  12.7 0.8 %rim_rows.1 = (bf16[512,256]{1,0:T(8,128)(2,1)S(1)}, bf16[512,256]{1,0:T(8,128)(2,1)S(1)}, bf16[136,256]{1,0:T(8,128)(2,1)S(1)}, f32[136,256]{1,0:T(8,128)S(1)}) custom-call(bf16[256,256]{1,0:T(8,128)(2,1)S(1)} %get-tuple-element.32.weight_ref, f32[1,256]{1,0:T(1,128)S(1)} %get-tuple-element.34.bias_ref, f32[512,256]{1,0:T(8,128)S(1)} %get-tuple-element.35.own_ref, ...), custom_call_target="tpu_custom_call" | custom-call | flops 240000000 | bytes 1200000 | tf_op jit(solution)/shard_map/rim_rows/pallas_call | solution.py:477
  13.5 0.1 collective-permute-start.2
  13.6 0.9 %rim_rows_back.1 = (bf16[1536,256]{1,0:T(8,128)(2,1)}, f32[8,256,128]{2,1,0:T(8,128)S(1)}, bf16[256,256]{1,0:T(8,128)(2,1)S(1)}, bf16[256,256]{1,0:T(8,128)(2,1)S(1)}, f32[8,128]{1,0:T(8,128)S(1)}) custom-call(bf16[256,256]{1,0:T(8,128)(2,1)S(1)} %get-tuple-element.32.weight_ref, ...), custom_call_target="tpu_custom_call", output_to_operand_aliasing={{0}: (4, {})} | custom-call | flops 240000000 | bytes 1200000 | tf_op jit(solution)/shard_map/rim_rows_back/pallas_call | solution.py:499
  14.5 0.4 %collective-permute-done.2.refs_1_ = bf16[136,256]{1,0:T(8,128)(2,1)S(1)} collective-permute-done((bf16[136,256]{1,0:T(8,128)(2,1)S(1)}, bf16[136,256]{1,0:T(8,128)(2,1)S(1)}, u32[]{:S(2)}, u32[]{:S(2)}) %collective-permute-start.2) | collective-permute-done | bytes 69664 | tf_op jit(solution)/shard_map/ppermute | solution.py:360
  14.9 0.1 collective-permute-start.5
  15.0 1.0 %collective-permute-start.4 = (bf16[136,256]{1,0:T(8,128)(2,1)S(1)}, bf16[136,256]{1,0:T(8,128)(2,1)S(1)}, u32[]{:S(2)}, u32[]{:S(2)}) collective-permute-start(bf16[136,256]{1,0:T(8,128)(2,1)S(1)} %add_halves.3.refs_0_), channel_id=1, source_target_pairs={{0,5},{1,4},{2,18},{3,19},{4,1},{5,0},{6,22},{7,23},{8,13},{9,12},... | collective-permute-start | bytes 208904 | tf_op jit(solution)/shard_map/ppermute | solution.py:360
  16.0 2.4 %collective-permute-start.3 = (bf16[136,256]{1,0:T(8,128)(2,1)S(1)}, bf16[136,256]{1,0:T(8,128)(2,1)S(1)}, u32[]{:S(2)}, u32[]{:S(2)}) collective-permute-start(bf16[136,256]{1,0:T(8,128)(2,1)S(1)} %add_halves.3.refs_0_), channel_id=1, source_target_pairs={{0,4},{1,5},{2,10},{3,11},{4,0},{5,1},{6,14},{7,15},{8,12},{9,13},... | collective-permute-start | bytes 208904 | tf_op jit(solution)/shard_map/ppermute | solution.py:360
  18.4 0.7 %collective-permute-start.9 = (bf16[256,256]{1,0:T(8,128)(2,1)S(1)}, bf16[256,256]{1,0:T(8,128)(2,1)S(1)}, u32[]{:S(2)}, u32[]{:S(2)}) collective-permute-start(bf16[256,256]{1,0:T(8,128)(2,1)S(1)} %get-tuple-element.53), channel_id=1, source_target_pairs={{1,2},{2,1},{3,4},{4,3},{5,6},{6,5},{7,8},{8,7},{9,10},{10,9},{11,... | collective-permute-start | bytes 393224 | tf_op jit(solution)/shard_map/ppermute | solution.py:365
  19.1 0.2 collective-permute-done.5.refs_3_
  19.2 1.0 %collective-permute-done.4.refs_2_ = bf16[136,256]{1,0:T(8,128)(2,1)S(1)} collective-permute-done((bf16[136,256]{1,0:T(8,128)(2,1)S(1)}, bf16[136,256]{1,0:T(8,128)(2,1)S(1)}, u32[]{:S(2)}, u32[]{:S(2)}) %collective-permute-start.4) | collective-permute-done | bytes 69664 | tf_op jit(solution)/shard_map/ppermute | solution.py:360
  20.2 1.2 %collective-permute-done.3.refs_1_ = bf16[136,256]{1,0:T(8,128)(2,1)S(1)} collective-permute-done((bf16[136,256]{1,0:T(8,128)(2,1)S(1)}, bf16[136,256]{1,0:T(8,128)(2,1)S(1)}, u32[]{:S(2)}, u32[]{:S(2)}) %collective-permute-start.3) | collective-permute-done | bytes 69664 | tf_op jit(solution)/shard_map/ppermute | solution.py:360
  21.5 2.9 %collective-permute-start.8 = (bf16[136,256]{1,0:T(8,128)(2,1)S(1)}, bf16[136,256]{1,0:T(8,128)(2,1)S(1)}, u32[]{:S(2)}, u32[]{:S(2)}) collective-permute-start(bf16[136,256]{1,0:T(8,128)(2,1)S(1)} %add_halves.4.refs_0_), channel_id=1, source_target_pairs={{0,24},{1,25},{2,3},{3,2},{4,28},{5,29},{6,7},{7,6},{8,16},{9,17},... | collective-permute-start | bytes 208904 | tf_op jit(solution)/shard_map/ppermute | solution.py:360
  24.4 0.0 collective-permute-start.7
  24.4 1.5 %collective-permute-start.6 = (bf16[136,256]{1,0:T(8,128)(2,1)S(1)}, bf16[136,256]{1,0:T(8,128)(2,1)S(1)}, u32[]{:S(2)}, u32[]{:S(2)}) collective-permute-start(bf16[136,256]{1,0:T(8,128)(2,1)S(1)} %add_halves.4.refs_0_), channel_id=1, source_target_pairs={{0,8},{1,9},{2,6},{3,7},{4,12},{5,13},{6,2},{7,3},{8,0},{9,1},{10,... | collective-permute-start | bytes 208904 | tf_op jit(solution)/shard_map/ppermute | solution.py:360
  25.9 0.8 %collective-permute-start.11 = (bf16[256,256]{1,0:T(8,128)(2,1)S(1)}, bf16[256,256]{1,0:T(8,128)(2,1)S(1)}, u32[]{:S(2)}, u32[]{:S(2)}) collective-permute-start(bf16[256,256]{1,0:T(8,128)(2,1)S(1)} %get-tuple-element.55), channel_id=1, source_target_pairs={{0,1},{1,0},{2,3},{3,2},{4,5},{5,4},{6,7},{7,6},{8,9},{9,8},{10,11... | collective-permute-start | bytes 393224 | tf_op jit(solution)/shard_map/ppermute | solution.py:360
  26.7 2.2 %inner_rows_back.1 = (bf16[1536,256]{1,0:T(8,128)(2,1)}, f32[512,256]{1,0:T(8,128)S(1)}, f32[8,128]{1,0:T(8,128)S(1)}) custom-call(s32[36]{0:T(128)S(1)} %get-tuple-element.48.place_in, bf16[256,256]{1,0:T(8,128)(2,1)S(1)} %get-tuple-element.32.weight_ref, bf16[8,3,128,128]{3,2,1,0:T(8,128)(2,1)S(1)} %get-tuple-element.49.adj_ref, ...), custom_call_target="tpu_custom_call" | custom-call | flops 360000000 | bytes 1800000 | tf_op jit(solution)/shard_map/inner_rows_back/pallas_call | solution.py:521
  29.0 0.0 collective-permute-done.9.refs_5_.second_ref
  29.0 0.0 collective-permute-done.8.refs_3_
  29.0 0.7 %collective-permute-done.7.refs_2_ = bf16[136,256]{1,0:T(8,128)(2,1)S(1)} collective-permute-done((bf16[136,256]{1,0:T(8,128)(2,1)S(1)}, bf16[136,256]{1,0:T(8,128)(2,1)S(1)}, u32[]{:S(2)}, u32[]{:S(2)}) %collective-permute-start.7) | collective-permute-done | bytes 69664 | tf_op jit(solution)/shard_map/ppermute | solution.py:360
  29.6 0.0 collective-permute-done.6.refs_1_
  29.7 0.1 collective-permute-start.10
  29.8 1.1 %collective-permute-done.11.first_ref = bf16[256,256]{1,0:T(8,128)(2,1)S(1)} collective-permute-done((bf16[256,256]{1,0:T(8,128)(2,1)S(1)}, bf16[256,256]{1,0:T(8,128)(2,1)S(1)}, u32[]{:S(2)}, u32[]{:S(2)}) %collective-permute-start.11) | collective-permute-done | bytes 131104 | tf_op jit(solution)/shard_map/ppermute | solution.py:360
  30.9 0.1 collective-permute-done.10.other_ref
  31.0 0.9 %last_step.1 = (f32[256,256]{1,0:T(8,128)}, f32[1,256]{1,0:T(1,128)}, bf16[1536,256]{1,0:T(8,128)(2,1)}) custom-call(bf16[136,256]{1,0:T(8,128)(2,1)S(1)} %add_halves.5.own_ref, bf16[136,256]{1,0:T(8,128)(2,1)S(1)} %collective-permute-done.10.other_ref, f32[512,256]{1,0:T(8,128)S(1)} %get-tuple-element.54.edge_ref, ...), custom_call_target="tpu_custom_call", output_to_operand_aliasing={{2}: (5, {})} | custom-call | tf_op jit(solution)/shard_map/last_step/pallas_call | solution.py:540
  (3 shorter events, 0.1 us)
Async XLA Ops:
  1.6 10.2 %collective-permute-start = (bf16[256,256]{1,0:T(8,128)(2,1)S(1)}, bf16[256,256]{1,0:T(8,128)(2,1)S(1)}, u32[]{:S(2)}, u32[]{:S(2)}) collective-permute-start(bf16[256,256]{1,0:T(8,128)(2,1)S(1)} %get-tuple-element.36), channel_id=1, source_target_pairs={{0,1},{1,0},{2,3},{3,2},{4,5},{5,4},{6,7},{7,6},{8,9},{9,8},{10,11... | collective-permute-start | bytes 393224 | tf_op jit(solution)/shard_map/ppermute | solution.py:360
  4.7 8.0 %collective-permute-start.1 = (bf16[256,256]{1,0:T(8,128)(2,1)S(1)}, bf16[256,256]{1,0:T(8,128)(2,1)S(1)}, u32[]{:S(2)}, u32[]{:S(2)}) collective-permute-start(bf16[256,256]{1,0:T(8,128)(2,1)S(1)} %get-tuple-element.37), channel_id=1, source_target_pairs={{0,31},{1,2},{2,1},{3,4},{4,3},{5,6},{6,5},{7,8},{8,7},{9,10},{10,... | collective-permute-start | bytes 393224 | tf_op jit(solution)/shard_map/ppermute | solution.py:365
  13.5 1.3 %collective-permute-start.2 = (bf16[136,256]{1,0:T(8,128)(2,1)S(1)}, bf16[136,256]{1,0:T(8,128)(2,1)S(1)}, u32[]{:S(2)}, u32[]{:S(2)}) collective-permute-start(bf16[136,256]{1,0:T(8,128)(2,1)S(1)} %get-tuple-element.46), channel_id=1, source_target_pairs={{0,2},{1,3},{2,0},{3,1},{4,6},{5,7},{6,4},{7,5},{8,10},{9,11},{10,... | collective-permute-start | bytes 208904 | tf_op jit(solution)/shard_map/ppermute | solution.py:360
  14.9 4.4 %collective-permute-start.5 = (bf16[136,256]{1,0:T(8,128)(2,1)S(1)}, bf16[136,256]{1,0:T(8,128)(2,1)S(1)}, u32[]{:S(2)}, u32[]{:S(2)}) collective-permute-start(bf16[136,256]{1,0:T(8,128)(2,1)S(1)} %add_halves.3.refs_0_), channel_id=1, source_target_pairs={{0,1},{1,0},{2,26},{3,27},{4,5},{5,4},{6,30},{7,31},{8,9},{9,8},{1... | collective-permute-start | bytes 208904 | tf_op jit(solution)/shard_map/ppermute | solution.py:360
  15.0 5.2 %collective-permute-start.4 = (bf16[136,256]{1,0:T(8,128)(2,1)S(1)}, bf16[136,256]{1,0:T(8,128)(2,1)S(1)}, u32[]{:S(2)}, u32[]{:S(2)}) collective-permute-start(bf16[136,256]{1,0:T(8,128)(2,1)S(1)} %add_halves.3.refs_0_), channel_id=1, source_target_pairs={{0,5},{1,4},{2,18},{3,19},{4,1},{5,0},{6,22},{7,23},{8,13},{9,12},... | collective-permute-start | bytes 208904 | tf_op jit(solution)/shard_map/ppermute | solution.py:360
  16.0 5.5 %collective-permute-start.3 = (bf16[136,256]{1,0:T(8,128)(2,1)S(1)}, bf16[136,256]{1,0:T(8,128)(2,1)S(1)}, u32[]{:S(2)}, u32[]{:S(2)}) collective-permute-start(bf16[136,256]{1,0:T(8,128)(2,1)S(1)} %add_halves.3.refs_0_), channel_id=1, source_target_pairs={{0,4},{1,5},{2,10},{3,11},{4,0},{5,1},{6,14},{7,15},{8,12},{9,13},... | collective-permute-start | bytes 208904 | tf_op jit(solution)/shard_map/ppermute | solution.py:360
  18.4 10.6 %collective-permute-start.9 = (bf16[256,256]{1,0:T(8,128)(2,1)S(1)}, bf16[256,256]{1,0:T(8,128)(2,1)S(1)}, u32[]{:S(2)}, u32[]{:S(2)}) collective-permute-start(bf16[256,256]{1,0:T(8,128)(2,1)S(1)} %get-tuple-element.53), channel_id=1, source_target_pairs={{1,2},{2,1},{3,4},{4,3},{5,6},{6,5},{7,8},{8,7},{9,10},{10,9},{11,... | collective-permute-start | bytes 393224 | tf_op jit(solution)/shard_map/ppermute | solution.py:365
  21.5 7.5 %collective-permute-start.8 = (bf16[136,256]{1,0:T(8,128)(2,1)S(1)}, bf16[136,256]{1,0:T(8,128)(2,1)S(1)}, u32[]{:S(2)}, u32[]{:S(2)}) collective-permute-start(bf16[136,256]{1,0:T(8,128)(2,1)S(1)} %add_halves.4.refs_0_), channel_id=1, source_target_pairs={{0,24},{1,25},{2,3},{3,2},{4,28},{5,29},{6,7},{7,6},{8,16},{9,17},... | collective-permute-start | bytes 208904 | tf_op jit(solution)/shard_map/ppermute | solution.py:360
  24.4 5.2 %collective-permute-start.7 = (bf16[136,256]{1,0:T(8,128)(2,1)S(1)}, bf16[136,256]{1,0:T(8,128)(2,1)S(1)}, u32[]{:S(2)}, u32[]{:S(2)}) collective-permute-start(bf16[136,256]{1,0:T(8,128)(2,1)S(1)} %add_halves.4.refs_0_), channel_id=1, source_target_pairs={{0,16},{1,17},{2,7},{3,6},{4,20},{5,21},{6,3},{7,2},{8,24},{9,25},... | collective-permute-start | bytes 208904 | tf_op jit(solution)/shard_map/ppermute | solution.py:360
  24.4 5.2 %collective-permute-start.6 = (bf16[136,256]{1,0:T(8,128)(2,1)S(1)}, bf16[136,256]{1,0:T(8,128)(2,1)S(1)}, u32[]{:S(2)}, u32[]{:S(2)}) collective-permute-start(bf16[136,256]{1,0:T(8,128)(2,1)S(1)} %add_halves.4.refs_0_), channel_id=1, source_target_pairs={{0,8},{1,9},{2,6},{3,7},{4,12},{5,13},{6,2},{7,3},{8,0},{9,1},{10,... | collective-permute-start | bytes 208904 | tf_op jit(solution)/shard_map/ppermute | solution.py:360
  25.9 5.0 %collective-permute-start.11 = (bf16[256,256]{1,0:T(8,128)(2,1)S(1)}, bf16[256,256]{1,0:T(8,128)(2,1)S(1)}, u32[]{:S(2)}, u32[]{:S(2)}) collective-permute-start(bf16[256,256]{1,0:T(8,128)(2,1)S(1)} %get-tuple-element.55), channel_id=1, source_target_pairs={{0,1},{1,0},{2,3},{3,2},{4,5},{5,4},{6,7},{7,6},{8,9},{9,8},{10,11... | collective-permute-start | bytes 393224 | tf_op jit(solution)/shard_map/ppermute | solution.py:360
  29.7 1.3 %collective-permute-start.10 = (bf16[136,256]{1,0:T(8,128)(2,1)S(1)}, bf16[136,256]{1,0:T(8,128)(2,1)S(1)}, u32[]{:S(2)}, u32[]{:S(2)}) collective-permute-start(bf16[136,256]{1,0:T(8,128)(2,1)S(1)} %add_halves.5.own_ref), channel_id=1, source_target_pairs={{0,2},{1,3},{2,0},{3,1},{4,6},{5,7},{6,4},{7,5},{8,10},{9,11},{10,... | collective-permute-start | bytes 208904 | tf_op jit(solution)/shard_map/ppermute | solution.py:360

commit v19 on v18

--- a/solution.py
+++ b/solution.py
@@ -181,7 +181,7 @@
 def rim_kernel(
     weight_ref, bias_ref, own_ref, first_ref, second_ref, dense, cot_ref, partial_ref, sums_ref,
     act_ref, grad_ref, send_ref, keep_ref,
-    halo, agg_all, payload,
+    halo, agg_all,
 ):
     rim, width = first_ref.shape
     odd = place_in_mesh() & 1
@@ -204,14 +204,12 @@
         sums = sums + column_sums(grad)
     half = width // 2
     partial = partial_ref[...] + weight_terms(agg_all[...], grad_ref[...])
-    payload[0, :half] = partial[:half]
-    payload[1, :half] = partial[half:]
-    tail = jnp.zeros((TAIL, width), jnp.float32)
-    payload[0, half:] = jnp.broadcast_to(jnp.sum(sums, axis=0, keepdims=True), tail.shape)
-    payload[1, half:] = tail
-    side = core_side()
-    keep_ref[...] = payload[side]
-    send_ref[...] = payload[1 - side].astype(send_ref.dtype)
+    bias_tail = jnp.broadcast_to(jnp.sum(sums, axis=0, keepdims=True), (TAIL, width))
+    upper = jnp.concatenate([partial[:half], bias_tail], 0)
+    lower = jnp.concatenate([partial[half:], jnp.zeros_like(bias_tail)], 0)
+    first = core_side() == 0
+    keep_ref[...] = jnp.where(first, upper, lower)
+    send_ref[...] = jnp.where(first, lower, upper).astype(send_ref.dtype)
 
 
 def scatter_rows(places, upstream, adj_ref, spread):
@@ -372,7 +370,7 @@
     total = add([keep, swap(send, [1 << core_bit] * count)], jnp.bfloat16, marks.get("core", ()))
     for step in range(len(groups)):
         masks = []
-        for group in (groups[step], groups[len(groups) - 1 - step]):
+        for group in (groups[len(groups) - 1 - step], groups[step]):
             if len(groups[0]) != len(groups[-1]):
                 group = groups[step]
             bits = [1 << bit for bit in group]
@@ -487,7 +485,6 @@
         scratch_shapes=[
             pltpu.VMEM((2 * rim, width), jnp.bfloat16),
             pltpu.VMEM((2 * rim, width), jnp.bfloat16),
-            pltpu.VMEM((2,) + half_shape, jnp.float32),
         ],
         compiler_params=params(12),
         cost_estimate=cost(0.2),

time: 32 us -> 32.4 us (1.012)
  starting transfers between devices: 16.3 us -> 16.7 us
    ppermute x10, starting transfers between devices: 12 us -> 12.4 us  [swap(): return lax.ppermute(value, AXES, pairs)]
  transfers between devices with their start and end apart: 12 -> 12, of which waited for: 8 -> 5; matrix products, arithmetic and copies ran while one was open for 0% -> 0% of each run, Pallas kernels for 21% -> 21%
where the time goes in v19:
time: 32.4 us; the launch traced here: 32.2 us
  starting transfers between devices  16.7 us (52%)
  Pallas kernels  9.4 us (29%)
  waiting for transfers between devices  5.3 us (16%)
  between operations  0.75 us (2%)
    ppermute x10, starting transfers between devices, swap(): return lax.ppermute(value, AXES, pairs)  12.4 us
    ppermute x10, waiting for transfers between devices, swap(): return lax.ppermute(value, AXES, pairs)  4.5 us
    ppermute x2, starting transfers between devices, with_next(): return lax.ppermute(value, AXES, pairs if closed else pairs[1:-1])  4.29 us
    pallas_call x1, Pallas kernels, on_device(): pl.pallas_call(inner_kernel, out_shape=(shape(rows, width), shape(blocks...  3.54 us
    pallas_call x1, Pallas kernels, on_device(): pl.pallas_call(inner_back_kernel, out_shape=(shape(rows, width), shape(2...  2.22 us
    pallas_call x1, Pallas kernels, on_device(): pl.pallas_call(halo_kernel, out_shape=(shape(rim, width), shape(rim, widt...  1 us
    pallas_call x1, Pallas kernels, on_device(): pl.pallas_call(rim_back_kernel, out_shape=(shape(rows, width), shape(4 *...  0.88 us
    pallas_call x1, Pallas kernels, on_device(): pl.pallas_call(functools.partial(last_kernel, norm_scale), out_shape=(sha...  0.85 us
  transfers between devices with their start and end apart: 12, of which 5 were waited for; matrix products, arithmetic and copies ran while one was open for 0% of the time, Pallas kernels for 21%

profile of v19, /device:TPU:0, one launch (start us, length us, event | category | flops | bytes accessed | tf_op | source)
XLA Modules:
  0.0 32.2 jit_solution(12322498092193890855)
XLA Ops:
  0.6 1.0 %halo_rows.1 = (bf16[256,256]{1,0:T(8,128)(2,1)S(1)}, bf16[256,256]{1,0:T(8,128)(2,1)S(1)}) custom-call(bf16[1536,256]{1,0:T(8,128)(2,1)} %feat_hbm.3), custom_call_target="tpu_custom_call" | custom-call | flops 60000000 | bytes 300000 | tf_op jit(solution)/shard_map/halo_rows/pallas_call | solution.py:424
  1.6 3.0 %collective-permute-start = (bf16[256,256]{1,0:T(8,128)(2,1)S(1)}, bf16[256,256]{1,0:T(8,128)(2,1)S(1)}, u32[]{:S(2)}, u32[]{:S(2)}) collective-permute-start(bf16[256,256]{1,0:T(8,128)(2,1)S(1)} %get-tuple-element.36), channel_id=1, source_target_pairs={{0,1},{1,0},{2,3},{3,2},{4,5},{5,4},{6,7},{7,6},{8,9},{9,8},{10,11... | collective-permute-start | bytes 393224 | tf_op jit(solution)/shard_map/ppermute | solution.py:358
  4.7 3.6 %collective-permute-start.1 = (bf16[256,256]{1,0:T(8,128)(2,1)S(1)}, bf16[256,256]{1,0:T(8,128)(2,1)S(1)}, u32[]{:S(2)}, u32[]{:S(2)}) collective-permute-start(bf16[256,256]{1,0:T(8,128)(2,1)S(1)} %get-tuple-element.37), channel_id=1, source_target_pairs={{0,31},{1,2},{2,1},{3,4},{4,3},{5,6},{6,5},{7,8},{8,7},{9,10},{10,... | collective-permute-start | bytes 393224 | tf_op jit(solution)/shard_map/ppermute | solution.py:363
  8.3 3.5 %inner_rows.1 = (bf16[1536,256]{1,0:T(8,128)(2,1)}, s32[36]{0:T(128)S(1)}, bf16[1024,256]{1,0:T(8,128)(2,1)S(1)}, f32[256,256]{1,0:T(8,128)S(1)}, f32[8,256]{1,0...) custom-call(s32[3,12]{1,0:T(4,128)} %bitcast.3, ...), custom_call_target="tpu_custom_call" | custom-call | flops 600000000 | bytes 3000000 | tf_op jit(solution)/shard_map/inner_rows/pallas_call | solution.py:439
  11.9 0.0 collective-permute-done.first_ref
  11.9 0.8 %collective-permute-done.1.second_ref = bf16[256,256]{1,0:T(8,128)(2,1)S(1)} collective-permute-done((bf16[256,256]{1,0:T(8,128)(2,1)S(1)}, bf16[256,256]{1,0:T(8,128)(2,1)S(1)}, u32[]{:S(2)}, u32[]{:S(2)}) %collective-permute-start.1) | collective-permute-done | bytes 131104 | tf_op jit(solution)/shard_map/ppermute | solution.py:363
  12.7 0.8 %rim_rows.1 = (bf16[512,256]{1,0:T(8,128)(2,1)S(1)}, bf16[512,256]{1,0:T(8,128)(2,1)S(1)}, bf16[136,256]{1,0:T(8,128)(2,1)S(1)}, f32[136,256]{1,0:T(8,128)S(1)}) custom-call(bf16[256,256]{1,0:T(8,128)(2,1)S(1)} %get-tuple-element.32.weight_ref, f32[1,256]{1,0:T(1,128)S(1)} %get-tuple-element.34.bias_ref, f32[512,256]{1,0:T(8,128)S(1)} %get-tuple-element.35.own_ref, ...), custom_call_target="tpu_custom_call" | custom-call | flops 240000000 | bytes 1200000 | tf_op jit(solution)/shard_map/rim_rows/pallas_call | solution.py:475
  13.5 0.1 collective-permute-start.2
  13.6 0.9 %rim_rows_back.1 = (bf16[1536,256]{1,0:T(8,128)(2,1)}, f32[8,256,128]{2,1,0:T(8,128)S(1)}, bf16[256,256]{1,0:T(8,128)(2,1)S(1)}, bf16[256,256]{1,0:T(8,128)(2,1)S(1)}, f32[8,128]{1,0:T(8,128)S(1)}) custom-call(bf16[256,256]{1,0:T(8,128)(2,1)S(1)} %get-tuple-element.32.weight_ref, ...), custom_call_target="tpu_custom_call", output_to_operand_aliasing={{0}: (4, {})} | custom-call | flops 240000000 | bytes 1200000 | tf_op jit(solution)/shard_map/rim_rows_back/pallas_call | solution.py:496
  14.4 0.4 %collective-permute-done.2.refs_1_ = bf16[136,256]{1,0:T(8,128)(2,1)S(1)} collective-permute-done((bf16[136,256]{1,0:T(8,128)(2,1)S(1)}, bf16[136,256]{1,0:T(8,128)(2,1)S(1)}, u32[]{:S(2)}, u32[]{:S(2)}) %collective-permute-start.2) | collective-permute-done | bytes 69664 | tf_op jit(solution)/shard_map/ppermute | solution.py:358
  14.8 2.0 %collective-permute-start.5 = (bf16[136,256]{1,0:T(8,128)(2,1)S(1)}, bf16[136,256]{1,0:T(8,128)(2,1)S(1)}, u32[]{:S(2)}, u32[]{:S(2)}) collective-permute-start(bf16[136,256]{1,0:T(8,128)(2,1)S(1)} %add_halves.3.refs_0_), channel_id=1, source_target_pairs={{0,24},{1,25},{2,3},{3,2},{4,28},{5,29},{6,7},{7,6},{8,16},{9,17},... | collective-permute-start | bytes 208904 | tf_op jit(solution)/shard_map/ppermute | solution.py:358
  16.8 0.0 collective-permute-start.4
  16.8 2.5 %collective-permute-start.3 = (bf16[136,256]{1,0:T(8,128)(2,1)S(1)}, bf16[136,256]{1,0:T(8,128)(2,1)S(1)}, u32[]{:S(2)}, u32[]{:S(2)}) collective-permute-start(bf16[136,256]{1,0:T(8,128)(2,1)S(1)} %add_halves.3.refs_0_), channel_id=1, source_target_pairs={{0,8},{1,9},{2,6},{3,7},{4,12},{5,13},{6,2},{7,3},{8,0},{9,1},{10,... | collective-permute-start | bytes 208904 | tf_op jit(solution)/shard_map/ppermute | solution.py:358
  19.3 0.7 %collective-permute-start.9 = (bf16[256,256]{1,0:T(8,128)(2,1)S(1)}, bf16[256,256]{1,0:T(8,128)(2,1)S(1)}, u32[]{:S(2)}, u32[]{:S(2)}) collective-permute-start(bf16[256,256]{1,0:T(8,128)(2,1)S(1)} %get-tuple-element.53), channel_id=1, source_target_pairs={{1,2},{2,1},{3,4},{4,3},{5,6},{6,5},{7,8},{8,7},{9,10},{10,9},{11,... | collective-permute-start | bytes 393224 | tf_op jit(solution)/shard_map/ppermute | solution.py:363
  19.9 1.1 %collective-permute-done.5.refs_3_ = bf16[136,256]{1,0:T(8,128)(2,1)S(1)} collective-permute-done((bf16[136,256]{1,0:T(8,128)(2,1)S(1)}, bf16[136,256]{1,0:T(8,128)(2,1)S(1)}, u32[]{:S(2)}, u32[]{:S(2)}) %collective-permute-start.5) | collective-permute-done | bytes 69664 | tf_op jit(solution)/shard_map/ppermute | solution.py:358
  21.0 1.5 %collective-permute-done.4.refs_2_ = bf16[136,256]{1,0:T(8,128)(2,1)S(1)} collective-permute-done((bf16[136,256]{1,0:T(8,128)(2,1)S(1)}, bf16[136,256]{1,0:T(8,128)(2,1)S(1)}, u32[]{:S(2)}, u32[]{:S(2)}) %collective-permute-start.4) | collective-permute-done | bytes 69664 | tf_op jit(solution)/shard_map/ppermute | solution.py:358
  22.5 0.0 collective-permute-done.3.refs_1_
  22.5 1.3 %collective-permute-start.8 = (bf16[136,256]{1,0:T(8,128)(2,1)S(1)}, bf16[136,256]{1,0:T(8,128)(2,1)S(1)}, u32[]{:S(2)}, u32[]{:S(2)}) collective-permute-start(bf16[136,256]{1,0:T(8,128)(2,1)S(1)} %add_halves.4.refs_0_), channel_id=1, source_target_pairs={{0,1},{1,0},{2,26},{3,27},{4,5},{5,4},{6,30},{7,31},{8,9},{9,8},{1... | collective-permute-start | bytes 208904 | tf_op jit(solution)/shard_map/ppermute | solution.py:358
  23.9 0.9 %collective-permute-start.7 = (bf16[136,256]{1,0:T(8,128)(2,1)S(1)}, bf16[136,256]{1,0:T(8,128)(2,1)S(1)}, u32[]{:S(2)}, u32[]{:S(2)}) collective-permute-start(bf16[136,256]{1,0:T(8,128)(2,1)S(1)} %add_halves.4.refs_0_), channel_id=1, source_target_pairs={{0,5},{1,4},{2,18},{3,19},{4,1},{5,0},{6,22},{7,23},{8,13},{9,12},... | collective-permute-start | bytes 208904 | tf_op jit(solution)/shard_map/ppermute | solution.py:358
  24.8 1.3 %collective-permute-start.6 = (bf16[136,256]{1,0:T(8,128)(2,1)S(1)}, bf16[136,256]{1,0:T(8,128)(2,1)S(1)}, u32[]{:S(2)}, u32[]{:S(2)}) collective-permute-start(bf16[136,256]{1,0:T(8,128)(2,1)S(1)} %add_halves.4.refs_0_), channel_id=1, source_target_pairs={{0,4},{1,5},{2,10},{3,11},{4,0},{5,1},{6,14},{7,15},{8,12},{9,13},... | collective-permute-start | bytes 208904 | tf_op jit(solution)/shard_map/ppermute | solution.py:358
  26.1 1.3 %collective-permute-start.11 = (bf16[256,256]{1,0:T(8,128)(2,1)S(1)}, bf16[256,256]{1,0:T(8,128)(2,1)S(1)}, u32[]{:S(2)}, u32[]{:S(2)}) collective-permute-start(bf16[256,256]{1,0:T(8,128)(2,1)S(1)} %get-tuple-element.55), channel_id=1, source_target_pairs={{0,1},{1,0},{2,3},{3,2},{4,5},{5,4},{6,7},{7,6},{8,9},{9,8},{10,11... | collective-permute-start | bytes 393224 | tf_op jit(solution)/shard_map/ppermute | solution.py:358
  27.4 2.2 %inner_rows_back.1 = (bf16[1536,256]{1,0:T(8,128)(2,1)}, f32[512,256]{1,0:T(8,128)S(1)}, f32[8,128]{1,0:T(8,128)S(1)}) custom-call(s32[36]{0:T(128)S(1)} %get-tuple-element.48.place_in, bf16[256,256]{1,0:T(8,128)(2,1)S(1)} %get-tuple-element.32.weight_ref, bf16[8,3,128,128]{3,2,1,0:T(8,128)(2,1)S(1)} %get-tuple-element.49.adj_ref, ...), custom_call_target="tpu_custom_call" | custom-call | flops 360000000 | bytes 1800000 | tf_op jit(solution)/shard_map/inner_rows_back/pallas_call | solution.py:518
  29.6 0.0 collective-permute-done.9.refs_5_.second_ref
  29.6 0.0 collective-permute-done.8.refs_3_
  29.6 0.0 collective-permute-done.7.refs_2_
  29.6 0.0 collective-permute-done.6.refs_1_
  29.7 0.1 collective-permute-start.10
  29.7 1.6 %collective-permute-done.11.first_ref = bf16[256,256]{1,0:T(8,128)(2,1)S(1)} collective-permute-done((bf16[256,256]{1,0:T(8,128)(2,1)S(1)}, bf16[256,256]{1,0:T(8,128)(2,1)S(1)}, u32[]{:S(2)}, u32[]{:S(2)}) %collective-permute-start.11) | collective-permute-done | bytes 131104 | tf_op jit(solution)/shard_map/ppermute | solution.py:358
  31.3 0.0 collective-permute-done.10.other_ref
  31.3 0.9 %last_step.1 = (f32[256,256]{1,0:T(8,128)}, f32[1,256]{1,0:T(1,128)}, bf16[1536,256]{1,0:T(8,128)(2,1)}) custom-call(bf16[136,256]{1,0:T(8,128)(2,1)S(1)} %add_halves.5.own_ref, bf16[136,256]{1,0:T(8,128)(2,1)S(1)} %collective-permute-done.10.other_ref, f32[512,256]{1,0:T(8,128)S(1)} %get-tuple-element.54.edge_ref, ...), custom_call_target="tpu_custom_call", output_to_operand_aliasing={{2}: (5, {})} | custom-call | tf_op jit(solution)/shard_map/last_step/pallas_call | solution.py:537
  (3 shorter events, 0.1 us)
Async XLA Ops:
  1.6 10.2 %collective-permute-start = (bf16[256,256]{1,0:T(8,128)(2,1)S(1)}, bf16[256,256]{1,0:T(8,128)(2,1)S(1)}, u32[]{:S(2)}, u32[]{:S(2)}) collective-permute-start(bf16[256,256]{1,0:T(8,128)(2,1)S(1)} %get-tuple-element.36), channel_id=1, source_target_pairs={{0,1},{1,0},{2,3},{3,2},{4,5},{5,4},{6,7},{7,6},{8,9},{9,8},{10,11... | collective-permute-start | bytes 393224 | tf_op jit(solution)/shard_map/ppermute | solution.py:358
  4.7 8.0 %collective-permute-start.1 = (bf16[256,256]{1,0:T(8,128)(2,1)S(1)}, bf16[256,256]{1,0:T(8,128)(2,1)S(1)}, u32[]{:S(2)}, u32[]{:S(2)}) collective-permute-start(bf16[256,256]{1,0:T(8,128)(2,1)S(1)} %get-tuple-element.37), channel_id=1, source_target_pairs={{0,31},{1,2},{2,1},{3,4},{4,3},{5,6},{6,5},{7,8},{8,7},{9,10},{10,... | collective-permute-start | bytes 393224 | tf_op jit(solution)/shard_map/ppermute | solution.py:363
  13.5 1.3 %collective-permute-start.2 = (bf16[136,256]{1,0:T(8,128)(2,1)S(1)}, bf16[136,256]{1,0:T(8,128)(2,1)S(1)}, u32[]{:S(2)}, u32[]{:S(2)}) collective-permute-start(bf16[136,256]{1,0:T(8,128)(2,1)S(1)} %get-tuple-element.46), channel_id=1, source_target_pairs={{0,2},{1,3},{2,0},{3,1},{4,6},{5,7},{6,4},{7,5},{8,10},{9,11},{10,... | collective-permute-start | bytes 208904 | tf_op jit(solution)/shard_map/ppermute | solution.py:358
  14.8 6.2 %collective-permute-start.5 = (bf16[136,256]{1,0:T(8,128)(2,1)S(1)}, bf16[136,256]{1,0:T(8,128)(2,1)S(1)}, u32[]{:S(2)}, u32[]{:S(2)}) collective-permute-start(bf16[136,256]{1,0:T(8,128)(2,1)S(1)} %add_halves.3.refs_0_), channel_id=1, source_target_pairs={{0,24},{1,25},{2,3},{3,2},{4,28},{5,29},{6,7},{7,6},{8,16},{9,17},... | collective-permute-start | bytes 208904 | tf_op jit(solution)/shard_map/ppermute | solution.py:358
  16.8 5.7 %collective-permute-start.4 = (bf16[136,256]{1,0:T(8,128)(2,1)S(1)}, bf16[136,256]{1,0:T(8,128)(2,1)S(1)}, u32[]{:S(2)}, u32[]{:S(2)}) collective-permute-start(bf16[136,256]{1,0:T(8,128)(2,1)S(1)} %add_halves.3.refs_0_), channel_id=1, source_target_pairs={{0,16},{1,17},{2,7},{3,6},{4,20},{5,21},{6,3},{7,2},{8,24},{9,25},... | collective-permute-start | bytes 208904 | tf_op jit(solution)/shard_map/ppermute | solution.py:358
  16.8 5.7 %collective-permute-start.3 = (bf16[136,256]{1,0:T(8,128)(2,1)S(1)}, bf16[136,256]{1,0:T(8,128)(2,1)S(1)}, u32[]{:S(2)}, u32[]{:S(2)}) collective-permute-start(bf16[136,256]{1,0:T(8,128)(2,1)S(1)} %add_halves.3.refs_0_), channel_id=1, source_target_pairs={{0,8},{1,9},{2,6},{3,7},{4,12},{5,13},{6,2},{7,3},{8,0},{9,1},{10,... | collective-permute-start | bytes 208904 | tf_op jit(solution)/shard_map/ppermute | solution.py:358
  19.3 10.3 %collective-permute-start.9 = (bf16[256,256]{1,0:T(8,128)(2,1)S(1)}, bf16[256,256]{1,0:T(8,128)(2,1)S(1)}, u32[]{:S(2)}, u32[]{:S(2)}) collective-permute-start(bf16[256,256]{1,0:T(8,128)(2,1)S(1)} %get-tuple-element.53), channel_id=1, source_target_pairs={{1,2},{2,1},{3,4},{4,3},{5,6},{6,5},{7,8},{8,7},{9,10},{10,9},{11,... | collective-permute-start | bytes 393224 | tf_op jit(solution)/shard_map/ppermute | solution.py:363
  22.5 7.1 %collective-permute-start.8 = (bf16[136,256]{1,0:T(8,128)(2,1)S(1)}, bf16[136,256]{1,0:T(8,128)(2,1)S(1)}, u32[]{:S(2)}, u32[]{:S(2)}) collective-permute-start(bf16[136,256]{1,0:T(8,128)(2,1)S(1)} %add_halves.4.refs_0_), channel_id=1, source_target_pairs={{0,1},{1,0},{2,26},{3,27},{4,5},{5,4},{6,30},{7,31},{8,9},{9,8},{1... | collective-permute-start | bytes 208904 | tf_op jit(solution)/shard_map/ppermute | solution.py:358
  23.9 5.7 %collective-permute-start.7 = (bf16[136,256]{1,0:T(8,128)(2,1)S(1)}, bf16[136,256]{1,0:T(8,128)(2,1)S(1)}, u32[]{:S(2)}, u32[]{:S(2)}) collective-permute-start(bf16[136,256]{1,0:T(8,128)(2,1)S(1)} %add_halves.4.refs_0_), channel_id=1, source_target_pairs={{0,5},{1,4},{2,18},{3,19},{4,1},{5,0},{6,22},{7,23},{8,13},{9,12},... | collective-permute-start | bytes 208904 | tf_op jit(solution)/shard_map/ppermute | solution.py:358
  24.8 4.9 %collective-permute-start.6 = (bf16[136,256]{1,0:T(8,128)(2,1)S(1)}, bf16[136,256]{1,0:T(8,128)(2,1)S(1)}, u32[]{:S(2)}, u32[]{:S(2)}) collective-permute-start(bf16[136,256]{1,0:T(8,128)(2,1)S(1)} %add_halves.4.refs_0_), channel_id=1, source_target_pairs={{0,4},{1,5},{2,10},{3,11},{4,0},{5,1},{6,14},{7,15},{8,12},{9,13},... | collective-permute-start | bytes 208904 | tf_op jit(solution)/shard_map/ppermute | solution.py:358
  26.1 5.2 %collective-permute-start.11 = (bf16[256,256]{1,0:T(8,128)(2,1)S(1)}, bf16[256,256]{1,0:T(8,128)(2,1)S(1)}, u32[]{:S(2)}, u32[]{:S(2)}) collective-permute-start(bf16[256,256]{1,0:T(8,128)(2,1)S(1)} %get-tuple-element.55), channel_id=1, source_target_pairs={{0,1},{1,0},{2,3},{3,2},{4,5},{5,4},{6,7},{7,6},{8,9},{9,8},{10,11... | collective-permute-start | bytes 393224 | tf_op jit(solution)/shard_map/ppermute | solution.py:358
  29.7 1.7 %collective-permute-start.10 = (bf16[136,256]{1,0:T(8,128)(2,1)S(1)}, bf16[136,256]{1,0:T(8,128)(2,1)S(1)}, u32[]{:S(2)}, u32[]{:S(2)}) collective-permute-start(bf16[136,256]{1,0:T(8,128)(2,1)S(1)} %add_halves.5.own_ref), channel_id=1, source_target_pairs={{0,2},{1,3},{2,0},{3,1},{4,6},{5,7},{6,4},{7,5},{8,10},{9,11},{10,... | collective-permute-start | bytes 208904 | tf_op jit(solution)/shard_map/ppermute | solution.py:358

commit v20 on v19

--- a/solution.py
+++ b/solution.py
@@ -370,7 +370,7 @@
     total = add([keep, swap(send, [1 << core_bit] * count)], jnp.bfloat16, marks.get("core", ()))
     for step in range(len(groups)):
         masks = []
-        for group in (groups[len(groups) - 1 - step], groups[step]):
+        for group in (groups[step], groups[len(groups) - 1 - step]):
             if len(groups[0]) != len(groups[-1]):
                 group = groups[step]
             bits = [1 << bit for bit in group]

time: 32.4 us -> 32 us (0.988)
  starting transfers between devices: 16.7 us -> 16.3 us
    ppermute x10, starting transfers between devices: 12.4 us -> 12 us  [swap(): return lax.ppermute(value, AXES, pairs)]
  transfers between devices with their start and end apart: 12 -> 12, of which waited for: 5 -> 8; matrix products, arithmetic and copies ran while one was open for 0% -> 0% of each run, Pallas kernels for 21% -> 21%
where the time goes in v20:
time: 32 us; the launch traced here: 31.8 us
  starting transfers between devices  16.3 us (51%)
  Pallas kernels  9.4 us (29%)
  waiting for transfers between devices  5.42 us (17%)
  between operations  0.73 us (2%)
    ppermute x10, starting transfers between devices, swap(): return lax.ppermute(value, AXES, pairs)  12 us
    ppermute x10, waiting for transfers between devices, swap(): return lax.ppermute(value, AXES, pairs)  4.63 us
    ppermute x2, starting transfers between devices, with_next(): return lax.ppermute(value, AXES, pairs if closed else pairs[1:-1])  4.29 us
    pallas_call x1, Pallas kernels, on_device(): pl.pallas_call(inner_kernel, out_shape=(shape(rows, width), shape(blocks...  3.54 us
    pallas_call x1, Pallas kernels, on_device(): pl.pallas_call(inner_back_kernel, out_shape=(shape(rows, width), shape(2...  2.22 us
    pallas_call x1, Pallas kernels, on_device(): pl.pallas_call(halo_kernel, out_shape=(shape(rim, width), shape(rim, widt...  1 us
    pallas_call x1, Pallas kernels, on_device(): pl.pallas_call(rim_back_kernel, out_shape=(shape(rows, width), shape(4 *...  0.88 us
    pallas_call x1, Pallas kernels, on_device(): pl.pallas_call(functools.partial(last_kernel, norm_scale), out_shape=(sha...  0.85 us
  transfers between devices with their start and end apart: 12, of which 8 were waited for; matrix products, arithmetic and copies ran while one was open for 0% of the time, Pallas kernels for 21%

profile of v20, /device:TPU:0, one launch (start us, length us, event | category | flops | bytes accessed | tf_op | source)
XLA Modules:
  0.0 31.8 jit_solution(3672206518989037587)
XLA Ops:
  0.6 1.0 %halo_rows.1 = (bf16[256,256]{1,0:T(8,128)(2,1)S(1)}, bf16[256,256]{1,0:T(8,128)(2,1)S(1)}) custom-call(bf16[1536,256]{1,0:T(8,128)(2,1)} %feat_hbm.3), custom_call_target="tpu_custom_call" | custom-call | flops 60000000 | bytes 300000 | tf_op jit(solution)/shard_map/halo_rows/pallas_call | solution.py:424
  1.6 3.0 %collective-permute-start = (bf16[256,256]{1,0:T(8,128)(2,1)S(1)}, bf16[256,256]{1,0:T(8,128)(2,1)S(1)}, u32[]{:S(2)}, u32[]{:S(2)}) collective-permute-start(bf16[256,256]{1,0:T(8,128)(2,1)S(1)} %get-tuple-element.36), channel_id=1, source_target_pairs={{0,1},{1,0},{2,3},{3,2},{4,5},{5,4},{6,7},{7,6},{8,9},{9,8},{10,11... | collective-permute-start | bytes 393224 | tf_op jit(solution)/shard_map/ppermute | solution.py:358
  4.7 3.6 %collective-permute-start.1 = (bf16[256,256]{1,0:T(8,128)(2,1)S(1)}, bf16[256,256]{1,0:T(8,128)(2,1)S(1)}, u32[]{:S(2)}, u32[]{:S(2)}) collective-permute-start(bf16[256,256]{1,0:T(8,128)(2,1)S(1)} %get-tuple-element.37), channel_id=1, source_target_pairs={{0,31},{1,2},{2,1},{3,4},{4,3},{5,6},{6,5},{7,8},{8,7},{9,10},{10,... | collective-permute-start | bytes 393224 | tf_op jit(solution)/shard_map/ppermute | solution.py:363
  8.3 3.5 %inner_rows.1 = (bf16[1536,256]{1,0:T(8,128)(2,1)}, s32[36]{0:T(128)S(1)}, bf16[1024,256]{1,0:T(8,128)(2,1)S(1)}, f32[256,256]{1,0:T(8,128)S(1)}, f32[8,256]{1,0...) custom-call(s32[3,12]{1,0:T(4,128)} %bitcast.3, ...), custom_call_target="tpu_custom_call" | custom-call | flops 600000000 | bytes 3000000 | tf_op jit(solution)/shard_map/inner_rows/pallas_call | solution.py:439
  11.9 0.0 collective-permute-done.first_ref
  11.9 0.8 %collective-permute-done.1.second_ref = bf16[256,256]{1,0:T(8,128)(2,1)S(1)} collective-permute-done((bf16[256,256]{1,0:T(8,128)(2,1)S(1)}, bf16[256,256]{1,0:T(8,128)(2,1)S(1)}, u32[]{:S(2)}, u32[]{:S(2)}) %collective-permute-start.1) | collective-permute-done | bytes 131104 | tf_op jit(solution)/shard_map/ppermute | solution.py:363
  12.7 0.8 %rim_rows.1 = (bf16[512,256]{1,0:T(8,128)(2,1)S(1)}, bf16[512,256]{1,0:T(8,128)(2,1)S(1)}, bf16[136,256]{1,0:T(8,128)(2,1)S(1)}, f32[136,256]{1,0:T(8,128)S(1)}) custom-call(bf16[256,256]{1,0:T(8,128)(2,1)S(1)} %get-tuple-element.32.weight_ref, f32[1,256]{1,0:T(1,128)S(1)} %get-tuple-element.34.bias_ref, f32[512,256]{1,0:T(8,128)S(1)} %get-tuple-element.35.own_ref, ...), custom_call_target="tpu_custom_call" | custom-call | flops 240000000 | bytes 1200000 | tf_op jit(solution)/shard_map/rim_rows/pallas_call | solution.py:475
  13.5 0.1 collective-permute-start.2
  13.6 0.9 %rim_rows_back.1 = (bf16[1536,256]{1,0:T(8,128)(2,1)}, f32[8,256,128]{2,1,0:T(8,128)S(1)}, bf16[256,256]{1,0:T(8,128)(2,1)S(1)}, bf16[256,256]{1,0:T(8,128)(2,1)S(1)}, f32[8,128]{1,0:T(8,128)S(1)}) custom-call(bf16[256,256]{1,0:T(8,128)(2,1)S(1)} %get-tuple-element.32.weight_ref, ...), custom_call_target="tpu_custom_call", output_to_operand_aliasing={{0}: (4, {})} | custom-call | flops 240000000 | bytes 1200000 | tf_op jit(solution)/shard_map/rim_rows_back/pallas_call | solution.py:496
  14.4 0.4 %collective-permute-done.2.refs_1_ = bf16[136,256]{1,0:T(8,128)(2,1)S(1)} collective-permute-done((bf16[136,256]{1,0:T(8,128)(2,1)S(1)}, bf16[136,256]{1,0:T(8,128)(2,1)S(1)}, u32[]{:S(2)}, u32[]{:S(2)}) %collective-permute-start.2) | collective-permute-done | bytes 69664 | tf_op jit(solution)/shard_map/ppermute | solution.py:358
  14.8 0.1 collective-permute-start.5
  14.9 1.0 %collective-permute-start.4 = (bf16[136,256]{1,0:T(8,128)(2,1)S(1)}, bf16[136,256]{1,0:T(8,128)(2,1)S(1)}, u32[]{:S(2)}, u32[]{:S(2)}) collective-permute-start(bf16[136,256]{1,0:T(8,128)(2,1)S(1)} %add_halves.3.refs_0_), channel_id=1, source_target_pairs={{0,5},{1,4},{2,18},{3,19},{4,1},{5,0},{6,22},{7,23},{8,13},{9,12},... | collective-permute-start | bytes 208904 | tf_op jit(solution)/shard_map/ppermute | solution.py:358
  15.9 2.4 %collective-permute-start.3 = (bf16[136,256]{1,0:T(8,128)(2,1)S(1)}, bf16[136,256]{1,0:T(8,128)(2,1)S(1)}, u32[]{:S(2)}, u32[]{:S(2)}) collective-permute-start(bf16[136,256]{1,0:T(8,128)(2,1)S(1)} %add_halves.3.refs_0_), channel_id=1, source_target_pairs={{0,4},{1,5},{2,10},{3,11},{4,0},{5,1},{6,14},{7,15},{8,12},{9,13},... | collective-permute-start | bytes 208904 | tf_op jit(solution)/shard_map/ppermute | solution.py:358
  18.4 0.7 %collective-permute-start.9 = (bf16[256,256]{1,0:T(8,128)(2,1)S(1)}, bf16[256,256]{1,0:T(8,128)(2,1)S(1)}, u32[]{:S(2)}, u32[]{:S(2)}) collective-permute-start(bf16[256,256]{1,0:T(8,128)(2,1)S(1)} %get-tuple-element.53), channel_id=1, source_target_pairs={{1,2},{2,1},{3,4},{4,3},{5,6},{6,5},{7,8},{8,7},{9,10},{10,9},{11,... | collective-permute-start | bytes 393224 | tf_op jit(solution)/shard_map/ppermute | solution.py:363
  19.0 0.2 collective-permute-done.5.refs_3_
  19.2 1.0 %collective-permute-done.4.refs_2_ = bf16[136,256]{1,0:T(8,128)(2,1)S(1)} collective-permute-done((bf16[136,256]{1,0:T(8,128)(2,1)S(1)}, bf16[136,256]{1,0:T(8,128)(2,1)S(1)}, u32[]{:S(2)}, u32[]{:S(2)}) %collective-permute-start.4) | collective-permute-done | bytes 69664 | tf_op jit(solution)/shard_map/ppermute | solution.py:358
  20.2 1.2 %collective-permute-done.3.refs_1_ = bf16[136,256]{1,0:T(8,128)(2,1)S(1)} collective-permute-done((bf16[136,256]{1,0:T(8,128)(2,1)S(1)}, bf16[136,256]{1,0:T(8,128)(2,1)S(1)}, u32[]{:S(2)}, u32[]{:S(2)}) %collective-permute-start.3) | collective-permute-done | bytes 69664 | tf_op jit(solution)/shard_map/ppermute | solution.py:358
  21.4 2.9 %collective-permute-start.8 = (bf16[136,256]{1,0:T(8,128)(2,1)S(1)}, bf16[136,256]{1,0:T(8,128)(2,1)S(1)}, u32[]{:S(2)}, u32[]{:S(2)}) collective-permute-start(bf16[136,256]{1,0:T(8,128)(2,1)S(1)} %add_halves.4.refs_0_), channel_id=1, source_target_pairs={{0,24},{1,25},{2,3},{3,2},{4,28},{5,29},{6,7},{7,6},{8,16},{9,17},... | collective-permute-start | bytes 208904 | tf_op jit(solution)/shard_map/ppermute | solution.py:358
  24.4 0.0 collective-permute-start.7
  24.4 1.5 %collective-permute-start.6 = (bf16[136,256]{1,0:T(8,128)(2,1)S(1)}, bf16[136,256]{1,0:T(8,128)(2,1)S(1)}, u32[]{:S(2)}, u32[]{:S(2)}) collective-permute-start(bf16[136,256]{1,0:T(8,128)(2,1)S(1)} %add_halves.4.refs_0_), channel_id=1, source_target_pairs={{0,8},{1,9},{2,6},{3,7},{4,12},{5,13},{6,2},{7,3},{8,0},{9,1},{10,... | collective-permute-start | bytes 208904 | tf_op jit(solution)/shard_map/ppermute | solution.py:358
  25.9 0.8 %collective-permute-start.11 = (bf16[256,256]{1,0:T(8,128)(2,1)S(1)}, bf16[256,256]{1,0:T(8,128)(2,1)S(1)}, u32[]{:S(2)}, u32[]{:S(2)}) collective-permute-start(bf16[256,256]{1,0:T(8,128)(2,1)S(1)} %get-tuple-element.55), channel_id=1, source_target_pairs={{0,1},{1,0},{2,3},{3,2},{4,5},{5,4},{6,7},{7,6},{8,9},{9,8},{10,11... | collective-permute-start | bytes 393224 | tf_op jit(solution)/shard_map/ppermute | solution.py:358
  26.7 2.2 %inner_rows_back.1 = (bf16[1536,256]{1,0:T(8,128)(2,1)}, f32[512,256]{1,0:T(8,128)S(1)}, f32[8,128]{1,0:T(8,128)S(1)}) custom-call(s32[36]{0:T(128)S(1)} %get-tuple-element.48.place_in, bf16[256,256]{1,0:T(8,128)(2,1)S(1)} %get-tuple-element.32.weight_ref, bf16[8,3,128,128]{3,2,1,0:T(8,128)(2,1)S(1)} %get-tuple-element.49.adj_ref, ...), custom_call_target="tpu_custom_call" | custom-call | flops 360000000 | bytes 1800000 | tf_op jit(solution)/shard_map/inner_rows_back/pallas_call | solution.py:518
  28.9 0.0 collective-permute-done.9.refs_5_.second_ref
  28.9 0.0 collective-permute-done.8.refs_3_
  29.0 0.6 %collective-permute-done.7.refs_2_ = bf16[136,256]{1,0:T(8,128)(2,1)S(1)} collective-permute-done((bf16[136,256]{1,0:T(8,128)(2,1)S(1)}, bf16[136,256]{1,0:T(8,128)(2,1)S(1)}, u32[]{:S(2)}, u32[]{:S(2)}) %collective-permute-start.7) | collective-permute-done | bytes 69664 | tf_op jit(solution)/shard_map/ppermute | solution.py:358
  29.6 0.0 collective-permute-done.6.refs_1_
  29.6 0.1 collective-permute-start.10
  29.7 1.1 %collective-permute-done.11.first_ref = bf16[256,256]{1,0:T(8,128)(2,1)S(1)} collective-permute-done((bf16[256,256]{1,0:T(8,128)(2,1)S(1)}, bf16[256,256]{1,0:T(8,128)(2,1)S(1)}, u32[]{:S(2)}, u32[]{:S(2)}) %collective-permute-start.11) | collective-permute-done | bytes 131104 | tf_op jit(solution)/shard_map/ppermute | solution.py:358
  30.9 0.1 collective-permute-done.10.other_ref
  31.0 0.9 %last_step.1 = (f32[256,256]{1,0:T(8,128)}, f32[1,256]{1,0:T(1,128)}, bf16[1536,256]{1,0:T(8,128)(2,1)}) custom-call(bf16[136,256]{1,0:T(8,128)(2,1)S(1)} %add_halves.5.own_ref, bf16[136,256]{1,0:T(8,128)(2,1)S(1)} %collective-permute-done.10.other_ref, f32[512,256]{1,0:T(8,128)S(1)} %get-tuple-element.54.edge_ref, ...), custom_call_target="tpu_custom_call", output_to_operand_aliasing={{2}: (5, {})} | custom-call | tf_op jit(solution)/shard_map/last_step/pallas_call | solution.py:537
  (3 shorter events, 0.1 us)
Async XLA Ops:
  1.6 10.2 %collective-permute-start = (bf16[256,256]{1,0:T(8,128)(2,1)S(1)}, bf16[256,256]{1,0:T(8,128)(2,1)S(1)}, u32[]{:S(2)}, u32[]{:S(2)}) collective-permute-start(bf16[256,256]{1,0:T(8,128)(2,1)S(1)} %get-tuple-element.36), channel_id=1, source_target_pairs={{0,1},{1,0},{2,3},{3,2},{4,5},{5,4},{6,7},{7,6},{8,9},{9,8},{10,11... | collective-permute-start | bytes 393224 | tf_op jit(solution)/shard_map/ppermute | solution.py:358
  4.7 8.0 %collective-permute-start.1 = (bf16[256,256]{1,0:T(8,128)(2,1)S(1)}, bf16[256,256]{1,0:T(8,128)(2,1)S(1)}, u32[]{:S(2)}, u32[]{:S(2)}) collective-permute-start(bf16[256,256]{1,0:T(8,128)(2,1)S(1)} %get-tuple-element.37), channel_id=1, source_target_pairs={{0,31},{1,2},{2,1},{3,4},{4,3},{5,6},{6,5},{7,8},{8,7},{9,10},{10,... | collective-permute-start | bytes 393224 | tf_op jit(solution)/shard_map/ppermute | solution.py:363
  13.5 1.3 %collective-permute-start.2 = (bf16[136,256]{1,0:T(8,128)(2,1)S(1)}, bf16[136,256]{1,0:T(8,128)(2,1)S(1)}, u32[]{:S(2)}, u32[]{:S(2)}) collective-permute-start(bf16[136,256]{1,0:T(8,128)(2,1)S(1)} %get-tuple-element.46), channel_id=1, source_target_pairs={{0,2},{1,3},{2,0},{3,1},{4,6},{5,7},{6,4},{7,5},{8,10},{9,11},{10,... | collective-permute-start | bytes 208904 | tf_op jit(solution)/shard_map/ppermute | solution.py:358
  14.8 4.4 %collective-permute-start.5 = (bf16[136,256]{1,0:T(8,128)(2,1)S(1)}, bf16[136,256]{1,0:T(8,128)(2,1)S(1)}, u32[]{:S(2)}, u32[]{:S(2)}) collective-permute-start(bf16[136,256]{1,0:T(8,128)(2,1)S(1)} %add_halves.3.refs_0_), channel_id=1, source_target_pairs={{0,1},{1,0},{2,26},{3,27},{4,5},{5,4},{6,30},{7,31},{8,9},{9,8},{1... | collective-permute-start | bytes 208904 | tf_op jit(solution)/shard_map/ppermute | solution.py:358
  14.9 5.2 %collective-permute-start.4 = (bf16[136,256]{1,0:T(8,128)(2,1)S(1)}, bf16[136,256]{1,0:T(8,128)(2,1)S(1)}, u32[]{:S(2)}, u32[]{:S(2)}) collective-permute-start(bf16[136,256]{1,0:T(8,128)(2,1)S(1)} %add_halves.3.refs_0_), channel_id=1, source_target_pairs={{0,5},{1,4},{2,18},{3,19},{4,1},{5,0},{6,22},{7,23},{8,13},{9,12},... | collective-permute-start | bytes 208904 | tf_op jit(solution)/shard_map/ppermute | solution.py:358
  15.9 5.5 %collective-permute-start.3 = (bf16[136,256]{1,0:T(8,128)(2,1)S(1)}, bf16[136,256]{1,0:T(8,128)(2,1)S(1)}, u32[]{:S(2)}, u32[]{:S(2)}) collective-permute-start(bf16[136,256]{1,0:T(8,128)(2,1)S(1)} %add_halves.3.refs_0_), channel_id=1, source_target_pairs={{0,4},{1,5},{2,10},{3,11},{4,0},{5,1},{6,14},{7,15},{8,12},{9,13},... | collective-permute-start | bytes 208904 | tf_op jit(solution)/shard_map/ppermute | solution.py:358
  18.4 10.6 %collective-permute-start.9 = (bf16[256,256]{1,0:T(8,128)(2,1)S(1)}, bf16[256,256]{1,0:T(8,128)(2,1)S(1)}, u32[]{:S(2)}, u32[]{:S(2)}) collective-permute-start(bf16[256,256]{1,0:T(8,128)(2,1)S(1)} %get-tuple-element.53), channel_id=1, source_target_pairs={{1,2},{2,1},{3,4},{4,3},{5,6},{6,5},{7,8},{8,7},{9,10},{10,9},{11,... | collective-permute-start | bytes 393224 | tf_op jit(solution)/shard_map/ppermute | solution.py:363
  21.4 7.5 %collective-permute-start.8 = (bf16[136,256]{1,0:T(8,128)(2,1)S(1)}, bf16[136,256]{1,0:T(8,128)(2,1)S(1)}, u32[]{:S(2)}, u32[]{:S(2)}) collective-permute-start(bf16[136,256]{1,0:T(8,128)(2,1)S(1)} %add_halves.4.refs_0_), channel_id=1, source_target_pairs={{0,24},{1,25},{2,3},{3,2},{4,28},{5,29},{6,7},{7,6},{8,16},{9,17},... | collective-permute-start | bytes 208904 | tf_op jit(solution)/shard_map/ppermute | solution.py:358
  24.4 5.2 %collective-permute-start.7 = (bf16[136,256]{1,0:T(8,128)(2,1)S(1)}, bf16[136,256]{1,0:T(8,128)(2,1)S(1)}, u32[]{:S(2)}, u32[]{:S(2)}) collective-permute-start(bf16[136,256]{1,0:T(8,128)(2,1)S(1)} %add_halves.4.refs_0_), channel_id=1, source_target_pairs={{0,16},{1,17},{2,7},{3,6},{4,20},{5,21},{6,3},{7,2},{8,24},{9,25},... | collective-permute-start | bytes 208904 | tf_op jit(solution)/shard_map/ppermute | solution.py:358
  24.4 5.2 %collective-permute-start.6 = (bf16[136,256]{1,0:T(8,128)(2,1)S(1)}, bf16[136,256]{1,0:T(8,128)(2,1)S(1)}, u32[]{:S(2)}, u32[]{:S(2)}) collective-permute-start(bf16[136,256]{1,0:T(8,128)(2,1)S(1)} %add_halves.4.refs_0_), channel_id=1, source_target_pairs={{0,8},{1,9},{2,6},{3,7},{4,12},{5,13},{6,2},{7,3},{8,0},{9,1},{10,... | collective-permute-start | bytes 208904 | tf_op jit(solution)/shard_map/ppermute | solution.py:358
  25.9 5.0 %collective-permute-start.11 = (bf16[256,256]{1,0:T(8,128)(2,1)S(1)}, bf16[256,256]{1,0:T(8,128)(2,1)S(1)}, u32[]{:S(2)}, u32[]{:S(2)}) collective-permute-start(bf16[256,256]{1,0:T(8,128)(2,1)S(1)} %get-tuple-element.55), channel_id=1, source_target_pairs={{0,1},{1,0},{2,3},{3,2},{4,5},{5,4},{6,7},{7,6},{8,9},{9,8},{10,11... | collective-permute-start | bytes 393224 | tf_op jit(solution)/shard_map/ppermute | solution.py:358
  29.6 1.3 %collective-permute-start.10 = (bf16[136,256]{1,0:T(8,128)(2,1)S(1)}, bf16[136,256]{1,0:T(8,128)(2,1)S(1)}, u32[]{:S(2)}, u32[]{:S(2)}) collective-permute-start(bf16[136,256]{1,0:T(8,128)(2,1)S(1)} %add_halves.5.own_ref), channel_id=1, source_target_pairs={{0,2},{1,3},{2,0},{3,1},{4,6},{5,7},{6,4},{7,5},{8,10},{9,11},{10,... | collective-permute-start | bytes 208904 | tf_op jit(solution)/shard_map/ppermute | solution.py:358

commit v21 on v20

--- a/solution.py
+++ b/solution.py
@@ -178,32 +178,34 @@
     place_copy.wait()
 
 
+def rim_side(order):
+    odd = place_in_mesh() & 1
+    return odd if order else 1 - odd
+
+
 def rim_kernel(
-    weight_ref, bias_ref, own_ref, first_ref, second_ref, dense, cot_ref, partial_ref, sums_ref,
-    act_ref, grad_ref, send_ref, keep_ref,
-    halo, agg_all,
+    order, weight_ref, bias_ref, own_ref, halo_ref, dense, cot_ref, partial_ref, sums_ref,
+    act_ref, grad_ref, *outs,
 ):
-    rim, width = first_ref.shape
-    odd = place_in_mesh() & 1
-    halo[pl.ds(pl.multiple_of((1 - odd) * rim, rim), rim)] = first_ref[...]
-    halo[pl.ds(pl.multiple_of(odd * rim, rim), rim)] = second_ref[...]
-    weight = weight_ref[...]
-    bias = bias_ref[...]
-    sums = sums_ref[...]
-    for side, first in enumerate((0, 2 * BAND)):
-        here = pl.ds(side * rim, rim)
-        agg = own_ref[here] + jnp.dot(
-            side_by_side(dense, side, first, first + BAND), halo[here],
-            preferred_element_type=jnp.float32,
-        )
-        agg = agg.astype(jnp.bfloat16)
-        agg_all[here] = agg
-        preact = jnp.dot(agg, weight, preferred_element_type=jnp.float32) + bias
-        act_ref[here], grad = activate(preact, cot_ref[here])
-        grad_ref[here] = grad
-        sums = sums + column_sums(grad)
-    half = width // 2
-    partial = partial_ref[...] + weight_terms(agg_all[...], grad_ref[...])
+    rim = halo_ref.shape[0]
+    side = rim_side(order)
+    here = pl.ds(pl.multiple_of(side * rim, rim), rim)
+    beyond = side * 2 * BAND
+    row = jnp.concatenate([dense[side, beyond + block] for block in range(BAND)], 1)
+    agg = own_ref[here] + jnp.dot(row, halo_ref[...], preferred_element_type=jnp.float32)
+    agg = agg.astype(jnp.bfloat16)
+    preact = jnp.dot(agg, weight_ref[...], preferred_element_type=jnp.float32) + bias_ref[...]
+    act_ref[...], grad = activate(preact, cot_ref[here])
+    grad_ref[...] = grad
+    sums = sums_ref[...] + column_sums(grad)
+    partial = partial_ref[...] + weight_terms(agg, grad)
+    if order == 0:
+        partial_out, sums_out = outs
+        partial_out[...] = partial
+        sums_out[...] = sums
+        return
+    send_ref, keep_ref = outs
+    half, width = partial.shape[0] // 2, partial.shape[1]
     bias_tail = jnp.broadcast_to(jnp.sum(sums, axis=0, keepdims=True), (TAIL, width))
     upper = jnp.concatenate([partial[:half], bias_tail], 0)
     lower = jnp.concatenate([partial[half:], jnp.zeros_like(bias_tail)], 0)
@@ -225,21 +227,25 @@
 
 
 def rim_back_kernel(
-    weight_ref, dense, grad_ref, act_ref, act_in,
+    weight_ref, dense, grad_first, grad_second, act_first, act_second, act_in,
     act_hbm, spread, first_ref, second_ref, mark_ref,
-    spill, sems,
+    grad_ref, spill, sems,
 ):
     block_rows = dense.shape[3]
     rim = BAND * block_rows
     rows = act_hbm.shape[0]
     copies = [
-        pltpu.make_async_copy(act_ref.at[pl.ds(0, rim)], act_hbm.at[pl.ds(0, rim)], sems.at[0]),
         pltpu.make_async_copy(
-            act_ref.at[pl.ds(rim, rim)], act_hbm.at[pl.ds(rows - rim, rim)], sems.at[1]
-        ),
+            act_ref,
+            act_hbm.at[pl.ds(pl.multiple_of(rim_side(order) * (rows - rim), rim), rim)],
+            sems.at[order],
+        )
+        for order, act_ref in enumerate((act_first, act_second))
     ]
     for copy in copies:
         copy.start()
+    for order, grad in enumerate((grad_first, grad_second)):
+        grad_ref[pl.ds(pl.multiple_of(rim_side(order) * rim, rim), rim)] = grad[...]
     weight = weight_ref[...]
     for side, (inside, outside) in enumerate(((BAND, 0), (0, 2 * BAND))):
         terms = jnp.dot(
@@ -472,25 +478,24 @@
         *(in_hbm(x) for x in (weight, bias_row, features, adj_values, cotangent)),
     )
     half_shape = (width // 2 + TAIL, width)
-    act_rim, grad_rim, send, keep = pl.pallas_call(
-        rim_kernel,
-        out_shape=(
-            shape(2 * rim, width),
-            shape(2 * rim, width),
-            shape(*half_shape),
-            shape(*half_shape, dtype=jnp.float32),
-        ),
-        in_specs=[vmem] * 9,
-        out_specs=(vmem,) * 4,
-        scratch_shapes=[
-            pltpu.VMEM((2 * rim, width), jnp.bfloat16),
-            pltpu.VMEM((2 * rim, width), jnp.bfloat16),
-        ],
-        compiler_params=params(12),
-        cost_estimate=cost(0.2),
-        name="rim_rows",
-    )(
-        weight_near, bias_near, own_part, first_halo, second_halo, dense, cot_rim, partial, sums,
+    def rim_rows(order, halo, partial, sums, *outs):
+        return pl.pallas_call(
+            functools.partial(rim_kernel, order),
+            out_shape=(shape(rim, width), shape(rim, width)) + outs,
+            in_specs=[vmem] * 8,
+            out_specs=(vmem,) * 4,
+            compiler_params=params(12),
+            cost_estimate=cost(0.1),
+            name="rim_rows",
+        )(weight_near, bias_near, own_part, halo, dense, cot_rim, partial, sums)
+
+    act_first, grad_first, partial, sums = rim_rows(
+        0, first_halo, partial, sums,
+        shape(width, width, dtype=jnp.float32), shape(8, width, dtype=jnp.float32),
+    )
+    act_second, grad_second, send, keep = rim_rows(
+        1, second_halo, partial, sums,
+        shape(*half_shape), shape(*half_shape, dtype=jnp.float32),
     )
     mark = shape(8, 128, dtype=jnp.float32)
     activated, rim_spread, first_spill, second_spill, first_mark = pl.pallas_call(
@@ -502,17 +507,20 @@
             shape(rim, width),
             mark,
         ),
-        in_specs=[vmem] * 4 + [hbm],
+        in_specs=[vmem] * 6 + [hbm],
         out_specs=(hbm,) + (vmem,) * 4,
         scratch_shapes=[
             pltpu.VMEM((2 * rim, width), jnp.bfloat16),
+            pltpu.VMEM((2 * rim, width), jnp.bfloat16),
             pltpu.SemaphoreType.DMA((2,)),
         ],
-        input_output_aliases={4: 0},
+        input_output_aliases={6: 0},
         compiler_params=params(12),
         cost_estimate=cost(0.2),
         name="rim_rows_back",
-    )(weight_near, dense, grad_rim, act_rim, activated)
+    )(
+        weight_near, dense, grad_first, grad_second, act_first, act_second, activated
+    )
     first_part = swap(first_spill, [1] * count)
     second_part = with_next(second_spill, count, False)
     grad_whole, edges, second_mark = pl.pallas_call(

time: 32 us -> 32.3 us (level)
  waiting for transfers between devices: 5.42 us -> 4.39 us
  Pallas kernels: 9.4 us -> 10.3 us
    ppermute x2, waiting for transfers between devices: 0.8 us -> 0.18 us  [with_next(): return lax.ppermute(value, AXES, pairs if closed else pairs[1:-1])]
    pallas_call x1, Pallas kernels: 0.88 us -> 1.42 us  [on_device(): pl.pallas_call(rim_back_kernel, out_shape=(shape(rows, width), shape(4 *...]
    ppermute x10, waiting for transfers between devices: 4.63 us -> 4.2 us  [swap(): return lax.ppermute(value, AXES, pairs)]
    pallas_call x1 -> x2, Pallas kernels: 0.81 us -> 1.21 us  [rim_rows(): pl.pallas_call(functools.partial(rim_kernel, order), out_shape=(shape(rim...]
    ppermute x10, starting transfers between devices: 12 us -> 12.4 us  [swap(): return lax.ppermute(value, AXES, pairs)]
  transfers between devices with their start and end apart: 12 -> 12, of which waited for: 8 -> 8; matrix products, arithmetic and copies ran while one was open for 0% -> 0% of each run, Pallas kernels for 21% -> 25%
where the time goes in v21:
time: 32.3 us; the launch traced here: 32.1 us
  starting transfers between devices  16.6 us (51%)
  Pallas kernels  10.3 us (32%)
  waiting for transfers between devices  4.39 us (14%)
  between operations  0.75 us (2%)
    ppermute x10, starting transfers between devices, swap(): return lax.ppermute(value, AXES, pairs)  12.4 us
    ppermute x2, starting transfers between devices, with_next(): return lax.ppermute(value, AXES, pairs if closed else pairs[1:-1])  4.29 us
    ppermute x10, waiting for transfers between devices, swap(): return lax.ppermute(value, AXES, pairs)  4.2 us
    pallas_call x1, Pallas kernels, on_device(): pl.pallas_call(inner_kernel, out_shape=(shape(rows, width), shape(blocks...  3.54 us
    pallas_call x1, Pallas kernels, on_device(): pl.pallas_call(inner_back_kernel, out_shape=(shape(rows, width), shape(2...  2.22 us
    pallas_call x1, Pallas kernels, on_device(): pl.pallas_call(rim_back_kernel, out_shape=(shape(rows, width), shape(4 *...  1.42 us
    pallas_call x2, Pallas kernels, rim_rows(): pl.pallas_call(functools.partial(rim_kernel, order), out_shape=(shape(rim...  1.21 us
    pallas_call x1, Pallas kernels, on_device(): pl.pallas_call(halo_kernel, out_shape=(shape(rim, width), shape(rim, widt...  1 us
  transfers between devices with their start and end apart: 12, of which 8 were waited for; matrix products, arithmetic and copies ran while one was open for 0% of the time, Pallas kernels for 25%

profile of v21, /device:TPU:0, one launch (start us, length us, event | category | flops | bytes accessed | tf_op | source)
XLA Modules:
  0.0 32.1 jit_solution(2443718072961119864)
XLA Ops:
  0.6 1.0 %halo_rows.1 = (bf16[256,256]{1,0:T(8,128)(2,1)S(1)}, bf16[256,256]{1,0:T(8,128)(2,1)S(1)}) custom-call(bf16[1536,256]{1,0:T(8,128)(2,1)} %feat_hbm.3), custom_call_target="tpu_custom_call" | custom-call | flops 60000000 | bytes 300000 | tf_op jit(solution)/shard_map/halo_rows/pallas_call | solution.py:430
  1.6 3.0 %collective-permute-start = (bf16[256,256]{1,0:T(8,128)(2,1)S(1)}, bf16[256,256]{1,0:T(8,128)(2,1)S(1)}, u32[]{:S(2)}, u32[]{:S(2)}) collective-permute-start(bf16[256,256]{1,0:T(8,128)(2,1)S(1)} %get-tuple-element.40), channel_id=1, source_target_pairs={{0,1},{1,0},{2,3},{3,2},{4,5},{5,4},{6,7},{7,6},{8,9},{9,8},{10,11... | collective-permute-start | bytes 393224 | tf_op jit(solution)/shard_map/ppermute | solution.py:364
  4.7 3.6 %collective-permute-start.1 = (bf16[256,256]{1,0:T(8,128)(2,1)S(1)}, bf16[256,256]{1,0:T(8,128)(2,1)S(1)}, u32[]{:S(2)}, u32[]{:S(2)}) collective-permute-start(bf16[256,256]{1,0:T(8,128)(2,1)S(1)} %get-tuple-element.45), channel_id=1, source_target_pairs={{0,31},{1,2},{2,1},{3,4},{4,3},{5,6},{6,5},{7,8},{8,7},{9,10},{10,... | collective-permute-start | bytes 393224 | tf_op jit(solution)/shard_map/ppermute | solution.py:369
  8.3 3.5 %inner_rows.1 = (bf16[1536,256]{1,0:T(8,128)(2,1)}, s32[36]{0:T(128)S(1)}, bf16[1024,256]{1,0:T(8,128)(2,1)S(1)}, f32[256,256]{1,0:T(8,128)S(1)}, f32[8,256]{1,0...) custom-call(s32[3,12]{1,0:T(4,128)} %bitcast.3, ...), custom_call_target="tpu_custom_call" | custom-call | flops 600000000 | bytes 3000000 | tf_op jit(solution)/shard_map/inner_rows/pallas_call | solution.py:445
  11.9 0.0 collective-permute-done.halo_ref
  11.9 0.6 %rim_rows.2 = (bf16[256,256]{1,0:T(8,128)(2,1)S(1)}, bf16[256,256]{1,0:T(8,128)(2,1)S(1)}, f32[256,256]{1,0:T(8,128)S(1)}, f32[8,256]{1,0:T(8,128)S(1)}) custom-call(bf16[256,256]{1,0:T(8,128)(2,1)S(1)} %get-tuple-element.36.weight_ref, f32[1,256]{1,0:T(1,128)S(1)} %get-tuple-element.38.bias_ref, f32[512,256]{1,0:T(8,128)S(1)} %get-tuple-element.39.own_ref, ...), custom_call_target="tpu_custom_call" | custom-call | flops 120000000 | bytes 600000 | tf_op jit(solution)/shard_map/rim_rows/pallas_call | solution.py:482
  12.5 0.2 collective-permute-done.1.halo_ref
  12.7 0.6 %rim_rows.3 = (bf16[256,256]{1,0:T(8,128)(2,1)S(1)}, bf16[256,256]{1,0:T(8,128)(2,1)S(1)}, bf16[136,256]{1,0:T(8,128)(2,1)S(1)}, f32[136,256]{1,0:T(8,128)S(1)}) custom-call(bf16[256,256]{1,0:T(8,128)(2,1)S(1)} %get-tuple-element.36.weight_ref, f32[1,256]{1,0:T(1,128)S(1)} %get-tuple-element.38.bias_ref, f32[512,256]{1,0:T(8,128)S(1)} %get-tuple-element.39.own_ref, ...), custom_call_target="tpu_custom_call" | custom-call | flops 120000000 | bytes 600000 | tf_op jit(solution)/shard_map/rim_rows/pallas_call | solution.py:482
  13.3 0.1 collective-permute-start.2
  13.3 1.4 %rim_rows_back.1 = (bf16[1536,256]{1,0:T(8,128)(2,1)}, f32[8,256,128]{2,1,0:T(8,128)S(1)}, bf16[256,256]{1,0:T(8,128)(2,1)S(1)}, bf16[256,256]{1,0:T(8,128)(2,1)S(1)}, f32[8,128]{1,0:T(8,128)S(1)}) custom-call(bf16[256,256]{1,0:T(8,128)(2,1)S(1)} %get-tuple-element.36.weight_ref, ...), custom_call_target="tpu_custom_call", output_to_operand_aliasing={{0}: (6, {})} | custom-call | flops 240000000 | bytes 1200000 | tf_op jit(solution)/shard_map/rim_rows_back/pallas_call | solution.py:501
  14.8 0.0 collective-permute-done.2.refs_1_
  14.8 0.5 %collective-permute-start.5 = (bf16[136,256]{1,0:T(8,128)(2,1)S(1)}, bf16[136,256]{1,0:T(8,128)(2,1)S(1)}, u32[]{:S(2)}, u32[]{:S(2)}) collective-permute-start(bf16[136,256]{1,0:T(8,128)(2,1)S(1)} %add_halves.3.refs_0_), channel_id=1, source_target_pairs={{0,1},{1,0},{2,26},{3,27},{4,5},{5,4},{6,30},{7,31},{8,9},{9,8},{1... | collective-permute-start | bytes 208904 | tf_op jit(solution)/shard_map/ppermute | solution.py:364
  15.3 1.0 %collective-permute-start.4 = (bf16[136,256]{1,0:T(8,128)(2,1)S(1)}, bf16[136,256]{1,0:T(8,128)(2,1)S(1)}, u32[]{:S(2)}, u32[]{:S(2)}) collective-permute-start(bf16[136,256]{1,0:T(8,128)(2,1)S(1)} %add_halves.3.refs_0_), channel_id=1, source_target_pairs={{0,5},{1,4},{2,18},{3,19},{4,1},{5,0},{6,22},{7,23},{8,13},{9,12},... | collective-permute-start | bytes 208904 | tf_op jit(solution)/shard_map/ppermute | solution.py:364
  16.3 2.1 %collective-permute-start.3 = (bf16[136,256]{1,0:T(8,128)(2,1)S(1)}, bf16[136,256]{1,0:T(8,128)(2,1)S(1)}, u32[]{:S(2)}, u32[]{:S(2)}) collective-permute-start(bf16[136,256]{1,0:T(8,128)(2,1)S(1)} %add_halves.3.refs_0_), channel_id=1, source_target_pairs={{0,4},{1,5},{2,10},{3,11},{4,0},{5,1},{6,14},{7,15},{8,12},{9,13},... | collective-permute-start | bytes 208904 | tf_op jit(solution)/shard_map/ppermute | solution.py:364
  18.4 0.7 %collective-permute-start.9 = (bf16[256,256]{1,0:T(8,128)(2,1)S(1)}, bf16[256,256]{1,0:T(8,128)(2,1)S(1)}, u32[]{:S(2)}, u32[]{:S(2)}) collective-permute-start(bf16[256,256]{1,0:T(8,128)(2,1)S(1)} %get-tuple-element.61), channel_id=1, source_target_pairs={{1,2},{2,1},{3,4},{4,3},{5,6},{6,5},{7,8},{8,7},{9,10},{10,9},{11,... | collective-permute-start | bytes 393224 | tf_op jit(solution)/shard_map/ppermute | solution.py:369
  19.0 0.2 collective-permute-done.5.refs_3_
  19.2 1.3 %collective-permute-done.4.refs_2_ = bf16[136,256]{1,0:T(8,128)(2,1)S(1)} collective-permute-done((bf16[136,256]{1,0:T(8,128)(2,1)S(1)}, bf16[136,256]{1,0:T(8,128)(2,1)S(1)}, u32[]{:S(2)}, u32[]{:S(2)}) %collective-permute-start.4) | collective-permute-done | bytes 69664 | tf_op jit(solution)/shard_map/ppermute | solution.py:364
  20.5 0.9 %collective-permute-done.3.refs_1_ = bf16[136,256]{1,0:T(8,128)(2,1)S(1)} collective-permute-done((bf16[136,256]{1,0:T(8,128)(2,1)S(1)}, bf16[136,256]{1,0:T(8,128)(2,1)S(1)}, u32[]{:S(2)}, u32[]{:S(2)}) %collective-permute-start.3) | collective-permute-done | bytes 69664 | tf_op jit(solution)/shard_map/ppermute | solution.py:364
  21.4 3.1 %collective-permute-start.8 = (bf16[136,256]{1,0:T(8,128)(2,1)S(1)}, bf16[136,256]{1,0:T(8,128)(2,1)S(1)}, u32[]{:S(2)}, u32[]{:S(2)}) collective-permute-start(bf16[136,256]{1,0:T(8,128)(2,1)S(1)} %add_halves.4.refs_0_), channel_id=1, source_target_pairs={{0,24},{1,25},{2,3},{3,2},{4,28},{5,29},{6,7},{7,6},{8,16},{9,17},... | collective-permute-start | bytes 208904 | tf_op jit(solution)/shard_map/ppermute | solution.py:364
  24.5 0.3 %collective-permute-start.7 = (bf16[136,256]{1,0:T(8,128)(2,1)S(1)}, bf16[136,256]{1,0:T(8,128)(2,1)S(1)}, u32[]{:S(2)}, u32[]{:S(2)}) collective-permute-start(bf16[136,256]{1,0:T(8,128)(2,1)S(1)} %add_halves.4.refs_0_), channel_id=1, source_target_pairs={{0,16},{1,17},{2,7},{3,6},{4,20},{5,21},{6,3},{7,2},{8,24},{9,25},... | collective-permute-start | bytes 208904 | tf_op jit(solution)/shard_map/ppermute | solution.py:364
  24.8 1.0 %collective-permute-start.6 = (bf16[136,256]{1,0:T(8,128)(2,1)S(1)}, bf16[136,256]{1,0:T(8,128)(2,1)S(1)}, u32[]{:S(2)}, u32[]{:S(2)}) collective-permute-start(bf16[136,256]{1,0:T(8,128)(2,1)S(1)} %add_halves.4.refs_0_), channel_id=1, source_target_pairs={{0,8},{1,9},{2,6},{3,7},{4,12},{5,13},{6,2},{7,3},{8,0},{9,1},{10,... | collective-permute-start | bytes 208904 | tf_op jit(solution)/shard_map/ppermute | solution.py:364
  25.9 1.2 %collective-permute-start.11 = (bf16[256,256]{1,0:T(8,128)(2,1)S(1)}, bf16[256,256]{1,0:T(8,128)(2,1)S(1)}, u32[]{:S(2)}, u32[]{:S(2)}) collective-permute-start(bf16[256,256]{1,0:T(8,128)(2,1)S(1)} %get-tuple-element.63), channel_id=1, source_target_pairs={{0,1},{1,0},{2,3},{3,2},{4,5},{5,4},{6,7},{7,6},{8,9},{9,8},{10,11... | collective-permute-start | bytes 393224 | tf_op jit(solution)/shard_map/ppermute | solution.py:364
  27.1 2.2 %inner_rows_back.1 = (bf16[1536,256]{1,0:T(8,128)(2,1)}, f32[512,256]{1,0:T(8,128)S(1)}, f32[8,128]{1,0:T(8,128)S(1)}) custom-call(s32[36]{0:T(128)S(1)} %get-tuple-element.56.place_in, bf16[256,256]{1,0:T(8,128)(2,1)S(1)} %get-tuple-element.36.weight_ref, bf16[8,3,128,128]{3,2,1,0:T(8,128)(2,1)S(1)} %get-tuple-element.57.adj_ref, ...), custom_call_target="tpu_custom_call" | custom-call | flops 360000000 | bytes 1800000 | tf_op jit(solution)/shard_map/inner_rows_back/pallas_call | solution.py:526
  29.3 0.0 collective-permute-done.9.refs_5_.second_ref
  29.3 0.0 collective-permute-done.8.refs_3_
  29.3 0.5 %collective-permute-done.7.refs_2_ = bf16[136,256]{1,0:T(8,128)(2,1)S(1)} collective-permute-done((bf16[136,256]{1,0:T(8,128)(2,1)S(1)}, bf16[136,256]{1,0:T(8,128)(2,1)S(1)}, u32[]{:S(2)}, u32[]{:S(2)}) %collective-permute-start.7) | collective-permute-done | bytes 69664 | tf_op jit(solution)/shard_map/ppermute | solution.py:364
  29.8 0.1 collective-permute-done.6.refs_1_
  29.9 0.1 collective-permute-start.10
  30.0 0.8 %collective-permute-done.11.first_ref = bf16[256,256]{1,0:T(8,128)(2,1)S(1)} collective-permute-done((bf16[256,256]{1,0:T(8,128)(2,1)S(1)}, bf16[256,256]{1,0:T(8,128)(2,1)S(1)}, u32[]{:S(2)}, u32[]{:S(2)}) %collective-permute-start.11) | collective-permute-done | bytes 131104 | tf_op jit(solution)/shard_map/ppermute | solution.py:364
  30.9 0.4 %collective-permute-done.10.other_ref = bf16[136,256]{1,0:T(8,128)(2,1)S(1)} collective-permute-done((bf16[136,256]{1,0:T(8,128)(2,1)S(1)}, bf16[136,256]{1,0:T(8,128)(2,1)S(1)}, u32[]{:S(2)}, u32[]{:S(2)}) %collective-permute-start.10) | collective-permute-done | bytes 69664 | tf_op jit(solution)/shard_map/ppermute | solution.py:364
  31.3 0.9 %last_step.1 = (f32[256,256]{1,0:T(8,128)}, f32[1,256]{1,0:T(1,128)}, bf16[1536,256]{1,0:T(8,128)(2,1)}) custom-call(bf16[136,256]{1,0:T(8,128)(2,1)S(1)} %add_halves.5.own_ref, bf16[136,256]{1,0:T(8,128)(2,1)S(1)} %collective-permute-done.10.other_ref, f32[512,256]{1,0:T(8,128)S(1)} %get-tuple-element.62.edge_ref, ...), custom_call_target="tpu_custom_call", output_to_operand_aliasing={{2}: (5, {})} | custom-call | tf_op jit(solution)/shard_map/last_step/pallas_call | solution.py:545
  (3 shorter events, 0.1 us)
Async XLA Ops:
  1.6 10.2 %collective-permute-start = (bf16[256,256]{1,0:T(8,128)(2,1)S(1)}, bf16[256,256]{1,0:T(8,128)(2,1)S(1)}, u32[]{:S(2)}, u32[]{:S(2)}) collective-permute-start(bf16[256,256]{1,0:T(8,128)(2,1)S(1)} %get-tuple-element.40), channel_id=1, source_target_pairs={{0,1},{1,0},{2,3},{3,2},{4,5},{5,4},{6,7},{7,6},{8,9},{9,8},{10,11... | collective-permute-start | bytes 393224 | tf_op jit(solution)/shard_map/ppermute | solution.py:364
  4.7 8.0 %collective-permute-start.1 = (bf16[256,256]{1,0:T(8,128)(2,1)S(1)}, bf16[256,256]{1,0:T(8,128)(2,1)S(1)}, u32[]{:S(2)}, u32[]{:S(2)}) collective-permute-start(bf16[256,256]{1,0:T(8,128)(2,1)S(1)} %get-tuple-element.45), channel_id=1, source_target_pairs={{0,31},{1,2},{2,1},{3,4},{4,3},{5,6},{6,5},{7,8},{8,7},{9,10},{10,... | collective-permute-start | bytes 393224 | tf_op jit(solution)/shard_map/ppermute | solution.py:369
  13.3 1.5 %collective-permute-start.2 = (bf16[136,256]{1,0:T(8,128)(2,1)S(1)}, bf16[136,256]{1,0:T(8,128)(2,1)S(1)}, u32[]{:S(2)}, u32[]{:S(2)}) collective-permute-start(bf16[136,256]{1,0:T(8,128)(2,1)S(1)} %get-tuple-element.54), channel_id=1, source_target_pairs={{0,2},{1,3},{2,0},{3,1},{4,6},{5,7},{6,4},{7,5},{8,10},{9,11},{10,... | collective-permute-start | bytes 208904 | tf_op jit(solution)/shard_map/ppermute | solution.py:364
  14.8 4.4 %collective-permute-start.5 = (bf16[136,256]{1,0:T(8,128)(2,1)S(1)}, bf16[136,256]{1,0:T(8,128)(2,1)S(1)}, u32[]{:S(2)}, u32[]{:S(2)}) collective-permute-start(bf16[136,256]{1,0:T(8,128)(2,1)S(1)} %add_halves.3.refs_0_), channel_id=1, source_target_pairs={{0,1},{1,0},{2,26},{3,27},{4,5},{5,4},{6,30},{7,31},{8,9},{9,8},{1... | collective-permute-start | bytes 208904 | tf_op jit(solution)/shard_map/ppermute | solution.py:364
  15.3 5.2 %collective-permute-start.4 = (bf16[136,256]{1,0:T(8,128)(2,1)S(1)}, bf16[136,256]{1,0:T(8,128)(2,1)S(1)}, u32[]{:S(2)}, u32[]{:S(2)}) collective-permute-start(bf16[136,256]{1,0:T(8,128)(2,1)S(1)} %add_halves.3.refs_0_), channel_id=1, source_target_pairs={{0,5},{1,4},{2,18},{3,19},{4,1},{5,0},{6,22},{7,23},{8,13},{9,12},... | collective-permute-start | bytes 208904 | tf_op jit(solution)/shard_map/ppermute | solution.py:364
  16.3 5.1 %collective-permute-start.3 = (bf16[136,256]{1,0:T(8,128)(2,1)S(1)}, bf16[136,256]{1,0:T(8,128)(2,1)S(1)}, u32[]{:S(2)}, u32[]{:S(2)}) collective-permute-start(bf16[136,256]{1,0:T(8,128)(2,1)S(1)} %add_halves.3.refs_0_), channel_id=1, source_target_pairs={{0,4},{1,5},{2,10},{3,11},{4,0},{5,1},{6,14},{7,15},{8,12},{9,13},... | collective-permute-start | bytes 208904 | tf_op jit(solution)/shard_map/ppermute | solution.py:364
  18.4 10.9 %collective-permute-start.9 = (bf16[256,256]{1,0:T(8,128)(2,1)S(1)}, bf16[256,256]{1,0:T(8,128)(2,1)S(1)}, u32[]{:S(2)}, u32[]{:S(2)}) collective-permute-start(bf16[256,256]{1,0:T(8,128)(2,1)S(1)} %get-tuple-element.61), channel_id=1, source_target_pairs={{1,2},{2,1},{3,4},{4,3},{5,6},{6,5},{7,8},{8,7},{9,10},{10,9},{11,... | collective-permute-start | bytes 393224 | tf_op jit(solution)/shard_map/ppermute | solution.py:369
  21.4 7.9 %collective-permute-start.8 = (bf16[136,256]{1,0:T(8,128)(2,1)S(1)}, bf16[136,256]{1,0:T(8,128)(2,1)S(1)}, u32[]{:S(2)}, u32[]{:S(2)}) collective-permute-start(bf16[136,256]{1,0:T(8,128)(2,1)S(1)} %add_halves.4.refs_0_), channel_id=1, source_target_pairs={{0,24},{1,25},{2,3},{3,2},{4,28},{5,29},{6,7},{7,6},{8,16},{9,17},... | collective-permute-start | bytes 208904 | tf_op jit(solution)/shard_map/ppermute | solution.py:364
  24.5 5.3 %collective-permute-start.7 = (bf16[136,256]{1,0:T(8,128)(2,1)S(1)}, bf16[136,256]{1,0:T(8,128)(2,1)S(1)}, u32[]{:S(2)}, u32[]{:S(2)}) collective-permute-start(bf16[136,256]{1,0:T(8,128)(2,1)S(1)} %add_halves.4.refs_0_), channel_id=1, source_target_pairs={{0,16},{1,17},{2,7},{3,6},{4,20},{5,21},{6,3},{7,2},{8,24},{9,25},... | collective-permute-start | bytes 208904 | tf_op jit(solution)/shard_map/ppermute | solution.py:364
  24.8 5.1 %collective-permute-start.6 = (bf16[136,256]{1,0:T(8,128)(2,1)S(1)}, bf16[136,256]{1,0:T(8,128)(2,1)S(1)}, u32[]{:S(2)}, u32[]{:S(2)}) collective-permute-start(bf16[136,256]{1,0:T(8,128)(2,1)S(1)} %add_halves.4.refs_0_), channel_id=1, source_target_pairs={{0,8},{1,9},{2,6},{3,7},{4,12},{5,13},{6,2},{7,3},{8,0},{9,1},{10,... | collective-permute-start | bytes 208904 | tf_op jit(solution)/shard_map/ppermute | solution.py:364
  25.9 5.0 %collective-permute-start.11 = (bf16[256,256]{1,0:T(8,128)(2,1)S(1)}, bf16[256,256]{1,0:T(8,128)(2,1)S(1)}, u32[]{:S(2)}, u32[]{:S(2)}) collective-permute-start(bf16[256,256]{1,0:T(8,128)(2,1)S(1)} %get-tuple-element.63), channel_id=1, source_target_pairs={{0,1},{1,0},{2,3},{3,2},{4,5},{5,4},{6,7},{7,6},{8,9},{9,8},{10,11... | collective-permute-start | bytes 393224 | tf_op jit(solution)/shard_map/ppermute | solution.py:364
  29.9 1.3 %collective-permute-start.10 = (bf16[136,256]{1,0:T(8,128)(2,1)S(1)}, bf16[136,256]{1,0:T(8,128)(2,1)S(1)}, u32[]{:S(2)}, u32[]{:S(2)}) collective-permute-start(bf16[136,256]{1,0:T(8,128)(2,1)S(1)} %add_halves.5.own_ref), channel_id=1, source_target_pairs={{0,2},{1,3},{2,0},{3,1},{4,6},{5,7},{6,4},{7,5},{8,10},{9,11},{10,... | collective-permute-start | bytes 208904 | tf_op jit(solution)/shard_map/ppermute | solution.py:364

commit v22 on v21

--- a/solution.py
+++ b/solution.py
@@ -229,7 +229,7 @@
 def rim_back_kernel(
     weight_ref, dense, grad_first, grad_second, act_first, act_second, act_in,
     act_hbm, spread, first_ref, second_ref, mark_ref,
-    grad_ref, spill, sems,
+    sems,
 ):
     block_rows = dense.shape[3]
     rim = BAND * block_rows
@@ -244,25 +244,20 @@
     ]
     for copy in copies:
         copy.start()
-    for order, grad in enumerate((grad_first, grad_second)):
-        grad_ref[pl.ds(pl.multiple_of(rim_side(order) * rim, rim), rim)] = grad[...]
     weight = weight_ref[...]
-    for side, (inside, outside) in enumerate(((BAND, 0), (0, 2 * BAND))):
+    exchanges = ((grad_first, first_ref), (grad_second, second_ref))
+    for order, (grad_ref, spill_ref) in enumerate(exchanges):
+        side = rim_side(order)
         terms = jnp.dot(
-            to_upstream(weight, grad_ref[side * rim : (side + 1) * rim]),
-            side_by_side(dense, side, 0, 3 * BAND),
+            to_upstream(weight, grad_ref[...]), side_by_side(dense, side, 0, 3 * BAND),
             preferred_element_type=jnp.float32,
         )
-        for block in range(2 * BAND):
-            lane = (inside + block) * block_rows
-            spread[side * 2 * BAND + block] = terms[:, lane : lane + block_rows]
+        for block in range(3 * BAND):
+            lane = block * block_rows
+            spread[order, block] = terms[:, lane : lane + block_rows]
         for block in range(BAND):
-            lane = (outside + block) * block_rows
-            here = pl.ds(side * rim + block * block_rows, block_rows)
-            spill[here] = terms[:, lane : lane + block_rows].T.astype(jnp.bfloat16)
-    odd = place_in_mesh() & 1
-    first_ref[...] = spill[pl.ds(pl.multiple_of((1 - odd) * rim, rim), rim)]
-    second_ref[...] = spill[pl.ds(pl.multiple_of(odd * rim, rim), rim)]
+            here = pl.ds(block * block_rows, block_rows)
+            spill_ref[here] = spread[order, side * 2 * BAND + block].T.astype(jnp.bfloat16)
     mark_ref[...] = jnp.zeros_like(mark_ref)
     for copy in copies:
         copy.wait()
@@ -278,9 +273,10 @@
     count, slots, block_rows, _ = adj_ref.shape
     blocks = place_ref.shape[0] // slots
     rim = BAND * block_rows
-    spread[: 2 * BAND] = rim_spread[: 2 * BAND]
+    odd = place_in_mesh() & 1
+    spread[: 2 * BAND] = rim_spread[1 - odd, BAND:]
     spread[2 * BAND :] = jnp.zeros_like(spread[2 * BAND :])
-    spread[blocks - 2 * BAND : blocks] = rim_spread[2 * BAND :]
+    spread[blocks - 2 * BAND : blocks] = rim_spread[odd, : 2 * BAND]
     upstream = to_upstream(weight_ref[...], grad_ref[...])
     fetch.wait()
     scatter_rows(
@@ -502,18 +498,14 @@
         rim_back_kernel,
         out_shape=(
             shape(rows, width),
-            shape(4 * BAND, width, block_rows, dtype=jnp.float32),
+            shape(2, 3 * BAND, width, block_rows, dtype=jnp.float32),
             shape(rim, width),
             shape(rim, width),
             mark,
         ),
         in_specs=[vmem] * 6 + [hbm],
         out_specs=(hbm,) + (vmem,) * 4,
-        scratch_shapes=[
-            pltpu.VMEM((2 * rim, width), jnp.bfloat16),
-            pltpu.VMEM((2 * rim, width), jnp.bfloat16),
-            pltpu.SemaphoreType.DMA((2,)),
-        ],
+        scratch_shapes=[pltpu.SemaphoreType.DMA((2,))],
         input_output_aliases={6: 0},
         compiler_params=params(12),
         cost_estimate=cost(0.2),

time: 32.3 us -> 32.4 us (level)
  no operation moved by 1% of the time
where the time goes in v22:
time: 32.4 us; the launch traced here: 32.2 us
  starting transfers between devices  16.6 us (51%)
  Pallas kernels  10.4 us (32%)
  waiting for transfers between devices  4.39 us (14%)
  between operations  0.75 us (2%)
    ppermute x10, starting transfers between devices, swap(): return lax.ppermute(value, AXES, pairs)  12.3 us
    ppermute x2, starting transfers between devices, with_next(): return lax.ppermute(value, AXES, pairs if closed else pairs[1:-1])  4.29 us
    ppermute x10, waiting for transfers between devices, swap(): return lax.ppermute(value, AXES, pairs)  4.21 us
    pallas_call x1, Pallas kernels, on_device(): pl.pallas_call(inner_kernel, out_shape=(shape(rows, width), shape(blocks...  3.54 us
    pallas_call x1, Pallas kernels, on_device(): pl.pallas_call(inner_back_kernel, out_shape=(shape(rows, width), shape(2...  2.22 us
    pallas_call x1, Pallas kernels, on_device(): pl.pallas_call(rim_back_kernel, out_shape=(shape(rows, width), shape(2, 3...  1.49 us
    pallas_call x2, Pallas kernels, rim_rows(): pl.pallas_call(functools.partial(rim_kernel, order), out_shape=(shape(rim...  1.21 us
    pallas_call x1, Pallas kernels, on_device(): pl.pallas_call(halo_kernel, out_shape=(shape(rim, width), shape(rim, widt...  1 us
  transfers between devices with their start and end apart: 12, of which 8 were waited for; matrix products, arithmetic and copies ran while one was open for 0% of the time, Pallas kernels for 25%

profile of v22, /device:TPU:0, one launch (start us, length us, event | category | flops | bytes accessed | tf_op | source)
XLA Modules:
  0.0 32.2 jit_solution(13354904402963175205)
XLA Ops:
  0.6 1.0 %halo_rows.1 = (bf16[256,256]{1,0:T(8,128)(2,1)S(1)}, bf16[256,256]{1,0:T(8,128)(2,1)S(1)}) custom-call(bf16[1536,256]{1,0:T(8,128)(2,1)} %feat_hbm.3), custom_call_target="tpu_custom_call" | custom-call | flops 60000000 | bytes 300000 | tf_op jit(solution)/shard_map/halo_rows/pallas_call | solution.py:426
  1.6 3.0 %collective-permute-start = (bf16[256,256]{1,0:T(8,128)(2,1)S(1)}, bf16[256,256]{1,0:T(8,128)(2,1)S(1)}, u32[]{:S(2)}, u32[]{:S(2)}) collective-permute-start(bf16[256,256]{1,0:T(8,128)(2,1)S(1)} %get-tuple-element.40), channel_id=1, source_target_pairs={{0,1},{1,0},{2,3},{3,2},{4,5},{5,4},{6,7},{7,6},{8,9},{9,8},{10,11... | collective-permute-start | bytes 393224 | tf_op jit(solution)/shard_map/ppermute | solution.py:360
  4.7 3.6 %collective-permute-start.1 = (bf16[256,256]{1,0:T(8,128)(2,1)S(1)}, bf16[256,256]{1,0:T(8,128)(2,1)S(1)}, u32[]{:S(2)}, u32[]{:S(2)}) collective-permute-start(bf16[256,256]{1,0:T(8,128)(2,1)S(1)} %get-tuple-element.45), channel_id=1, source_target_pairs={{0,31},{1,2},{2,1},{3,4},{4,3},{5,6},{6,5},{7,8},{8,7},{9,10},{10,... | collective-permute-start | bytes 393224 | tf_op jit(solution)/shard_map/ppermute | solution.py:365
  8.3 3.5 %inner_rows.1 = (bf16[1536,256]{1,0:T(8,128)(2,1)}, s32[36]{0:T(128)S(1)}, bf16[1024,256]{1,0:T(8,128)(2,1)S(1)}, f32[256,256]{1,0:T(8,128)S(1)}, f32[8,256]{1,0...) custom-call(s32[3,12]{1,0:T(4,128)} %bitcast.3, ...), custom_call_target="tpu_custom_call" | custom-call | flops 600000000 | bytes 3000000 | tf_op jit(solution)/shard_map/inner_rows/pallas_call | solution.py:441
  11.9 0.0 collective-permute-done.halo_ref
  11.9 0.6 %rim_rows.2 = (bf16[256,256]{1,0:T(8,128)(2,1)S(1)}, bf16[256,256]{1,0:T(8,128)(2,1)S(1)}, f32[256,256]{1,0:T(8,128)S(1)}, f32[8,256]{1,0:T(8,128)S(1)}) custom-call(bf16[256,256]{1,0:T(8,128)(2,1)S(1)} %get-tuple-element.36.weight_ref, f32[1,256]{1,0:T(1,128)S(1)} %get-tuple-element.38.bias_ref, f32[512,256]{1,0:T(8,128)S(1)} %get-tuple-element.39.own_ref, ...), custom_call_target="tpu_custom_call" | custom-call | flops 120000000 | bytes 600000 | tf_op jit(solution)/shard_map/rim_rows/pallas_call | solution.py:478
  12.5 0.2 collective-permute-done.1.halo_ref
  12.7 0.6 %rim_rows.3 = (bf16[256,256]{1,0:T(8,128)(2,1)S(1)}, bf16[256,256]{1,0:T(8,128)(2,1)S(1)}, bf16[136,256]{1,0:T(8,128)(2,1)S(1)}, f32[136,256]{1,0:T(8,128)S(1)}) custom-call(bf16[256,256]{1,0:T(8,128)(2,1)S(1)} %get-tuple-element.36.weight_ref, f32[1,256]{1,0:T(1,128)S(1)} %get-tuple-element.38.bias_ref, f32[512,256]{1,0:T(8,128)S(1)} %get-tuple-element.39.own_ref, ...), custom_call_target="tpu_custom_call" | custom-call | flops 120000000 | bytes 600000 | tf_op jit(solution)/shard_map/rim_rows/pallas_call | solution.py:478
  13.3 0.1 collective-permute-start.2
  13.3 1.5 %rim_rows_back.1 = (bf16[1536,256]{1,0:T(8,128)(2,1)}, f32[2,6,256,128]{3,2,1,0:T(8,128)S(1)}, bf16[256,256]{1,0:T(8,128)(2,1)S(1)}, bf16[256,256]{1,0:T(8,128)(2,1)S(1)}, f32[8,128]{1,0:T(8,128)S(1)}) custom-call(bf16[256,256]{1,0:T(8,128)(2,1)S(1)} %get-tuple-element.36.weight_ref, ...), custom_call_target="tpu_custom_call", output_to_operand_aliasing={{0}: (6, {})} | custom-call | flops 240000000 | bytes 1200000 | tf_op jit(solution)/shard_map/rim_rows_back/pallas_call | solution.py:497
  14.8 0.0 collective-permute-done.2.refs_1_
  14.9 0.5 %collective-permute-start.5 = (bf16[136,256]{1,0:T(8,128)(2,1)S(1)}, bf16[136,256]{1,0:T(8,128)(2,1)S(1)}, u32[]{:S(2)}, u32[]{:S(2)}) collective-permute-start(bf16[136,256]{1,0:T(8,128)(2,1)S(1)} %add_halves.3.refs_0_), channel_id=1, source_target_pairs={{0,1},{1,0},{2,26},{3,27},{4,5},{5,4},{6,30},{7,31},{8,9},{9,8},{1... | collective-permute-start | bytes 208904 | tf_op jit(solution)/shard_map/ppermute | solution.py:360
  15.4 1.0 %collective-permute-start.4 = (bf16[136,256]{1,0:T(8,128)(2,1)S(1)}, bf16[136,256]{1,0:T(8,128)(2,1)S(1)}, u32[]{:S(2)}, u32[]{:S(2)}) collective-permute-start(bf16[136,256]{1,0:T(8,128)(2,1)S(1)} %add_halves.3.refs_0_), channel_id=1, source_target_pairs={{0,5},{1,4},{2,18},{3,19},{4,1},{5,0},{6,22},{7,23},{8,13},{9,12},... | collective-permute-start | bytes 208904 | tf_op jit(solution)/shard_map/ppermute | solution.py:360
  16.4 2.1 %collective-permute-start.3 = (bf16[136,256]{1,0:T(8,128)(2,1)S(1)}, bf16[136,256]{1,0:T(8,128)(2,1)S(1)}, u32[]{:S(2)}, u32[]{:S(2)}) collective-permute-start(bf16[136,256]{1,0:T(8,128)(2,1)S(1)} %add_halves.3.refs_0_), channel_id=1, source_target_pairs={{0,4},{1,5},{2,10},{3,11},{4,0},{5,1},{6,14},{7,15},{8,12},{9,13},... | collective-permute-start | bytes 208904 | tf_op jit(solution)/shard_map/ppermute | solution.py:360
  18.4 0.7 %collective-permute-start.9 = (bf16[256,256]{1,0:T(8,128)(2,1)S(1)}, bf16[256,256]{1,0:T(8,128)(2,1)S(1)}, u32[]{:S(2)}, u32[]{:S(2)}) collective-permute-start(bf16[256,256]{1,0:T(8,128)(2,1)S(1)} %get-tuple-element.61), channel_id=1, source_target_pairs={{1,2},{2,1},{3,4},{4,3},{5,6},{6,5},{7,8},{8,7},{9,10},{10,9},{11,... | collective-permute-start | bytes 393224 | tf_op jit(solution)/shard_map/ppermute | solution.py:365
  19.1 0.2 collective-permute-done.5.refs_3_
  19.3 1.3 %collective-permute-done.4.refs_2_ = bf16[136,256]{1,0:T(8,128)(2,1)S(1)} collective-permute-done((bf16[136,256]{1,0:T(8,128)(2,1)S(1)}, bf16[136,256]{1,0:T(8,128)(2,1)S(1)}, u32[]{:S(2)}, u32[]{:S(2)}) %collective-permute-start.4) | collective-permute-done | bytes 69664 | tf_op jit(solution)/shard_map/ppermute | solution.py:360
  20.6 0.9 %collective-permute-done.3.refs_1_ = bf16[136,256]{1,0:T(8,128)(2,1)S(1)} collective-permute-done((bf16[136,256]{1,0:T(8,128)(2,1)S(1)}, bf16[136,256]{1,0:T(8,128)(2,1)S(1)}, u32[]{:S(2)}, u32[]{:S(2)}) %collective-permute-start.3) | collective-permute-done | bytes 69664 | tf_op jit(solution)/shard_map/ppermute | solution.py:360
  21.5 3.1 %collective-permute-start.8 = (bf16[136,256]{1,0:T(8,128)(2,1)S(1)}, bf16[136,256]{1,0:T(8,128)(2,1)S(1)}, u32[]{:S(2)}, u32[]{:S(2)}) collective-permute-start(bf16[136,256]{1,0:T(8,128)(2,1)S(1)} %add_halves.4.refs_0_), channel_id=1, source_target_pairs={{0,24},{1,25},{2,3},{3,2},{4,28},{5,29},{6,7},{7,6},{8,16},{9,17},... | collective-permute-start | bytes 208904 | tf_op jit(solution)/shard_map/ppermute | solution.py:360
  24.6 0.3 %collective-permute-start.7 = (bf16[136,256]{1,0:T(8,128)(2,1)S(1)}, bf16[136,256]{1,0:T(8,128)(2,1)S(1)}, u32[]{:S(2)}, u32[]{:S(2)}) collective-permute-start(bf16[136,256]{1,0:T(8,128)(2,1)S(1)} %add_halves.4.refs_0_), channel_id=1, source_target_pairs={{0,16},{1,17},{2,7},{3,6},{4,20},{5,21},{6,3},{7,2},{8,24},{9,25},... | collective-permute-start | bytes 208904 | tf_op jit(solution)/shard_map/ppermute | solution.py:360
  24.9 1.0 %collective-permute-start.6 = (bf16[136,256]{1,0:T(8,128)(2,1)S(1)}, bf16[136,256]{1,0:T(8,128)(2,1)S(1)}, u32[]{:S(2)}, u32[]{:S(2)}) collective-permute-start(bf16[136,256]{1,0:T(8,128)(2,1)S(1)} %add_halves.4.refs_0_), channel_id=1, source_target_pairs={{0,8},{1,9},{2,6},{3,7},{4,12},{5,13},{6,2},{7,3},{8,0},{9,1},{10,... | collective-permute-start | bytes 208904 | tf_op jit(solution)/shard_map/ppermute | solution.py:360
  26.0 1.2 %collective-permute-start.11 = (bf16[256,256]{1,0:T(8,128)(2,1)S(1)}, bf16[256,256]{1,0:T(8,128)(2,1)S(1)}, u32[]{:S(2)}, u32[]{:S(2)}) collective-permute-start(bf16[256,256]{1,0:T(8,128)(2,1)S(1)} %get-tuple-element.63), channel_id=1, source_target_pairs={{0,1},{1,0},{2,3},{3,2},{4,5},{5,4},{6,7},{7,6},{8,9},{9,8},{10,11... | collective-permute-start | bytes 393224 | tf_op jit(solution)/shard_map/ppermute | solution.py:360
  27.1 2.2 %inner_rows_back.1 = (bf16[1536,256]{1,0:T(8,128)(2,1)}, f32[512,256]{1,0:T(8,128)S(1)}, f32[8,128]{1,0:T(8,128)S(1)}) custom-call(s32[36]{0:T(128)S(1)} %get-tuple-element.56.place_in, bf16[256,256]{1,0:T(8,128)(2,1)S(1)} %get-tuple-element.36.weight_ref, bf16[8,3,128,128]{3,2,1,0:T(8,128)(2,1)S(1)} %get-tuple-element.57.adj_ref, ...), custom_call_target="tpu_custom_call" | custom-call | flops 360000000 | bytes 1800000 | tf_op jit(solution)/shard_map/inner_rows_back/pallas_call | solution.py:518
  29.4 0.0 collective-permute-done.9.refs_5_.second_ref
  29.4 0.0 collective-permute-done.8.refs_3_
  29.4 0.5 %collective-permute-done.7.refs_2_ = bf16[136,256]{1,0:T(8,128)(2,1)S(1)} collective-permute-done((bf16[136,256]{1,0:T(8,128)(2,1)S(1)}, bf16[136,256]{1,0:T(8,128)(2,1)S(1)}, u32[]{:S(2)}, u32[]{:S(2)}) %collective-permute-start.7) | collective-permute-done | bytes 69664 | tf_op jit(solution)/shard_map/ppermute | solution.py:360
  29.9 0.1 collective-permute-done.6.refs_1_
  30.0 0.1 collective-permute-start.10
  30.1 0.8 %collective-permute-done.11.first_ref = bf16[256,256]{1,0:T(8,128)(2,1)S(1)} collective-permute-done((bf16[256,256]{1,0:T(8,128)(2,1)S(1)}, bf16[256,256]{1,0:T(8,128)(2,1)S(1)}, u32[]{:S(2)}, u32[]{:S(2)}) %collective-permute-start.11) | collective-permute-done | bytes 131104 | tf_op jit(solution)/shard_map/ppermute | solution.py:360
  30.9 0.4 %collective-permute-done.10.other_ref = bf16[136,256]{1,0:T(8,128)(2,1)S(1)} collective-permute-done((bf16[136,256]{1,0:T(8,128)(2,1)S(1)}, bf16[136,256]{1,0:T(8,128)(2,1)S(1)}, u32[]{:S(2)}, u32[]{:S(2)}) %collective-permute-start.10) | collective-permute-done | bytes 69664 | tf_op jit(solution)/shard_map/ppermute | solution.py:360
  31.3 0.9 %last_step.1 = (f32[256,256]{1,0:T(8,128)}, f32[1,256]{1,0:T(1,128)}, bf16[1536,256]{1,0:T(8,128)(2,1)}) custom-call(bf16[136,256]{1,0:T(8,128)(2,1)S(1)} %add_halves.5.own_ref, bf16[136,256]{1,0:T(8,128)(2,1)S(1)} %collective-permute-done.10.other_ref, f32[512,256]{1,0:T(8,128)S(1)} %get-tuple-element.62.edge_ref, ...), custom_call_target="tpu_custom_call", output_to_operand_aliasing={{2}: (5, {})} | custom-call | tf_op jit(solution)/shard_map/last_step/pallas_call | solution.py:537
  (3 shorter events, 0.1 us)
Async XLA Ops:
  1.6 10.2 %collective-permute-start = (bf16[256,256]{1,0:T(8,128)(2,1)S(1)}, bf16[256,256]{1,0:T(8,128)(2,1)S(1)}, u32[]{:S(2)}, u32[]{:S(2)}) collective-permute-start(bf16[256,256]{1,0:T(8,128)(2,1)S(1)} %get-tuple-element.40), channel_id=1, source_target_pairs={{0,1},{1,0},{2,3},{3,2},{4,5},{5,4},{6,7},{7,6},{8,9},{9,8},{10,11... | collective-permute-start | bytes 393224 | tf_op jit(solution)/shard_map/ppermute | solution.py:360
  4.7 8.0 %collective-permute-start.1 = (bf16[256,256]{1,0:T(8,128)(2,1)S(1)}, bf16[256,256]{1,0:T(8,128)(2,1)S(1)}, u32[]{:S(2)}, u32[]{:S(2)}) collective-permute-start(bf16[256,256]{1,0:T(8,128)(2,1)S(1)} %get-tuple-element.45), channel_id=1, source_target_pairs={{0,31},{1,2},{2,1},{3,4},{4,3},{5,6},{6,5},{7,8},{8,7},{9,10},{10,... | collective-permute-start | bytes 393224 | tf_op jit(solution)/shard_map/ppermute | solution.py:365
  13.3 1.6 %collective-permute-start.2 = (bf16[136,256]{1,0:T(8,128)(2,1)S(1)}, bf16[136,256]{1,0:T(8,128)(2,1)S(1)}, u32[]{:S(2)}, u32[]{:S(2)}) collective-permute-start(bf16[136,256]{1,0:T(8,128)(2,1)S(1)} %get-tuple-element.54), channel_id=1, source_target_pairs={{0,2},{1,3},{2,0},{3,1},{4,6},{5,7},{6,4},{7,5},{8,10},{9,11},{10,... | collective-permute-start | bytes 208904 | tf_op jit(solution)/shard_map/ppermute | solution.py:360
  14.9 4.4 %collective-permute-start.5 = (bf16[136,256]{1,0:T(8,128)(2,1)S(1)}, bf16[136,256]{1,0:T(8,128)(2,1)S(1)}, u32[]{:S(2)}, u32[]{:S(2)}) collective-permute-start(bf16[136,256]{1,0:T(8,128)(2,1)S(1)} %add_halves.3.refs_0_), channel_id=1, source_target_pairs={{0,1},{1,0},{2,26},{3,27},{4,5},{5,4},{6,30},{7,31},{8,9},{9,8},{1... | collective-permute-start | bytes 208904 | tf_op jit(solution)/shard_map/ppermute | solution.py:360
  15.4 5.2 %collective-permute-start.4 = (bf16[136,256]{1,0:T(8,128)(2,1)S(1)}, bf16[136,256]{1,0:T(8,128)(2,1)S(1)}, u32[]{:S(2)}, u32[]{:S(2)}) collective-permute-start(bf16[136,256]{1,0:T(8,128)(2,1)S(1)} %add_halves.3.refs_0_), channel_id=1, source_target_pairs={{0,5},{1,4},{2,18},{3,19},{4,1},{5,0},{6,22},{7,23},{8,13},{9,12},... | collective-permute-start | bytes 208904 | tf_op jit(solution)/shard_map/ppermute | solution.py:360
  16.4 5.1 %collective-permute-start.3 = (bf16[136,256]{1,0:T(8,128)(2,1)S(1)}, bf16[136,256]{1,0:T(8,128)(2,1)S(1)}, u32[]{:S(2)}, u32[]{:S(2)}) collective-permute-start(bf16[136,256]{1,0:T(8,128)(2,1)S(1)} %add_halves.3.refs_0_), channel_id=1, source_target_pairs={{0,4},{1,5},{2,10},{3,11},{4,0},{5,1},{6,14},{7,15},{8,12},{9,13},... | collective-permute-start | bytes 208904 | tf_op jit(solution)/shard_map/ppermute | solution.py:360
  18.4 10.9 %collective-permute-start.9 = (bf16[256,256]{1,0:T(8,128)(2,1)S(1)}, bf16[256,256]{1,0:T(8,128)(2,1)S(1)}, u32[]{:S(2)}, u32[]{:S(2)}) collective-permute-start(bf16[256,256]{1,0:T(8,128)(2,1)S(1)} %get-tuple-element.61), channel_id=1, source_target_pairs={{1,2},{2,1},{3,4},{4,3},{5,6},{6,5},{7,8},{8,7},{9,10},{10,9},{11,... | collective-permute-start | bytes 393224 | tf_op jit(solution)/shard_map/ppermute | solution.py:365
  21.5 7.9 %collective-permute-start.8 = (bf16[136,256]{1,0:T(8,128)(2,1)S(1)}, bf16[136,256]{1,0:T(8,128)(2,1)S(1)}, u32[]{:S(2)}, u32[]{:S(2)}) collective-permute-start(bf16[136,256]{1,0:T(8,128)(2,1)S(1)} %add_halves.4.refs_0_), channel_id=1, source_target_pairs={{0,24},{1,25},{2,3},{3,2},{4,28},{5,29},{6,7},{7,6},{8,16},{9,17},... | collective-permute-start | bytes 208904 | tf_op jit(solution)/shard_map/ppermute | solution.py:360
  24.6 5.3 %collective-permute-start.7 = (bf16[136,256]{1,0:T(8,128)(2,1)S(1)}, bf16[136,256]{1,0:T(8,128)(2,1)S(1)}, u32[]{:S(2)}, u32[]{:S(2)}) collective-permute-start(bf16[136,256]{1,0:T(8,128)(2,1)S(1)} %add_halves.4.refs_0_), channel_id=1, source_target_pairs={{0,16},{1,17},{2,7},{3,6},{4,20},{5,21},{6,3},{7,2},{8,24},{9,25},... | collective-permute-start | bytes 208904 | tf_op jit(solution)/shard_map/ppermute | solution.py:360
  24.9 5.1 %collective-permute-start.6 = (bf16[136,256]{1,0:T(8,128)(2,1)S(1)}, bf16[136,256]{1,0:T(8,128)(2,1)S(1)}, u32[]{:S(2)}, u32[]{:S(2)}) collective-permute-start(bf16[136,256]{1,0:T(8,128)(2,1)S(1)} %add_halves.4.refs_0_), channel_id=1, source_target_pairs={{0,8},{1,9},{2,6},{3,7},{4,12},{5,13},{6,2},{7,3},{8,0},{9,1},{10,... | collective-permute-start | bytes 208904 | tf_op jit(solution)/shard_map/ppermute | solution.py:360
  26.0 5.0 %collective-permute-start.11 = (bf16[256,256]{1,0:T(8,128)(2,1)S(1)}, bf16[256,256]{1,0:T(8,128)(2,1)S(1)}, u32[]{:S(2)}, u32[]{:S(2)}) collective-permute-start(bf16[256,256]{1,0:T(8,128)(2,1)S(1)} %get-tuple-element.63), channel_id=1, source_target_pairs={{0,1},{1,0},{2,3},{3,2},{4,5},{5,4},{6,7},{7,6},{8,9},{9,8},{10,11... | collective-permute-start | bytes 393224 | tf_op jit(solution)/shard_map/ppermute | solution.py:360
  30.0 1.3 %collective-permute-start.10 = (bf16[136,256]{1,0:T(8,128)(2,1)S(1)}, bf16[136,256]{1,0:T(8,128)(2,1)S(1)}, u32[]{:S(2)}, u32[]{:S(2)}) collective-permute-start(bf16[136,256]{1,0:T(8,128)(2,1)S(1)} %add_halves.5.own_ref), channel_id=1, source_target_pairs={{0,2},{1,3},{2,0},{3,1},{4,6},{5,7},{6,4},{7,5},{8,10},{9,11},{10,... | collective-permute-start | bytes 208904 | tf_op jit(solution)/shard_map/ppermute | solution.py:360

commit v23 on v20

--- a/solution.py
+++ b/solution.py
@@ -514,7 +514,7 @@
         name="rim_rows_back",
     )(weight_near, dense, grad_rim, act_rim, activated)
     first_part = swap(first_spill, [1] * count)
-    second_part = with_next(second_spill, count, False)
+    second_part = with_next(second_spill, count, True)
     grad_whole, edges, second_mark = pl.pallas_call(
         inner_back_kernel,
         out_shape=(shape(rows, width), shape(2 * rim, width, dtype=jnp.float32), mark),

time: 32 us -> 32.6 us (1.019)
  starting transfers between devices: 16.3 us -> 18.8 us
  waiting for transfers between devices: 5.42 us -> 3.47 us
    ppermute x2, starting transfers between devices: 4.29 us -> 7.32 us  [with_next(): return lax.ppermute(value, AXES, pairs if closed else pairs[1:-1])]
    ppermute x10, waiting for transfers between devices: 4.63 us -> 2.68 us  [swap(): return lax.ppermute(value, AXES, pairs)]
    ppermute x10, starting transfers between devices: 12 us -> 11.5 us  [swap(): return lax.ppermute(value, AXES, pairs)]
  transfers between devices with their start and end apart: 12 -> 12, of which waited for: 8 -> 4; matrix products, arithmetic and copies ran while one was open for 0% -> 0% of each run, Pallas kernels for 21% -> 21%
where the time goes in v23:
time: 32.6 us; the launch traced here: 32.4 us
  starting transfers between devices  18.8 us (58%)
  Pallas kernels  9.4 us (29%)
  waiting for transfers between devices  3.47 us (11%)
  between operations  0.73 us (2%)
    ppermute x10, starting transfers between devices, swap(): return lax.ppermute(value, AXES, pairs)  11.5 us
    ppermute x2, starting transfers between devices, with_next(): return lax.ppermute(value, AXES, pairs if closed else pairs[1:-1])  7.32 us
    pallas_call x1, Pallas kernels, on_device(): pl.pallas_call(inner_kernel, out_shape=(shape(rows, width), shape(blocks...  3.54 us
    ppermute x10, waiting for transfers between devices, swap(): return lax.ppermute(value, AXES, pairs)  2.68 us
    pallas_call x1, Pallas kernels, on_device(): pl.pallas_call(inner_back_kernel, out_shape=(shape(rows, width), shape(2...  2.22 us
    pallas_call x1, Pallas kernels, on_device(): pl.pallas_call(halo_kernel, out_shape=(shape(rim, width), shape(rim, widt...  1 us
    pallas_call x1, Pallas kernels, on_device(): pl.pallas_call(rim_back_kernel, out_shape=(shape(rows, width), shape(4 *...  0.88 us
    pallas_call x1, Pallas kernels, on_device(): pl.pallas_call(functools.partial(last_kernel, norm_scale), out_shape=(sha...  0.85 us
  transfers between devices with their start and end apart: 12, of which 4 were waited for; matrix products, arithmetic and copies ran while one was open for 0% of the time, Pallas kernels for 21%

profile of v23, /device:TPU:0, one launch (start us, length us, event | category | flops | bytes accessed | tf_op | source)
XLA Modules:
  0.0 32.4 jit_solution(6294805966148194754)
XLA Ops:
  0.6 1.0 %halo_rows.1 = (bf16[256,256]{1,0:T(8,128)(2,1)S(1)}, bf16[256,256]{1,0:T(8,128)(2,1)S(1)}) custom-call(bf16[1536,256]{1,0:T(8,128)(2,1)} %feat_hbm.3), custom_call_target="tpu_custom_call" | custom-call | flops 60000000 | bytes 300000 | tf_op jit(solution)/shard_map/halo_rows/pallas_call | solution.py:424
  1.6 3.0 %collective-permute-start = (bf16[256,256]{1,0:T(8,128)(2,1)S(1)}, bf16[256,256]{1,0:T(8,128)(2,1)S(1)}, u32[]{:S(2)}, u32[]{:S(2)}) collective-permute-start(bf16[256,256]{1,0:T(8,128)(2,1)S(1)} %get-tuple-element.36), channel_id=1, source_target_pairs={{0,1},{1,0},{2,3},{3,2},{4,5},{5,4},{6,7},{7,6},{8,9},{9,8},{10,11... | collective-permute-start | bytes 393224 | tf_op jit(solution)/shard_map/ppermute | solution.py:358
  4.7 3.6 %collective-permute-start.1 = (bf16[256,256]{1,0:T(8,128)(2,1)S(1)}, bf16[256,256]{1,0:T(8,128)(2,1)S(1)}, u32[]{:S(2)}, u32[]{:S(2)}) collective-permute-start(bf16[256,256]{1,0:T(8,128)(2,1)S(1)} %get-tuple-element.37), channel_id=1, source_target_pairs={{0,31},{1,2},{2,1},{3,4},{4,3},{5,6},{6,5},{7,8},{8,7},{9,10},{10,... | collective-permute-start | bytes 393224 | tf_op jit(solution)/shard_map/ppermute | solution.py:363
  8.3 3.5 %inner_rows.1 = (bf16[1536,256]{1,0:T(8,128)(2,1)}, s32[36]{0:T(128)S(1)}, bf16[1024,256]{1,0:T(8,128)(2,1)S(1)}, f32[256,256]{1,0:T(8,128)S(1)}, f32[8,256]{1,0...) custom-call(s32[3,12]{1,0:T(4,128)} %bitcast.3, ...), custom_call_target="tpu_custom_call" | custom-call | flops 600000000 | bytes 3000000 | tf_op jit(solution)/shard_map/inner_rows/pallas_call | solution.py:439
  11.9 0.0 collective-permute-done.first_ref
  11.9 0.8 %collective-permute-done.1.second_ref = bf16[256,256]{1,0:T(8,128)(2,1)S(1)} collective-permute-done((bf16[256,256]{1,0:T(8,128)(2,1)S(1)}, bf16[256,256]{1,0:T(8,128)(2,1)S(1)}, u32[]{:S(2)}, u32[]{:S(2)}) %collective-permute-start.1) | collective-permute-done | bytes 131104 | tf_op jit(solution)/shard_map/ppermute | solution.py:363
  12.7 0.8 %rim_rows.1 = (bf16[512,256]{1,0:T(8,128)(2,1)S(1)}, bf16[512,256]{1,0:T(8,128)(2,1)S(1)}, bf16[136,256]{1,0:T(8,128)(2,1)S(1)}, f32[136,256]{1,0:T(8,128)S(1)}) custom-call(bf16[256,256]{1,0:T(8,128)(2,1)S(1)} %get-tuple-element.32.weight_ref, f32[1,256]{1,0:T(1,128)S(1)} %get-tuple-element.34.bias_ref, f32[512,256]{1,0:T(8,128)S(1)} %get-tuple-element.35.own_ref, ...), custom_call_target="tpu_custom_call" | custom-call | flops 240000000 | bytes 1200000 | tf_op jit(solution)/shard_map/rim_rows/pallas_call | solution.py:475
  13.5 0.1 collective-permute-start.2
  13.6 0.9 %rim_rows_back.1 = (bf16[1536,256]{1,0:T(8,128)(2,1)}, f32[8,256,128]{2,1,0:T(8,128)S(1)}, bf16[256,256]{1,0:T(8,128)(2,1)S(1)}, bf16[256,256]{1,0:T(8,128)(2,1)S(1)}, f32[8,128]{1,0:T(8,128)S(1)}) custom-call(bf16[256,256]{1,0:T(8,128)(2,1)S(1)} %get-tuple-element.32.weight_ref, ...), custom_call_target="tpu_custom_call", output_to_operand_aliasing={{0}: (4, {})} | custom-call | flops 240000000 | bytes 1200000 | tf_op jit(solution)/shard_map/rim_rows_back/pallas_call | solution.py:496
  14.4 0.4 %collective-permute-done.2.refs_1_ = bf16[136,256]{1,0:T(8,128)(2,1)S(1)} collective-permute-done((bf16[136,256]{1,0:T(8,128)(2,1)S(1)}, bf16[136,256]{1,0:T(8,128)(2,1)S(1)}, u32[]{:S(2)}, u32[]{:S(2)}) %collective-permute-start.2) | collective-permute-done | bytes 69664 | tf_op jit(solution)/shard_map/ppermute | solution.py:358
  14.8 0.1 collective-permute-start.5
  14.9 1.0 %collective-permute-start.4 = (bf16[136,256]{1,0:T(8,128)(2,1)S(1)}, bf16[136,256]{1,0:T(8,128)(2,1)S(1)}, u32[]{:S(2)}, u32[]{:S(2)}) collective-permute-start(bf16[136,256]{1,0:T(8,128)(2,1)S(1)} %add_halves.3.refs_0_), channel_id=1, source_target_pairs={{0,5},{1,4},{2,18},{3,19},{4,1},{5,0},{6,22},{7,23},{8,13},{9,12},... | collective-permute-start | bytes 208904 | tf_op jit(solution)/shard_map/ppermute | solution.py:358
  15.9 2.4 %collective-permute-start.3 = (bf16[136,256]{1,0:T(8,128)(2,1)S(1)}, bf16[136,256]{1,0:T(8,128)(2,1)S(1)}, u32[]{:S(2)}, u32[]{:S(2)}) collective-permute-start(bf16[136,256]{1,0:T(8,128)(2,1)S(1)} %add_halves.3.refs_0_), channel_id=1, source_target_pairs={{0,4},{1,5},{2,10},{3,11},{4,0},{5,1},{6,14},{7,15},{8,12},{9,13},... | collective-permute-start | bytes 208904 | tf_op jit(solution)/shard_map/ppermute | solution.py:358
  18.4 3.7 %collective-permute-start.9 = (bf16[256,256]{1,0:T(8,128)(2,1)S(1)}, bf16[256,256]{1,0:T(8,128)(2,1)S(1)}, u32[]{:S(2)}, u32[]{:S(2)}) collective-permute-start(bf16[256,256]{1,0:T(8,128)(2,1)S(1)} %get-tuple-element.53), channel_id=1, source_target_pairs={{0,31},{1,2},{2,1},{3,4},{4,3},{5,6},{6,5},{7,8},{8,7},{9,10},{10,... | collective-permute-start | bytes 393224 | tf_op jit(solution)/shard_map/ppermute | solution.py:363
  22.1 0.0 collective-permute-done.5.refs_3_
  22.1 0.0 collective-permute-done.4.refs_2_
  22.1 0.0 collective-permute-done.3.refs_1_
  22.1 1.7 %collective-permute-start.8 = (bf16[136,256]{1,0:T(8,128)(2,1)S(1)}, bf16[136,256]{1,0:T(8,128)(2,1)S(1)}, u32[]{:S(2)}, u32[]{:S(2)}) collective-permute-start(bf16[136,256]{1,0:T(8,128)(2,1)S(1)} %add_halves.4.refs_0_), channel_id=1, source_target_pairs={{0,24},{1,25},{2,3},{3,2},{4,28},{5,29},{6,7},{7,6},{8,16},{9,17},... | collective-permute-start | bytes 208904 | tf_op jit(solution)/shard_map/ppermute | solution.py:358
  23.9 0.0 collective-permute-start.7
  23.9 2.7 %collective-permute-start.6 = (bf16[136,256]{1,0:T(8,128)(2,1)S(1)}, bf16[136,256]{1,0:T(8,128)(2,1)S(1)}, u32[]{:S(2)}, u32[]{:S(2)}) collective-permute-start(bf16[136,256]{1,0:T(8,128)(2,1)S(1)} %add_halves.4.refs_0_), channel_id=1, source_target_pairs={{0,8},{1,9},{2,6},{3,7},{4,12},{5,13},{6,2},{7,3},{8,0},{9,1},{10,... | collective-permute-start | bytes 208904 | tf_op jit(solution)/shard_map/ppermute | solution.py:358
  26.6 0.3 collective-permute-start.11
  26.9 2.2 %inner_rows_back.1 = (bf16[1536,256]{1,0:T(8,128)(2,1)}, f32[512,256]{1,0:T(8,128)S(1)}, f32[8,128]{1,0:T(8,128)S(1)}) custom-call(s32[36]{0:T(128)S(1)} %get-tuple-element.48.place_in, bf16[256,256]{1,0:T(8,128)(2,1)S(1)} %get-tuple-element.32.weight_ref, bf16[8,3,128,128]{3,2,1,0:T(8,128)(2,1)S(1)} %get-tuple-element.49.adj_ref, ...), custom_call_target="tpu_custom_call" | custom-call | flops 360000000 | bytes 1800000 | tf_op jit(solution)/shard_map/inner_rows_back/pallas_call | solution.py:518
  29.1 0.0 collective-permute-done.9.refs_5_.second_ref
  29.1 0.0 collective-permute-done.8.refs_3_
  29.1 0.7 %collective-permute-done.7.refs_2_ = bf16[136,256]{1,0:T(8,128)(2,1)S(1)} collective-permute-done((bf16[136,256]{1,0:T(8,128)(2,1)S(1)}, bf16[136,256]{1,0:T(8,128)(2,1)S(1)}, u32[]{:S(2)}, u32[]{:S(2)}) %collective-permute-start.7) | collective-permute-done | bytes 69664 | tf_op jit(solution)/shard_map/ppermute | solution.py:358
  29.8 0.0 collective-permute-done.6.refs_1_
  29.8 0.1 collective-permute-start.10
  29.9 1.6 %collective-permute-done.11.first_ref = bf16[256,256]{1,0:T(8,128)(2,1)S(1)} collective-permute-done((bf16[256,256]{1,0:T(8,128)(2,1)S(1)}, bf16[256,256]{1,0:T(8,128)(2,1)S(1)}, u32[]{:S(2)}, u32[]{:S(2)}) %collective-permute-start.11) | collective-permute-done | bytes 131104 | tf_op jit(solution)/shard_map/ppermute | solution.py:358
  31.5 0.0 collective-permute-done.10.other_ref
  31.5 0.9 %last_step.1 = (f32[256,256]{1,0:T(8,128)}, f32[1,256]{1,0:T(1,128)}, bf16[1536,256]{1,0:T(8,128)(2,1)}) custom-call(bf16[136,256]{1,0:T(8,128)(2,1)S(1)} %add_halves.5.own_ref, bf16[136,256]{1,0:T(8,128)(2,1)S(1)} %collective-permute-done.10.other_ref, f32[512,256]{1,0:T(8,128)S(1)} %get-tuple-element.54.edge_ref, ...), custom_call_target="tpu_custom_call", output_to_operand_aliasing={{2}: (5, {})} | custom-call | tf_op jit(solution)/shard_map/last_step/pallas_call | solution.py:537
  (3 shorter events, 0.1 us)
Async XLA Ops:
  1.6 10.2 %collective-permute-start = (bf16[256,256]{1,0:T(8,128)(2,1)S(1)}, bf16[256,256]{1,0:T(8,128)(2,1)S(1)}, u32[]{:S(2)}, u32[]{:S(2)}) collective-permute-start(bf16[256,256]{1,0:T(8,128)(2,1)S(1)} %get-tuple-element.36), channel_id=1, source_target_pairs={{0,1},{1,0},{2,3},{3,2},{4,5},{5,4},{6,7},{7,6},{8,9},{9,8},{10,11... | collective-permute-start | bytes 393224 | tf_op jit(solution)/shard_map/ppermute | solution.py:358
  4.7 8.0 %collective-permute-start.1 = (bf16[256,256]{1,0:T(8,128)(2,1)S(1)}, bf16[256,256]{1,0:T(8,128)(2,1)S(1)}, u32[]{:S(2)}, u32[]{:S(2)}) collective-permute-start(bf16[256,256]{1,0:T(8,128)(2,1)S(1)} %get-tuple-element.37), channel_id=1, source_target_pairs={{0,31},{1,2},{2,1},{3,4},{4,3},{5,6},{6,5},{7,8},{8,7},{9,10},{10,... | collective-permute-start | bytes 393224 | tf_op jit(solution)/shard_map/ppermute | solution.py:363
  13.5 1.3 %collective-permute-start.2 = (bf16[136,256]{1,0:T(8,128)(2,1)S(1)}, bf16[136,256]{1,0:T(8,128)(2,1)S(1)}, u32[]{:S(2)}, u32[]{:S(2)}) collective-permute-start(bf16[136,256]{1,0:T(8,128)(2,1)S(1)} %get-tuple-element.46), channel_id=1, source_target_pairs={{0,2},{1,3},{2,0},{3,1},{4,6},{5,7},{6,4},{7,5},{8,10},{9,11},{10,... | collective-permute-start | bytes 208904 | tf_op jit(solution)/shard_map/ppermute | solution.py:358
  14.8 7.2 %collective-permute-start.5 = (bf16[136,256]{1,0:T(8,128)(2,1)S(1)}, bf16[136,256]{1,0:T(8,128)(2,1)S(1)}, u32[]{:S(2)}, u32[]{:S(2)}) collective-permute-start(bf16[136,256]{1,0:T(8,128)(2,1)S(1)} %add_halves.3.refs_0_), channel_id=1, source_target_pairs={{0,1},{1,0},{2,26},{3,27},{4,5},{5,4},{6,30},{7,31},{8,9},{9,8},{1... | collective-permute-start | bytes 208904 | tf_op jit(solution)/shard_map/ppermute | solution.py:358
  14.9 7.1 %collective-permute-start.4 = (bf16[136,256]{1,0:T(8,128)(2,1)S(1)}, bf16[136,256]{1,0:T(8,128)(2,1)S(1)}, u32[]{:S(2)}, u32[]{:S(2)}) collective-permute-start(bf16[136,256]{1,0:T(8,128)(2,1)S(1)} %add_halves.3.refs_0_), channel_id=1, source_target_pairs={{0,5},{1,4},{2,18},{3,19},{4,1},{5,0},{6,22},{7,23},{8,13},{9,12},... | collective-permute-start | bytes 208904 | tf_op jit(solution)/shard_map/ppermute | solution.py:358
  15.9 6.1 %collective-permute-start.3 = (bf16[136,256]{1,0:T(8,128)(2,1)S(1)}, bf16[136,256]{1,0:T(8,128)(2,1)S(1)}, u32[]{:S(2)}, u32[]{:S(2)}) collective-permute-start(bf16[136,256]{1,0:T(8,128)(2,1)S(1)} %add_halves.3.refs_0_), channel_id=1, source_target_pairs={{0,4},{1,5},{2,10},{3,11},{4,0},{5,1},{6,14},{7,15},{8,12},{9,13},... | collective-permute-start | bytes 208904 | tf_op jit(solution)/shard_map/ppermute | solution.py:358
  18.4 10.7 %collective-permute-start.9 = (bf16[256,256]{1,0:T(8,128)(2,1)S(1)}, bf16[256,256]{1,0:T(8,128)(2,1)S(1)}, u32[]{:S(2)}, u32[]{:S(2)}) collective-permute-start(bf16[256,256]{1,0:T(8,128)(2,1)S(1)} %get-tuple-element.53), channel_id=1, source_target_pairs={{0,31},{1,2},{2,1},{3,4},{4,3},{5,6},{6,5},{7,8},{8,7},{9,10},{10,... | collective-permute-start | bytes 393224 | tf_op jit(solution)/shard_map/ppermute | solution.py:363
  22.1 7.0 %collective-permute-start.8 = (bf16[136,256]{1,0:T(8,128)(2,1)S(1)}, bf16[136,256]{1,0:T(8,128)(2,1)S(1)}, u32[]{:S(2)}, u32[]{:S(2)}) collective-permute-start(bf16[136,256]{1,0:T(8,128)(2,1)S(1)} %add_halves.4.refs_0_), channel_id=1, source_target_pairs={{0,24},{1,25},{2,3},{3,2},{4,28},{5,29},{6,7},{7,6},{8,16},{9,17},... | collective-permute-start | bytes 208904 | tf_op jit(solution)/shard_map/ppermute | solution.py:358
  23.9 5.9 %collective-permute-start.7 = (bf16[136,256]{1,0:T(8,128)(2,1)S(1)}, bf16[136,256]{1,0:T(8,128)(2,1)S(1)}, u32[]{:S(2)}, u32[]{:S(2)}) collective-permute-start(bf16[136,256]{1,0:T(8,128)(2,1)S(1)} %add_halves.4.refs_0_), channel_id=1, source_target_pairs={{0,16},{1,17},{2,7},{3,6},{4,20},{5,21},{6,3},{7,2},{8,24},{9,25},... | collective-permute-start | bytes 208904 | tf_op jit(solution)/shard_map/ppermute | solution.py:358
  23.9 5.9 %collective-permute-start.6 = (bf16[136,256]{1,0:T(8,128)(2,1)S(1)}, bf16[136,256]{1,0:T(8,128)(2,1)S(1)}, u32[]{:S(2)}, u32[]{:S(2)}) collective-permute-start(bf16[136,256]{1,0:T(8,128)(2,1)S(1)} %add_halves.4.refs_0_), channel_id=1, source_target_pairs={{0,8},{1,9},{2,6},{3,7},{4,12},{5,13},{6,2},{7,3},{8,0},{9,1},{10,... | collective-permute-start | bytes 208904 | tf_op jit(solution)/shard_map/ppermute | solution.py:358
  26.6 5.0 %collective-permute-start.11 = (bf16[256,256]{1,0:T(8,128)(2,1)S(1)}, bf16[256,256]{1,0:T(8,128)(2,1)S(1)}, u32[]{:S(2)}, u32[]{:S(2)}) collective-permute-start(bf16[256,256]{1,0:T(8,128)(2,1)S(1)} %get-tuple-element.55), channel_id=1, source_target_pairs={{0,1},{1,0},{2,3},{3,2},{4,5},{5,4},{6,7},{7,6},{8,9},{9,8},{10,11... | collective-permute-start | bytes 393224 | tf_op jit(solution)/shard_map/ppermute | solution.py:358
  29.8 1.7 %collective-permute-start.10 = (bf16[136,256]{1,0:T(8,128)(2,1)S(1)}, bf16[136,256]{1,0:T(8,128)(2,1)S(1)}, u32[]{:S(2)}, u32[]{:S(2)}) collective-permute-start(bf16[136,256]{1,0:T(8,128)(2,1)S(1)} %add_halves.5.own_ref), channel_id=1, source_target_pairs={{0,2},{1,3},{2,0},{3,1},{4,6},{5,7},{6,4},{7,5},{8,10},{9,11},{10,... | collective-permute-start | bytes 208904 | tf_op jit(solution)/shard_map/ppermute | solution.py:358

commit v24 on v20

--- a/solution.py
+++ b/solution.py
@@ -179,7 +179,7 @@
 
 
 def rim_kernel(
-    weight_ref, bias_ref, own_ref, first_ref, second_ref, dense, cot_ref, partial_ref, sums_ref,
+    weight_ref, bias_ref, own_ref, second_ref, first_ref, dense, cot_ref, partial_ref, sums_ref,
     act_ref, grad_ref, send_ref, keep_ref,
     halo, agg_all,
 ):
@@ -431,8 +431,8 @@
         cost_estimate=cost(0.05),
         name="halo_rows",
     )(in_hbm(features))
+    second_halo = with_next(second_rim, count, True)
     first_halo = swap(first_rim, [1] * count)
-    second_halo = with_next(second_rim, count, True)
     (
         activated, places, grad_inner, partial, sums, weight_near, bias_near, dense, own_part,
         cot_rim, adj_inner,
@@ -490,7 +490,7 @@
         cost_estimate=cost(0.2),
         name="rim_rows",
     )(
-        weight_near, bias_near, own_part, first_halo, second_halo, dense, cot_rim, partial, sums,
+        weight_near, bias_near, own_part, second_halo, first_halo, dense, cot_rim, partial, sums,
     )
     mark = shape(8, 128, dtype=jnp.float32)
     activated, rim_spread, first_spill, second_spill, first_mark = pl.pallas_call(

time: 32 us -> 32.6 us (1.019)
  waiting for transfers between devices: 5.42 us -> 6.33 us
    ppermute x10, starting transfers between devices: 12 us -> 8.91 us  [swap(): return lax.ppermute(value, AXES, pairs)]
    ppermute x2, starting transfers between devices: 4.29 us -> 7.09 us  [with_next(): return lax.ppermute(value, AXES, pairs if closed else pairs[1:-1])]
    ppermute x10, waiting for transfers between devices: 4.63 us -> 6.33 us  [swap(): return lax.ppermute(value, AXES, pairs)]
    ppermute x2, waiting for transfers between devices: 0.8 us -> 0.01 us  [with_next(): return lax.ppermute(value, AXES, pairs if closed else pairs[1:-1])]
where the time goes in v24:
time: 32.6 us; the launch traced here: 32.5 us
  starting transfers between devices  16 us (49%)
  Pallas kernels  9.39 us (29%)
  waiting for transfers between devices  6.33 us (19%)
  between operations  0.73 us (2%)
    ppermute x10, starting transfers between devices, swap(): return lax.ppermute(value, AXES, pairs)  8.91 us
    ppermute x2, starting transfers between devices, with_next(): return lax.ppermute(value, AXES, pairs if closed else pairs[1:-1])  7.09 us
    ppermute x10, waiting for transfers between devices, swap(): return lax.ppermute(value, AXES, pairs)  6.33 us
    pallas_call x1, Pallas kernels, on_device(): pl.pallas_call(inner_kernel, out_shape=(shape(rows, width), shape(blocks...  3.54 us
    pallas_call x1, Pallas kernels, on_device(): pl.pallas_call(inner_back_kernel, out_shape=(shape(rows, width), shape(2...  2.21 us
    pallas_call x1, Pallas kernels, on_device(): pl.pallas_call(halo_kernel, out_shape=(shape(rim, width), shape(rim, widt...  1 us
    pallas_call x1, Pallas kernels, on_device(): pl.pallas_call(rim_back_kernel, out_shape=(shape(rows, width), shape(4 *...  0.88 us
    pallas_call x1, Pallas kernels, on_device(): pl.pallas_call(functools.partial(last_kernel, norm_scale), out_shape=(sha...  0.85 us
  transfers between devices with their start and end apart: 12, of which 8 were waited for; matrix products, arithmetic and copies ran while one was open for 0% of the time, Pallas kernels for 21%

profile of v24, /device:TPU:0, one launch (start us, length us, event | category | flops | bytes accessed | tf_op | source)
XLA Modules:
  0.0 32.5 jit_solution(17690400489439595995)
XLA Ops:
  0.6 1.0 %halo_rows.1 = (bf16[256,256]{1,0:T(8,128)(2,1)S(1)}, bf16[256,256]{1,0:T(8,128)(2,1)S(1)}) custom-call(bf16[1536,256]{1,0:T(8,128)(2,1)} %feat_hbm.3), custom_call_target="tpu_custom_call" | custom-call | flops 60000000 | bytes 300000 | tf_op jit(solution)/shard_map/halo_rows/pallas_call | solution.py:424
  1.6 6.4 %collective-permute-start = (bf16[256,256]{1,0:T(8,128)(2,1)S(1)}, bf16[256,256]{1,0:T(8,128)(2,1)S(1)}, u32[]{:S(2)}, u32[]{:S(2)}) collective-permute-start(bf16[256,256]{1,0:T(8,128)(2,1)S(1)} %get-tuple-element.36), channel_id=1, source_target_pairs={{0,31},{1,2},{2,1},{3,4},{4,3},{5,6},{6,5},{7,8},{8,7},{9,10},{10,... | collective-permute-start | bytes 393224 | tf_op jit(solution)/shard_map/ppermute | solution.py:363
  8.1 0.0 collective-permute-start.1
  8.1 3.5 %inner_rows.1 = (bf16[1536,256]{1,0:T(8,128)(2,1)}, s32[36]{0:T(128)S(1)}, bf16[1024,256]{1,0:T(8,128)(2,1)S(1)}, f32[256,256]{1,0:T(8,128)S(1)}, f32[8,256]{1,0...) custom-call(s32[3,12]{1,0:T(4,128)} %bitcast.3, ...), custom_call_target="tpu_custom_call" | custom-call | flops 600000000 | bytes 3000000 | tf_op jit(solution)/shard_map/inner_rows/pallas_call | solution.py:439
  11.6 0.0 collective-permute-done.second_ref
  11.6 1.4 %collective-permute-done.1.first_ref = bf16[256,256]{1,0:T(8,128)(2,1)S(1)} collective-permute-done((bf16[256,256]{1,0:T(8,128)(2,1)S(1)}, bf16[256,256]{1,0:T(8,128)(2,1)S(1)}, u32[]{:S(2)}, u32[]{:S(2)}) %collective-permute-start.1) | collective-permute-done | bytes 131104 | tf_op jit(solution)/shard_map/ppermute | solution.py:358
  13.0 0.8 %rim_rows.1 = (bf16[512,256]{1,0:T(8,128)(2,1)S(1)}, bf16[512,256]{1,0:T(8,128)(2,1)S(1)}, bf16[136,256]{1,0:T(8,128)(2,1)S(1)}, f32[136,256]{1,0:T(8,128)S(1)}) custom-call(bf16[256,256]{1,0:T(8,128)(2,1)S(1)} %get-tuple-element.32.weight_ref, f32[1,256]{1,0:T(1,128)S(1)} %get-tuple-element.34.bias_ref, f32[512,256]{1,0:T(8,128)S(1)} %get-tuple-element.35.own_ref, ...), custom_call_target="tpu_custom_call" | custom-call | flops 240000000 | bytes 1200000 | tf_op jit(solution)/shard_map/rim_rows/pallas_call | solution.py:475
  13.9 0.1 collective-permute-start.2
  13.9 0.9 %rim_rows_back.1 = (bf16[1536,256]{1,0:T(8,128)(2,1)}, f32[8,256,128]{2,1,0:T(8,128)S(1)}, bf16[256,256]{1,0:T(8,128)(2,1)S(1)}, bf16[256,256]{1,0:T(8,128)(2,1)S(1)}, f32[8,128]{1,0:T(8,128)S(1)}) custom-call(bf16[256,256]{1,0:T(8,128)(2,1)S(1)} %get-tuple-element.32.weight_ref, ...), custom_call_target="tpu_custom_call", output_to_operand_aliasing={{0}: (4, {})} | custom-call | flops 240000000 | bytes 1200000 | tf_op jit(solution)/shard_map/rim_rows_back/pallas_call | solution.py:496
  14.8 0.4 %collective-permute-done.2.refs_1_ = bf16[136,256]{1,0:T(8,128)(2,1)S(1)} collective-permute-done((bf16[136,256]{1,0:T(8,128)(2,1)S(1)}, bf16[136,256]{1,0:T(8,128)(2,1)S(1)}, u32[]{:S(2)}, u32[]{:S(2)}) %collective-permute-start.2) | collective-permute-done | bytes 69664 | tf_op jit(solution)/shard_map/ppermute | solution.py:358
  15.2 0.7 %collective-permute-start.5 = (bf16[136,256]{1,0:T(8,128)(2,1)S(1)}, bf16[136,256]{1,0:T(8,128)(2,1)S(1)}, u32[]{:S(2)}, u32[]{:S(2)}) collective-permute-start(bf16[136,256]{1,0:T(8,128)(2,1)S(1)} %add_halves.3.refs_0_), channel_id=1, source_target_pairs={{0,1},{1,0},{2,26},{3,27},{4,5},{5,4},{6,30},{7,31},{8,9},{9,8},{1... | collective-permute-start | bytes 208904 | tf_op jit(solution)/shard_map/ppermute | solution.py:358
  15.9 1.1 %collective-permute-start.4 = (bf16[136,256]{1,0:T(8,128)(2,1)S(1)}, bf16[136,256]{1,0:T(8,128)(2,1)S(1)}, u32[]{:S(2)}, u32[]{:S(2)}) collective-permute-start(bf16[136,256]{1,0:T(8,128)(2,1)S(1)} %add_halves.3.refs_0_), channel_id=1, source_target_pairs={{0,5},{1,4},{2,18},{3,19},{4,1},{5,0},{6,22},{7,23},{8,13},{9,12},... | collective-permute-start | bytes 208904 | tf_op jit(solution)/shard_map/ppermute | solution.py:358
  17.0 1.8 %collective-permute-start.3 = (bf16[136,256]{1,0:T(8,128)(2,1)S(1)}, bf16[136,256]{1,0:T(8,128)(2,1)S(1)}, u32[]{:S(2)}, u32[]{:S(2)}) collective-permute-start(bf16[136,256]{1,0:T(8,128)(2,1)S(1)} %add_halves.3.refs_0_), channel_id=1, source_target_pairs={{0,4},{1,5},{2,10},{3,11},{4,0},{5,1},{6,14},{7,15},{8,12},{9,13},... | collective-permute-start | bytes 208904 | tf_op jit(solution)/shard_map/ppermute | solution.py:358
  18.8 0.7 %collective-permute-start.9 = (bf16[256,256]{1,0:T(8,128)(2,1)S(1)}, bf16[256,256]{1,0:T(8,128)(2,1)S(1)}, u32[]{:S(2)}, u32[]{:S(2)}) collective-permute-start(bf16[256,256]{1,0:T(8,128)(2,1)S(1)} %get-tuple-element.53), channel_id=1, source_target_pairs={{1,2},{2,1},{3,4},{4,3},{5,6},{6,5},{7,8},{8,7},{9,10},{10,9},{11,... | collective-permute-start | bytes 393224 | tf_op jit(solution)/shard_map/ppermute | solution.py:363
  19.4 0.2 collective-permute-done.5.refs_3_
  19.6 1.5 %collective-permute-done.4.refs_2_ = bf16[136,256]{1,0:T(8,128)(2,1)S(1)} collective-permute-done((bf16[136,256]{1,0:T(8,128)(2,1)S(1)}, bf16[136,256]{1,0:T(8,128)(2,1)S(1)}, u32[]{:S(2)}, u32[]{:S(2)}) %collective-permute-start.4) | collective-permute-done | bytes 69664 | tf_op jit(solution)/shard_map/ppermute | solution.py:358
  21.1 0.7 %collective-permute-done.3.refs_1_ = bf16[136,256]{1,0:T(8,128)(2,1)S(1)} collective-permute-done((bf16[136,256]{1,0:T(8,128)(2,1)S(1)}, bf16[136,256]{1,0:T(8,128)(2,1)S(1)}, u32[]{:S(2)}, u32[]{:S(2)}) %collective-permute-start.3) | collective-permute-done | bytes 69664 | tf_op jit(solution)/shard_map/ppermute | solution.py:358
  21.8 3.2 %collective-permute-start.8 = (bf16[136,256]{1,0:T(8,128)(2,1)S(1)}, bf16[136,256]{1,0:T(8,128)(2,1)S(1)}, u32[]{:S(2)}, u32[]{:S(2)}) collective-permute-start(bf16[136,256]{1,0:T(8,128)(2,1)S(1)} %add_halves.4.refs_0_), channel_id=1, source_target_pairs={{0,24},{1,25},{2,3},{3,2},{4,28},{5,29},{6,7},{7,6},{8,16},{9,17},... | collective-permute-start | bytes 208904 | tf_op jit(solution)/shard_map/ppermute | solution.py:358
  25.0 0.0 collective-permute-start.7
  25.0 1.3 %collective-permute-start.6 = (bf16[136,256]{1,0:T(8,128)(2,1)S(1)}, bf16[136,256]{1,0:T(8,128)(2,1)S(1)}, u32[]{:S(2)}, u32[]{:S(2)}) collective-permute-start(bf16[136,256]{1,0:T(8,128)(2,1)S(1)} %add_halves.4.refs_0_), channel_id=1, source_target_pairs={{0,8},{1,9},{2,6},{3,7},{4,12},{5,13},{6,2},{7,3},{8,0},{9,1},{10,... | collective-permute-start | bytes 208904 | tf_op jit(solution)/shard_map/ppermute | solution.py:358
  26.3 0.8 %collective-permute-start.11 = (bf16[256,256]{1,0:T(8,128)(2,1)S(1)}, bf16[256,256]{1,0:T(8,128)(2,1)S(1)}, u32[]{:S(2)}, u32[]{:S(2)}) collective-permute-start(bf16[256,256]{1,0:T(8,128)(2,1)S(1)} %get-tuple-element.55), channel_id=1, source_target_pairs={{0,1},{1,0},{2,3},{3,2},{4,5},{5,4},{6,7},{7,6},{8,9},{9,8},{10,11... | collective-permute-start | bytes 393224 | tf_op jit(solution)/shard_map/ppermute | solution.py:358
  27.0 2.2 %inner_rows_back.1 = (bf16[1536,256]{1,0:T(8,128)(2,1)}, f32[512,256]{1,0:T(8,128)S(1)}, f32[8,128]{1,0:T(8,128)S(1)}) custom-call(s32[36]{0:T(128)S(1)} %get-tuple-element.48.place_in, bf16[256,256]{1,0:T(8,128)(2,1)S(1)} %get-tuple-element.32.weight_ref, bf16[8,3,128,128]{3,2,1,0:T(8,128)(2,1)S(1)} %get-tuple-element.49.adj_ref, ...), custom_call_target="tpu_custom_call" | custom-call | flops 360000000 | bytes 1800000 | tf_op jit(solution)/shard_map/inner_rows_back/pallas_call | solution.py:518
  29.3 0.0 collective-permute-done.9.refs_5_.second_ref
  29.3 0.0 collective-permute-done.8.refs_3_
  29.3 0.9 %collective-permute-done.7.refs_2_ = bf16[136,256]{1,0:T(8,128)(2,1)S(1)} collective-permute-done((bf16[136,256]{1,0:T(8,128)(2,1)S(1)}, bf16[136,256]{1,0:T(8,128)(2,1)S(1)}, u32[]{:S(2)}, u32[]{:S(2)}) %collective-permute-start.7) | collective-permute-done | bytes 69664 | tf_op jit(solution)/shard_map/ppermute | solution.py:358
  30.2 0.0 collective-permute-done.6.refs_1_
  30.3 0.1 collective-permute-start.10
  30.4 0.9 %collective-permute-done.11.first_ref = bf16[256,256]{1,0:T(8,128)(2,1)S(1)} collective-permute-done((bf16[256,256]{1,0:T(8,128)(2,1)S(1)}, bf16[256,256]{1,0:T(8,128)(2,1)S(1)}, u32[]{:S(2)}, u32[]{:S(2)}) %collective-permute-start.11) | collective-permute-done | bytes 131104 | tf_op jit(solution)/shard_map/ppermute | solution.py:358
  31.3 0.4 %collective-permute-done.10.other_ref = bf16[136,256]{1,0:T(8,128)(2,1)S(1)} collective-permute-done((bf16[136,256]{1,0:T(8,128)(2,1)S(1)}, bf16[136,256]{1,0:T(8,128)(2,1)S(1)}, u32[]{:S(2)}, u32[]{:S(2)}) %collective-permute-start.10) | collective-permute-done | bytes 69664 | tf_op jit(solution)/shard_map/ppermute | solution.py:358
  31.6 0.9 %last_step.1 = (f32[256,256]{1,0:T(8,128)}, f32[1,256]{1,0:T(1,128)}, bf16[1536,256]{1,0:T(8,128)(2,1)}) custom-call(bf16[136,256]{1,0:T(8,128)(2,1)S(1)} %add_halves.5.own_ref, bf16[136,256]{1,0:T(8,128)(2,1)S(1)} %collective-permute-done.10.other_ref, f32[512,256]{1,0:T(8,128)S(1)} %get-tuple-element.54.edge_ref, ...), custom_call_target="tpu_custom_call", output_to_operand_aliasing={{2}: (5, {})} | custom-call | tf_op jit(solution)/shard_map/last_step/pallas_call | solution.py:537
  (3 shorter events, 0.1 us)
Async XLA Ops:
  1.6 10.0 %collective-permute-start = (bf16[256,256]{1,0:T(8,128)(2,1)S(1)}, bf16[256,256]{1,0:T(8,128)(2,1)S(1)}, u32[]{:S(2)}, u32[]{:S(2)}) collective-permute-start(bf16[256,256]{1,0:T(8,128)(2,1)S(1)} %get-tuple-element.36), channel_id=1, source_target_pairs={{0,31},{1,2},{2,1},{3,4},{4,3},{5,6},{6,5},{7,8},{8,7},{9,10},{10,... | collective-permute-start | bytes 393224 | tf_op jit(solution)/shard_map/ppermute | solution.py:363
  8.1 5.0 %collective-permute-start.1 = (bf16[256,256]{1,0:T(8,128)(2,1)S(1)}, bf16[256,256]{1,0:T(8,128)(2,1)S(1)}, u32[]{:S(2)}, u32[]{:S(2)}) collective-permute-start(bf16[256,256]{1,0:T(8,128)(2,1)S(1)} %get-tuple-element.37), channel_id=1, source_target_pairs={{0,1},{1,0},{2,3},{3,2},{4,5},{5,4},{6,7},{7,6},{8,9},{9,8},{10,11... | collective-permute-start | bytes 393224 | tf_op jit(solution)/shard_map/ppermute | solution.py:358
  13.9 1.3 %collective-permute-start.2 = (bf16[136,256]{1,0:T(8,128)(2,1)S(1)}, bf16[136,256]{1,0:T(8,128)(2,1)S(1)}, u32[]{:S(2)}, u32[]{:S(2)}) collective-permute-start(bf16[136,256]{1,0:T(8,128)(2,1)S(1)} %get-tuple-element.46), channel_id=1, source_target_pairs={{0,2},{1,3},{2,0},{3,1},{4,6},{5,7},{6,4},{7,5},{8,10},{9,11},{10,... | collective-permute-start | bytes 208904 | tf_op jit(solution)/shard_map/ppermute | solution.py:358
  15.2 4.4 %collective-permute-start.5 = (bf16[136,256]{1,0:T(8,128)(2,1)S(1)}, bf16[136,256]{1,0:T(8,128)(2,1)S(1)}, u32[]{:S(2)}, u32[]{:S(2)}) collective-permute-start(bf16[136,256]{1,0:T(8,128)(2,1)S(1)} %add_halves.3.refs_0_), channel_id=1, source_target_pairs={{0,1},{1,0},{2,26},{3,27},{4,5},{5,4},{6,30},{7,31},{8,9},{9,8},{1... | collective-permute-start | bytes 208904 | tf_op jit(solution)/shard_map/ppermute | solution.py:358
  15.9 5.2 %collective-permute-start.4 = (bf16[136,256]{1,0:T(8,128)(2,1)S(1)}, bf16[136,256]{1,0:T(8,128)(2,1)S(1)}, u32[]{:S(2)}, u32[]{:S(2)}) collective-permute-start(bf16[136,256]{1,0:T(8,128)(2,1)S(1)} %add_halves.3.refs_0_), channel_id=1, source_target_pairs={{0,5},{1,4},{2,18},{3,19},{4,1},{5,0},{6,22},{7,23},{8,13},{9,12},... | collective-permute-start | bytes 208904 | tf_op jit(solution)/shard_map/ppermute | solution.py:358
  17.0 4.8 %collective-permute-start.3 = (bf16[136,256]{1,0:T(8,128)(2,1)S(1)}, bf16[136,256]{1,0:T(8,128)(2,1)S(1)}, u32[]{:S(2)}, u32[]{:S(2)}) collective-permute-start(bf16[136,256]{1,0:T(8,128)(2,1)S(1)} %add_halves.3.refs_0_), channel_id=1, source_target_pairs={{0,4},{1,5},{2,10},{3,11},{4,0},{5,1},{6,14},{7,15},{8,12},{9,13},... | collective-permute-start | bytes 208904 | tf_op jit(solution)/shard_map/ppermute | solution.py:358
  18.8 10.5 %collective-permute-start.9 = (bf16[256,256]{1,0:T(8,128)(2,1)S(1)}, bf16[256,256]{1,0:T(8,128)(2,1)S(1)}, u32[]{:S(2)}, u32[]{:S(2)}) collective-permute-start(bf16[256,256]{1,0:T(8,128)(2,1)S(1)} %get-tuple-element.53), channel_id=1, source_target_pairs={{1,2},{2,1},{3,4},{4,3},{5,6},{6,5},{7,8},{8,7},{9,10},{10,9},{11,... | collective-permute-start | bytes 393224 | tf_op jit(solution)/shard_map/ppermute | solution.py:363
  21.8 7.4 %collective-permute-start.8 = (bf16[136,256]{1,0:T(8,128)(2,1)S(1)}, bf16[136,256]{1,0:T(8,128)(2,1)S(1)}, u32[]{:S(2)}, u32[]{:S(2)}) collective-permute-start(bf16[136,256]{1,0:T(8,128)(2,1)S(1)} %add_halves.4.refs_0_), channel_id=1, source_target_pairs={{0,24},{1,25},{2,3},{3,2},{4,28},{5,29},{6,7},{7,6},{8,16},{9,17},... | collective-permute-start | bytes 208904 | tf_op jit(solution)/shard_map/ppermute | solution.py:358
  25.0 5.2 %collective-permute-start.7 = (bf16[136,256]{1,0:T(8,128)(2,1)S(1)}, bf16[136,256]{1,0:T(8,128)(2,1)S(1)}, u32[]{:S(2)}, u32[]{:S(2)}) collective-permute-start(bf16[136,256]{1,0:T(8,128)(2,1)S(1)} %add_halves.4.refs_0_), channel_id=1, source_target_pairs={{0,16},{1,17},{2,7},{3,6},{4,20},{5,21},{6,3},{7,2},{8,24},{9,25},... | collective-permute-start | bytes 208904 | tf_op jit(solution)/shard_map/ppermute | solution.py:358
  25.0 5.2 %collective-permute-start.6 = (bf16[136,256]{1,0:T(8,128)(2,1)S(1)}, bf16[136,256]{1,0:T(8,128)(2,1)S(1)}, u32[]{:S(2)}, u32[]{:S(2)}) collective-permute-start(bf16[136,256]{1,0:T(8,128)(2,1)S(1)} %add_halves.4.refs_0_), channel_id=1, source_target_pairs={{0,8},{1,9},{2,6},{3,7},{4,12},{5,13},{6,2},{7,3},{8,0},{9,1},{10,... | collective-permute-start | bytes 208904 | tf_op jit(solution)/shard_map/ppermute | solution.py:358
  26.3 5.0 %collective-permute-start.11 = (bf16[256,256]{1,0:T(8,128)(2,1)S(1)}, bf16[256,256]{1,0:T(8,128)(2,1)S(1)}, u32[]{:S(2)}, u32[]{:S(2)}) collective-permute-start(bf16[256,256]{1,0:T(8,128)(2,1)S(1)} %get-tuple-element.55), channel_id=1, source_target_pairs={{0,1},{1,0},{2,3},{3,2},{4,5},{5,4},{6,7},{7,6},{8,9},{9,8},{10,11... | collective-permute-start | bytes 393224 | tf_op jit(solution)/shard_map/ppermute | solution.py:358
  30.3 1.3 %collective-permute-start.10 = (bf16[136,256]{1,0:T(8,128)(2,1)S(1)}, bf16[136,256]{1,0:T(8,128)(2,1)S(1)}, u32[]{:S(2)}, u32[]{:S(2)}) collective-permute-start(bf16[136,256]{1,0:T(8,128)(2,1)S(1)} %add_halves.5.own_ref), channel_id=1, source_target_pairs={{0,2},{1,3},{2,0},{3,1},{4,6},{5,7},{6,4},{7,5},{8,10},{9,11},{10,... | collective-permute-start | bytes 208904 | tf_op jit(solution)/shard_map/ppermute | solution.py:358

commit v25 on v20

--- a/solution.py
+++ b/solution.py
@@ -365,7 +365,8 @@
 
 def sum_halves(send, keep, count, core_bit, marks):
     others = [bit for bit in range(count.bit_length() - 1) if bit != core_bit]
-    groups = [others[i : i + 2] for i in range(0, len(others), 2)]
+    half = (len(others) + 1) // 2
+    groups = [others[i::half] for i in range(half)]
     groups[0] = groups[0][::-1]
     total = add([keep, swap(send, [1 << core_bit] * count)], jnp.bfloat16, marks.get("core", ()))
     for step in range(len(groups)):

time: 32 us -> 32.6 us (1.019)
  waiting for transfers between devices: 5.42 us -> 5.99 us
    ppermute x10, waiting for transfers between devices: 4.63 us -> 5.19 us  [swap(): return lax.ppermute(value, AXES, pairs)]
  transfers between devices with their start and end apart: 12 -> 12, of which waited for: 8 -> 7; matrix products, arithmetic and copies ran while one was open for 0% -> 0% of each run, Pallas kernels for 21% -> 21%
where the time goes in v25:
time: 32.6 us; the launch traced here: 32.5 us
  starting transfers between devices  16.4 us (50%)
  Pallas kernels  9.39 us (29%)
  waiting for transfers between devices  5.99 us (18%)
  between operations  0.73 us (2%)
    ppermute x10, starting transfers between devices, swap(): return lax.ppermute(value, AXES, pairs)  12.1 us
    ppermute x10, waiting for transfers between devices, swap(): return lax.ppermute(value, AXES, pairs)  5.19 us
    ppermute x2, starting transfers between devices, with_next(): return lax.ppermute(value, AXES, pairs if closed else pairs[1:-1])  4.29 us
    pallas_call x1, Pallas kernels, on_device(): pl.pallas_call(inner_kernel, out_shape=(shape(rows, width), shape(blocks...  3.54 us
    pallas_call x1, Pallas kernels, on_device(): pl.pallas_call(inner_back_kernel, out_shape=(shape(rows, width), shape(2...  2.22 us
    pallas_call x1, Pallas kernels, on_device(): pl.pallas_call(halo_kernel, out_shape=(shape(rim, width), shape(rim, widt...  1 us
    pallas_call x1, Pallas kernels, on_device(): pl.pallas_call(rim_back_kernel, out_shape=(shape(rows, width), shape(4 *...  0.88 us
    pallas_call x1, Pallas kernels, on_device(): pl.pallas_call(functools.partial(last_kernel, norm_scale), out_shape=(sha...  0.85 us
  transfers between devices with their start and end apart: 12, of which 7 were waited for; matrix products, arithmetic and copies ran while one was open for 0% of the time, Pallas kernels for 21%

profile of v25, /device:TPU:0, one launch (start us, length us, event | category | flops | bytes accessed | tf_op | source)
XLA Modules:
  0.0 32.5 jit_solution(1619009809426783175)
XLA Ops:
  0.6 1.0 %halo_rows.1 = (bf16[256,256]{1,0:T(8,128)(2,1)S(1)}, bf16[256,256]{1,0:T(8,128)(2,1)S(1)}) custom-call(bf16[1536,256]{1,0:T(8,128)(2,1)} %feat_hbm.3), custom_call_target="tpu_custom_call" | custom-call | flops 60000000 | bytes 300000 | tf_op jit(solution)/shard_map/halo_rows/pallas_call | solution.py:425
  1.6 3.0 %collective-permute-start = (bf16[256,256]{1,0:T(8,128)(2,1)S(1)}, bf16[256,256]{1,0:T(8,128)(2,1)S(1)}, u32[]{:S(2)}, u32[]{:S(2)}) collective-permute-start(bf16[256,256]{1,0:T(8,128)(2,1)S(1)} %get-tuple-element.36), channel_id=1, source_target_pairs={{0,1},{1,0},{2,3},{3,2},{4,5},{5,4},{6,7},{7,6},{8,9},{9,8},{10,11... | collective-permute-start | bytes 393224 | tf_op jit(solution)/shard_map/ppermute | solution.py:358
  4.7 3.6 %collective-permute-start.1 = (bf16[256,256]{1,0:T(8,128)(2,1)S(1)}, bf16[256,256]{1,0:T(8,128)(2,1)S(1)}, u32[]{:S(2)}, u32[]{:S(2)}) collective-permute-start(bf16[256,256]{1,0:T(8,128)(2,1)S(1)} %get-tuple-element.37), channel_id=1, source_target_pairs={{0,31},{1,2},{2,1},{3,4},{4,3},{5,6},{6,5},{7,8},{8,7},{9,10},{10,... | collective-permute-start | bytes 393224 | tf_op jit(solution)/shard_map/ppermute | solution.py:363
  8.3 3.5 %inner_rows.1 = (bf16[1536,256]{1,0:T(8,128)(2,1)}, s32[36]{0:T(128)S(1)}, bf16[1024,256]{1,0:T(8,128)(2,1)S(1)}, f32[256,256]{1,0:T(8,128)S(1)}, f32[8,256]{1,0...) custom-call(s32[3,12]{1,0:T(4,128)} %bitcast.3, ...), custom_call_target="tpu_custom_call" | custom-call | flops 600000000 | bytes 3000000 | tf_op jit(solution)/shard_map/inner_rows/pallas_call | solution.py:440
  11.9 0.0 collective-permute-done.first_ref
  11.9 0.8 %collective-permute-done.1.second_ref = bf16[256,256]{1,0:T(8,128)(2,1)S(1)} collective-permute-done((bf16[256,256]{1,0:T(8,128)(2,1)S(1)}, bf16[256,256]{1,0:T(8,128)(2,1)S(1)}, u32[]{:S(2)}, u32[]{:S(2)}) %collective-permute-start.1) | collective-permute-done | bytes 131104 | tf_op jit(solution)/shard_map/ppermute | solution.py:363
  12.7 0.8 %rim_rows.1 = (bf16[512,256]{1,0:T(8,128)(2,1)S(1)}, bf16[512,256]{1,0:T(8,128)(2,1)S(1)}, bf16[136,256]{1,0:T(8,128)(2,1)S(1)}, f32[136,256]{1,0:T(8,128)S(1)}) custom-call(bf16[256,256]{1,0:T(8,128)(2,1)S(1)} %get-tuple-element.32.weight_ref, f32[1,256]{1,0:T(1,128)S(1)} %get-tuple-element.34.bias_ref, f32[512,256]{1,0:T(8,128)S(1)} %get-tuple-element.35.own_ref, ...), custom_call_target="tpu_custom_call" | custom-call | flops 240000000 | bytes 1200000 | tf_op jit(solution)/shard_map/rim_rows/pallas_call | solution.py:476
  13.5 0.1 collective-permute-start.2
  13.6 0.9 %rim_rows_back.1 = (bf16[1536,256]{1,0:T(8,128)(2,1)}, f32[8,256,128]{2,1,0:T(8,128)S(1)}, bf16[256,256]{1,0:T(8,128)(2,1)S(1)}, bf16[256,256]{1,0:T(8,128)(2,1)S(1)}, f32[8,128]{1,0:T(8,128)S(1)}) custom-call(bf16[256,256]{1,0:T(8,128)(2,1)S(1)} %get-tuple-element.32.weight_ref, ...), custom_call_target="tpu_custom_call", output_to_operand_aliasing={{0}: (4, {})} | custom-call | flops 240000000 | bytes 1200000 | tf_op jit(solution)/shard_map/rim_rows_back/pallas_call | solution.py:497
  14.4 0.4 %collective-permute-done.2.refs_1_ = bf16[136,256]{1,0:T(8,128)(2,1)S(1)} collective-permute-done((bf16[136,256]{1,0:T(8,128)(2,1)S(1)}, bf16[136,256]{1,0:T(8,128)(2,1)S(1)}, u32[]{:S(2)}, u32[]{:S(2)}) %collective-permute-start.2) | collective-permute-done | bytes 69664 | tf_op jit(solution)/shard_map/ppermute | solution.py:358
  14.8 0.1 collective-permute-start.5
  14.9 1.3 %collective-permute-start.4 = (bf16[136,256]{1,0:T(8,128)(2,1)S(1)}, bf16[136,256]{1,0:T(8,128)(2,1)S(1)}, u32[]{:S(2)}, u32[]{:S(2)}) collective-permute-start(bf16[136,256]{1,0:T(8,128)(2,1)S(1)} %add_halves.3.refs_0_), channel_id=1, source_target_pairs={{0,9},{1,8},{2,18},{3,19},{4,13},{5,12},{6,22},{7,23},{8,1},{9,0},... | collective-permute-start | bytes 208904 | tf_op jit(solution)/shard_map/ppermute | solution.py:358
  16.2 2.1 %collective-permute-start.3 = (bf16[136,256]{1,0:T(8,128)(2,1)S(1)}, bf16[136,256]{1,0:T(8,128)(2,1)S(1)}, u32[]{:S(2)}, u32[]{:S(2)}) collective-permute-start(bf16[136,256]{1,0:T(8,128)(2,1)S(1)} %add_halves.3.refs_0_), channel_id=1, source_target_pairs={{0,8},{1,9},{2,6},{3,7},{4,12},{5,13},{6,2},{7,3},{8,0},{9,1},{10,... | collective-permute-start | bytes 208904 | tf_op jit(solution)/shard_map/ppermute | solution.py:358
  18.4 0.7 %collective-permute-start.9 = (bf16[256,256]{1,0:T(8,128)(2,1)S(1)}, bf16[256,256]{1,0:T(8,128)(2,1)S(1)}, u32[]{:S(2)}, u32[]{:S(2)}) collective-permute-start(bf16[256,256]{1,0:T(8,128)(2,1)S(1)} %get-tuple-element.53), channel_id=1, source_target_pairs={{1,2},{2,1},{3,4},{4,3},{5,6},{6,5},{7,8},{8,7},{9,10},{10,9},{11,... | collective-permute-start | bytes 393224 | tf_op jit(solution)/shard_map/ppermute | solution.py:363
  19.0 0.2 collective-permute-done.5.refs_3_
  19.2 1.3 %collective-permute-done.4.refs_2_ = bf16[136,256]{1,0:T(8,128)(2,1)S(1)} collective-permute-done((bf16[136,256]{1,0:T(8,128)(2,1)S(1)}, bf16[136,256]{1,0:T(8,128)(2,1)S(1)}, u32[]{:S(2)}, u32[]{:S(2)}) %collective-permute-start.4) | collective-permute-done | bytes 69664 | tf_op jit(solution)/shard_map/ppermute | solution.py:358
  20.4 1.7 %collective-permute-done.3.refs_1_ = bf16[136,256]{1,0:T(8,128)(2,1)S(1)} collective-permute-done((bf16[136,256]{1,0:T(8,128)(2,1)S(1)}, bf16[136,256]{1,0:T(8,128)(2,1)S(1)}, u32[]{:S(2)}, u32[]{:S(2)}) %collective-permute-start.3) | collective-permute-done | bytes 69664 | tf_op jit(solution)/shard_map/ppermute | solution.py:358
  22.2 2.2 %collective-permute-start.8 = (bf16[136,256]{1,0:T(8,128)(2,1)S(1)}, bf16[136,256]{1,0:T(8,128)(2,1)S(1)}, u32[]{:S(2)}, u32[]{:S(2)}) collective-permute-start(bf16[136,256]{1,0:T(8,128)(2,1)S(1)} %add_halves.4.refs_0_), channel_id=1, source_target_pairs={{0,20},{1,21},{2,3},{3,2},{4,16},{5,17},{6,7},{7,6},{8,28},{9,29},... | collective-permute-start | bytes 208904 | tf_op jit(solution)/shard_map/ppermute | solution.py:358
  24.4 0.6 %collective-permute-start.7 = (bf16[136,256]{1,0:T(8,128)(2,1)S(1)}, bf16[136,256]{1,0:T(8,128)(2,1)S(1)}, u32[]{:S(2)}, u32[]{:S(2)}) collective-permute-start(bf16[136,256]{1,0:T(8,128)(2,1)S(1)} %add_halves.4.refs_0_), channel_id=1, source_target_pairs={{0,16},{1,17},{2,11},{3,10},{4,20},{5,21},{6,15},{7,14},{8,24},{9,... | collective-permute-start | bytes 208904 | tf_op jit(solution)/shard_map/ppermute | solution.py:358
  25.0 1.6 %collective-permute-start.6 = (bf16[136,256]{1,0:T(8,128)(2,1)S(1)}, bf16[136,256]{1,0:T(8,128)(2,1)S(1)}, u32[]{:S(2)}, u32[]{:S(2)}) collective-permute-start(bf16[136,256]{1,0:T(8,128)(2,1)S(1)} %add_halves.4.refs_0_), channel_id=1, source_target_pairs={{0,4},{1,5},{2,10},{3,11},{4,0},{5,1},{6,14},{7,15},{8,12},{9,13},... | collective-permute-start | bytes 208904 | tf_op jit(solution)/shard_map/ppermute | solution.py:358
  26.6 0.9 %collective-permute-start.11 = (bf16[256,256]{1,0:T(8,128)(2,1)S(1)}, bf16[256,256]{1,0:T(8,128)(2,1)S(1)}, u32[]{:S(2)}, u32[]{:S(2)}) collective-permute-start(bf16[256,256]{1,0:T(8,128)(2,1)S(1)} %get-tuple-element.55), channel_id=1, source_target_pairs={{0,1},{1,0},{2,3},{3,2},{4,5},{5,4},{6,7},{7,6},{8,9},{9,8},{10,11... | collective-permute-start | bytes 393224 | tf_op jit(solution)/shard_map/ppermute | solution.py:358
  27.5 2.2 %inner_rows_back.1 = (bf16[1536,256]{1,0:T(8,128)(2,1)}, f32[512,256]{1,0:T(8,128)S(1)}, f32[8,128]{1,0:T(8,128)S(1)}) custom-call(s32[36]{0:T(128)S(1)} %get-tuple-element.48.place_in, bf16[256,256]{1,0:T(8,128)(2,1)S(1)} %get-tuple-element.32.weight_ref, bf16[8,3,128,128]{3,2,1,0:T(8,128)(2,1)S(1)} %get-tuple-element.49.adj_ref, ...), custom_call_target="tpu_custom_call" | custom-call | flops 360000000 | bytes 1800000 | tf_op jit(solution)/shard_map/inner_rows_back/pallas_call | solution.py:519
  29.8 0.0 collective-permute-done.9.refs_5_.second_ref
  29.8 0.0 collective-permute-done.8.refs_3_
  29.8 0.4 %collective-permute-done.7.refs_2_ = bf16[136,256]{1,0:T(8,128)(2,1)S(1)} collective-permute-done((bf16[136,256]{1,0:T(8,128)(2,1)S(1)}, bf16[136,256]{1,0:T(8,128)(2,1)S(1)}, u32[]{:S(2)}, u32[]{:S(2)}) %collective-permute-start.7) | collective-permute-done | bytes 69664 | tf_op jit(solution)/shard_map/ppermute | solution.py:358
  30.1 0.0 collective-permute-done.6.refs_1_
  30.2 0.1 collective-permute-start.10
  30.3 1.3 %collective-permute-done.11.first_ref = bf16[256,256]{1,0:T(8,128)(2,1)S(1)} collective-permute-done((bf16[256,256]{1,0:T(8,128)(2,1)S(1)}, bf16[256,256]{1,0:T(8,128)(2,1)S(1)}, u32[]{:S(2)}, u32[]{:S(2)}) %collective-permute-start.11) | collective-permute-done | bytes 131104 | tf_op jit(solution)/shard_map/ppermute | solution.py:358
  31.6 0.0 collective-permute-done.10.other_ref
  31.6 0.9 %last_step.1 = (f32[256,256]{1,0:T(8,128)}, f32[1,256]{1,0:T(1,128)}, bf16[1536,256]{1,0:T(8,128)(2,1)}) custom-call(bf16[136,256]{1,0:T(8,128)(2,1)S(1)} %add_halves.5.own_ref, bf16[136,256]{1,0:T(8,128)(2,1)S(1)} %collective-permute-done.10.other_ref, f32[512,256]{1,0:T(8,128)S(1)} %get-tuple-element.54.edge_ref, ...), custom_call_target="tpu_custom_call", output_to_operand_aliasing={{2}: (5, {})} | custom-call | tf_op jit(solution)/shard_map/last_step/pallas_call | solution.py:538
  (3 shorter events, 0.1 us)
Async XLA Ops:
  1.6 10.2 %collective-permute-start = (bf16[256,256]{1,0:T(8,128)(2,1)S(1)}, bf16[256,256]{1,0:T(8,128)(2,1)S(1)}, u32[]{:S(2)}, u32[]{:S(2)}) collective-permute-start(bf16[256,256]{1,0:T(8,128)(2,1)S(1)} %get-tuple-element.36), channel_id=1, source_target_pairs={{0,1},{1,0},{2,3},{3,2},{4,5},{5,4},{6,7},{7,6},{8,9},{9,8},{10,11... | collective-permute-start | bytes 393224 | tf_op jit(solution)/shard_map/ppermute | solution.py:358
  4.7 8.0 %collective-permute-start.1 = (bf16[256,256]{1,0:T(8,128)(2,1)S(1)}, bf16[256,256]{1,0:T(8,128)(2,1)S(1)}, u32[]{:S(2)}, u32[]{:S(2)}) collective-permute-start(bf16[256,256]{1,0:T(8,128)(2,1)S(1)} %get-tuple-element.37), channel_id=1, source_target_pairs={{0,31},{1,2},{2,1},{3,4},{4,3},{5,6},{6,5},{7,8},{8,7},{9,10},{10,... | collective-permute-start | bytes 393224 | tf_op jit(solution)/shard_map/ppermute | solution.py:363
  13.5 1.3 %collective-permute-start.2 = (bf16[136,256]{1,0:T(8,128)(2,1)S(1)}, bf16[136,256]{1,0:T(8,128)(2,1)S(1)}, u32[]{:S(2)}, u32[]{:S(2)}) collective-permute-start(bf16[136,256]{1,0:T(8,128)(2,1)S(1)} %get-tuple-element.46), channel_id=1, source_target_pairs={{0,2},{1,3},{2,0},{3,1},{4,6},{5,7},{6,4},{7,5},{8,10},{9,11},{10,... | collective-permute-start | bytes 208904 | tf_op jit(solution)/shard_map/ppermute | solution.py:358
  14.8 4.4 %collective-permute-start.5 = (bf16[136,256]{1,0:T(8,128)(2,1)S(1)}, bf16[136,256]{1,0:T(8,128)(2,1)S(1)}, u32[]{:S(2)}, u32[]{:S(2)}) collective-permute-start(bf16[136,256]{1,0:T(8,128)(2,1)S(1)} %add_halves.3.refs_0_), channel_id=1, source_target_pairs={{0,1},{1,0},{2,22},{3,23},{4,5},{5,4},{6,18},{7,19},{8,9},{9,8},{1... | collective-permute-start | bytes 208904 | tf_op jit(solution)/shard_map/ppermute | solution.py:358
  14.9 5.5 %collective-permute-start.4 = (bf16[136,256]{1,0:T(8,128)(2,1)S(1)}, bf16[136,256]{1,0:T(8,128)(2,1)S(1)}, u32[]{:S(2)}, u32[]{:S(2)}) collective-permute-start(bf16[136,256]{1,0:T(8,128)(2,1)S(1)} %add_halves.3.refs_0_), channel_id=1, source_target_pairs={{0,9},{1,8},{2,18},{3,19},{4,13},{5,12},{6,22},{7,23},{8,1},{9,0},... | collective-permute-start | bytes 208904 | tf_op jit(solution)/shard_map/ppermute | solution.py:358
  16.2 5.9 %collective-permute-start.3 = (bf16[136,256]{1,0:T(8,128)(2,1)S(1)}, bf16[136,256]{1,0:T(8,128)(2,1)S(1)}, u32[]{:S(2)}, u32[]{:S(2)}) collective-permute-start(bf16[136,256]{1,0:T(8,128)(2,1)S(1)} %add_halves.3.refs_0_), channel_id=1, source_target_pairs={{0,8},{1,9},{2,6},{3,7},{4,12},{5,13},{6,2},{7,3},{8,0},{9,1},{10,... | collective-permute-start | bytes 208904 | tf_op jit(solution)/shard_map/ppermute | solution.py:358
  18.4 11.4 %collective-permute-start.9 = (bf16[256,256]{1,0:T(8,128)(2,1)S(1)}, bf16[256,256]{1,0:T(8,128)(2,1)S(1)}, u32[]{:S(2)}, u32[]{:S(2)}) collective-permute-start(bf16[256,256]{1,0:T(8,128)(2,1)S(1)} %get-tuple-element.53), channel_id=1, source_target_pairs={{1,2},{2,1},{3,4},{4,3},{5,6},{6,5},{7,8},{8,7},{9,10},{10,9},{11,... | collective-permute-start | bytes 393224 | tf_op jit(solution)/shard_map/ppermute | solution.py:363
  22.2 7.6 %collective-permute-start.8 = (bf16[136,256]{1,0:T(8,128)(2,1)S(1)}, bf16[136,256]{1,0:T(8,128)(2,1)S(1)}, u32[]{:S(2)}, u32[]{:S(2)}) collective-permute-start(bf16[136,256]{1,0:T(8,128)(2,1)S(1)} %add_halves.4.refs_0_), channel_id=1, source_target_pairs={{0,20},{1,21},{2,3},{3,2},{4,16},{5,17},{6,7},{7,6},{8,28},{9,29},... | collective-permute-start | bytes 208904 | tf_op jit(solution)/shard_map/ppermute | solution.py:358
  24.4 5.7 %collective-permute-start.7 = (bf16[136,256]{1,0:T(8,128)(2,1)S(1)}, bf16[136,256]{1,0:T(8,128)(2,1)S(1)}, u32[]{:S(2)}, u32[]{:S(2)}) collective-permute-start(bf16[136,256]{1,0:T(8,128)(2,1)S(1)} %add_halves.4.refs_0_), channel_id=1, source_target_pairs={{0,16},{1,17},{2,11},{3,10},{4,20},{5,21},{6,15},{7,14},{8,24},{9,... | collective-permute-start | bytes 208904 | tf_op jit(solution)/shard_map/ppermute | solution.py:358
  25.0 5.1 %collective-permute-start.6 = (bf16[136,256]{1,0:T(8,128)(2,1)S(1)}, bf16[136,256]{1,0:T(8,128)(2,1)S(1)}, u32[]{:S(2)}, u32[]{:S(2)}) collective-permute-start(bf16[136,256]{1,0:T(8,128)(2,1)S(1)} %add_halves.4.refs_0_), channel_id=1, source_target_pairs={{0,4},{1,5},{2,10},{3,11},{4,0},{5,1},{6,14},{7,15},{8,12},{9,13},... | collective-permute-start | bytes 208904 | tf_op jit(solution)/shard_map/ppermute | solution.py:358
  26.6 5.0 %collective-permute-start.11 = (bf16[256,256]{1,0:T(8,128)(2,1)S(1)}, bf16[256,256]{1,0:T(8,128)(2,1)S(1)}, u32[]{:S(2)}, u32[]{:S(2)}) collective-permute-start(bf16[256,256]{1,0:T(8,128)(2,1)S(1)} %get-tuple-element.55), channel_id=1, source_target_pairs={{0,1},{1,0},{2,3},{3,2},{4,5},{5,4},{6,7},{7,6},{8,9},{9,8},{10,11... | collective-permute-start | bytes 393224 | tf_op jit(solution)/shard_map/ppermute | solution.py:358
  30.2 1.4 %collective-permute-start.10 = (bf16[136,256]{1,0:T(8,128)(2,1)S(1)}, bf16[136,256]{1,0:T(8,128)(2,1)S(1)}, u32[]{:S(2)}, u32[]{:S(2)}) collective-permute-start(bf16[136,256]{1,0:T(8,128)(2,1)S(1)} %add_halves.5.own_ref), channel_id=1, source_target_pairs={{0,2},{1,3},{2,0},{3,1},{4,6},{5,7},{6,4},{7,5},{8,10},{9,11},{10,... | collective-permute-start | bytes 208904 | tf_op jit(solution)/shard_map/ppermute | solution.py:358

commit v26 on v18

--- a/solution.py
+++ b/solution.py
@@ -63,12 +63,16 @@
     rim = first_ref.shape[0]
     odd = place_in_mesh() & 1
     last = rows - rim
+    piece = rim // 4
     starts = ((1 - odd) * last, odd * last)
     copies = [
         pltpu.make_async_copy(
-            feat_hbm.at[pl.ds(pl.multiple_of(start, rim), rim)], out_ref, sems.at[i]
+            feat_hbm.at[pl.ds(pl.multiple_of(start + part * piece, piece), piece)],
+            out_ref.at[pl.ds(part * piece, piece)],
+            sems.at[4 * i + part],
         )
         for i, (start, out_ref) in enumerate(zip(starts, (first_ref, second_ref)))
+        for part in range(4)
     ]
     for copy in copies:
         copy.start()
@@ -428,7 +432,7 @@
         out_shape=(shape(rim, width), shape(rim, width)),
         in_specs=[hbm],
         out_specs=(vmem, vmem),
-        scratch_shapes=[pltpu.SemaphoreType.DMA((2,))],
+        scratch_shapes=[pltpu.SemaphoreType.DMA((8,))],
         compiler_params=params(2),
         cost_estimate=cost(0.05),
         name="halo_rows",

time: 32 us -> 32.1 us (level)
  no operation moved by 1% of the time
where the time goes in v26:
time: 32.1 us; the launch traced here: 31.8 us
  starting transfers between devices  16.3 us (51%)
  Pallas kernels  9.39 us (29%)
  waiting for transfers between devices  5.43 us (17%)
  between operations  0.73 us (2%)
    ppermute x10, starting transfers between devices, swap(): return lax.ppermute(value, AXES, pairs)  12 us
    ppermute x10, waiting for transfers between devices, swap(): return lax.ppermute(value, AXES, pairs)  4.63 us
    ppermute x2, starting transfers between devices, with_next(): return lax.ppermute(value, AXES, pairs if closed else pairs[1:-1])  4.29 us
    pallas_call x1, Pallas kernels, on_device(): pl.pallas_call(inner_kernel, out_shape=(shape(rows, width), shape(blocks...  3.54 us
    pallas_call x1, Pallas kernels, on_device(): pl.pallas_call(inner_back_kernel, out_shape=(shape(rows, width), shape(2...  2.22 us
    pallas_call x1, Pallas kernels, on_device(): pl.pallas_call(halo_kernel, out_shape=(shape(rim, width), shape(rim, widt...  0.96 us
    pallas_call x1, Pallas kernels, on_device(): pl.pallas_call(rim_back_kernel, out_shape=(shape(rows, width), shape(4 *...  0.88 us
    pallas_call x1, Pallas kernels, on_device(): pl.pallas_call(functools.partial(last_kernel, norm_scale), out_shape=(sha...  0.85 us
  transfers between devices with their start and end apart: 12, of which 8 were waited for; matrix products, arithmetic and copies ran while one was open for 0% of the time, Pallas kernels for 21%

profile of v26, /device:TPU:0, one launch (start us, length us, event | category | flops | bytes accessed | tf_op | source)
XLA Modules:
  0.0 31.8 jit_solution(9940276928458863104)
XLA Ops:
  0.6 1.0 %halo_rows.1 = (bf16[256,256]{1,0:T(8,128)(2,1)S(1)}, bf16[256,256]{1,0:T(8,128)(2,1)S(1)}) custom-call(bf16[1536,256]{1,0:T(8,128)(2,1)} %feat_hbm.3), custom_call_target="tpu_custom_call" | custom-call | flops 60000000 | bytes 300000 | tf_op jit(solution)/shard_map/halo_rows/pallas_call | solution.py:430
  1.6 3.0 %collective-permute-start = (bf16[256,256]{1,0:T(8,128)(2,1)S(1)}, bf16[256,256]{1,0:T(8,128)(2,1)S(1)}, u32[]{:S(2)}, u32[]{:S(2)}) collective-permute-start(bf16[256,256]{1,0:T(8,128)(2,1)S(1)} %get-tuple-element.36), channel_id=1, source_target_pairs={{0,1},{1,0},{2,3},{3,2},{4,5},{5,4},{6,7},{7,6},{8,9},{9,8},{10,11... | collective-permute-start | bytes 393224 | tf_op jit(solution)/shard_map/ppermute | solution.py:364
  4.6 3.6 %collective-permute-start.1 = (bf16[256,256]{1,0:T(8,128)(2,1)S(1)}, bf16[256,256]{1,0:T(8,128)(2,1)S(1)}, u32[]{:S(2)}, u32[]{:S(2)}) collective-permute-start(bf16[256,256]{1,0:T(8,128)(2,1)S(1)} %get-tuple-element.37), channel_id=1, source_target_pairs={{0,31},{1,2},{2,1},{3,4},{4,3},{5,6},{6,5},{7,8},{8,7},{9,10},{10,... | collective-permute-start | bytes 393224 | tf_op jit(solution)/shard_map/ppermute | solution.py:369
  8.3 3.5 %inner_rows.1 = (bf16[1536,256]{1,0:T(8,128)(2,1)}, s32[36]{0:T(128)S(1)}, bf16[1024,256]{1,0:T(8,128)(2,1)S(1)}, f32[256,256]{1,0:T(8,128)S(1)}, f32[8,256]{1,0...) custom-call(s32[3,12]{1,0:T(4,128)} %bitcast.3, ...), custom_call_target="tpu_custom_call" | custom-call | flops 600000000 | bytes 3000000 | tf_op jit(solution)/shard_map/inner_rows/pallas_call | solution.py:445
  11.8 0.0 collective-permute-done.first_ref
  11.8 0.8 %collective-permute-done.1.second_ref = bf16[256,256]{1,0:T(8,128)(2,1)S(1)} collective-permute-done((bf16[256,256]{1,0:T(8,128)(2,1)S(1)}, bf16[256,256]{1,0:T(8,128)(2,1)S(1)}, u32[]{:S(2)}, u32[]{:S(2)}) %collective-permute-start.1) | collective-permute-done | bytes 131104 | tf_op jit(solution)/shard_map/ppermute | solution.py:369
  12.6 0.8 %rim_rows.1 = (bf16[512,256]{1,0:T(8,128)(2,1)S(1)}, bf16[512,256]{1,0:T(8,128)(2,1)S(1)}, bf16[136,256]{1,0:T(8,128)(2,1)S(1)}, f32[136,256]{1,0:T(8,128)S(1)}) custom-call(bf16[256,256]{1,0:T(8,128)(2,1)S(1)} %get-tuple-element.32.weight_ref, f32[1,256]{1,0:T(1,128)S(1)} %get-tuple-element.34.bias_ref, f32[512,256]{1,0:T(8,128)S(1)} %get-tuple-element.35.own_ref, ...), custom_call_target="tpu_custom_call" | custom-call | flops 240000000 | bytes 1200000 | tf_op jit(solution)/shard_map/rim_rows/pallas_call | solution.py:481
  13.5 0.1 collective-permute-start.2
  13.5 0.9 %rim_rows_back.1 = (bf16[1536,256]{1,0:T(8,128)(2,1)}, f32[8,256,128]{2,1,0:T(8,128)S(1)}, bf16[256,256]{1,0:T(8,128)(2,1)S(1)}, bf16[256,256]{1,0:T(8,128)(2,1)S(1)}, f32[8,128]{1,0:T(8,128)S(1)}) custom-call(bf16[256,256]{1,0:T(8,128)(2,1)S(1)} %get-tuple-element.32.weight_ref, ...), custom_call_target="tpu_custom_call", output_to_operand_aliasing={{0}: (4, {})} | custom-call | flops 240000000 | bytes 1200000 | tf_op jit(solution)/shard_map/rim_rows_back/pallas_call | solution.py:503
  14.4 0.4 %collective-permute-done.2.refs_1_ = bf16[136,256]{1,0:T(8,128)(2,1)S(1)} collective-permute-done((bf16[136,256]{1,0:T(8,128)(2,1)S(1)}, bf16[136,256]{1,0:T(8,128)(2,1)S(1)}, u32[]{:S(2)}, u32[]{:S(2)}) %collective-permute-start.2) | collective-permute-done | bytes 69664 | tf_op jit(solution)/shard_map/ppermute | solution.py:364
  14.8 0.1 collective-permute-start.5
  14.9 1.0 %collective-permute-start.4 = (bf16[136,256]{1,0:T(8,128)(2,1)S(1)}, bf16[136,256]{1,0:T(8,128)(2,1)S(1)}, u32[]{:S(2)}, u32[]{:S(2)}) collective-permute-start(bf16[136,256]{1,0:T(8,128)(2,1)S(1)} %add_halves.3.refs_0_), channel_id=1, source_target_pairs={{0,5},{1,4},{2,18},{3,19},{4,1},{5,0},{6,22},{7,23},{8,13},{9,12},... | collective-permute-start | bytes 208904 | tf_op jit(solution)/shard_map/ppermute | solution.py:364
  15.9 2.4 %collective-permute-start.3 = (bf16[136,256]{1,0:T(8,128)(2,1)S(1)}, bf16[136,256]{1,0:T(8,128)(2,1)S(1)}, u32[]{:S(2)}, u32[]{:S(2)}) collective-permute-start(bf16[136,256]{1,0:T(8,128)(2,1)S(1)} %add_halves.3.refs_0_), channel_id=1, source_target_pairs={{0,4},{1,5},{2,10},{3,11},{4,0},{5,1},{6,14},{7,15},{8,12},{9,13},... | collective-permute-start | bytes 208904 | tf_op jit(solution)/shard_map/ppermute | solution.py:364
  18.4 0.7 %collective-permute-start.9 = (bf16[256,256]{1,0:T(8,128)(2,1)S(1)}, bf16[256,256]{1,0:T(8,128)(2,1)S(1)}, u32[]{:S(2)}, u32[]{:S(2)}) collective-permute-start(bf16[256,256]{1,0:T(8,128)(2,1)S(1)} %get-tuple-element.53), channel_id=1, source_target_pairs={{1,2},{2,1},{3,4},{4,3},{5,6},{6,5},{7,8},{8,7},{9,10},{10,9},{11,... | collective-permute-start | bytes 393224 | tf_op jit(solution)/shard_map/ppermute | solution.py:369
  19.0 0.2 collective-permute-done.5.refs_3_
  19.2 1.0 %collective-permute-done.4.refs_2_ = bf16[136,256]{1,0:T(8,128)(2,1)S(1)} collective-permute-done((bf16[136,256]{1,0:T(8,128)(2,1)S(1)}, bf16[136,256]{1,0:T(8,128)(2,1)S(1)}, u32[]{:S(2)}, u32[]{:S(2)}) %collective-permute-start.4) | collective-permute-done | bytes 69664 | tf_op jit(solution)/shard_map/ppermute | solution.py:364
  20.2 1.2 %collective-permute-done.3.refs_1_ = bf16[136,256]{1,0:T(8,128)(2,1)S(1)} collective-permute-done((bf16[136,256]{1,0:T(8,128)(2,1)S(1)}, bf16[136,256]{1,0:T(8,128)(2,1)S(1)}, u32[]{:S(2)}, u32[]{:S(2)}) %collective-permute-start.3) | collective-permute-done | bytes 69664 | tf_op jit(solution)/shard_map/ppermute | solution.py:364
  21.4 3.0 %collective-permute-start.8 = (bf16[136,256]{1,0:T(8,128)(2,1)S(1)}, bf16[136,256]{1,0:T(8,128)(2,1)S(1)}, u32[]{:S(2)}, u32[]{:S(2)}) collective-permute-start(bf16[136,256]{1,0:T(8,128)(2,1)S(1)} %add_halves.4.refs_0_), channel_id=1, source_target_pairs={{0,24},{1,25},{2,3},{3,2},{4,28},{5,29},{6,7},{7,6},{8,16},{9,17},... | collective-permute-start | bytes 208904 | tf_op jit(solution)/shard_map/ppermute | solution.py:364
  24.4 0.0 collective-permute-start.7
  24.4 1.5 %collective-permute-start.6 = (bf16[136,256]{1,0:T(8,128)(2,1)S(1)}, bf16[136,256]{1,0:T(8,128)(2,1)S(1)}, u32[]{:S(2)}, u32[]{:S(2)}) collective-permute-start(bf16[136,256]{1,0:T(8,128)(2,1)S(1)} %add_halves.4.refs_0_), channel_id=1, source_target_pairs={{0,8},{1,9},{2,6},{3,7},{4,12},{5,13},{6,2},{7,3},{8,0},{9,1},{10,... | collective-permute-start | bytes 208904 | tf_op jit(solution)/shard_map/ppermute | solution.py:364
  25.9 0.8 %collective-permute-start.11 = (bf16[256,256]{1,0:T(8,128)(2,1)S(1)}, bf16[256,256]{1,0:T(8,128)(2,1)S(1)}, u32[]{:S(2)}, u32[]{:S(2)}) collective-permute-start(bf16[256,256]{1,0:T(8,128)(2,1)S(1)} %get-tuple-element.55), channel_id=1, source_target_pairs={{0,1},{1,0},{2,3},{3,2},{4,5},{5,4},{6,7},{7,6},{8,9},{9,8},{10,11... | collective-permute-start | bytes 393224 | tf_op jit(solution)/shard_map/ppermute | solution.py:364
  26.7 2.2 %inner_rows_back.1 = (bf16[1536,256]{1,0:T(8,128)(2,1)}, f32[512,256]{1,0:T(8,128)S(1)}, f32[8,128]{1,0:T(8,128)S(1)}) custom-call(s32[36]{0:T(128)S(1)} %get-tuple-element.48.place_in, bf16[256,256]{1,0:T(8,128)(2,1)S(1)} %get-tuple-element.32.weight_ref, bf16[8,3,128,128]{3,2,1,0:T(8,128)(2,1)S(1)} %get-tuple-element.49.adj_ref, ...), custom_call_target="tpu_custom_call" | custom-call | flops 360000000 | bytes 1800000 | tf_op jit(solution)/shard_map/inner_rows_back/pallas_call | solution.py:525
  28.9 0.0 collective-permute-done.9.refs_5_.second_ref
  28.9 0.0 collective-permute-done.8.refs_3_
  28.9 0.7 %collective-permute-done.7.refs_2_ = bf16[136,256]{1,0:T(8,128)(2,1)S(1)} collective-permute-done((bf16[136,256]{1,0:T(8,128)(2,1)S(1)}, bf16[136,256]{1,0:T(8,128)(2,1)S(1)}, u32[]{:S(2)}, u32[]{:S(2)}) %collective-permute-start.7) | collective-permute-done | bytes 69664 | tf_op jit(solution)/shard_map/ppermute | solution.py:364
  29.6 0.0 collective-permute-done.6.refs_1_
  29.6 0.1 collective-permute-start.10
  29.7 1.1 %collective-permute-done.11.first_ref = bf16[256,256]{1,0:T(8,128)(2,1)S(1)} collective-permute-done((bf16[256,256]{1,0:T(8,128)(2,1)S(1)}, bf16[256,256]{1,0:T(8,128)(2,1)S(1)}, u32[]{:S(2)}, u32[]{:S(2)}) %collective-permute-start.11) | collective-permute-done | bytes 131104 | tf_op jit(solution)/shard_map/ppermute | solution.py:364
  30.9 0.1 collective-permute-done.10.other_ref
  31.0 0.9 %last_step.1 = (f32[256,256]{1,0:T(8,128)}, f32[1,256]{1,0:T(1,128)}, bf16[1536,256]{1,0:T(8,128)(2,1)}) custom-call(bf16[136,256]{1,0:T(8,128)(2,1)S(1)} %add_halves.5.own_ref, bf16[136,256]{1,0:T(8,128)(2,1)S(1)} %collective-permute-done.10.other_ref, f32[512,256]{1,0:T(8,128)S(1)} %get-tuple-element.54.edge_ref, ...), custom_call_target="tpu_custom_call", output_to_operand_aliasing={{2}: (5, {})} | custom-call | tf_op jit(solution)/shard_map/last_step/pallas_call | solution.py:544
  (3 shorter events, 0.1 us)
Async XLA Ops:
  1.6 10.2 %collective-permute-start = (bf16[256,256]{1,0:T(8,128)(2,1)S(1)}, bf16[256,256]{1,0:T(8,128)(2,1)S(1)}, u32[]{:S(2)}, u32[]{:S(2)}) collective-permute-start(bf16[256,256]{1,0:T(8,128)(2,1)S(1)} %get-tuple-element.36), channel_id=1, source_target_pairs={{0,1},{1,0},{2,3},{3,2},{4,5},{5,4},{6,7},{7,6},{8,9},{9,8},{10,11... | collective-permute-start | bytes 393224 | tf_op jit(solution)/shard_map/ppermute | solution.py:364
  4.6 8.0 %collective-permute-start.1 = (bf16[256,256]{1,0:T(8,128)(2,1)S(1)}, bf16[256,256]{1,0:T(8,128)(2,1)S(1)}, u32[]{:S(2)}, u32[]{:S(2)}) collective-permute-start(bf16[256,256]{1,0:T(8,128)(2,1)S(1)} %get-tuple-element.37), channel_id=1, source_target_pairs={{0,31},{1,2},{2,1},{3,4},{4,3},{5,6},{6,5},{7,8},{8,7},{9,10},{10,... | collective-permute-start | bytes 393224 | tf_op jit(solution)/shard_map/ppermute | solution.py:369
  13.5 1.3 %collective-permute-start.2 = (bf16[136,256]{1,0:T(8,128)(2,1)S(1)}, bf16[136,256]{1,0:T(8,128)(2,1)S(1)}, u32[]{:S(2)}, u32[]{:S(2)}) collective-permute-start(bf16[136,256]{1,0:T(8,128)(2,1)S(1)} %get-tuple-element.46), channel_id=1, source_target_pairs={{0,2},{1,3},{2,0},{3,1},{4,6},{5,7},{6,4},{7,5},{8,10},{9,11},{10,... | collective-permute-start | bytes 208904 | tf_op jit(solution)/shard_map/ppermute | solution.py:364
  14.8 4.4 %collective-permute-start.5 = (bf16[136,256]{1,0:T(8,128)(2,1)S(1)}, bf16[136,256]{1,0:T(8,128)(2,1)S(1)}, u32[]{:S(2)}, u32[]{:S(2)}) collective-permute-start(bf16[136,256]{1,0:T(8,128)(2,1)S(1)} %add_halves.3.refs_0_), channel_id=1, source_target_pairs={{0,1},{1,0},{2,26},{3,27},{4,5},{5,4},{6,30},{7,31},{8,9},{9,8},{1... | collective-permute-start | bytes 208904 | tf_op jit(solution)/shard_map/ppermute | solution.py:364
  14.9 5.2 %collective-permute-start.4 = (bf16[136,256]{1,0:T(8,128)(2,1)S(1)}, bf16[136,256]{1,0:T(8,128)(2,1)S(1)}, u32[]{:S(2)}, u32[]{:S(2)}) collective-permute-start(bf16[136,256]{1,0:T(8,128)(2,1)S(1)} %add_halves.3.refs_0_), channel_id=1, source_target_pairs={{0,5},{1,4},{2,18},{3,19},{4,1},{5,0},{6,22},{7,23},{8,13},{9,12},... | collective-permute-start | bytes 208904 | tf_op jit(solution)/shard_map/ppermute | solution.py:364
  15.9 5.5 %collective-permute-start.3 = (bf16[136,256]{1,0:T(8,128)(2,1)S(1)}, bf16[136,256]{1,0:T(8,128)(2,1)S(1)}, u32[]{:S(2)}, u32[]{:S(2)}) collective-permute-start(bf16[136,256]{1,0:T(8,128)(2,1)S(1)} %add_halves.3.refs_0_), channel_id=1, source_target_pairs={{0,4},{1,5},{2,10},{3,11},{4,0},{5,1},{6,14},{7,15},{8,12},{9,13},... | collective-permute-start | bytes 208904 | tf_op jit(solution)/shard_map/ppermute | solution.py:364
  18.4 10.6 %collective-permute-start.9 = (bf16[256,256]{1,0:T(8,128)(2,1)S(1)}, bf16[256,256]{1,0:T(8,128)(2,1)S(1)}, u32[]{:S(2)}, u32[]{:S(2)}) collective-permute-start(bf16[256,256]{1,0:T(8,128)(2,1)S(1)} %get-tuple-element.53), channel_id=1, source_target_pairs={{1,2},{2,1},{3,4},{4,3},{5,6},{6,5},{7,8},{8,7},{9,10},{10,9},{11,... | collective-permute-start | bytes 393224 | tf_op jit(solution)/shard_map/ppermute | solution.py:369
  21.4 7.5 %collective-permute-start.8 = (bf16[136,256]{1,0:T(8,128)(2,1)S(1)}, bf16[136,256]{1,0:T(8,128)(2,1)S(1)}, u32[]{:S(2)}, u32[]{:S(2)}) collective-permute-start(bf16[136,256]{1,0:T(8,128)(2,1)S(1)} %add_halves.4.refs_0_), channel_id=1, source_target_pairs={{0,24},{1,25},{2,3},{3,2},{4,28},{5,29},{6,7},{7,6},{8,16},{9,17},... | collective-permute-start | bytes 208904 | tf_op jit(solution)/shard_map/ppermute | solution.py:364
  24.4 5.2 %collective-permute-start.7 = (bf16[136,256]{1,0:T(8,128)(2,1)S(1)}, bf16[136,256]{1,0:T(8,128)(2,1)S(1)}, u32[]{:S(2)}, u32[]{:S(2)}) collective-permute-start(bf16[136,256]{1,0:T(8,128)(2,1)S(1)} %add_halves.4.refs_0_), channel_id=1, source_target_pairs={{0,16},{1,17},{2,7},{3,6},{4,20},{5,21},{6,3},{7,2},{8,24},{9,25},... | collective-permute-start | bytes 208904 | tf_op jit(solution)/shard_map/ppermute | solution.py:364
  24.4 5.2 %collective-permute-start.6 = (bf16[136,256]{1,0:T(8,128)(2,1)S(1)}, bf16[136,256]{1,0:T(8,128)(2,1)S(1)}, u32[]{:S(2)}, u32[]{:S(2)}) collective-permute-start(bf16[136,256]{1,0:T(8,128)(2,1)S(1)} %add_halves.4.refs_0_), channel_id=1, source_target_pairs={{0,8},{1,9},{2,6},{3,7},{4,12},{5,13},{6,2},{7,3},{8,0},{9,1},{10,... | collective-permute-start | bytes 208904 | tf_op jit(solution)/shard_map/ppermute | solution.py:364
  25.9 5.0 %collective-permute-start.11 = (bf16[256,256]{1,0:T(8,128)(2,1)S(1)}, bf16[256,256]{1,0:T(8,128)(2,1)S(1)}, u32[]{:S(2)}, u32[]{:S(2)}) collective-permute-start(bf16[256,256]{1,0:T(8,128)(2,1)S(1)} %get-tuple-element.55), channel_id=1, source_target_pairs={{0,1},{1,0},{2,3},{3,2},{4,5},{5,4},{6,7},{7,6},{8,9},{9,8},{10,11... | collective-permute-start | bytes 393224 | tf_op jit(solution)/shard_map/ppermute | solution.py:364
  29.6 1.3 %collective-permute-start.10 = (bf16[136,256]{1,0:T(8,128)(2,1)S(1)}, bf16[136,256]{1,0:T(8,128)(2,1)S(1)}, u32[]{:S(2)}, u32[]{:S(2)}) collective-permute-start(bf16[136,256]{1,0:T(8,128)(2,1)S(1)} %add_halves.5.own_ref), channel_id=1, source_target_pairs={{0,2},{1,3},{2,0},{3,1},{4,6},{5,7},{6,4},{7,5},{8,10},{9,11},{10,... | collective-permute-start | bytes 208904 | tf_op jit(solution)/shard_map/ppermute | solution.py:364
